TPU v7x, 32 devices: a whole 2x2x4 slice. The times are simulated.
32 devices in a mesh: real: 2 (over y), comp: 4 (over z), space: 4 (over x, core).
Axes of the slice: x: 2, y: 2, z: 4, core: 2. Of those that a mesh axis runs over, the one named last changes fastest.
Arguments:
- concentration: float32 [256, 32, 2048], P(('real', 'comp'), None, 'space'), parts along dimension 0, may hold values from -12 to 12
- face_rate: float32 [2, 64, 2048], P(None, 'real', 'space'), parts along dimension 1, may hold values from 0.02 to 0.15
- face_flag: int32 [2, 64, 2048], P(None, 'real', 'space'), parts along dimension 1, may hold values from 0 to 1
- retardation: float32 [16], replicated, may hold values from 1 to 3
- dispersion: float32 [16], replicated, may hold values from 0.01 to 0.08
- mixing: float32 [16, 16], replicated, may hold values from -0.08 to 2.5
- mixing_inverse: float32 [16, 16], replicated, may hold values from -0.05 to 0.5
- affinity: float32 [16], replicated, may hold values from 0.5 to 3
- mineral: float32 [16], replicated, may hold values from 0.3 to 1.5
- stiff_mask: int32 [8, 64, 2048], P(None, ('real', 'comp'), 'space'), parts along dimension 1, may hold values from 0 to 1, as said below
Outputs:
- concentration_out: float32 [256, 32, 2048], P(('real', 'comp'), None, 'space'), parts along dimension 0
There are 2 independent parts, one for each index of `real`. A program takes and returns all parts, laid end to end along the dimension named above; an argument that names none is the same for every part. Nothing has to cross between parts.
Inputs may be any that keep to these rules, and one draw needn't show every extreme that they name: `stiff_mask`: in every block of cells made of all 8 layers, x rows k * 8 to (k + 1) * 8 - 1 and y columns l * 512 to (l + 1) * 512 - 1, at most 8192 cells are stiff, and some block has exactly 8192.
All inputs are finite; a program needn't handle non-finite values.
Results may differ from a plain program's by a relative error of at most 0.00011.
Values sent between devices are 32-bit elements; how exact they have to be, the bound alone decides.
No kernel may reach another device: no remote copies, remote signals or barrier semaphores. Data moves between devices by JAX's collectives and lax.ppermute only.
A program may use at most 64 MiB of HBM per device.

v0:
```python
import functools

import jax
import jax.numpy as jnp
from jax import lax
from jax.experimental import pallas as pl
from jax.experimental.pallas import tpu as pltpu
from jax.sharding import PartitionSpec as P

NC = 16
NZ = 8
STEPS = 2
NEWT = 4
STIFF = 4


highest = lax.Precision.HIGHEST


def shifted(shard, axis, by):
    devices = lax.axis_size(axis)
    pairs = [(i, i + by) for i in range(devices) if 0 <= i + by < devices]
    return lax.ppermute(shard, axis, pairs)


def extended(block, sides, width):
    for axis, dim in sides:
        count = lax.axis_size(axis)
        forward = [(i, i + 1) for i in range(count - 1)]
        backward = [(target, source) for source, target in forward]
        low = lax.ppermute(
            lax.slice_in_dim(block, block.shape[dim] - width, None, axis=dim), axis, forward
        )
        high = lax.ppermute(lax.slice_in_dim(block, 0, width, axis=dim), axis, backward)
        block = jnp.concatenate([low, block, high], axis=dim)
    return block


def shift_down(values, axis_index):
    size_along = values.shape[axis_index]
    zero_row = jnp.zeros_like(lax.slice_in_dim(values, 0, 1, axis=axis_index))
    kept = lax.slice_in_dim(values, 0, size_along - 1, axis=axis_index)
    return jnp.concatenate([zero_row, kept], axis=axis_index)


def face_weights(face_rate, face_flag):
    flag_values = face_flag.astype(jnp.float32)
    weight_plus = face_rate * flag_values
    weight_minus = face_rate * (1.0 - flag_values)
    return (weight_plus, weight_minus)


def advance(
    values, lower_row, upper_row, lower_col, upper_col, coefficients, retard_planes, spread_planes
):
    divergence = (
        coefficients[0] * lower_row
        + coefficients[1] * upper_row
        + coefficients[2] * lower_col
        + coefficients[3] * upper_col
        - coefficients[4] * values
    )
    laplace = lower_row + upper_row + lower_col + upper_col - 4.0 * values
    return values + (divergence + spread_planes * laplace) / retard_planes


def residual_of(species, target, mixing, affinity, mineral, stiff):
    total = jnp.dot(
        mixing, species, precision=highest, preferred_element_type=jnp.float32
    ) + affinity[:, None] * jnp.tanh(species)
    if stiff:
        total = total + mineral[:, None] * jnp.tanh(2.0 * species)
    return total - target


def newton_steps(species, target, repeats, stiff, mixing, mixing_inverse, affinity, mineral):
    for iteration in range(repeats):
        update = residual_of(species, target, mixing, affinity, mineral, stiff)
        species = species - jnp.dot(
            mixing_inverse, update, precision=highest, preferred_element_type=jnp.float32
        )
    return species


def speciate(cell_block, stiff_mask, mixing, mixing_inverse, affinity, mineral):
    target = cell_block.reshape(NC, -1)
    flat_mask = stiff_mask.reshape(-1) > 0
    species = jnp.zeros_like(target)
    species = newton_steps(species, target, NEWT, False, mixing, mixing_inverse, affinity, mineral)
    stiffer = newton_steps(species, target, STIFF, True, mixing, mixing_inverse, affinity, mineral)
    species = jnp.where(flat_mask[None, :], stiffer, species)
    return species.reshape(cell_block.shape)


def by_rows(
    concentration,
    face_rate,
    face_flag,
    retardation,
    dispersion,
    mixing,
    mixing_inverse,
    affinity,
    mineral,
    stiff_mask,
):
    weight_plus, weight_minus = face_weights(face_rate, face_flag)
    rim_weights = jnp.stack([weight_plus[1, :, -1], weight_minus[1, :, -1]])
    left_rims = shifted(rim_weights, "space", 1)
    side_plus = jnp.concatenate([left_rims[0][:, None], weight_plus[1, :, :-1]], axis=1)
    side_minus = jnp.concatenate([left_rims[1][:, None], weight_minus[1, :, :-1]], axis=1)
    down_plus = shift_down(weight_plus[0], 0)
    down_minus = shift_down(weight_minus[0], 0)
    centre = down_minus + weight_plus[0] + side_minus + weight_plus[1]
    coefficients = jnp.stack([down_plus, weight_minus[0], side_plus, weight_minus[1], centre])
    retard_all = jnp.repeat(retardation, NZ)
    spread_all = jnp.repeat(dispersion, NZ)
    rows_held = stiff_mask.shape[1]
    row_start = lax.axis_index("comp") * rows_held
    cell_coefficients = lax.dynamic_slice_in_dim(coefficients, row_start, rows_held, 1)
    retard_planes = retard_all[:, None, None]
    spread_planes = spread_all[:, None, None]
    cell_block = lax.all_to_all(concentration, "comp", split_axis=1, concat_axis=0, tiled=True)
    for step_index in range(STEPS):
        padded = extended(cell_block, (("comp", 1), ("space", 2)), 1)
        cell_block = advance(
            cell_block,
            padded[:, :-2, 1:-1],
            padded[:, 2:, 1:-1],
            padded[:, 1:-1, :-2],
            padded[:, 1:-1, 2:],
            cell_coefficients,
            retard_planes,
            spread_planes,
        )
        cell_block = speciate(cell_block, stiff_mask, mixing, mixing_inverse, affinity, mineral)
    return lax.all_to_all(cell_block, "comp", split_axis=0, concat_axis=1, tiled=True)


TILE = 8
LANES = 128


def step_kernel(
    held,
    layer,
    with_rim,
    place_ref,
    scale_ref,
    *refs,
):
    pieces = len(held)
    value_refs, refs = refs[:pieces], refs[pieces:]
    (low_ref, high_ref, rate_ref, flag_ref, stiff_ref, ratio_ref, first_ref, both_ref), refs = (
        refs[:8],
        refs[8:],
    )
    out_refs, refs = refs[:pieces], refs[pieces:]
    if with_rim:
        rim_ref, refs = refs[0], refs[1:]
    offset_ref, species_ref, plain_ref, first_split, both_split = refs
    groups, stacked, cols = species_ref.shape
    rows = groups * TILE
    components = stacked // TILE
    row_at = lax.broadcasted_iota(jnp.int32, (rows, cols), 0)
    col_at = lax.broadcasted_iota(jnp.int32, (rows, cols), 1)

    def split(value):
        high = value.astype(jnp.bfloat16)
        return high, (value - high.astype(jnp.float32)).astype(jnp.bfloat16)

    for source, target in ((first_ref, first_split), (both_ref, both_split)):
        high, low = split(source[...])
        target[...] = jnp.concatenate([high, low, high], axis=1)

    def product(weights, parts):
        highs, lows = zip(*[split(part) for part in parts])
        operand = jnp.concatenate(highs + highs + lows, axis=0)
        return jnp.dot(weights[...], operand, preferred_element_type=jnp.float32)

    weight_plus, weight_minus = face_weights(rate_ref[...], flag_ref[...])
    low_side, high_side = low_ref[...], high_ref[...]

    def column(side, at):
        return jnp.broadcast_to(side[:, at : at + 1], (rows, cols))

    def from_lower_row(value):
        return jnp.where(row_at == 0, 0.0, pltpu.roll(value, 1, 0))

    def from_upper_row(value):
        return jnp.where(row_at == rows - 1, 0.0, pltpu.roll(value, rows - 1, 0))

    def from_lower_col(value, edge):
        return jnp.where(col_at == 0, edge, pltpu.roll(value, 1, 1))

    def from_upper_col(value, edge):
        return jnp.where(col_at == cols - 1, edge, pltpu.roll(value, cols - 1, 1))

    rim_at = 2 * components
    down_plus = from_lower_row(weight_plus[0])
    down_minus = from_lower_row(weight_minus[0])
    side_plus = from_lower_col(weight_plus[1], column(low_side, rim_at))
    side_minus = from_lower_col(weight_minus[1], column(low_side, rim_at + 1))
    centre = down_minus + weight_plus[0] + side_minus + weight_plus[1]
    at = 0
    for value_ref, count in zip(value_refs, held):
        for index in range(count):
            value = value_ref[index]
            spread, retard = scale_ref[0, at], scale_ref[1, at]
            change = (
                (down_plus + spread) * from_lower_row(value)
                + (weight_minus[0] + spread) * from_upper_row(value)
                + (side_plus + spread) * from_lower_col(value, column(low_side, components + at))
                + (weight_minus[1] + spread) * from_upper_col(value, column(high_side, at))
                - (centre + 4.0 * spread) * value
            )
            value = value + change * retard
            for group in range(groups):
                offset_ref[group, at * TILE : (at + 1) * TILE, :] = value[
                    group * TILE : (group + 1) * TILE
                ]
            at += 1

    for group in range(groups):
        offset = product(first_split, [offset_ref[group]])
        offset_ref[group] = offset
        species_ref[group] = offset

    def plain_step(_, carry):
        for group in range(groups):
            species = species_ref[group]
            species_ref[group] = offset_ref[group] + product(
                both_split, [species, jnp.tanh(species)]
            )
        return carry

    lax.fori_loop(0, NEWT - 1, plain_step, 0)
    plain_ref[...] = species_ref[...]
    ratio = jnp.concatenate([ratio_ref[...]] * (cols // LANES), axis=1)

    def stiff_step(_, carry):
        for group in range(groups):
            species = species_ref[group]
            reaction = jnp.tanh(species) + ratio * jnp.tanh(species + species)
            species_ref[group] = offset_ref[group] + product(both_split, [species, reaction])
        return carry

    lax.fori_loop(0, STIFF, stiff_step, 0)
    ranks, block = stiff_ref.shape[0], rows // stiff_ref.shape[0]
    for group in range(groups):
        rank = lax.rem(place_ref[0] + ranks - (group * TILE) // block, ranks)
        inside = (group * TILE) % block
        stiff = stiff_ref[rank, layer, inside : inside + TILE, :] > 0.0
        at = 0
        for out_ref, count in zip(out_refs, held):
            for index in range(count):
                spot = slice(at * TILE, (at + 1) * TILE)
                out_ref[index, group * TILE : (group + 1) * TILE, :] = jnp.where(
                    stiff, species_ref[group, spot, :], plain_ref[group, spot, :]
                )
                at += 1
    if with_rim:
        lane_at = lax.broadcasted_iota(jnp.int32, (rows, LANES), 1)
        edges = [out_ref[i] for out_ref, count in zip(out_refs, held) for i in range(count)]
        columns = [value[:, :1] for value in edges] + [value[:, cols - 1 :] for value in edges]
        columns += [weight_plus[1][:, cols - 1 :], weight_minus[1][:, cols - 1 :]]
        rim = jnp.zeros((rows, LANES), jnp.float32)
        for lane, edge in enumerate(columns):
            rim = jnp.where(lane_at == lane, jnp.broadcast_to(edge, (rows, LANES)), rim)
        rim_ref[...] = rim


def layer_step(values, low, high, shared, layer, with_rim):
    place, scales, face_rate, face_flag, stiff, ratio, first, both = shared
    held = [value.shape[0] for value in values]
    components = sum(held)
    rows, cols = values[0].shape[1:]
    groups = rows // TILE
    stacked = components * TILE
    whole = pl.BlockSpec(memory_space=pltpu.VMEM)
    scalar = pl.BlockSpec(memory_space=pltpu.SMEM)
    out_shape = [jax.ShapeDtypeStruct(value.shape, jnp.float32) for value in values]
    if with_rim:
        out_shape.append(jax.ShapeDtypeStruct((rows, LANES), jnp.float32))
    field = pltpu.VMEM((groups, stacked, cols), jnp.float32)
    cells = rows * cols
    operands = [place, scales, *values, low, high, face_rate, face_flag, stiff, ratio, first, both]
    results = pl.pallas_call(
        functools.partial(step_kernel, held, layer, with_rim),
        out_shape=out_shape,
        in_specs=[scalar, scalar] + [whole] * (len(operands) - 2),
        out_specs=[whole] * len(out_shape),
        scratch_shapes=[
            field,
            field,
            field,
            pltpu.VMEM((stacked, 3 * stacked), jnp.bfloat16),
            pltpu.VMEM((stacked, 6 * stacked), jnp.bfloat16),
        ],
        compiler_params=pltpu.CompilerParams(vmem_limit_bytes=24 * 1024 * 1024),
        cost_estimate=pl.CostEstimate(
            flops=2 * (NEWT + STIFF) * 6 * stacked * components * cells,
            bytes_accessed=8 * components * cells,
            transcendentals=(NEWT + 2 * STIFF) * components * cells,
        ),
        name="layer_step",
    )(*operands)
    return (results[:-1], results[-1]) if with_rim else (results, None)


def by_layers(
    concentration,
    face_rate,
    face_flag,
    retardation,
    dispersion,
    mixing,
    mixing_inverse,
    affinity,
    mineral,
    stiff_mask,
):
    ranks = lax.axis_size("comp")
    me = lax.axis_index("comp")
    planes, rows, cols = concentration.shape
    held = planes // NZ
    layers = NZ // ranks
    block = stiff_mask.shape[1]
    own = concentration.reshape(held, ranks, layers, rows, cols)

    def send(value, by):
        return lax.ppermute(value, "comp", [(i, (i + by) % ranks) for i in range(ranks)])

    arrived = []
    for layer in range(layers):
        values = []
        for q in range(ranks):
            piece = lax.dynamic_slice(
                own, (0, (me + q) % ranks, layer, 0, 0), (held, 1, 1, rows, cols)
            ).reshape(held, rows, cols)
            if layer > 0 and q > 0:
                piece, arrived[layer - 1][q] = lax.optimization_barrier(
                    (piece, arrived[layer - 1][q])
                )
            values.append(send(piece, q) if q else piece)
        arrived.append(values)

    rim_rate = face_rate[1, :, -1]
    rim_flag = face_flag[1, :, -1]
    rim = jnp.stack(face_weights(rim_rate, rim_flag))
    from_low = shifted(jnp.concatenate([concentration[:, :, -1], rim]), "space", 1)
    from_high = shifted(concentration[:, :, 0], "space", -1)
    sides = jnp.stack([from_high, from_low[:planes]]).reshape(2, held, ranks, layers, rows)
    sides = sides.transpose(2, 3, 0, 1, 4).reshape(ranks, layers, -1)
    edge_rows = -(-sides.shape[-1] // cols)
    sides = jnp.pad(sides, ((0, 0), (0, 0), (0, edge_rows * cols - sides.shape[-1])))
    sides = sides.reshape(ranks, layers, edge_rows, cols)
    marks = stiff_mask.astype(jnp.float32).reshape(ranks, layers, block, cols)
    small = jnp.concatenate([marks, sides], axis=2)
    small = [
        lax.dynamic_index_in_dim(small, (me + q) % ranks, 0, keepdims=False) for q in range(ranks)
    ]
    small = jnp.stack([send(piece, q) if q else piece for q, piece in enumerate(small)])
    sides = small[:, :, block:].reshape(ranks, layers, -1)[:, :, : 2 * held * rows]
    sides = sides.reshape(ranks, layers, 2, held, rows).transpose(1, 2, 0, 3, 4)
    sides = sides.reshape(layers, 2 * ranks * held, rows)
    rims = jnp.broadcast_to(from_low[planes:], (layers, 2, rows))
    sides = jnp.concatenate([sides, rims], axis=1)
    sides = jnp.pad(sides, ((0, 0), (0, LANES - sides.shape[1]), (0, 0))).transpose(0, 2, 1)

    order = ((me - jnp.arange(ranks)) % ranks)[:, None] * held + jnp.arange(held)
    order = order.reshape(-1)
    inverse = mixing_inverse[order][:, order]
    amounts = affinity[order]
    blend = jnp.eye(NC, dtype=jnp.float32) - jnp.dot(
        inverse, mixing[order][:, order], precision=highest
    )
    tile = jnp.eye(TILE, dtype=jnp.float32)
    first = jnp.kron(inverse, tile)
    both = jnp.concatenate([jnp.kron(blend, tile), jnp.kron(-inverse * amounts, tile)], axis=1)
    ratio = jnp.repeat(mineral[order] / amounts, TILE)
    ratio = jnp.broadcast_to(ratio[:, None], (NC * TILE, LANES))
    scales = jnp.stack([dispersion[order], 1.0 / retardation[order]])
    place = me.astype(jnp.int32).reshape(1)
    shared = (place, scales, face_rate, face_flag, small, ratio, first, both)

    result = jnp.zeros((held, NZ, rows, cols), jnp.float32)
    for layer in range(layers):
        values, low, high = arrived[layer], sides[layer], sides[layer]
        for step in range(STEPS):
            values, rims = layer_step(values, low, high, shared, layer, step < STEPS - 1)
            if step < STEPS - 1:
                low, high = shifted(rims, "space", 1), shifted(rims, "space", -1)
        for q in range(ranks):
            piece = send(values[q], -q) if q else values[q]
            result = lax.dynamic_update_slice(
                result, piece[:, None], (0, (me + q) % ranks * layers + layer, 0, 0)
            )
    return result.reshape(planes, rows, cols)


def shards(concentration, face_rate, face_flag, *parameters):
    ranks = lax.axis_size("comp")
    planes, rows, cols = concentration.shape
    whole = NZ % ranks == 0 and planes % NZ == 0 and 2 * NC + 2 <= LANES
    even = rows % (ranks * TILE) == 0 and cols % LANES == 0
    plan = by_layers if whole and even else by_rows
    return plan(concentration, face_rate, face_flag, *parameters)


def solution(mesh):
    in_specs = (
        P(("real", "comp"), None, "space"),
        P(None, "real", "space"),
        P(None, "real", "space"),
        P(),
        P(),
        P(),
        P(),
        P(),
        P(),
        P(None, ("real", "comp"), "space"),
    )
    out_specs = P(("real", "comp"), None, "space")
    return jax.shard_map(shards, mesh=mesh, in_specs=in_specs, out_specs=out_specs, check_vma=False)
```

profile of v0, /device:TPU:1, one launch (start us, length us, event | category | flops | bytes accessed | tf_op | source)
XLA Modules:
  0.0 143.2 jit_solution(4590383774791351071)
XLA Ops:
  0.0 2.5 %fusion.13 = (f32[32,32,1]{2,1,0:T(8,128)}, f32[32,32,1]{2,1,0:T(8,128)}) fusion(f32[32,32,512]{2,1,0:T(8,128)} %param.10), kind=kLoop, calls=%fused_computation.74 | loop fusion | bytes 16384 | tf_op jit(solution)/shard_map/slice | solution.py:352
  4.0 4.5 %collective-permute-start.4 = (f32[34,32]{1,0:T(8,128)S(1)}, f32[34,32]{1,0:T(8,128)S(1)}, u32[]{:S(2)}, u32[]{:S(2)}) collective-permute-start(f32[34,32]{1,0:T(8,128)S(1)} %pad_maximum_fusion.1), channel_id=1, source_target_pairs={{0,1},{1,2},{2,3},{4,5},{5,6},{6,7},{8,9},{9,10},{10,11},{12,13},{... | collective-permute-start | bytes 13064 | tf_op jit(solution)/shard_map/ppermute | solution.py:23
  9.8 1.9 %collective-permute-start.3 = (f32[32,32]{1,0:T(8,128)S(1)}, f32[32,32]{1,0:T(8,128)S(1)}, u32[]{:S(2)}, u32[]{:S(2)}) collective-permute-start(f32[32,32]{1,0:T(8,128)S(1)} %bitcast.113), channel_id=1, source_target_pairs={{1,0},{2,1},{3,2},{5,4},{6,5},{7,6},{9,8},{10,9},{11,10},{13,12},{... | collective-permute-start | bytes 12296 | tf_op jit(solution)/shard_map/ppermute | solution.py:23
  12.9 3.3 %collective-permute-start.2 = (f32[4,32,512]{2,1,0:T(8,128)}, f32[4,32,512]{2,1,0:T(8,128)S(1)}, u32[]{:S(2)}, u32[]{:S(2)}) collective-permute-start(f32[4,32,512]{2,1,0:T(8,128)} %get-tuple-element.54), channel_id=1, source_target_pairs={{0,12},{4,0},{8,4},{12,8},{1,13},{5,1},{9,5},{13,9},{2,14},{6,2},{... | collective-permute-start | bytes 786440 | tf_op jit(solution)/shard_map/ppermute | solution.py:332
  21.5 1.7 %mul.123 = f32[128,128]{1,0:T(8,128)S(1)} reshape(f32[16,8,16,8]{3,2,1,0:T(8,128)} %get-tuple-element.70) | data formatting | bytes 131072 | tf_op jit(solution)/shard_map/jit(kron)/mul | solution.py:380
  23.3 1.7 %mul.128 = f32[128,128]{1,0:T(8,128)S(1)} reshape(f32[16,8,16,8]{3,2,1,0:T(8,128)} %get-tuple-element.69) | data formatting | bytes 131072 | tf_op jit(solution)/shard_map/jit(kron)/mul | solution.py:380
  27.0 2.0 %collective-permute-start.6 = (f32[2,9,512]{2,1,0:T(8,128)S(1)}, f32[2,9,512]{2,1,0:T(8,128)S(1)}, u32[]{:S(2)}, u32[]{:S(2)}) collective-permute-start(f32[2,9,512]{2,1,0:T(8,128)S(1)} %get-tuple-element.65), channel_id=1, source_target_pairs={{0,8},{4,12},{8,0},{12,4},{1,9},{5,13},{9,1},{13,5},{2,10},{6,14},... | collective-permute-start | bytes 110600 | tf_op jit(solution)/shard_map/ppermute | solution.py:332
  29.0 2.3 %collective-permute-start.7 = (f32[2,9,512]{2,1,0:T(8,128)S(1)}, f32[2,9,512]{2,1,0:T(8,128)}, u32[]{:S(2)}, u32[]{:S(2)}) collective-permute-start(f32[2,9,512]{2,1,0:T(8,128)S(1)} %get-tuple-element.66), channel_id=1, source_target_pairs={{0,12},{4,0},{8,4},{12,8},{1,13},{5,1},{9,5},{13,9},{2,14},{6,2},{... | collective-permute-start | bytes 110600 | tf_op jit(solution)/shard_map/ppermute | solution.py:332
  32.8 5.2 %collective-permute-start = (f32[4,32,512]{2,1,0:T(8,128)}, f32[4,32,512]{2,1,0:T(8,128)S(1)}, u32[]{:S(2)}, u32[]{:S(2)}) collective-permute-start(f32[4,32,512]{2,1,0:T(8,128)} %get-tuple-element.58), channel_id=1, source_target_pairs={{0,4},{4,8},{8,12},{12,0},{1,5},{5,9},{9,13},{13,1},{2,6},{6,10},{... | collective-permute-start | bytes 786440 | tf_op jit(solution)/shard_map/ppermute | solution.py:332
  39.8 4.3 %collective-permute-done.refs_1_ = f32[4,32,512]{2,1,0:T(8,128)S(1)} collective-permute-done((f32[4,32,512]{2,1,0:T(8,128)}, f32[4,32,512]{2,1,0:T(8,128)S(1)}, u32[]{:S(2)}, u32[]{:S(2)}) %collective-permute-start) | collective-permute-done | bytes 262176 | tf_op jit(solution)/shard_map/ppermute | solution.py:332
  44.2 7.5 %layer_step.4 = (f32[4,32,512]{2,1,0:T(8,128)S(1)}, f32[4,32,512]{2,1,0:T(8,128)S(1)}, f32[4,32,512]{2,1,0:T(8,128)S(1)}, f32[4,32,512]{2,1,0:T(8,128)S(1)}, f32[32,128]{1,0:T(8,128)S(1)}) custom-call(s32[1]{0:T(128)} %bitcast.place_ref, f32[2,16]{1,0:T(2,128)S(1)} %pad_maximum_fusion.2.scale_ref, f32[4,32,512]{2,1,0:T(8,128)S(1)} %get-tuple-element.60.refs_0_, ...), custom_call_target="tpu_custom_call" | custom-call | flops 3221225472 | bytes 2097152 | tf_op jit(solution)/shard_map/layer_step/pallas_call | solution.py:288
  51.7 4.4 %collective-permute-start.8 = (f32[32,128]{1,0:T(8,128)S(1)}, f32[32,128]{1,0:T(8,128)S(1)}, u32[]{:S(2)}, u32[]{:S(2)}) collective-permute-start(f32[32,128]{1,0:T(8,128)S(1)} %get-tuple-element.36), channel_id=1, source_target_pairs={{0,1},{1,2},{2,3},{4,5},{5,6},{6,7},{8,9},{9,10},{10,11},{12,13},{... | collective-permute-start | bytes 49160 | tf_op jit(solution)/shard_map/ppermute | solution.py:23
  56.0 1.9 %collective-permute-start.9 = (f32[32,128]{1,0:T(8,128)S(1)}, f32[32,128]{1,0:T(8,128)S(1)}, u32[]{:S(2)}, u32[]{:S(2)}) collective-permute-start(f32[32,128]{1,0:T(8,128)S(1)} %get-tuple-element.36), channel_id=1, source_target_pairs={{1,0},{2,1},{3,2},{5,4},{6,5},{7,6},{9,8},{10,9},{11,10},{13,12},{... | collective-permute-start | bytes 49160 | tf_op jit(solution)/shard_map/ppermute | solution.py:23
  58.0 2.1 %collective-permute-start.15 = (f32[4,32,512]{2,1,0:T(8,128)}, f32[4,32,512]{2,1,0:T(8,128)S(1)}, u32[]{:S(2)}, u32[]{:S(2)}) collective-permute-start(f32[4,32,512]{2,1,0:T(8,128)} %get-tuple-element.43), channel_id=1, source_target_pairs={{0,12},{4,0},{8,4},{12,8},{1,13},{5,1},{9,5},{13,9},{2,14},{6,2},{... | collective-permute-start | bytes 786440 | tf_op jit(solution)/shard_map/ppermute | solution.py:332
  61.5 7.3 %layer_step.5 = (f32[4,32,512]{2,1,0:T(8,128)S(1)}, f32[4,32,512]{2,1,0:T(8,128)S(1)}, f32[4,32,512]{2,1,0:T(8,128)S(1)}, f32[4,32,512]{2,1,0:T(8,128)S(1)}) custom-call(s32[1]{0:T(128)} %bitcast.place_ref, f32[2,16]{1,0:T(2,128)S(1)} %pad_maximum_fusion.2.scale_ref, f32[4,32,512]{2,1,0:T(8,128)S(1)} %get-tuple-element.32.refs_0_, ...), custom_call_target="tpu_custom_call" | custom-call | flops 3221225472 | bytes 2097152 | tf_op jit(solution)/shard_map/layer_step/pallas_call | solution.py:288
  68.8 1.9 %collective-permute-start.10 = (f32[4,32,512]{2,1,0:T(8,128)S(1)}, f32[4,32,512]{2,1,0:T(8,128)S(1)}, u32[]{:S(2)}, u32[]{:S(2)}) collective-permute-start(f32[4,32,512]{2,1,0:T(8,128)S(1)} %get-tuple-element.38), channel_id=1, source_target_pairs={{0,12},{4,0},{8,4},{12,8},{1,13},{5,1},{9,5},{13,9},{2,14},{6,2},{... | collective-permute-start | bytes 786440 | tf_op jit(solution)/shard_map/ppermute | solution.py:332
  71.8 11.8 %collective-permute-done.14.refs_2_ = f32[4,32,512]{2,1,0:T(8,128)S(1)} collective-permute-done((f32[4,32,512]{2,1,0:T(8,128)}, f32[4,32,512]{2,1,0:T(8,128)S(1)}, u32[]{:S(2)}, u32[]{:S(2)}) %collective-permute-start.14) | collective-permute-done | bytes 262176 | tf_op jit(solution)/shard_map/ppermute | solution.py:332
  83.7 7.5 %layer_step.6 = (f32[4,32,512]{2,1,0:T(8,128)S(1)}, f32[4,32,512]{2,1,0:T(8,128)S(1)}, f32[4,32,512]{2,1,0:T(8,128)S(1)}, f32[4,32,512]{2,1,0:T(8,128)S(1)}, f32[32,128]{1,0:T(8,128)S(1)}) custom-call(s32[1]{0:T(128)} %bitcast.place_ref, f32[2,16]{1,0:T(2,128)S(1)} %pad_maximum_fusion.2.scale_ref, f32[4,32,512]{2,1,0:T(8,128)S(1)} %get-tuple-element.53.refs_0_, ...), custom_call_target="tpu_custom_call" | custom-call | flops 3221225472 | bytes 2097152 | tf_op jit(solution)/shard_map/layer_step/pallas_call | solution.py:288
  91.2 15.8 %collective-permute-start.16 = (f32[32,128]{1,0:T(8,128)S(1)}, f32[32,128]{1,0:T(8,128)S(1)}, u32[]{:S(2)}, u32[]{:S(2)}) collective-permute-start(f32[32,128]{1,0:T(8,128)S(1)} %get-tuple-element.48), channel_id=1, source_target_pairs={{0,1},{1,2},{2,3},{4,5},{5,6},{6,7},{8,9},{9,10},{10,11},{12,13},{... | collective-permute-start | bytes 49160 | tf_op jit(solution)/shard_map/ppermute | solution.py:23
  107.0 1.9 %collective-permute-start.17 = (f32[32,128]{1,0:T(8,128)S(1)}, f32[32,128]{1,0:T(8,128)S(1)}, u32[]{:S(2)}, u32[]{:S(2)}) collective-permute-start(f32[32,128]{1,0:T(8,128)S(1)} %get-tuple-element.48), channel_id=1, source_target_pairs={{1,0},{2,1},{3,2},{5,4},{6,5},{7,6},{9,8},{10,9},{11,10},{13,12},{... | collective-permute-start | bytes 49160 | tf_op jit(solution)/shard_map/ppermute | solution.py:23
  109.2 2.8 %collective-permute-done.17.refs_5_ = f32[32,128]{1,0:T(8,128)S(1)} collective-permute-done((f32[32,128]{1,0:T(8,128)S(1)}, f32[32,128]{1,0:T(8,128)S(1)}, u32[]{:S(2)}, u32[]{:S(2)}) %collective-permute-start.17) | collective-permute-done | bytes 16416 | tf_op jit(solution)/shard_map/ppermute | solution.py:23
  112.0 7.2 %layer_step.7 = (f32[4,32,512]{2,1,0:T(8,128)S(1)}, f32[4,32,512]{2,1,0:T(8,128)S(1)}, f32[4,32,512]{2,1,0:T(8,128)S(1)}, f32[4,32,512]{2,1,0:T(8,128)S(1)}) custom-call(s32[1]{0:T(128)} %bitcast.place_ref, f32[2,16]{1,0:T(2,128)S(1)} %pad_maximum_fusion.2.scale_ref, f32[4,32,512]{2,1,0:T(8,128)S(1)} %get-tuple-element.44.refs_0_, ...), custom_call_target="tpu_custom_call" | custom-call | flops 3221225472 | bytes 2097152 | tf_op jit(solution)/shard_map/layer_step/pallas_call | solution.py:288
  121.6 6.1 %collective-permute-done.18 = f32[4,32,512]{2,1,0:T(8,128)S(1)} collective-permute-done((f32[4,32,512]{2,1,0:T(8,128)S(1)}, f32[4,32,512]{2,1,0:T(8,128)S(1)}, u32[]{:S(2)}, u32[]{:S(2)}) %collective-permute-start.18) | collective-permute-done | bytes 262176 | tf_op jit(solution)/shard_map/ppermute | solution.py:332
  127.7 13.9 %collective-permute-done.19 = f32[4,32,512]{2,1,0:T(8,128)S(1)} collective-permute-done((f32[4,32,512]{2,1,0:T(8,128)S(1)}, f32[4,32,512]{2,1,0:T(8,128)S(1)}, u32[]{:S(2)}, u32[]{:S(2)}) %collective-permute-start.19) | collective-permute-done | bytes 262176 | tf_op jit(solution)/shard_map/ppermute | solution.py:332
  (118 shorter events, 21.1 us)
Async XLA Ops:
  0.0 16.5 %copy-start = (f32[16,16]{1,0:T(8,128)S(1)}, f32[16,16]{1,0:T(8,128)}, u32[]{:S(2)}) copy-start(f32[16,16]{1,0:T(8,128)} %param.16) | copy-start | bytes 3076
  0.0 11.8 %copy-start.7 = (f32[32,32,512]{2,1,0:T(8,128)S(1)}, f32[32,32,512]{2,1,0:T(8,128)}, u32[]{:S(2)}) copy-start(f32[32,32,512]{2,1,0:T(8,128)} %param.10) | copy-start | bytes 6291460
  4.0 22.3 %collective-permute-start.4 = (f32[34,32]{1,0:T(8,128)S(1)}, f32[34,32]{1,0:T(8,128)S(1)}, u32[]{:S(2)}, u32[]{:S(2)}) collective-permute-start(f32[34,32]{1,0:T(8,128)S(1)} %pad_maximum_fusion.1), channel_id=1, source_target_pairs={{0,1},{1,2},{2,3},{4,5},{5,6},{6,7},{8,9},{9,10},{10,11},{12,13},{... | collective-permute-start | bytes 13064 | tf_op jit(solution)/shard_map/ppermute | solution.py:23
  9.8 16.5 %collective-permute-start.3 = (f32[32,32]{1,0:T(8,128)S(1)}, f32[32,32]{1,0:T(8,128)S(1)}, u32[]{:S(2)}, u32[]{:S(2)}) collective-permute-start(f32[32,32]{1,0:T(8,128)S(1)} %bitcast.113), channel_id=1, source_target_pairs={{1,0},{2,1},{3,2},{5,4},{6,5},{7,6},{9,8},{10,9},{11,10},{13,12},{... | collective-permute-start | bytes 12296 | tf_op jit(solution)/shard_map/ppermute | solution.py:23
  12.9 26.9 %collective-permute-start.2 = (f32[4,32,512]{2,1,0:T(8,128)}, f32[4,32,512]{2,1,0:T(8,128)S(1)}, u32[]{:S(2)}, u32[]{:S(2)}) collective-permute-start(f32[4,32,512]{2,1,0:T(8,128)} %get-tuple-element.54), channel_id=1, source_target_pairs={{0,12},{4,0},{8,4},{12,8},{1,13},{5,1},{9,5},{13,9},{2,14},{6,2},{... | collective-permute-start | bytes 786440 | tf_op jit(solution)/shard_map/ppermute | solution.py:332
  16.3 23.6 %collective-permute-start.1 = (f32[4,32,512]{2,1,0:T(8,128)}, f32[4,32,512]{2,1,0:T(8,128)S(1)}, u32[]{:S(2)}, u32[]{:S(2)}) collective-permute-start(f32[4,32,512]{2,1,0:T(8,128)} %get-tuple-element.56), channel_id=1, source_target_pairs={{0,8},{4,12},{8,0},{12,4},{1,9},{5,13},{9,1},{13,5},{2,10},{6,14},... | collective-permute-start | bytes 786440 | tf_op jit(solution)/shard_map/ppermute | solution.py:332
  23.2 8.6 %copy-start.6 = (f32[16]{0:T(128)S(1)}, f32[16]{0:T(128)}, u32[]{:S(2)}) copy-start(f32[16]{0:T(128)} %param.18) | copy-start | bytes 196
  26.5 6.2 %collective-permute-start.5 = (f32[2,9,512]{2,1,0:T(8,128)S(1)}, f32[2,9,512]{2,1,0:T(8,128)S(1)}, u32[]{:S(2)}, u32[]{:S(2)}) collective-permute-start(f32[2,9,512]{2,1,0:T(8,128)S(1)} %get-tuple-element.64), channel_id=1, source_target_pairs={{0,4},{4,8},{8,12},{12,0},{1,5},{5,9},{9,13},{13,1},{2,6},{6,10},{... | collective-permute-start | bytes 110600 | tf_op jit(solution)/shard_map/ppermute | solution.py:332
  27.0 10.9 %collective-permute-start.6 = (f32[2,9,512]{2,1,0:T(8,128)S(1)}, f32[2,9,512]{2,1,0:T(8,128)S(1)}, u32[]{:S(2)}, u32[]{:S(2)}) collective-permute-start(f32[2,9,512]{2,1,0:T(8,128)S(1)} %get-tuple-element.65), channel_id=1, source_target_pairs={{0,8},{4,12},{8,0},{12,4},{1,9},{5,13},{9,1},{13,5},{2,10},{6,14},... | collective-permute-start | bytes 110600 | tf_op jit(solution)/shard_map/ppermute | solution.py:332
  29.0 8.9 %collective-permute-start.7 = (f32[2,9,512]{2,1,0:T(8,128)S(1)}, f32[2,9,512]{2,1,0:T(8,128)}, u32[]{:S(2)}, u32[]{:S(2)}) collective-permute-start(f32[2,9,512]{2,1,0:T(8,128)S(1)} %get-tuple-element.66), channel_id=1, source_target_pairs={{0,12},{4,0},{8,4},{12,8},{1,13},{5,1},{9,5},{13,9},{2,14},{6,2},{... | collective-permute-start | bytes 110600 | tf_op jit(solution)/shard_map/ppermute | solution.py:332
  32.8 11.3 %collective-permute-start = (f32[4,32,512]{2,1,0:T(8,128)}, f32[4,32,512]{2,1,0:T(8,128)S(1)}, u32[]{:S(2)}, u32[]{:S(2)}) collective-permute-start(f32[4,32,512]{2,1,0:T(8,128)} %get-tuple-element.58), channel_id=1, source_target_pairs={{0,4},{4,8},{8,12},{12,0},{1,5},{5,9},{9,13},{13,1},{2,6},{6,10},{... | collective-permute-start | bytes 786440 | tf_op jit(solution)/shard_map/ppermute | solution.py:332
  51.7 9.9 %collective-permute-start.8 = (f32[32,128]{1,0:T(8,128)S(1)}, f32[32,128]{1,0:T(8,128)S(1)}, u32[]{:S(2)}, u32[]{:S(2)}) collective-permute-start(f32[32,128]{1,0:T(8,128)S(1)} %get-tuple-element.36), channel_id=1, source_target_pairs={{0,1},{1,2},{2,3},{4,5},{5,6},{6,7},{8,9},{9,10},{10,11},{12,13},{... | collective-permute-start | bytes 49160 | tf_op jit(solution)/shard_map/ppermute | solution.py:23
  56.0 5.5 %collective-permute-start.9 = (f32[32,128]{1,0:T(8,128)S(1)}, f32[32,128]{1,0:T(8,128)S(1)}, u32[]{:S(2)}, u32[]{:S(2)}) collective-permute-start(f32[32,128]{1,0:T(8,128)S(1)} %get-tuple-element.36), channel_id=1, source_target_pairs={{1,0},{2,1},{3,2},{5,4},{6,5},{7,6},{9,8},{10,9},{11,10},{13,12},{... | collective-permute-start | bytes 49160 | tf_op jit(solution)/shard_map/ppermute | solution.py:23
  58.0 13.3 %collective-permute-start.15 = (f32[4,32,512]{2,1,0:T(8,128)}, f32[4,32,512]{2,1,0:T(8,128)S(1)}, u32[]{:S(2)}, u32[]{:S(2)}) collective-permute-start(f32[4,32,512]{2,1,0:T(8,128)} %get-tuple-element.43), channel_id=1, source_target_pairs={{0,12},{4,0},{8,4},{12,8},{1,13},{5,1},{9,5},{13,9},{2,14},{6,2},{... | collective-permute-start | bytes 786440 | tf_op jit(solution)/shard_map/ppermute | solution.py:332
  60.1 23.5 %collective-permute-start.14 = (f32[4,32,512]{2,1,0:T(8,128)}, f32[4,32,512]{2,1,0:T(8,128)S(1)}, u32[]{:S(2)}, u32[]{:S(2)}) collective-permute-start(f32[4,32,512]{2,1,0:T(8,128)} %get-tuple-element.42), channel_id=1, source_target_pairs={{0,8},{4,12},{8,0},{12,4},{1,9},{5,13},{9,1},{13,5},{2,10},{6,14},... | collective-permute-start | bytes 786440 | tf_op jit(solution)/shard_map/ppermute | solution.py:332
  60.1 23.5 %collective-permute-start.13 = (f32[4,32,512]{2,1,0:T(8,128)S(1)}, f32[4,32,512]{2,1,0:T(8,128)S(1)}, u32[]{:S(2)}, u32[]{:S(2)}) collective-permute-start(f32[4,32,512]{2,1,0:T(8,128)S(1)} %get-tuple-element.41), channel_id=1, source_target_pairs={{0,4},{4,8},{8,12},{12,0},{1,5},{5,9},{9,13},{13,1},{2,6},{6,10},{... | collective-permute-start | bytes 786440 | tf_op jit(solution)/shard_map/ppermute | solution.py:332
  68.8 51.3 %collective-permute-start.10 = (f32[4,32,512]{2,1,0:T(8,128)S(1)}, f32[4,32,512]{2,1,0:T(8,128)S(1)}, u32[]{:S(2)}, u32[]{:S(2)}) collective-permute-start(f32[4,32,512]{2,1,0:T(8,128)S(1)} %get-tuple-element.38), channel_id=1, source_target_pairs={{0,12},{4,0},{8,4},{12,8},{1,13},{5,1},{9,5},{13,9},{2,14},{6,2},{... | collective-permute-start | bytes 786440 | tf_op jit(solution)/shard_map/ppermute | solution.py:332
  70.7 50.8 %collective-permute-start.11 = (f32[4,32,512]{2,1,0:T(8,128)S(1)}, f32[4,32,512]{2,1,0:T(8,128)S(1)}, u32[]{:S(2)}, u32[]{:S(2)}) collective-permute-start(f32[4,32,512]{2,1,0:T(8,128)S(1)} %get-tuple-element.39), channel_id=1, source_target_pairs={{0,8},{4,12},{8,0},{12,4},{1,9},{5,13},{9,1},{13,5},{2,10},{6,14},... | collective-permute-start | bytes 786440 | tf_op jit(solution)/shard_map/ppermute | solution.py:332
  71.3 50.2 %collective-permute-start.12 = (f32[4,32,512]{2,1,0:T(8,128)S(1)}, f32[4,32,512]{2,1,0:T(8,128)S(1)}, u32[]{:S(2)}, u32[]{:S(2)}) collective-permute-start(f32[4,32,512]{2,1,0:T(8,128)S(1)} %get-tuple-element.40), channel_id=1, source_target_pairs={{0,4},{4,8},{8,12},{12,0},{1,5},{5,9},{9,13},{13,1},{2,6},{6,10},{... | collective-permute-start | bytes 786440 | tf_op jit(solution)/shard_map/ppermute | solution.py:332
  91.2 18.0 %collective-permute-start.16 = (f32[32,128]{1,0:T(8,128)S(1)}, f32[32,128]{1,0:T(8,128)S(1)}, u32[]{:S(2)}, u32[]{:S(2)}) collective-permute-start(f32[32,128]{1,0:T(8,128)S(1)} %get-tuple-element.48), channel_id=1, source_target_pairs={{0,1},{1,2},{2,3},{4,5},{5,6},{6,7},{8,9},{9,10},{10,11},{12,13},{... | collective-permute-start | bytes 49160 | tf_op jit(solution)/shard_map/ppermute | solution.py:23
  107.0 5.1 %collective-permute-start.17 = (f32[32,128]{1,0:T(8,128)S(1)}, f32[32,128]{1,0:T(8,128)S(1)}, u32[]{:S(2)}, u32[]{:S(2)}) collective-permute-start(f32[32,128]{1,0:T(8,128)S(1)} %get-tuple-element.48), channel_id=1, source_target_pairs={{1,0},{2,1},{3,2},{5,4},{6,5},{7,6},{9,8},{10,9},{11,10},{13,12},{... | collective-permute-start | bytes 49160 | tf_op jit(solution)/shard_map/ppermute | solution.py:23
  119.3 8.4 %collective-permute-start.18 = (f32[4,32,512]{2,1,0:T(8,128)S(1)}, f32[4,32,512]{2,1,0:T(8,128)S(1)}, u32[]{:S(2)}, u32[]{:S(2)}) collective-permute-start(f32[4,32,512]{2,1,0:T(8,128)S(1)} %get-tuple-element.50), channel_id=1, source_target_pairs={{0,12},{4,0},{8,4},{12,8},{1,13},{5,1},{9,5},{13,9},{2,14},{6,2},{... | collective-permute-start | bytes 786440 | tf_op jit(solution)/shard_map/ppermute | solution.py:332
  119.4 22.3 %collective-permute-start.19 = (f32[4,32,512]{2,1,0:T(8,128)S(1)}, f32[4,32,512]{2,1,0:T(8,128)S(1)}, u32[]{:S(2)}, u32[]{:S(2)}) collective-permute-start(f32[4,32,512]{2,1,0:T(8,128)S(1)} %get-tuple-element.51), channel_id=1, source_target_pairs={{0,8},{4,12},{8,0},{12,4},{1,9},{5,13},{9,1},{13,5},{2,10},{6,14},... | collective-permute-start | bytes 786440 | tf_op jit(solution)/shard_map/ppermute | solution.py:332
  120.1 21.8 %collective-permute-start.20 = (f32[4,32,512]{2,1,0:T(8,128)S(1)}, f32[4,32,512]{2,1,0:T(8,128)S(1)}, u32[]{:S(2)}, u32[]{:S(2)}) collective-permute-start(f32[4,32,512]{2,1,0:T(8,128)S(1)} %get-tuple-element.52), channel_id=1, source_target_pairs={{0,4},{4,8},{8,12},{12,0},{1,5},{5,9},{9,13},{13,1},{2,6},{6,10},{... | collective-permute-start | bytes 786440 | tf_op jit(solution)/shard_map/ppermute | solution.py:332
  (10 other events, 40.7 us)
where the time goes:
time: 144 us; the launch traced here: 143 us
  starting transfers between devices  52.4 us (36%)
  waiting for transfers between devices  39 us (27%)
  Pallas kernels  29.4 us (20%)
  local copies, waits for them, and re-layouts  18.5 us (13%)
  other arithmetic  3.04 us (2%)
    ppermute x15, waiting for transfers between devices, send(): lax.ppermute(value, 'comp', [(i, (i + by) % ranks) for i in range(ranks)])  36.1 us
    ppermute x6, starting transfers between devices, shifted(): return lax.ppermute(shard, axis, pairs)  30.5 us
    pallas_call x4, Pallas kernels, layer_step(): pl.pallas_call(functools.partial(step_kernel, held, layer, with_rim), out...  29.4 us
    ppermute x15, starting transfers between devices, send(): lax.ppermute(value, 'comp', [(i, (i + by) % ranks) for i in range(ranks)])  22 us
    unnamed x30, local copies, waits for them, and re-layouts  4.57 us
  transfers between devices with their start and end apart: 21, of which 5 were waited for; matrix products, arithmetic and copies ran while one was open for 11% of the time, Pallas kernels for 15%

commit v1 on v0

--- a/solution.py
+++ b/solution.py
@@ -141,27 +141,24 @@
 LANES = 128
 
 
-def step_kernel(
-    held,
-    layer,
-    with_rim,
-    place_ref,
-    scale_ref,
-    *refs,
-):
-    pieces = len(held)
+def step_kernel(pieces, is_first, with_rim, place_ref, scale_ref, *refs):
     value_refs, refs = refs[:pieces], refs[pieces:]
-    (low_ref, high_ref, rate_ref, flag_ref, stiff_ref, ratio_ref, first_ref, both_ref), refs = (
-        refs[:8],
-        refs[8:],
+    (low_ref, high_ref, rate_ref, flag_ref, ratio_ref, first_ref, both_ref), refs = (
+        refs[:7],
+        refs[7:],
     )
+    if not is_first:
+        stiff_ref, refs = refs[0], refs[1:]
     out_refs, refs = refs[:pieces], refs[pieces:]
     if with_rim:
         rim_ref, refs = refs[0], refs[1:]
+    if is_first:
+        stiff_ref, refs = refs[0], refs[1:]
     offset_ref, species_ref, plain_ref, first_split, both_split = refs
     groups, stacked, cols = species_ref.shape
     rows = groups * TILE
     components = stacked // TILE
+    held = components // pieces
     row_at = lax.broadcasted_iota(jnp.int32, (rows, cols), 0)
     col_at = lax.broadcasted_iota(jnp.int32, (rows, cols), 1)
 
@@ -203,9 +200,9 @@
     side_minus = from_lower_col(weight_minus[1], column(low_side, rim_at + 1))
     centre = down_minus + weight_plus[0] + side_minus + weight_plus[1]
     at = 0
-    for value_ref, count in zip(value_refs, held):
-        for index in range(count):
-            value = value_ref[index]
+    for value_ref in value_refs:
+        for index in range(held):
+            value = value_ref[index * rows : (index + 1) * rows, :]
             spread, retard = scale_ref[0, at], scale_ref[1, at]
             change = (
                 (down_plus + spread) * from_lower_row(value)
@@ -246,22 +243,24 @@
         return carry
 
     lax.fori_loop(0, STIFF, stiff_step, 0)
-    ranks, block = stiff_ref.shape[0], rows // stiff_ref.shape[0]
+    if is_first:
+        block = rows // pieces
+        for q, value_ref in enumerate(value_refs):
+            rank = lax.rem(place_ref[0] + pieces - q, pieces)
+            spot = pl.ds(pl.multiple_of(rank * block, TILE), block)
+            stiff_ref[spot, :] = value_ref[held * rows :, :]
     for group in range(groups):
-        rank = lax.rem(place_ref[0] + ranks - (group * TILE) // block, ranks)
-        inside = (group * TILE) % block
-        stiff = stiff_ref[rank, layer, inside : inside + TILE, :] > 0.0
-        at = 0
-        for out_ref, count in zip(out_refs, held):
-            for index in range(count):
-                spot = slice(at * TILE, (at + 1) * TILE)
-                out_ref[index, group * TILE : (group + 1) * TILE, :] = jnp.where(
-                    stiff, species_ref[group, spot, :], plain_ref[group, spot, :]
-                )
-                at += 1
+        spot = slice(group * TILE, (group + 1) * TILE)
+        stiff = stiff_ref[spot, :] > 0.0
+        for at in range(components):
+            lane = slice(at * TILE, (at + 1) * TILE)
+            start = at % held * rows + group * TILE
+            out_refs[at // held][start : start + TILE, :] = jnp.where(
+                stiff, species_ref[group, lane, :], plain_ref[group, lane, :]
+            )
     if with_rim:
         lane_at = lax.broadcasted_iota(jnp.int32, (rows, LANES), 1)
-        edges = [out_ref[i] for out_ref, count in zip(out_refs, held) for i in range(count)]
+        edges = [ref[i * rows : (i + 1) * rows, :] for ref in out_refs for i in range(held)]
         columns = [value[:, :1] for value in edges] + [value[:, cols - 1 :] for value in edges]
         columns += [weight_plus[1][:, cols - 1 :], weight_minus[1][:, cols - 1 :]]
         rim = jnp.zeros((rows, LANES), jnp.float32)
@@ -270,23 +269,28 @@
         rim_ref[...] = rim
 
 
-def layer_step(values, low, high, shared, layer, with_rim):
-    place, scales, face_rate, face_flag, stiff, ratio, first, both = shared
-    held = [value.shape[0] for value in values]
-    components = sum(held)
-    rows, cols = values[0].shape[1:]
+def layer_step(values, stiff, low, high, shared, with_rim):
+    place, scales, face_rate, face_flag, ratio, first, both = shared
+    pieces = len(values)
+    rows, cols = face_rate.shape[1:]
     groups = rows // TILE
-    stacked = components * TILE
+    stacked = ratio.shape[0]
+    components = stacked // TILE
     whole = pl.BlockSpec(memory_space=pltpu.VMEM)
     scalar = pl.BlockSpec(memory_space=pltpu.SMEM)
-    out_shape = [jax.ShapeDtypeStruct(value.shape, jnp.float32) for value in values]
+    plane = jax.ShapeDtypeStruct((components // pieces * rows, cols), jnp.float32)
+    out_shape = [plane] * pieces
     if with_rim:
         out_shape.append(jax.ShapeDtypeStruct((rows, LANES), jnp.float32))
+    if stiff is None:
+        out_shape.append(jax.ShapeDtypeStruct((rows, cols), jnp.float32))
     field = pltpu.VMEM((groups, stacked, cols), jnp.float32)
     cells = rows * cols
-    operands = [place, scales, *values, low, high, face_rate, face_flag, stiff, ratio, first, both]
+    operands = [place, scales, *values, low, high, face_rate, face_flag, ratio, first, both]
+    if stiff is not None:
+        operands.append(stiff)
     results = pl.pallas_call(
-        functools.partial(step_kernel, held, layer, with_rim),
+        functools.partial(step_kernel, pieces, stiff is None, with_rim),
         out_shape=out_shape,
         in_specs=[scalar, scalar] + [whole] * (len(operands) - 2),
         out_specs=[whole] * len(out_shape),
@@ -305,7 +309,9 @@
         ),
         name="layer_step",
     )(*operands)
-    return (results[:-1], results[-1]) if with_rim else (results, None)
+    values, results = results[:pieces], results[pieces:]
+    rims = results[0] if with_rim else None
+    return values, (results[-1] if stiff is None else stiff), rims
 
 
 def by_layers(
@@ -327,46 +333,51 @@
     layers = NZ // ranks
     block = stiff_mask.shape[1]
     own = concentration.reshape(held, ranks, layers, rows, cols)
+    marks = stiff_mask.astype(jnp.float32).reshape(ranks, layers, block, cols)
 
     def send(value, by):
         return lax.ppermute(value, "comp", [(i, (i + by) % ranks) for i in range(ranks)])
 
-    arrived = []
+    messages, arrived = [], []
     for layer in range(layers):
-        values = []
+        parts = []
         for q in range(ranks):
-            piece = lax.dynamic_slice(
-                own, (0, (me + q) % ranks, layer, 0, 0), (held, 1, 1, rows, cols)
-            ).reshape(held, rows, cols)
+            target = (me + q) % ranks
+            piece = lax.dynamic_slice(own, (0, target, layer, 0, 0), (held, 1, 1, rows, cols))
+            mark = lax.dynamic_slice(marks, (target, layer, 0, 0), (1, 1, block, cols))
+            part = jnp.concatenate([piece.reshape(-1, cols), mark.reshape(-1, cols)])
             if layer > 0 and q > 0:
-                piece, arrived[layer - 1][q] = lax.optimization_barrier(
-                    (piece, arrived[layer - 1][q])
+                part, arrived[layer - 1][q] = lax.optimization_barrier(
+                    (part, arrived[layer - 1][q])
                 )
-            values.append(send(piece, q) if q else piece)
-        arrived.append(values)
-
-    rim_rate = face_rate[1, :, -1]
-    rim_flag = face_flag[1, :, -1]
-    rim = jnp.stack(face_weights(rim_rate, rim_flag))
-    from_low = shifted(jnp.concatenate([concentration[:, :, -1], rim]), "space", 1)
-    from_high = shifted(concentration[:, :, 0], "space", -1)
-    sides = jnp.stack([from_high, from_low[:planes]]).reshape(2, held, ranks, layers, rows)
-    sides = sides.transpose(2, 3, 0, 1, 4).reshape(ranks, layers, -1)
-    edge_rows = -(-sides.shape[-1] // cols)
-    sides = jnp.pad(sides, ((0, 0), (0, 0), (0, edge_rows * cols - sides.shape[-1])))
-    sides = sides.reshape(ranks, layers, edge_rows, cols)
-    marks = stiff_mask.astype(jnp.float32).reshape(ranks, layers, block, cols)
-    small = jnp.concatenate([marks, sides], axis=2)
-    small = [
-        lax.dynamic_index_in_dim(small, (me + q) % ranks, 0, keepdims=False) for q in range(ranks)
-    ]
-    small = jnp.stack([send(piece, q) if q else piece for q, piece in enumerate(small)])
-    sides = small[:, :, block:].reshape(ranks, layers, -1)[:, :, : 2 * held * rows]
-    sides = sides.reshape(ranks, layers, 2, held, rows).transpose(1, 2, 0, 3, 4)
-    sides = sides.reshape(layers, 2 * ranks * held, rows)
-    rims = jnp.broadcast_to(from_low[planes:], (layers, 2, rows))
-    sides = jnp.concatenate([sides, rims], axis=1)
-    sides = jnp.pad(sides, ((0, 0), (0, LANES - sides.shape[1]), (0, 0))).transpose(0, 2, 1)
+            parts.append(part)
+        messages.append(parts)
+        arrived.append([send(part, q) if q else part for q, part in enumerate(parts)])
+
+    planes_after, messages[0] = lax.optimization_barrier((concentration, messages[0]))
+    rim = jnp.stack(face_weights(face_rate[1, :, -1], face_flag[1, :, -1]))
+    edges = jnp.concatenate([planes_after[:, :, 0], planes_after[:, :, -1], rim])
+    edges = lax.all_gather(edges, ("comp", "space"))
+    spaces = lax.axis_size("space")
+    mine = lax.axis_index("space")
+    edges = edges.reshape(ranks, spaces, 2 * planes + 2, rows)
+    edges = jnp.pad(edges, ((0, 0), (1, 1), (0, 0), (0, 0)))
+    below = lax.dynamic_index_in_dim(edges, mine, 1, keepdims=False)
+    above = lax.dynamic_index_in_dim(edges, mine + 2, 1, keepdims=False)
+
+    def sides_of(values):
+        values = values.reshape(ranks, held, ranks, layers, rows)
+        values = lax.dynamic_index_in_dim(values, me, 2, keepdims=False)
+        return values[(me - jnp.arange(ranks)) % ranks].reshape(NC, layers, rows)
+
+    sides = jnp.concatenate(
+        [
+            sides_of(above[:, :planes]),
+            sides_of(below[:, planes : 2 * planes]),
+            jnp.broadcast_to(below[0, 2 * planes :, None], (2, layers, rows)),
+            jnp.zeros((LANES - 2 * NC - 2, layers, rows), jnp.float32),
+        ]
+    ).transpose(1, 2, 0)
 
     order = ((me - jnp.arange(ranks)) % ranks)[:, None] * held + jnp.arange(held)
     order = order.reshape(-1)
@@ -382,19 +393,19 @@
     ratio = jnp.broadcast_to(ratio[:, None], (NC * TILE, LANES))
     scales = jnp.stack([dispersion[order], 1.0 / retardation[order]])
     place = me.astype(jnp.int32).reshape(1)
-    shared = (place, scales, face_rate, face_flag, small, ratio, first, both)
+    shared = (place, scales, face_rate, face_flag, ratio, first, both)
 
     result = jnp.zeros((held, NZ, rows, cols), jnp.float32)
     for layer in range(layers):
-        values, low, high = arrived[layer], sides[layer], sides[layer]
+        values, stiff, low, high = arrived[layer], None, sides[layer], sides[layer]
         for step in range(STEPS):
-            values, rims = layer_step(values, low, high, shared, layer, step < STEPS - 1)
+            values, stiff, rims = layer_step(values, stiff, low, high, shared, step < STEPS - 1)
             if step < STEPS - 1:
                 low, high = shifted(rims, "space", 1), shifted(rims, "space", -1)
         for q in range(ranks):
             piece = send(values[q], -q) if q else values[q]
             result = lax.dynamic_update_slice(
-                result, piece[:, None], (0, (me + q) % ranks * layers + layer, 0, 0)
+                result, piece.reshape(held, 1, rows, cols), (0, (me + q) % ranks * layers + layer, 0, 0)
             )
     return result.reshape(planes, rows, cols)
 

time: 144 us -> 165 us (1.15)
  starting transfers between devices: 52.4 us -> 27.5 us
  blocking collectives: 0 us -> 22.9 us
  local copies, waits for them, and re-layouts: 18.5 us -> 34.6 us
  other arithmetic: 3.04 us -> 7.5 us
  waiting for transfers between devices: 39 us -> 41.4 us
    all_gather x0 -> x1, blocking collectives: none -> 22.9 us  [by_layers(): edges = lax.all_gather(edges, ('comp', 'space'))]
    ppermute x6 -> x4, starting transfers between devices: 30.5 us -> 10.6 us  [shifted(): return lax.ppermute(shard, axis, pairs)]
    optimization_barrier x0 -> x2, local copies, waits for them, and re-layouts: none -> 16.8 us  [by_layers(): lax.optimization_barrier((concentration, messages[0]))]
    ppermute x15 -> x12, starting transfers between devices: 22 us -> 16.9 us  [send(): lax.ppermute(value, 'comp', [(i, (i + by) % ranks) for i in range(ranks)])]
    concatenate x2 -> x6, other arithmetic: 0.04 us -> 3.77 us  [by_layers(): part = jnp.concatenate([piece.reshape(-1, cols), mark.reshape(-1, cols)])]
    unnamed x30 -> x28, local copies, waits for them, and re-layouts: 4.57 us -> 1.75 us
    slice x6 -> x2, local copies, waits for them, and re-layouts: 2.59 us -> 0.01 us  [the longest x1 0.01 us: by_layers(): below[:, planes:2 * planes]]
    dynamic_slice x0 -> x4, local copies, waits for them, and re-layouts: none -> 1.76 us  [the longest x1 1.74 us: by_layers(): lax.dynamic_slice(own, (0, target, layer, 0, 0), (held, 1, 1, rows, cols))]
  transfers between devices with their start and end apart: 21 -> 16, of which waited for: 5 -> 5; matrix products, arithmetic and copies ran while one was open for 11% -> 22% of each run, Pallas kernels for 15% -> 13%
where the time goes in v1:
time: 165 us; the launch traced here: 164 us
  waiting for transfers between devices  41.4 us (25%)
  local copies, waits for them, and re-layouts  34.6 us (21%)
  Pallas kernels  29.5 us (18%)
  starting transfers between devices  27.5 us (17%)
  blocking collectives  22.9 us (14%)
  other arithmetic  7.5 us (5%)
    ppermute x12, waiting for transfers between devices, send(): lax.ppermute(value, 'comp', [(i, (i + by) % ranks) for i in range(ranks)])  37 us
    pallas_call x4, Pallas kernels, layer_step(): pl.pallas_call(functools.partial(step_kernel, pieces, stiff is None, with...  29.5 us
    all_gather x1, blocking collectives, by_layers(): edges = lax.all_gather(edges, ('comp', 'space'))  22.9 us
    ppermute x12, starting transfers between devices, send(): lax.ppermute(value, 'comp', [(i, (i + by) % ranks) for i in range(ranks)])  16.9 us
    optimization_barrier x2, local copies, waits for them, and re-layouts, by_layers(): lax.optimization_barrier((concentration, messages[0]))  16.8 us
    ppermute x4, starting transfers between devices, shifted(): return lax.ppermute(shard, axis, pairs)  10.6 us
    ppermute x4, waiting for transfers between devices, shifted(): return lax.ppermute(shard, axis, pairs)  4.4 us
    concatenate x6, other arithmetic, by_layers(): part = jnp.concatenate([piece.reshape(-1, cols), mark.reshape(-1, cols)])  3.77 us
  transfers between devices with their start and end apart: 16, of which 5 were waited for; matrix products, arithmetic and copies ran while one was open for 22% of the time, Pallas kernels for 13%

profile of v1, /device:TPU:1, one launch (start us, length us, event | category | flops | bytes accessed | tf_op | source)
XLA Modules:
  0.0 164.2 jit_solution(6836922539331124058)
XLA Ops:
  1.0 1.7 %constant_dynamic-slice_fusion = (f32[4,1,1,32,512]{4,3,2,1,0:T(8,128)S(1)}, f32[4,1,1,32,512]{4,3,2,1,0:T(8,128)S(1)}, f32[4,1,1,32,512]{4,3,2,1,0:T(8,128)S(1)...) fusion(f32[4,4,2,32,512]{4,3,2,1,0:T(8,128)} %bitcast.124, ...), kind=kLoop, calls=%fused_computation.50 | loop fusion | bytes 4194320 | tf_op jit(solution)/shard_map/dynamic_slice | solution.py:346
  4.0 4.2 %collective-permute-start.2 = (f32[136,512]{1,0:T(8,128)}, f32[136,512]{1,0:T(8,128)S(1)}, u32[]{:S(2)}, u32[]{:S(2)}) collective-permute-start(f32[136,512]{1,0:T(8,128)} %pad_maximum_fusion.6), channel_id=1, source_target_pairs={{0,12},{4,0},{8,4},{12,8},{1,13},{5,1},{9,5},{13,9},{2,14},{6,2},{... | collective-permute-start | bytes 835592 | tf_op jit(solution)/shard_map/ppermute | solution.py:339
  10.8 8.4 %copy.98 = f32[32,32,512]{1,0,2:T(8,128)} copy(f32[32,32,512]{2,1,0:T(8,128)} %param.10) | data formatting | bytes 4194304 | tf_op jit(solution)/shard_map/optimization_barrier | solution.py:357
  19.3 8.4 %copy.97 = f32[32,32,512]{0,1,2:T(8,128)} copy(f32[32,32,512]{2,1,0:T(8,128)} %param.10) | data formatting | bytes 4194304 | tf_op jit(solution)/shard_map/optimization_barrier | solution.py:357
  29.7 22.9 %all-gather.1 = f32[16,66,32]{1,2,0:T(8,128)S(1)} all-gather(f32[1,66,32]{1,2,0:T(8,128)S(1)} %maximum_bitcast_fusion.1), channel_id=2, replica_groups=mesh['real'=2,'comp'=4,'space'=4] {'comp','space'}, dimensions={0}, use_global_device_ids=true | all-gather | bytes 143616 | tf_op jit(solution)/shard_map/all_gather | solution.py:360
  58.5 1.6 broadcast_multiply_fusion
  60.1 1.7 %mul.123 = f32[128,128]{1,0:T(8,128)S(1)} reshape(f32[16,8,16,8]{3,2,1,0:T(8,128)} %get-tuple-element.80) | data formatting | bytes 131072 | tf_op jit(solution)/shard_map/jit(kron)/mul | solution.py:391
  61.7 1.7 %mul.128 = f32[128,128]{1,0:T(8,128)S(1)} reshape(f32[16,8,16,8]{3,2,1,0:T(8,128)} %get-tuple-element.79) | data formatting | bytes 131072 | tf_op jit(solution)/shard_map/jit(kron)/mul | solution.py:391
  68.3 7.5 %layer_step.4 = (f32[128,512]{1,0:T(8,128)S(1)}, f32[128,512]{1,0:T(8,128)S(1)}, f32[128,512]{1,0:T(8,128)S(1)}, f32[128,512]{1,0:T(8,128)S(1)}, f32[32,128]{1,0:T(8,128)S(1)}, /*index=5*/f32[32,512]{1,0:T(8,128)S(1)}) custom-call(s32[1]{0:T(128)} %bitcast.place_ref, f32[2,16]{1,0:T(2,128)S(1)} %pad_maximum_fusion.8.scale_ref, ...), custom_call_target="tpu_custom_call" | custom-call | flops 3221225472 | bytes 2097152 | tf_op jit(solution)/shard_map/layer_step/pallas_call | solution.py:292
  75.8 1.9 %collective-permute-start.3 = (f32[32,128]{1,0:T(8,128)S(1)}, f32[32,128]{1,0:T(8,128)S(1)}, u32[]{:S(2)}, u32[]{:S(2)}) collective-permute-start(f32[32,128]{1,0:T(8,128)S(1)} %get-tuple-element.40), channel_id=1, source_target_pairs={{0,1},{1,2},{2,3},{4,5},{5,6},{6,7},{8,9},{9,10},{10,11},{12,13},{... | collective-permute-start | bytes 49160 | tf_op jit(solution)/shard_map/ppermute | solution.py:23
  77.7 2.4 %collective-permute-start.4 = (f32[32,128]{1,0:T(8,128)S(1)}, f32[32,128]{1,0:T(8,128)S(1)}, u32[]{:S(2)}, u32[]{:S(2)}) collective-permute-start(f32[32,128]{1,0:T(8,128)S(1)} %get-tuple-element.40), channel_id=1, source_target_pairs={{1,0},{2,1},{3,2},{5,4},{6,5},{7,6},{9,8},{10,9},{11,10},{13,12},{... | collective-permute-start | bytes 49160 | tf_op jit(solution)/shard_map/ppermute | solution.py:23
  80.4 1.4 collective-permute-start.8
  81.7 1.3 collective-permute-done.4.refs_5_
  83.1 7.3 %layer_step.5 = (f32[128,512]{1,0:T(8,128)S(1)}, f32[128,512]{1,0:T(8,128)S(1)}, f32[128,512]{1,0:T(8,128)S(1)}, f32[128,512]{1,0:T(8,128)S(1)}) custom-call(s32[1]{0:T(128)} %bitcast.place_ref, f32[2,16]{1,0:T(2,128)S(1)} %pad_maximum_fusion.8.scale_ref, f32[128,512]{1,0:T(8,128)S(1)} %get-tuple-element.36.refs_0_, ...), custom_call_target="tpu_custom_call" | custom-call | flops 3221225472 | bytes 2097152 | tf_op jit(solution)/shard_map/layer_step/pallas_call | solution.py:292
  91.8 7.8 %collective-permute-start.7 = (f32[128,512]{1,0:T(8,128)S(1)}, f32[128,512]{1,0:T(8,128)S(1)}, u32[]{:S(2)}, u32[]{:S(2)}) collective-permute-start(f32[128,512]{1,0:T(8,128)S(1)} %get-tuple-element.45), channel_id=1, source_target_pairs={{0,4},{4,8},{8,12},{12,0},{1,5},{5,9},{9,13},{13,1},{2,6},{6,10},{... | collective-permute-start | bytes 786440 | tf_op jit(solution)/shard_map/ppermute | solution.py:339
  99.6 16.6 %collective-permute-done.9.refs_2_ = f32[136,512]{1,0:T(8,128)S(1)} collective-permute-done((f32[136,512]{1,0:T(8,128)}, f32[136,512]{1,0:T(8,128)S(1)}, u32[]{:S(2)}, u32[]{:S(2)}) %collective-permute-start.9) | collective-permute-done | bytes 278560 | tf_op jit(solution)/shard_map/ppermute | solution.py:339
  116.2 7.5 %layer_step.6 = (f32[128,512]{1,0:T(8,128)S(1)}, f32[128,512]{1,0:T(8,128)S(1)}, f32[128,512]{1,0:T(8,128)S(1)}, f32[128,512]{1,0:T(8,128)S(1)}, f32[32,128]{1,0:T(8,128)S(1)}, /*index=5*/f32[32,512]{1,0:T(8,128)S(1)}) custom-call(s32[1]{0:T(128)} %bitcast.place_ref, f32[2,16]{1,0:T(2,128)S(1)} %pad_maximum_fusion.8.scale_ref, ...), custom_call_target="tpu_custom_call" | custom-call | flops 3221225472 | bytes 2097152 | tf_op jit(solution)/shard_map/layer_step/pallas_call | solution.py:292
  123.7 4.3 %collective-permute-start.11 = (f32[32,128]{1,0:T(8,128)S(1)}, f32[32,128]{1,0:T(8,128)S(1)}, u32[]{:S(2)}, u32[]{:S(2)}) collective-permute-start(f32[32,128]{1,0:T(8,128)S(1)} %get-tuple-element.53), channel_id=1, source_target_pairs={{0,1},{1,2},{2,3},{4,5},{5,6},{6,7},{8,9},{9,10},{10,11},{12,13},{... | collective-permute-start | bytes 49160 | tf_op jit(solution)/shard_map/ppermute | solution.py:23
  128.0 1.9 %collective-permute-start.12 = (f32[32,128]{1,0:T(8,128)S(1)}, f32[32,128]{1,0:T(8,128)S(1)}, u32[]{:S(2)}, u32[]{:S(2)}) collective-permute-start(f32[32,128]{1,0:T(8,128)S(1)} %get-tuple-element.53), channel_id=1, source_target_pairs={{1,0},{2,1},{3,2},{5,4},{6,5},{7,6},{9,8},{10,9},{11,10},{13,12},{... | collective-permute-start | bytes 49160 | tf_op jit(solution)/shard_map/ppermute | solution.py:23
  130.0 3.1 %collective-permute-done.12.refs_5_ = f32[32,128]{1,0:T(8,128)S(1)} collective-permute-done((f32[32,128]{1,0:T(8,128)S(1)}, f32[32,128]{1,0:T(8,128)S(1)}, u32[]{:S(2)}, u32[]{:S(2)}) %collective-permute-start.12) | collective-permute-done | bytes 16416 | tf_op jit(solution)/shard_map/ppermute | solution.py:23
  133.1 7.3 %layer_step.7 = (f32[128,512]{1,0:T(8,128)S(1)}, f32[128,512]{1,0:T(8,128)S(1)}, f32[128,512]{1,0:T(8,128)S(1)}, f32[128,512]{1,0:T(8,128)S(1)}) custom-call(s32[1]{0:T(128)} %bitcast.place_ref, f32[2,16]{1,0:T(2,128)S(1)} %pad_maximum_fusion.8.scale_ref, f32[128,512]{1,0:T(8,128)S(1)} %get-tuple-element.49.refs_0_, ...), custom_call_target="tpu_custom_call" | custom-call | flops 3221225472 | bytes 2097152 | tf_op jit(solution)/shard_map/layer_step/pallas_call | solution.py:292
  140.8 1.5 collective-permute-start.15
  142.3 6.3 %collective-permute-done.13 = f32[128,512]{1,0:T(8,128)S(1)} collective-permute-done((f32[128,512]{1,0:T(8,128)S(1)}, f32[128,512]{1,0:T(8,128)S(1)}, u32[]{:S(2)}, u32[]{:S(2)}) %collective-permute-start.13) | collective-permute-done | bytes 262176 | tf_op jit(solution)/shard_map/ppermute | solution.py:339
  148.7 14.1 %collective-permute-done.14 = f32[128,512]{1,0:T(8,128)S(1)} collective-permute-done((f32[128,512]{1,0:T(8,128)S(1)}, f32[128,512]{1,0:T(8,128)S(1)}, u32[]{:S(2)}, u32[]{:S(2)}) %collective-permute-start.14) | collective-permute-done | bytes 262176 | tf_op jit(solution)/shard_map/ppermute | solution.py:339
  (121 shorter events, 21.0 us)
Async XLA Ops:
  0.0 54.6 %copy-start = (f32[16,16]{1,0:T(8,128)S(1)}, f32[16,16]{1,0:T(8,128)}, u32[]{:S(2)}) copy-start(f32[16,16]{1,0:T(8,128)} %param.16) | copy-start | bytes 3076
  4.0 64.1 %collective-permute-start.2 = (f32[136,512]{1,0:T(8,128)}, f32[136,512]{1,0:T(8,128)S(1)}, u32[]{:S(2)}, u32[]{:S(2)}) collective-permute-start(f32[136,512]{1,0:T(8,128)} %pad_maximum_fusion.6), channel_id=1, source_target_pairs={{0,12},{4,0},{8,4},{12,8},{1,13},{5,1},{9,5},{13,9},{2,14},{6,2},{... | collective-permute-start | bytes 835592 | tf_op jit(solution)/shard_map/ppermute | solution.py:339
  8.9 59.2 %collective-permute-start.1 = (f32[136,512]{1,0:T(8,128)}, f32[136,512]{1,0:T(8,128)S(1)}, u32[]{:S(2)}, u32[]{:S(2)}) collective-permute-start(f32[136,512]{1,0:T(8,128)} %pad_maximum_fusion.4), channel_id=1, source_target_pairs={{0,8},{4,12},{8,0},{12,4},{1,9},{5,13},{9,1},{13,5},{2,10},{6,14},... | collective-permute-start | bytes 835592 | tf_op jit(solution)/shard_map/ppermute | solution.py:339
  9.6 58.5 %collective-permute-start = (f32[136,512]{1,0:T(8,128)}, f32[136,512]{1,0:T(8,128)S(1)}, u32[]{:S(2)}, u32[]{:S(2)}) collective-permute-start(f32[136,512]{1,0:T(8,128)} %pad_maximum_fusion.2), channel_id=1, source_target_pairs={{0,4},{4,8},{8,12},{12,0},{1,5},{5,9},{9,13},{13,1},{2,6},{6,10},{... | collective-permute-start | bytes 835592 | tf_op jit(solution)/shard_map/ppermute | solution.py:339
  19.3 10.0 %copy-start.1 = (s32[2,32,512]{2,1,0:T(8,128)S(1)}, s32[2,32,512]{2,1,0:T(8,128)}, u32[]{:S(2)}) copy-start(s32[2,32,512]{2,1,0:T(8,128)} %refs_7_.7) | copy-start | bytes 393220
  19.3 10.0 %copy-start.2 = (f32[2,32,512]{2,1,0:T(8,128)S(1)}, f32[2,32,512]{2,1,0:T(8,128)}, u32[]{:S(2)}) copy-start(f32[2,32,512]{2,1,0:T(8,128)} %refs_6_.7) | copy-start | bytes 393220
  27.7 28.1 %copy-start.8 = (f32[16,16]{1,0:T(8,128)S(1)}, f32[16,16]{1,0:T(8,128)}, u32[]{:S(2)}) copy-start(f32[16,16]{1,0:T(8,128)} %param.15) | copy-start | bytes 3076
  27.7 29.3 %copy-start.3 = (f32[16]{0:T(128)S(1)}, f32[16]{0:T(128)}, u32[]{:S(2)}) copy-start(f32[16]{0:T(128)} %param.17) | copy-start | bytes 196
  58.5 4.9 %copy-start.4 = (f32[16]{0:T(128)S(1)}, f32[16]{0:T(128)}, u32[]{:S(2)}) copy-start(f32[16]{0:T(128)} %param.13) | copy-start | bytes 196
  68.3 11.9 %copy-start.10 = (f32[8,512]{1,0:T(8,128)S(1)}, f32[8,512]{1,0:T(8,128)}, u32[]{:S(2)}) copy-start(f32[8,512]{1,0:T(8,128)} %get-tuple-element.69) | copy-start | bytes 49156
  68.3 12.1 %copy-start.9 = (f32[136,512]{1,0:T(8,128)S(1)}, f32[136,512]{1,0:T(8,128)}, u32[]{:S(2)}) copy-start(f32[136,512]{1,0:T(8,128)} %get-tuple-element.46) | copy-start | bytes 835588
  75.8 6.0 %collective-permute-start.3 = (f32[32,128]{1,0:T(8,128)S(1)}, f32[32,128]{1,0:T(8,128)S(1)}, u32[]{:S(2)}, u32[]{:S(2)}) collective-permute-start(f32[32,128]{1,0:T(8,128)S(1)} %get-tuple-element.40), channel_id=1, source_target_pairs={{0,1},{1,2},{2,3},{4,5},{5,6},{6,7},{8,9},{9,10},{10,11},{12,13},{... | collective-permute-start | bytes 49160 | tf_op jit(solution)/shard_map/ppermute | solution.py:23
  77.7 5.4 %collective-permute-start.4 = (f32[32,128]{1,0:T(8,128)S(1)}, f32[32,128]{1,0:T(8,128)S(1)}, u32[]{:S(2)}, u32[]{:S(2)}) collective-permute-start(f32[32,128]{1,0:T(8,128)S(1)} %get-tuple-element.40), channel_id=1, source_target_pairs={{1,0},{2,1},{3,2},{5,4},{6,5},{7,6},{9,8},{10,9},{11,10},{13,12},{... | collective-permute-start | bytes 49160 | tf_op jit(solution)/shard_map/ppermute | solution.py:23
  80.2 11.6 %collective-permute-start.10 = (f32[136,512]{1,0:T(8,128)}, f32[136,512]{1,0:T(8,128)S(1)}, u32[]{:S(2)}, u32[]{:S(2)}) collective-permute-start(f32[136,512]{1,0:T(8,128)} %get-tuple-element.48), channel_id=1, source_target_pairs={{0,12},{4,0},{8,4},{12,8},{1,13},{5,1},{9,5},{13,9},{2,14},{6,2},{... | collective-permute-start | bytes 835592 | tf_op jit(solution)/shard_map/ppermute | solution.py:339
  80.3 35.9 %collective-permute-start.9 = (f32[136,512]{1,0:T(8,128)}, f32[136,512]{1,0:T(8,128)S(1)}, u32[]{:S(2)}, u32[]{:S(2)}) collective-permute-start(f32[136,512]{1,0:T(8,128)} %get-tuple-element.47), channel_id=1, source_target_pairs={{0,8},{4,12},{8,0},{12,4},{1,9},{5,13},{9,1},{13,5},{2,10},{6,14},... | collective-permute-start | bytes 835592 | tf_op jit(solution)/shard_map/ppermute | solution.py:339
  80.4 35.8 %collective-permute-start.8 = (f32[136,512]{1,0:T(8,128)S(1)}, f32[136,512]{1,0:T(8,128)S(1)}, u32[]{:S(2)}, u32[]{:S(2)}) collective-permute-start(f32[136,512]{1,0:T(8,128)S(1)} %copy-done.9), channel_id=1, source_target_pairs={{0,4},{4,8},{8,12},{12,0},{1,5},{5,9},{9,13},{13,1},{2,6},{6,10},{... | collective-permute-start | bytes 835592 | tf_op jit(solution)/shard_map/ppermute | solution.py:339
  90.3 39.6 %collective-permute-start.5 = (f32[128,512]{1,0:T(8,128)S(1)}, f32[128,512]{1,0:T(8,128)S(1)}, u32[]{:S(2)}, u32[]{:S(2)}) collective-permute-start(f32[128,512]{1,0:T(8,128)S(1)} %get-tuple-element.43), channel_id=1, source_target_pairs={{0,12},{4,0},{8,4},{12,8},{1,13},{5,1},{9,5},{13,9},{2,14},{6,2},{... | collective-permute-start | bytes 786440 | tf_op jit(solution)/shard_map/ppermute | solution.py:339
  91.2 49.2 %collective-permute-start.6 = (f32[128,512]{1,0:T(8,128)S(1)}, f32[128,512]{1,0:T(8,128)S(1)}, u32[]{:S(2)}, u32[]{:S(2)}) collective-permute-start(f32[128,512]{1,0:T(8,128)S(1)} %get-tuple-element.44), channel_id=1, source_target_pairs={{0,8},{4,12},{8,0},{12,4},{1,9},{5,13},{9,1},{13,5},{2,10},{6,14},... | collective-permute-start | bytes 786440 | tf_op jit(solution)/shard_map/ppermute | solution.py:339
  91.8 49.0 %collective-permute-start.7 = (f32[128,512]{1,0:T(8,128)S(1)}, f32[128,512]{1,0:T(8,128)S(1)}, u32[]{:S(2)}, u32[]{:S(2)}) collective-permute-start(f32[128,512]{1,0:T(8,128)S(1)} %get-tuple-element.45), channel_id=1, source_target_pairs={{0,4},{4,8},{8,12},{12,0},{1,5},{5,9},{9,13},{13,1},{2,6},{6,10},{... | collective-permute-start | bytes 786440 | tf_op jit(solution)/shard_map/ppermute | solution.py:339
  123.7 6.3 %collective-permute-start.11 = (f32[32,128]{1,0:T(8,128)S(1)}, f32[32,128]{1,0:T(8,128)S(1)}, u32[]{:S(2)}, u32[]{:S(2)}) collective-permute-start(f32[32,128]{1,0:T(8,128)S(1)} %get-tuple-element.53), channel_id=1, source_target_pairs={{0,1},{1,2},{2,3},{4,5},{5,6},{6,7},{8,9},{9,10},{10,11},{12,13},{... | collective-permute-start | bytes 49160 | tf_op jit(solution)/shard_map/ppermute | solution.py:23
  128.0 5.1 %collective-permute-start.12 = (f32[32,128]{1,0:T(8,128)S(1)}, f32[32,128]{1,0:T(8,128)S(1)}, u32[]{:S(2)}, u32[]{:S(2)}) collective-permute-start(f32[32,128]{1,0:T(8,128)S(1)} %get-tuple-element.53), channel_id=1, source_target_pairs={{1,0},{2,1},{3,2},{5,4},{6,5},{7,6},{9,8},{10,9},{11,10},{13,12},{... | collective-permute-start | bytes 49160 | tf_op jit(solution)/shard_map/ppermute | solution.py:23
  140.4 8.3 %collective-permute-start.13 = (f32[128,512]{1,0:T(8,128)S(1)}, f32[128,512]{1,0:T(8,128)S(1)}, u32[]{:S(2)}, u32[]{:S(2)}) collective-permute-start(f32[128,512]{1,0:T(8,128)S(1)} %get-tuple-element.56), channel_id=1, source_target_pairs={{0,12},{4,0},{8,4},{12,8},{1,13},{5,1},{9,5},{13,9},{2,14},{6,2},{... | collective-permute-start | bytes 786440 | tf_op jit(solution)/shard_map/ppermute | solution.py:339
  140.5 22.3 %collective-permute-start.14 = (f32[128,512]{1,0:T(8,128)S(1)}, f32[128,512]{1,0:T(8,128)S(1)}, u32[]{:S(2)}, u32[]{:S(2)}) collective-permute-start(f32[128,512]{1,0:T(8,128)S(1)} %get-tuple-element.57), channel_id=1, source_target_pairs={{0,8},{4,12},{8,0},{12,4},{1,9},{5,13},{9,1},{13,5},{2,10},{6,14},... | collective-permute-start | bytes 786440 | tf_op jit(solution)/shard_map/ppermute | solution.py:339
  140.8 22.0 %collective-permute-start.15 = (f32[128,512]{1,0:T(8,128)S(1)}, f32[128,512]{1,0:T(8,128)S(1)}, u32[]{:S(2)}, u32[]{:S(2)}) collective-permute-start(f32[128,512]{1,0:T(8,128)S(1)} %get-tuple-element.58), channel_id=1, source_target_pairs={{0,4},{4,8},{8,12},{12,0},{1,5},{5,9},{9,13},{13,1},{2,6},{6,10},{... | collective-permute-start | bytes 786440 | tf_op jit(solution)/shard_map/ppermute | solution.py:339
  (5 other events, 14.7 us)

commit v2 on v1

v2 whole, which is shorter than its diff:
```python
import functools

import jax
import jax.numpy as jnp
from jax import lax
from jax.experimental import pallas as pl
from jax.experimental.pallas import tpu as pltpu
from jax.sharding import PartitionSpec as P

NC = 16
NZ = 8
STEPS = 2
NEWT = 4
STIFF = 4


highest = lax.Precision.HIGHEST


def shifted(shard, axis, by):
    devices = lax.axis_size(axis)
    pairs = [(i, i + by) for i in range(devices) if 0 <= i + by < devices]
    return lax.ppermute(shard, axis, pairs)


def extended(block, sides, width):
    for axis, dim in sides:
        count = lax.axis_size(axis)
        forward = [(i, i + 1) for i in range(count - 1)]
        backward = [(target, source) for source, target in forward]
        low = lax.ppermute(
            lax.slice_in_dim(block, block.shape[dim] - width, None, axis=dim), axis, forward
        )
        high = lax.ppermute(lax.slice_in_dim(block, 0, width, axis=dim), axis, backward)
        block = jnp.concatenate([low, block, high], axis=dim)
    return block


def shift_down(values, axis_index):
    size_along = values.shape[axis_index]
    zero_row = jnp.zeros_like(lax.slice_in_dim(values, 0, 1, axis=axis_index))
    kept = lax.slice_in_dim(values, 0, size_along - 1, axis=axis_index)
    return jnp.concatenate([zero_row, kept], axis=axis_index)


def face_weights(face_rate, face_flag):
    flag_values = face_flag.astype(jnp.float32)
    weight_plus = face_rate * flag_values
    weight_minus = face_rate * (1.0 - flag_values)
    return (weight_plus, weight_minus)


def advance(
    values, lower_row, upper_row, lower_col, upper_col, coefficients, retard_planes, spread_planes
):
    divergence = (
        coefficients[0] * lower_row
        + coefficients[1] * upper_row
        + coefficients[2] * lower_col
        + coefficients[3] * upper_col
        - coefficients[4] * values
    )
    laplace = lower_row + upper_row + lower_col + upper_col - 4.0 * values
    return values + (divergence + spread_planes * laplace) / retard_planes


def residual_of(species, target, mixing, affinity, mineral, stiff):
    total = jnp.dot(
        mixing, species, precision=highest, preferred_element_type=jnp.float32
    ) + affinity[:, None] * jnp.tanh(species)
    if stiff:
        total = total + mineral[:, None] * jnp.tanh(2.0 * species)
    return total - target


def newton_steps(species, target, repeats, stiff, mixing, mixing_inverse, affinity, mineral):
    for iteration in range(repeats):
        update = residual_of(species, target, mixing, affinity, mineral, stiff)
        species = species - jnp.dot(
            mixing_inverse, update, precision=highest, preferred_element_type=jnp.float32
        )
    return species


def speciate(cell_block, stiff_mask, mixing, mixing_inverse, affinity, mineral):
    target = cell_block.reshape(NC, -1)
    flat_mask = stiff_mask.reshape(-1) > 0
    species = jnp.zeros_like(target)
    species = newton_steps(species, target, NEWT, False, mixing, mixing_inverse, affinity, mineral)
    stiffer = newton_steps(species, target, STIFF, True, mixing, mixing_inverse, affinity, mineral)
    species = jnp.where(flat_mask[None, :], stiffer, species)
    return species.reshape(cell_block.shape)


def by_rows(
    concentration,
    face_rate,
    face_flag,
    retardation,
    dispersion,
    mixing,
    mixing_inverse,
    affinity,
    mineral,
    stiff_mask,
):
    weight_plus, weight_minus = face_weights(face_rate, face_flag)
    rim_weights = jnp.stack([weight_plus[1, :, -1], weight_minus[1, :, -1]])
    left_rims = shifted(rim_weights, "space", 1)
    side_plus = jnp.concatenate([left_rims[0][:, None], weight_plus[1, :, :-1]], axis=1)
    side_minus = jnp.concatenate([left_rims[1][:, None], weight_minus[1, :, :-1]], axis=1)
    down_plus = shift_down(weight_plus[0], 0)
    down_minus = shift_down(weight_minus[0], 0)
    centre = down_minus + weight_plus[0] + side_minus + weight_plus[1]
    coefficients = jnp.stack([down_plus, weight_minus[0], side_plus, weight_minus[1], centre])
    retard_all = jnp.repeat(retardation, NZ)
    spread_all = jnp.repeat(dispersion, NZ)
    rows_held = stiff_mask.shape[1]
    row_start = lax.axis_index("comp") * rows_held
    cell_coefficients = lax.dynamic_slice_in_dim(coefficients, row_start, rows_held, 1)
    retard_planes = retard_all[:, None, None]
    spread_planes = spread_all[:, None, None]
    cell_block = lax.all_to_all(concentration, "comp", split_axis=1, concat_axis=0, tiled=True)
    for step_index in range(STEPS):
        padded = extended(cell_block, (("comp", 1), ("space", 2)), 1)
        cell_block = advance(
            cell_block,
            padded[:, :-2, 1:-1],
            padded[:, 2:, 1:-1],
            padded[:, 1:-1, :-2],
            padded[:, 1:-1, 2:],
            cell_coefficients,
            retard_planes,
            spread_planes,
        )
        cell_block = speciate(cell_block, stiff_mask, mixing, mixing_inverse, affinity, mineral)
    return lax.all_to_all(cell_block, "comp", split_axis=0, concat_axis=1, tiled=True)


TILE = 8
LANES = 128
VMEM_LIMIT = 24 * 1024 * 1024


def whole_spec():
    return pl.BlockSpec(memory_space=pltpu.VMEM)


def any_spec():
    return pl.BlockSpec(memory_space=pl.ANY)


def split(value):
    high = value.astype(jnp.bfloat16)
    return high, (value - high.astype(jnp.float32)).astype(jnp.bfloat16)


def gather_columns(columns, rows):
    lane_at = lax.broadcasted_iota(jnp.int32, (rows, LANES), 1)
    gathered = jnp.zeros((rows, LANES), jnp.float32)
    for lane, column in enumerate(columns):
        gathered = jnp.where(lane_at == lane, jnp.broadcast_to(column, (rows, LANES)), gathered)
    return gathered


def pack_kernel(ranks, layer, with_edges, plane_ref, mask_ref, after_ref, *refs):
    if with_edges:
        (rate_ref, flag_ref), refs = refs[:2], refs[2:]
    out_refs, refs = refs[:ranks], refs[ranks:]
    if with_edges:
        (edge_ref,), refs = refs[:1], refs[1:]
    mark_ref, low_ref, high_ref, sems = refs
    planes, rows, cols = plane_ref.shape
    layers = mask_ref.shape[0] // ranks
    block = mask_ref.shape[1]
    held = planes // mask_ref.shape[0]
    me = lax.axis_index("comp")
    copies = []

    def start(source, target):
        copies.append(pltpu.make_async_copy(source, target, sems.at[len(copies)]))
        copies[-1].start()
        return copies[-1]

    if with_edges:
        low = start(plane_ref.at[:, :, pl.ds(0, LANES)], low_ref)
        high = start(plane_ref.at[:, :, pl.ds(cols - LANES, LANES)], high_ref)
    for q, out_ref in enumerate(out_refs):
        at = lax.rem(me + q, ranks) * layers + layer
        for index in range(held):
            start(
                plane_ref.at[index * mask_ref.shape[0] + at],
                out_ref.at[pl.ds(index * rows, rows)],
            )
    for q, out_ref in enumerate(out_refs):
        at = lax.rem(me + q, ranks) * layers + layer
        mark_ref[q] = mask_ref[at].astype(jnp.float32)
        start(mark_ref.at[q], out_ref.at[pl.ds(held * rows, block)])
    if with_edges:
        low.wait()
        high.wait()
        copies = copies[2:]
        last = pl.ds(cols - LANES, LANES)
        weight_plus, weight_minus = face_weights(rate_ref[1, :, last], flag_ref[1, :, last])
        columns = [low_ref[plane][:, :1] for plane in range(planes)]
        columns += [high_ref[plane][:, LANES - 1 :] for plane in range(planes)]
        columns += [weight_plus[:, LANES - 1 :], weight_minus[:, LANES - 1 :]]
        edge_ref[...] = gather_columns(columns, rows)
    for copy in copies:
        copy.wait()


def pack(concentration, stiff_mask, layer, ranks, after, faces):
    planes, rows, cols = concentration.shape
    held = planes // NZ
    block = stiff_mask.shape[1]
    message = jax.ShapeDtypeStruct((held * rows + block, cols), jnp.float32)
    out_shape, out_specs = [message] * ranks, [any_spec()] * ranks
    if faces:
        out_shape.append(jax.ShapeDtypeStruct((rows, LANES), jnp.float32))
        out_specs.append(whole_spec())
    results = pl.pallas_call(
        functools.partial(pack_kernel, ranks, layer, bool(faces)),
        out_shape=out_shape,
        in_specs=[any_spec(), whole_spec(), any_spec()] + [whole_spec()] * len(faces),
        out_specs=out_specs,
        scratch_shapes=[
            pltpu.VMEM((ranks, block, cols), jnp.float32),
            pltpu.VMEM((planes, rows, LANES), jnp.float32),
            pltpu.VMEM((planes, rows, LANES), jnp.float32),
            pltpu.SemaphoreType.DMA((ranks * (held + 1) + 2,)),
        ],
        compiler_params=pltpu.CompilerParams(vmem_limit_bytes=VMEM_LIMIT),
        cost_estimate=pl.CostEstimate(
            flops=0, bytes_accessed=8 * ranks * held * rows * cols, transcendentals=0
        ),
        name="pack",
    )(concentration, stiff_mask, after, *faces)
    return list(results[:ranks]), results[ranks:]


def spread_kernel(ranks, mixing_ref, inverse_ref, affinity_ref, mineral_ref, *refs):
    _, first_ref, both_ref, ratio_ref = refs
    components = mixing_ref.shape[0]
    stacked = components * TILE
    held = components // ranks
    me = lax.axis_index("comp")

    def dot(left, right):
        return jnp.dot(left, right, precision=highest, preferred_element_type=jnp.float32)

    def pick(shape, stacked_dim):
        at = lax.broadcasted_iota(jnp.int32, shape, stacked_dim) // TILE
        component = lax.rem(me + ranks - at // held, ranks) * held + lax.rem(at, held)
        held_at = lax.broadcasted_iota(jnp.int32, shape, 1 - stacked_dim)
        return jnp.where(component == held_at, 1.0, 0.0)

    rows = pick((stacked, components), 0)
    cols = pick((components, stacked), 1)
    inner = (stacked, stacked)
    same = lax.rem(lax.broadcasted_iota(jnp.int32, inner, 0), TILE) == lax.rem(
        lax.broadcasted_iota(jnp.int32, inner, 1), TILE
    )

    def spread(matrix):
        return jnp.where(same, dot(dot(rows, matrix), cols), 0.0)

    inverse = inverse_ref[...]
    square = (components, components)
    unit = jnp.where(
        lax.broadcasted_iota(jnp.int32, square, 0) == lax.broadcasted_iota(jnp.int32, square, 1),
        1.0,
        0.0,
    )
    blend = unit - dot(inverse, mixing_ref[...])
    high, low = split(spread(inverse))
    first_ref[...] = jnp.concatenate([high, low, high], axis=1)
    high, low = split(
        jnp.concatenate([spread(blend), spread(-inverse * affinity_ref[...])], axis=1)
    )
    both_ref[...] = jnp.concatenate([high, low, high], axis=1)
    ratio = jnp.sum(rows * (mineral_ref[...] / affinity_ref[...]), axis=1, keepdims=True)
    ratio_ref[...] = jnp.broadcast_to(ratio, (stacked, LANES))


def spread_parameters(ranks, mixing, mixing_inverse, affinity, mineral, after):
    components = mixing.shape[0]
    stacked = components * TILE
    return pl.pallas_call(
        functools.partial(spread_kernel, ranks),
        out_shape=[
            jax.ShapeDtypeStruct((stacked, 3 * stacked), jnp.bfloat16),
            jax.ShapeDtypeStruct((stacked, 6 * stacked), jnp.bfloat16),
            jax.ShapeDtypeStruct((stacked, LANES), jnp.float32),
        ],
        in_specs=[whole_spec()] * 4 + [any_spec()],
        out_specs=[whole_spec()] * 3,
        compiler_params=pltpu.CompilerParams(vmem_limit_bytes=VMEM_LIMIT),
        cost_estimate=pl.CostEstimate(
            flops=12 * stacked * stacked * components,
            bytes_accessed=32 * stacked * stacked,
            transcendentals=0,
        ),
        name="spread_parameters",
    )(mixing, mixing_inverse, affinity.reshape(1, -1), mineral.reshape(1, -1), after)


def step_kernel(pieces, is_first, with_rim, layer, layers, spread_ref, retard_ref, *refs):
    value_refs, refs = refs[:pieces], refs[pieces:]
    (low_ref, high_ref, rate_ref, flag_ref, ratio_ref, first_ref, both_ref), refs = (
        refs[:7],
        refs[7:],
    )
    if not is_first:
        stiff_ref, refs = refs[0], refs[1:]
    out_refs, refs = refs[:pieces], refs[pieces:]
    if with_rim:
        rim_ref, refs = refs[0], refs[1:]
    if is_first:
        stiff_ref, refs = refs[0], refs[1:]
    offset_ref, species_ref, plain_ref = refs
    groups, stacked, cols = species_ref.shape
    rows = groups * TILE
    components = stacked // TILE
    held = components // pieces
    me = lax.axis_index("comp")
    ranks = [lax.rem(me + pieces - q, pieces) for q in range(pieces)]
    row_at = lax.broadcasted_iota(jnp.int32, (rows, cols), 0)
    col_at = lax.broadcasted_iota(jnp.int32, (rows, cols), 1)

    def product(weights, parts):
        highs, lows = zip(*[split(part) for part in parts])
        operand = jnp.concatenate(highs + highs + lows, axis=0)
        return jnp.dot(weights[...], operand, preferred_element_type=jnp.float32)

    weight_plus, weight_minus = face_weights(rate_ref[...], flag_ref[...])

    def column(side, at):
        return jnp.broadcast_to(side[:, at : at + 1], (rows, cols))

    def from_lower_row(value):
        return jnp.where(row_at == 0, 0.0, pltpu.roll(value, 1, 0))

    def from_upper_row(value):
        return jnp.where(row_at == rows - 1, 0.0, pltpu.roll(value, rows - 1, 0))

    def from_lower_col(value, edge):
        return jnp.where(col_at == 0, edge, pltpu.roll(value, 1, 1))

    def from_upper_col(value, edge):
        return jnp.where(col_at == cols - 1, edge, pltpu.roll(value, cols - 1, 1))

    if is_first:
        planes = held * layers * pieces
        rim_side, rim_at = low_ref[0], 2 * planes
        turn = LANES - (me * layers + layer)
        sides = []
        for rank in ranks:
            side = pltpu.roll(low_ref[jnp.bitwise_xor(me, rank)], turn, 1)
            for index in range(held):
                at = index * layers * pieces
                sides.append((side, planes + at, side, at))
    else:
        rim_side, rim_at = low_ref[...], 2 * components
        low_side, high_side = low_ref[...], high_ref[...]
        sides = [(low_side, components + at, high_side, at) for at in range(components)]
    down_plus = from_lower_row(weight_plus[0])
    down_minus = from_lower_row(weight_minus[0])
    side_plus = from_lower_col(weight_plus[1], column(rim_side, rim_at))
    side_minus = from_lower_col(weight_minus[1], column(rim_side, rim_at + 1))
    centre = down_minus + weight_plus[0] + side_minus + weight_plus[1]
    for at, (low_side, low_at, high_side, high_at) in enumerate(sides):
        q, index = divmod(at, held)
        value = value_refs[q][index * rows : (index + 1) * rows, :]
        component = ranks[q] * held + index
        spread = spread_ref[component]
        retard = 1.0 / jnp.full((rows, cols), retard_ref[component], jnp.float32)
        change = (
            (down_plus + spread) * from_lower_row(value)
            + (weight_minus[0] + spread) * from_upper_row(value)
            + (side_plus + spread) * from_lower_col(value, column(low_side, low_at))
            + (weight_minus[1] + spread) * from_upper_col(value, column(high_side, high_at))
            - (centre + 4.0 * spread) * value
        )
        value = value + change * retard
        for group in range(groups):
            offset_ref[group, at * TILE : (at + 1) * TILE, :] = value[
                group * TILE : (group + 1) * TILE
            ]

    for group in range(groups):
        offset = product(first_ref, [offset_ref[group]])
        offset_ref[group] = offset
        species_ref[group] = offset

    def plain_step(_, carry):
        for group in range(groups):
            species = species_ref[group]
            species_ref[group] = offset_ref[group] + product(both_ref, [species, jnp.tanh(species)])
        return carry

    lax.fori_loop(0, NEWT - 1, plain_step, 0)
    plain_ref[...] = species_ref[...]
    ratio = jnp.concatenate([ratio_ref[...]] * (cols // LANES), axis=1)

    def stiff_step(_, carry):
        for group in range(groups):
            species = species_ref[group]
            reaction = jnp.tanh(species) + ratio * jnp.tanh(species + species)
            species_ref[group] = offset_ref[group] + product(both_ref, [species, reaction])
        return carry

    lax.fori_loop(0, STIFF, stiff_step, 0)
    if is_first:
        block = rows // pieces
        for rank, value_ref in zip(ranks, value_refs):
            spot = pl.ds(pl.multiple_of(rank * block, TILE), block)
            stiff_ref[spot, :] = value_ref[held * rows :, :]
    for group in range(groups):
        spot = slice(group * TILE, (group + 1) * TILE)
        stiff = stiff_ref[spot, :] > 0.0
        for at in range(components):
            lane = slice(at * TILE, (at + 1) * TILE)
            start = at % held * rows + group * TILE
            out_refs[at // held][start : start + TILE, :] = jnp.where(
                stiff, species_ref[group, lane, :], plain_ref[group, lane, :]
            )
    if with_rim:
        edges = [ref[i * rows : (i + 1) * rows, :] for ref in out_refs for i in range(held)]
        columns = [value[:, :1] for value in edges] + [value[:, cols - 1 :] for value in edges]
        columns += [weight_plus[1][:, cols - 1 :], weight_minus[1][:, cols - 1 :]]
        rim_ref[...] = gather_columns(columns, rows)


def layer_step(values, stiff, low, high, shared, layer, layers, with_rim):
    dispersion, retardation, face_rate, face_flag, ratio, first, both = shared
    pieces = len(values)
    rows, cols = face_rate.shape[1:]
    groups = rows // TILE
    stacked = ratio.shape[0]
    components = stacked // TILE
    scalar = pl.BlockSpec(memory_space=pltpu.SMEM)
    plane = jax.ShapeDtypeStruct((components // pieces * rows, cols), jnp.float32)
    out_shape = [plane] * pieces
    if with_rim:
        out_shape.append(jax.ShapeDtypeStruct((rows, LANES), jnp.float32))
    if stiff is None:
        out_shape.append(jax.ShapeDtypeStruct((rows, cols), jnp.float32))
    field = pltpu.VMEM((groups, stacked, cols), jnp.float32)
    cells = rows * cols
    operands = [dispersion, retardation, *values, low, high, face_rate, face_flag]
    operands += [ratio, first, both]
    if stiff is not None:
        operands.append(stiff)
    results = pl.pallas_call(
        functools.partial(step_kernel, pieces, stiff is None, with_rim, layer, layers),
        out_shape=out_shape,
        in_specs=[scalar, scalar] + [whole_spec()] * (len(operands) - 2),
        out_specs=[whole_spec()] * len(out_shape),
        scratch_shapes=[field, field, field],
        compiler_params=pltpu.CompilerParams(vmem_limit_bytes=VMEM_LIMIT),
        cost_estimate=pl.CostEstimate(
            flops=0, bytes_accessed=8 * components * cells, transcendentals=0
        ),
        name="layer_step",
    )(*operands)
    values, results = results[:pieces], results[pieces:]
    rims = results[0] if with_rim else None
    return values, (results[-1] if stiff is None else stiff), rims


def by_layers(
    concentration,
    face_rate,
    face_flag,
    retardation,
    dispersion,
    mixing,
    mixing_inverse,
    affinity,
    mineral,
    stiff_mask,
):
    ranks = lax.axis_size("comp")
    me = lax.axis_index("comp")
    planes, rows, cols = concentration.shape
    held = planes // NZ
    layers = NZ // ranks

    def send(value, by):
        return lax.ppermute(value, "comp", [(i, (i + by) % ranks) for i in range(ranks)])

    faces = (face_rate, face_flag)
    messages, (edges,) = pack(concentration, stiff_mask, 0, ranks, face_rate, faces)
    arrived = [[send(part, q) if q else part for q, part in enumerate(messages)]]

    from_low, from_high = shifted(edges, "space", 1), shifted(edges, "space", -1)
    lane_at = lax.broadcasted_iota(jnp.int32, edges.shape, 1)
    sides = jnp.where(lane_at < planes, from_high, from_low)[None]
    span = 1
    while span < ranks:
        other = lax.ppermute(sides, "comp", [(i, i ^ span) for i in range(ranks)])
        sides = jnp.concatenate([sides, other])
        span *= 2

    first, both, ratio = spread_parameters(
        ranks, mixing, mixing_inverse, affinity, mineral, edges
    )
    shared = (dispersion, retardation, face_rate, face_flag, ratio, first, both)

    for layer in range(1, layers):
        messages, _ = pack(concentration, stiff_mask, layer, ranks, sides, ())
        arrived.append([send(part, q) if q else part for q, part in enumerate(messages)])

    result = jnp.zeros((held, NZ, rows, cols), jnp.float32)
    for layer in range(layers):
        values, stiff, low, high = arrived[layer], None, sides, sides
        for step in range(STEPS):
            last = step == STEPS - 1
            values, stiff, rims = layer_step(
                values, stiff, low, high, shared, layer, layers, not last
            )
            if not last:
                low, high = shifted(rims, "space", 1), shifted(rims, "space", -1)
        for q in range(ranks):
            piece = send(values[q], -q) if q else values[q]
            result = lax.dynamic_update_slice(
                result,
                piece.reshape(held, 1, rows, cols),
                (0, (me + q) % ranks * layers + layer, 0, 0),
            )
    return result.reshape(planes, rows, cols)


def shards(concentration, face_rate, face_flag, *parameters):
    ranks = lax.axis_size("comp")
    planes, rows, cols = concentration.shape
    whole = NZ % ranks == 0 and planes % NZ == 0 and ranks & (ranks - 1) == 0
    narrow = 2 * max(NC, planes) + 2 <= LANES
    even = rows % (ranks * TILE) == 0 and cols % LANES == 0
    plan = by_layers if whole and narrow and even else by_rows
    return plan(concentration, face_rate, face_flag, *parameters)


def solution(mesh):
    in_specs = (
        P(("real", "comp"), None, "space"),
        P(None, "real", "space"),
        P(None, "real", "space"),
        P(),
        P(),
        P(),
        P(),
        P(),
        P(),
        P(None, ("real", "comp"), "space"),
    )
    out_specs = P(("real", "comp"), None, "space")
    return jax.shard_map(shards, mesh=mesh, in_specs=in_specs, out_specs=out_specs, check_vma=False)
```

time: 165 us -> 122 us (0.74)
  local copies, waits for them, and re-layouts: 34.6 us -> 7.98 us
  blocking collectives: 22.9 us -> 0 us
  waiting for transfers between devices: 41.4 us -> 49 us
  other arithmetic: 7.5 us -> 0.02 us
  Pallas kernels: 29.5 us -> 34.8 us
  starting transfers between devices: 27.5 us -> 29.8 us
    ppermute x0 -> x2, waiting for transfers between devices: none -> 23.8 us  [by_layers(): other = lax.ppermute(sides, 'comp', [(i, i ^ span) for i in range(ranks)])]
    all_gather x1 -> x0, blocking collectives: 22.9 us -> none  [by_layers(): edges = lax.all_gather(edges, ('comp', 'space'))]
    ppermute x12, waiting for transfers between devices: 37 us -> 18.7 us  [send(): lax.ppermute(value, 'comp', [(i, (i + by) % ranks) for i in range(ranks)])]
    optimization_barrier x2 -> x0, local copies, waits for them, and re-layouts: 16.8 us -> none  [by_layers(): lax.optimization_barrier((concentration, messages[0]))]
    gather x15 -> x0, local copies, waits for them, and re-layouts: 6.61 us -> none  [the longest x2 1.56 us: by_layers(): scales = jnp.stack([dispersion[order], 1.0 / retardation[order]])]
    ppermute x4 -> x6, starting transfers between devices: 10.6 us -> 15.6 us  [shifted(): return lax.ppermute(shard, axis, pairs)]
    ppermute x12, starting transfers between devices: 16.9 us -> 12.1 us  [send(): lax.ppermute(value, 'comp', [(i, (i + by) % ranks) for i in range(ranks)])]
    pallas_call x0 -> x3, Pallas kernels: none -> 4.68 us  [the longest x2 3.87 us: pack(): pl.pallas_call(functools.partial(pack_kernel, ranks, layer, bool(faces)),...]
  transfers between devices with their start and end apart: 16 -> 20, of which waited for: 5 -> 6; matrix products, arithmetic and copies ran while one was open for 22% -> 2% of each run, Pallas kernels for 13% -> 27%
where the time goes in v2:
time: 122 us
  waiting for transfers between devices  49 us (40%)
  Pallas kernels  34.8 us (29%)
  starting transfers between devices  29.8 us (24%)
  local copies, waits for them, and re-layouts  7.98 us (7%)
    pallas_call x4, Pallas kernels, layer_step(): pl.pallas_call(functools.partial(step_kernel, pieces, stiff is None, with...  30.1 us
    ppermute x2, waiting for transfers between devices, by_layers(): other = lax.ppermute(sides, 'comp', [(i, i ^ span) for i in range(ranks)])  23.8 us
    ppermute x12, waiting for transfers between devices, send(): lax.ppermute(value, 'comp', [(i, (i + by) % ranks) for i in range(ranks)])  18.7 us
    ppermute x6, starting transfers between devices, shifted(): return lax.ppermute(shard, axis, pairs)  15.6 us
    ppermute x12, starting transfers between devices, send(): lax.ppermute(value, 'comp', [(i, (i + by) % ranks) for i in range(ranks)])  12.1 us
    ppermute x6, waiting for transfers between devices, shifted(): return lax.ppermute(shard, axis, pairs)  6.47 us
    unnamed x26, local copies, waits for them, and re-layouts  5.65 us
    pallas_call x2, Pallas kernels, pack(): pl.pallas_call(functools.partial(pack_kernel, ranks, layer, bool(faces)),...  3.87 us
  transfers between devices with their start and end apart: 20, of which 6 were waited for; matrix products, arithmetic and copies ran while one was open for 2% of the time, Pallas kernels for 27%

profile of v2, /device:TPU:1, one launch (start us, length us, event | category | flops | bytes accessed | tf_op | source)
XLA Modules:
  0.0 121.8 jit_solution(13410161180786687361)
XLA Ops:
  0.0 1.6 %copy-done = f32[32,32,512]{2,1,0:T(8,128)S(1)} copy-done((f32[32,32,512]{2,1,0:T(8,128)S(1)}, f32[32,32,512]{2,1,0:T(8,128)}, u32[]{:S(2)}) %copy-start) | copy-done | bytes 2097176
  4.4 2.2 %pack.2 = (f32[136,512]{1,0:T(8,128)S(1)}, f32[136,512]{1,0:T(8,128)S(1)}, f32[136,512]{1,0:T(8,128)S(1)}, f32[136,512]{1,0:T(8,128)S(1)}, f32[32,128]{1,0:T(8,128)S(1)}) custom-call(f32[32,32,512]{2,1,0:T(8,128)S(1)} %copy-done, s32[8,8,512]{2,1,0:T(8,128)S(1)} %copy-done.5, f32[2,32,512]{2,1,0:T(8,128)S(1)} %copy-done.1, f32[2,32,512]{2,1,0:T(8,128)S(1)} %copy-done.1, ...), custom_call_target="tpu_custom_call" | custom-call | bytes 2097152 | tf_op jit(solution)/shard_map/pack/pallas_call | solution.py:222
  6.6 2.0 %collective-permute-start.3 = (f32[32,128]{1,0:T(8,128)S(1)}, f32[32,128]{1,0:T(8,128)S(1)}, u32[]{:S(2)}, u32[]{:S(2)}) collective-permute-start(f32[32,128]{1,0:T(8,128)S(1)} %get-tuple-element.41.refs_0_), channel_id=1, source_target_pairs={{1,0},{2,1},{3,2},{5,4},{6,5},{7,6},{9,8},{10,9},{11,10},{13,12},{... | collective-permute-start | bytes 49160 | tf_op jit(solution)/shard_map/ppermute | solution.py:23
  8.5 4.5 %collective-permute-start.4 = (f32[32,128]{1,0:T(8,128)S(1)}, f32[32,128]{1,0:T(8,128)S(1)}, u32[]{:S(2)}, u32[]{:S(2)}) collective-permute-start(f32[32,128]{1,0:T(8,128)S(1)} %get-tuple-element.41.refs_0_), channel_id=1, source_target_pairs={{0,1},{1,2},{2,3},{4,5},{5,6},{6,7},{8,9},{9,10},{10,11},{12,13},{... | collective-permute-start | bytes 49160 | tf_op jit(solution)/shard_map/ppermute | solution.py:23
  15.7 1.7 %collective-permute-start.1 = (f32[136,512]{1,0:T(8,128)S(1)}, f32[136,512]{1,0:T(8,128)S(1)}, u32[]{:S(2)}, u32[]{:S(2)}) collective-permute-start(f32[136,512]{1,0:T(8,128)S(1)} %get-tuple-element.39), channel_id=1, source_target_pairs={{0,8},{4,12},{8,0},{12,4},{1,9},{5,13},{9,1},{13,5},{2,10},{6,14},... | collective-permute-start | bytes 835592 | tf_op jit(solution)/shard_map/ppermute | solution.py:491
  18.0 5.5 %collective-permute-done.5 = f32[1,32,128]{2,1,0:T(8,128)S(1)} collective-permute-done((f32[1,32,128]{2,1,0:T(8,128)S(1)}, f32[1,32,128]{2,1,0:T(8,128)S(1)}, u32[]{:S(2)}, u32[]{:S(2)}) %collective-permute-start.5) | collective-permute-done | bytes 16416 | tf_op jit(solution)/shard_map/ppermute | solution.py:502
  24.2 18.3 %collective-permute-done.6 = f32[2,32,128]{2,1,0:T(8,128)S(1)} collective-permute-done((f32[2,32,128]{2,1,0:T(8,128)S(1)}, f32[2,32,128]{2,1,0:T(8,128)S(1)}, u32[]{:S(2)}, u32[]{:S(2)}) %collective-permute-start.6) | collective-permute-done | bytes 32800 | tf_op jit(solution)/shard_map/ppermute | solution.py:502
  42.5 1.7 %pack.3 = (f32[136,512]{1,0:T(8,128)S(1)}, f32[136,512]{1,0:T(8,128)S(1)}, f32[136,512]{1,0:T(8,128)S(1)}, f32[136,512]{1,0:T(8,128)S(1)}) custom-call(f32[32,32,512]{2,1,0:T(8,128)S(1)} %copy-done, s32[8,8,512]{2,1,0:T(8,128)S(1)} %copy-done.5, f32[4,32,128]{2,1,0:T(8,128)S(1)} %pad_maximum_fusion.refs_4_.refs_5_.after_ref), custom_call_target="tpu_custom_call" | custom-call | bytes 2097152 | tf_op jit(solution)/shard_map/pack/pallas_call | solution.py:222
  44.3 1.7 %collective-permute-start.13 = (f32[136,512]{1,0:T(8,128)S(1)}, f32[136,512]{1,0:T(8,128)S(1)}, u32[]{:S(2)}, u32[]{:S(2)}) collective-permute-start(f32[136,512]{1,0:T(8,128)S(1)} %get-tuple-element.57), channel_id=1, source_target_pairs={{0,8},{4,12},{8,0},{12,4},{1,9},{5,13},{9,1},{13,5},{2,10},{6,14},... | collective-permute-start | bytes 835592 | tf_op jit(solution)/shard_map/ppermute | solution.py:491
  46.0 1.6 %collective-permute-start.14 = (f32[136,512]{1,0:T(8,128)S(1)}, f32[136,512]{1,0:T(8,128)S(1)}, u32[]{:S(2)}, u32[]{:S(2)}) collective-permute-start(f32[136,512]{1,0:T(8,128)S(1)} %get-tuple-element.58), channel_id=1, source_target_pairs={{0,12},{4,0},{8,4},{12,8},{1,13},{5,1},{9,5},{13,9},{2,14},{6,2},{... | collective-permute-start | bytes 835592 | tf_op jit(solution)/shard_map/ppermute | solution.py:491
  48.4 7.5 %layer_step.4 = (f32[128,512]{1,0:T(8,128)S(1)}, f32[128,512]{1,0:T(8,128)S(1)}, f32[128,512]{1,0:T(8,128)S(1)}, f32[128,512]{1,0:T(8,128)S(1)}, f32[32,128]{1,0:T(8,128)S(1)}, /*index=5*/f32[32,512]{1,0:T(8,128)S(1)}) custom-call(f32[16]{0:T(128)S(1)} %copy-done.6, f32[16]{0:T(128)S(1)} %copy-done.7, f32[136,512]{1,0:T(8,128)S(1)} %get-tuple-element.37.refs_0_, ...), custom_call_target="tpu_custom_call" | custom-call | bytes 2097152 | tf_op jit(solution)/shard_map/layer_step/pallas_call | solution.py:455
  55.9 2.7 %collective-permute-start.7 = (f32[32,128]{1,0:T(8,128)S(1)}, f32[32,128]{1,0:T(8,128)S(1)}, u32[]{:S(2)}, u32[]{:S(2)}) collective-permute-start(f32[32,128]{1,0:T(8,128)S(1)} %get-tuple-element.49), channel_id=1, source_target_pairs={{0,1},{1,2},{2,3},{4,5},{5,6},{6,7},{8,9},{9,10},{10,11},{12,13},{... | collective-permute-start | bytes 49160 | tf_op jit(solution)/shard_map/ppermute | solution.py:23
  58.6 1.9 %collective-permute-start.8 = (f32[32,128]{1,0:T(8,128)S(1)}, f32[32,128]{1,0:T(8,128)S(1)}, u32[]{:S(2)}, u32[]{:S(2)}) collective-permute-start(f32[32,128]{1,0:T(8,128)S(1)} %get-tuple-element.49), channel_id=1, source_target_pairs={{1,0},{2,1},{3,2},{5,4},{6,5},{7,6},{9,8},{10,9},{11,10},{13,12},{... | collective-permute-start | bytes 49160 | tf_op jit(solution)/shard_map/ppermute | solution.py:23
  60.5 3.4 %collective-permute-done.8.refs_5_ = f32[32,128]{1,0:T(8,128)S(1)} collective-permute-done((f32[32,128]{1,0:T(8,128)S(1)}, f32[32,128]{1,0:T(8,128)S(1)}, u32[]{:S(2)}, u32[]{:S(2)}) %collective-permute-start.8) | collective-permute-done | bytes 16416 | tf_op jit(solution)/shard_map/ppermute | solution.py:23
  64.0 7.9 %layer_step.5 = (f32[128,512]{1,0:T(8,128)S(1)}, f32[128,512]{1,0:T(8,128)}, f32[128,512]{1,0:T(8,128)S(1)}, f32[128,512]{1,0:T(8,128)S(1)}) custom-call(f32[16]{0:T(128)S(1)} %copy-done.6, f32[16]{0:T(128)S(1)} %copy-done.7, f32[128,512]{1,0:T(8,128)S(1)} %get-tuple-element.45.refs_0_, f32[128,512]{1,0:T(8,128)S(1)} %get-tuple-element.46.refs_1_, ...), custom_call_target="tpu_custom_call" | custom-call | bytes 2097152 | tf_op jit(solution)/shard_map/layer_step/pallas_call | solution.py:455
  73.6 1.5 %collective-permute-start.11 = (f32[128,512]{1,0:T(8,128)S(1)}, f32[128,512]{1,0:T(8,128)S(1)}, u32[]{:S(2)}, u32[]{:S(2)}) collective-permute-start(f32[128,512]{1,0:T(8,128)S(1)} %get-tuple-element.54), channel_id=1, source_target_pairs={{0,4},{4,8},{8,12},{12,0},{1,5},{5,9},{9,13},{13,1},{2,6},{6,10},{... | collective-permute-start | bytes 786440 | tf_op jit(solution)/shard_map/ppermute | solution.py:491
  75.1 7.4 %layer_step.6 = (f32[128,512]{1,0:T(8,128)S(1)}, f32[128,512]{1,0:T(8,128)S(1)}, f32[128,512]{1,0:T(8,128)S(1)}, f32[128,512]{1,0:T(8,128)S(1)}, f32[32,128]{1,0:T(8,128)S(1)}, /*index=5*/f32[32,512]{1,0:T(8,128)S(1)}) custom-call(f32[16]{0:T(128)S(1)} %copy-done.6, f32[16]{0:T(128)S(1)} %copy-done.7, f32[136,512]{1,0:T(8,128)S(1)} %get-tuple-element.55.refs_0_, ...), custom_call_target="tpu_custom_call" | custom-call | bytes 2097152 | tf_op jit(solution)/shard_map/layer_step/pallas_call | solution.py:455
  82.5 2.5 %collective-permute-start.15 = (f32[32,128]{1,0:T(8,128)S(1)}, f32[32,128]{1,0:T(8,128)S(1)}, u32[]{:S(2)}, u32[]{:S(2)}) collective-permute-start(f32[32,128]{1,0:T(8,128)S(1)} %get-tuple-element.63), channel_id=1, source_target_pairs={{0,1},{1,2},{2,3},{4,5},{5,6},{6,7},{8,9},{9,10},{10,11},{12,13},{... | collective-permute-start | bytes 49160 | tf_op jit(solution)/shard_map/ppermute | solution.py:23
  85.0 2.1 %collective-permute-start.16 = (f32[32,128]{1,0:T(8,128)S(1)}, f32[32,128]{1,0:T(8,128)S(1)}, u32[]{:S(2)}, u32[]{:S(2)}) collective-permute-start(f32[32,128]{1,0:T(8,128)S(1)} %get-tuple-element.63), channel_id=1, source_target_pairs={{1,0},{2,1},{3,2},{5,4},{6,5},{7,6},{9,8},{10,9},{11,10},{13,12},{... | collective-permute-start | bytes 49160 | tf_op jit(solution)/shard_map/ppermute | solution.py:23
  87.4 3.0 %collective-permute-done.16.refs_5_ = f32[32,128]{1,0:T(8,128)S(1)} collective-permute-done((f32[32,128]{1,0:T(8,128)S(1)}, f32[32,128]{1,0:T(8,128)S(1)}, u32[]{:S(2)}, u32[]{:S(2)}) %collective-permute-start.16) | collective-permute-done | bytes 16416 | tf_op jit(solution)/shard_map/ppermute | solution.py:23
  90.5 7.3 %layer_step.7 = (f32[128,512]{1,0:T(8,128)S(1)}, f32[128,512]{1,0:T(8,128)S(1)}, f32[128,512]{1,0:T(8,128)S(1)}, f32[128,512]{1,0:T(8,128)S(1)}) custom-call(f32[16]{0:T(128)S(1)} %copy-done.6, f32[16]{0:T(128)S(1)} %copy-done.7, f32[128,512]{1,0:T(8,128)S(1)} %get-tuple-element.59.refs_0_, f32[128,512]{1,0:T(8,128)S(1)} %get-tuple-element.60.refs_1_, ...), custom_call_target="tpu_custom_call" | custom-call | bytes 2097152 | tf_op jit(solution)/shard_map/layer_step/pallas_call | solution.py:455
  97.7 1.6 %collective-permute-start.17 = (f32[128,512]{1,0:T(8,128)S(1)}, f32[128,512]{1,0:T(8,128)S(1)}, u32[]{:S(2)}, u32[]{:S(2)}) collective-permute-start(f32[128,512]{1,0:T(8,128)S(1)} %get-tuple-element.66), channel_id=1, source_target_pairs={{0,12},{4,0},{8,4},{12,8},{1,13},{5,1},{9,5},{13,9},{2,14},{6,2},{... | collective-permute-start | bytes 786440 | tf_op jit(solution)/shard_map/ppermute | solution.py:491
  101.8 3.8 %collective-permute-done.17 = f32[128,512]{1,0:T(8,128)S(1)} collective-permute-done((f32[128,512]{1,0:T(8,128)S(1)}, f32[128,512]{1,0:T(8,128)S(1)}, u32[]{:S(2)}, u32[]{:S(2)}) %collective-permute-start.17) | collective-permute-done | bytes 262176 | tf_op jit(solution)/shard_map/ppermute | solution.py:491
  105.6 14.8 %collective-permute-done.18 = f32[128,512]{1,0:T(8,128)S(1)} collective-permute-done((f32[128,512]{1,0:T(8,128)S(1)}, f32[128,512]{1,0:T(8,128)S(1)}, u32[]{:S(2)}, u32[]{:S(2)}) %collective-permute-start.18) | collective-permute-done | bytes 262176 | tf_op jit(solution)/shard_map/ppermute | solution.py:491
  (62 shorter events, 13.4 us)
Async XLA Ops:
  4.3 44.1 %copy-start.2 = (f32[2,32,512]{2,1,0:T(8,128)S(1)}, f32[2,32,512]{2,1,0:T(8,128)}, u32[]{:S(2)}) copy-start(f32[2,32,512]{2,1,0:T(8,128)} %refs_6_.7) | copy-start | bytes 393220
  4.3 44.1 %copy-start.4 = (s32[2,32,512]{2,1,0:T(8,128)S(1)}, s32[2,32,512]{2,1,0:T(8,128)}, u32[]{:S(2)}) copy-start(s32[2,32,512]{2,1,0:T(8,128)} %refs_7_.7) | copy-start | bytes 393220
  4.3 44.1 %copy-start.6 = (f32[16]{0:T(128)S(1)}, f32[16]{0:T(128)}, u32[]{:S(2)}) copy-start(f32[16]{0:T(128)} %spread_ref.7) | copy-start | bytes 196
  4.3 44.1 %copy-start.7 = (f32[16]{0:T(128)S(1)}, f32[16]{0:T(128)}, u32[]{:S(2)}) copy-start(f32[16]{0:T(128)} %retard_ref.7) | copy-start | bytes 196
  6.6 7.8 %collective-permute-start.3 = (f32[32,128]{1,0:T(8,128)S(1)}, f32[32,128]{1,0:T(8,128)S(1)}, u32[]{:S(2)}, u32[]{:S(2)}) collective-permute-start(f32[32,128]{1,0:T(8,128)S(1)} %get-tuple-element.41.refs_0_), channel_id=1, source_target_pairs={{1,0},{2,1},{3,2},{5,4},{6,5},{7,6},{9,8},{10,9},{11,10},{13,12},{... | collective-permute-start | bytes 49160 | tf_op jit(solution)/shard_map/ppermute | solution.py:23
  8.5 5.8 %collective-permute-start.4 = (f32[32,128]{1,0:T(8,128)S(1)}, f32[32,128]{1,0:T(8,128)S(1)}, u32[]{:S(2)}, u32[]{:S(2)}) collective-permute-start(f32[32,128]{1,0:T(8,128)S(1)} %get-tuple-element.41.refs_0_), channel_id=1, source_target_pairs={{0,1},{1,2},{2,3},{4,5},{5,6},{6,7},{8,9},{9,10},{10,11},{12,13},{... | collective-permute-start | bytes 49160 | tf_op jit(solution)/shard_map/ppermute | solution.py:23
  13.0 33.0 %collective-permute-start = (f32[136,512]{1,0:T(8,128)S(1)}, f32[136,512]{1,0:T(8,128)S(1)}, u32[]{:S(2)}, u32[]{:S(2)}) collective-permute-start(f32[136,512]{1,0:T(8,128)S(1)} %get-tuple-element.38), channel_id=1, source_target_pairs={{0,4},{4,8},{8,12},{12,0},{1,5},{5,9},{9,13},{13,1},{2,6},{6,10},{... | collective-permute-start | bytes 835592 | tf_op jit(solution)/shard_map/ppermute | solution.py:491
  14.4 9.1 %collective-permute-start.5 = (f32[1,32,128]{2,1,0:T(8,128)S(1)}, f32[1,32,128]{2,1,0:T(8,128)S(1)}, u32[]{:S(2)}, u32[]{:S(2)}) collective-permute-start(f32[1,32,128]{2,1,0:T(8,128)S(1)} %select_bitcast_fusion), channel_id=1, source_target_pairs={{0,4},{4,0},{8,12},{12,8},{1,5},{5,1},{9,13},{13,9},{2,6},{6,2},{1... | collective-permute-start | bytes 49160 | tf_op jit(solution)/shard_map/ppermute | solution.py:502
  15.7 32.6 %collective-permute-start.1 = (f32[136,512]{1,0:T(8,128)S(1)}, f32[136,512]{1,0:T(8,128)S(1)}, u32[]{:S(2)}, u32[]{:S(2)}) collective-permute-start(f32[136,512]{1,0:T(8,128)S(1)} %get-tuple-element.39), channel_id=1, source_target_pairs={{0,8},{4,12},{8,0},{12,4},{1,9},{5,13},{9,1},{13,5},{2,10},{6,14},... | collective-permute-start | bytes 835592 | tf_op jit(solution)/shard_map/ppermute | solution.py:491
  17.5 30.9 %collective-permute-start.2 = (f32[136,512]{1,0:T(8,128)S(1)}, f32[136,512]{1,0:T(8,128)S(1)}, u32[]{:S(2)}, u32[]{:S(2)}) collective-permute-start(f32[136,512]{1,0:T(8,128)S(1)} %get-tuple-element.40), channel_id=1, source_target_pairs={{0,12},{4,0},{8,4},{12,8},{1,13},{5,1},{9,5},{13,9},{2,14},{6,2},{... | collective-permute-start | bytes 835592 | tf_op jit(solution)/shard_map/ppermute | solution.py:491
  23.5 19.0 %collective-permute-start.6 = (f32[2,32,128]{2,1,0:T(8,128)S(1)}, f32[2,32,128]{2,1,0:T(8,128)S(1)}, u32[]{:S(2)}, u32[]{:S(2)}) collective-permute-start(f32[2,32,128]{2,1,0:T(8,128)S(1)} %pad_maximum_fusion.1), channel_id=1, source_target_pairs={{0,8},{4,12},{8,0},{12,4},{1,9},{5,13},{9,1},{13,5},{2,10},{6,14},... | collective-permute-start | bytes 98312 | tf_op jit(solution)/shard_map/ppermute | solution.py:502
  44.2 29.4 %collective-permute-start.12 = (f32[136,512]{1,0:T(8,128)S(1)}, f32[136,512]{1,0:T(8,128)S(1)}, u32[]{:S(2)}, u32[]{:S(2)}) collective-permute-start(f32[136,512]{1,0:T(8,128)S(1)} %get-tuple-element.56), channel_id=1, source_target_pairs={{0,4},{4,8},{8,12},{12,0},{1,5},{5,9},{9,13},{13,1},{2,6},{6,10},{... | collective-permute-start | bytes 835592 | tf_op jit(solution)/shard_map/ppermute | solution.py:491
  44.3 30.8 %collective-permute-start.13 = (f32[136,512]{1,0:T(8,128)S(1)}, f32[136,512]{1,0:T(8,128)S(1)}, u32[]{:S(2)}, u32[]{:S(2)}) collective-permute-start(f32[136,512]{1,0:T(8,128)S(1)} %get-tuple-element.57), channel_id=1, source_target_pairs={{0,8},{4,12},{8,0},{12,4},{1,9},{5,13},{9,1},{13,5},{2,10},{6,14},... | collective-permute-start | bytes 835592 | tf_op jit(solution)/shard_map/ppermute | solution.py:491
  46.0 29.1 %collective-permute-start.14 = (f32[136,512]{1,0:T(8,128)S(1)}, f32[136,512]{1,0:T(8,128)S(1)}, u32[]{:S(2)}, u32[]{:S(2)}) collective-permute-start(f32[136,512]{1,0:T(8,128)S(1)} %get-tuple-element.58), channel_id=1, source_target_pairs={{0,12},{4,0},{8,4},{12,8},{1,13},{5,1},{9,5},{13,9},{2,14},{6,2},{... | collective-permute-start | bytes 835592 | tf_op jit(solution)/shard_map/ppermute | solution.py:491
  55.9 4.6 %collective-permute-start.7 = (f32[32,128]{1,0:T(8,128)S(1)}, f32[32,128]{1,0:T(8,128)S(1)}, u32[]{:S(2)}, u32[]{:S(2)}) collective-permute-start(f32[32,128]{1,0:T(8,128)S(1)} %get-tuple-element.49), channel_id=1, source_target_pairs={{0,1},{1,2},{2,3},{4,5},{5,6},{6,7},{8,9},{9,10},{10,11},{12,13},{... | collective-permute-start | bytes 49160 | tf_op jit(solution)/shard_map/ppermute | solution.py:23
  58.6 5.4 %collective-permute-start.8 = (f32[32,128]{1,0:T(8,128)S(1)}, f32[32,128]{1,0:T(8,128)S(1)}, u32[]{:S(2)}, u32[]{:S(2)}) collective-permute-start(f32[32,128]{1,0:T(8,128)S(1)} %get-tuple-element.49), channel_id=1, source_target_pairs={{1,0},{2,1},{3,2},{5,4},{6,5},{7,6},{9,8},{10,9},{11,10},{13,12},{... | collective-permute-start | bytes 49160 | tf_op jit(solution)/shard_map/ppermute | solution.py:23
  71.9 27.5 %collective-permute-start.9 = (f32[128,512]{1,0:T(8,128)}, f32[128,512]{1,0:T(8,128)}, u32[]{:S(2)}, u32[]{:S(2)}) collective-permute-start(f32[128,512]{1,0:T(8,128)} %get-tuple-element.52), channel_id=1, source_target_pairs={{0,12},{4,0},{8,4},{12,8},{1,13},{5,1},{9,5},{13,9},{2,14},{6,2},{... | collective-permute-start | bytes 786440 | tf_op jit(solution)/shard_map/ppermute | solution.py:491
  72.2 28.5 %collective-permute-start.10 = (f32[128,512]{1,0:T(8,128)S(1)}, f32[128,512]{1,0:T(8,128)}, u32[]{:S(2)}, u32[]{:S(2)}) collective-permute-start(f32[128,512]{1,0:T(8,128)S(1)} %get-tuple-element.53), channel_id=1, source_target_pairs={{0,8},{4,12},{8,0},{12,4},{1,9},{5,13},{9,1},{13,5},{2,10},{6,14},... | collective-permute-start | bytes 786440 | tf_op jit(solution)/shard_map/ppermute | solution.py:491
  73.6 28.1 %collective-permute-start.11 = (f32[128,512]{1,0:T(8,128)S(1)}, f32[128,512]{1,0:T(8,128)S(1)}, u32[]{:S(2)}, u32[]{:S(2)}) collective-permute-start(f32[128,512]{1,0:T(8,128)S(1)} %get-tuple-element.54), channel_id=1, source_target_pairs={{0,4},{4,8},{8,12},{12,0},{1,5},{5,9},{9,13},{13,1},{2,6},{6,10},{... | collective-permute-start | bytes 786440 | tf_op jit(solution)/shard_map/ppermute | solution.py:491
  82.5 4.9 %collective-permute-start.15 = (f32[32,128]{1,0:T(8,128)S(1)}, f32[32,128]{1,0:T(8,128)S(1)}, u32[]{:S(2)}, u32[]{:S(2)}) collective-permute-start(f32[32,128]{1,0:T(8,128)S(1)} %get-tuple-element.63), channel_id=1, source_target_pairs={{0,1},{1,2},{2,3},{4,5},{5,6},{6,7},{8,9},{9,10},{10,11},{12,13},{... | collective-permute-start | bytes 49160 | tf_op jit(solution)/shard_map/ppermute | solution.py:23
  85.0 5.5 %collective-permute-start.16 = (f32[32,128]{1,0:T(8,128)S(1)}, f32[32,128]{1,0:T(8,128)S(1)}, u32[]{:S(2)}, u32[]{:S(2)}) collective-permute-start(f32[32,128]{1,0:T(8,128)S(1)} %get-tuple-element.63), channel_id=1, source_target_pairs={{1,0},{2,1},{3,2},{5,4},{6,5},{7,6},{9,8},{10,9},{11,10},{13,12},{... | collective-permute-start | bytes 49160 | tf_op jit(solution)/shard_map/ppermute | solution.py:23
  97.7 7.8 %collective-permute-start.17 = (f32[128,512]{1,0:T(8,128)S(1)}, f32[128,512]{1,0:T(8,128)S(1)}, u32[]{:S(2)}, u32[]{:S(2)}) collective-permute-start(f32[128,512]{1,0:T(8,128)S(1)} %get-tuple-element.66), channel_id=1, source_target_pairs={{0,12},{4,0},{8,4},{12,8},{1,13},{5,1},{9,5},{13,9},{2,14},{6,2},{... | collective-permute-start | bytes 786440 | tf_op jit(solution)/shard_map/ppermute | solution.py:491
  99.4 21.1 %collective-permute-start.18 = (f32[128,512]{1,0:T(8,128)S(1)}, f32[128,512]{1,0:T(8,128)S(1)}, u32[]{:S(2)}, u32[]{:S(2)}) collective-permute-start(f32[128,512]{1,0:T(8,128)S(1)} %get-tuple-element.67), channel_id=1, source_target_pairs={{0,8},{4,12},{8,0},{12,4},{1,9},{5,13},{9,1},{13,5},{2,10},{6,14},... | collective-permute-start | bytes 786440 | tf_op jit(solution)/shard_map/ppermute | solution.py:491
  99.4 21.1 %collective-permute-start.19 = (f32[128,512]{1,0:T(8,128)S(1)}, f32[128,512]{1,0:T(8,128)S(1)}, u32[]{:S(2)}, u32[]{:S(2)}) collective-permute-start(f32[128,512]{1,0:T(8,128)S(1)} %get-tuple-element.68), channel_id=1, source_target_pairs={{0,4},{4,8},{8,12},{12,0},{1,5},{5,9},{9,13},{13,1},{2,6},{6,10},{... | collective-permute-start | bytes 786440 | tf_op jit(solution)/shard_map/ppermute | solution.py:491
  (9 other events, 178.6 us)

commit v3 on v2

--- a/solution.py
+++ b/solution.py
@@ -140,6 +140,7 @@
 TILE = 8
 LANES = 128
 VMEM_LIMIT = 24 * 1024 * 1024
+MOST_VMEM = 60 * 1024 * 1024
 
 
 def whole_spec():
@@ -148,6 +149,10 @@
 
 def any_spec():
     return pl.BlockSpec(memory_space=pl.ANY)
+
+
+def hbm_spec():
+    return pl.BlockSpec(memory_space=pltpu.HBM)
 
 
 def split(value):
@@ -163,80 +168,130 @@
     return gathered
 
 
-def pack_kernel(ranks, layer, with_edges, plane_ref, mask_ref, after_ref, *refs):
-    if with_edges:
+def bands(rows, cols):
+    return -(-rows * LANES // (TILE * cols)) * TILE
+
+
+def band_spots(rows, cols):
+    wide = cols // LANES
+    return [
+        (group, group // wide * TILE, group % wide * LANES) for group in range(rows // TILE)
+    ]
+
+
+def pack_kernel(layer, plane_ref, mask_ref, *refs):
+    if layer:
+        (low_ref, high_ref), refs = refs[:2], refs[2:]
+    else:
         (rate_ref, flag_ref), refs = refs[:2], refs[2:]
-    out_refs, refs = refs[:ranks], refs[ranks:]
-    if with_edges:
-        (edge_ref,), refs = refs[:1], refs[1:]
-    mark_ref, low_ref, high_ref, sems = refs
+    refs, scratch = refs[:-6], refs[-6:]
+    mask_part, mark_ref, first_ref, last_ref, mask_sems, sems = scratch
+    if layer:
+        out_refs = refs
+    else:
+        out_refs, edge_ref = refs[:-1], refs[-1]
+    ranks = len(out_refs)
     planes, rows, cols = plane_ref.shape
-    layers = mask_ref.shape[0] // ranks
-    block = mask_ref.shape[1]
-    held = planes // mask_ref.shape[0]
+    levels, block, _ = mask_ref.shape
+    held = planes // levels
     me = lax.axis_index("comp")
-    copies = []
+    copies, masks = [], []
 
     def start(source, target):
         copies.append(pltpu.make_async_copy(source, target, sems.at[len(copies)]))
         copies[-1].start()
-        return copies[-1]
-
-    if with_edges:
-        low = start(plane_ref.at[:, :, pl.ds(0, LANES)], low_ref)
-        high = start(plane_ref.at[:, :, pl.ds(cols - LANES, LANES)], high_ref)
+
     for q, out_ref in enumerate(out_refs):
-        at = lax.rem(me + q, ranks) * layers + layer
+        at = lax.rem(me + q, ranks) * (levels // ranks) + layer
+        masks.append(pltpu.make_async_copy(mask_ref.at[at], mask_part.at[q], mask_sems.at[q]))
+        masks[-1].start()
         for index in range(held):
-            start(
-                plane_ref.at[index * mask_ref.shape[0] + at],
-                out_ref.at[pl.ds(index * rows, rows)],
-            )
+            start(plane_ref.at[index * levels + at], out_ref.at[pl.ds(index * rows, rows)])
+    if layer:
+        lane_at = lax.broadcasted_iota(jnp.int32, (rows, LANES), 1)
+        sides = jnp.where(lane_at < planes, high_ref[...], low_ref[...])
+        for group, row, lane in band_spots(rows, cols):
+            part = sides[group * TILE : (group + 1) * TILE]
+            for q in range(ranks):
+                mark_ref[q, block + row : block + row + TILE, lane : lane + LANES] = part
+    else:
+        start(plane_ref.at[:, :, pl.ds(0, LANES)], first_ref)
+        start(plane_ref.at[:, :, pl.ds(cols - LANES, LANES)], last_ref)
     for q, out_ref in enumerate(out_refs):
-        at = lax.rem(me + q, ranks) * layers + layer
-        mark_ref[q] = mask_ref[at].astype(jnp.float32)
-        start(mark_ref.at[q], out_ref.at[pl.ds(held * rows, block)])
-    if with_edges:
-        low.wait()
-        high.wait()
-        copies = copies[2:]
-        last = pl.ds(cols - LANES, LANES)
-        weight_plus, weight_minus = face_weights(rate_ref[1, :, last], flag_ref[1, :, last])
-        columns = [low_ref[plane][:, :1] for plane in range(planes)]
-        columns += [high_ref[plane][:, LANES - 1 :] for plane in range(planes)]
+        masks[q].wait()
+        mark_ref[q, :block, :] = mask_part[q].astype(jnp.float32)
+        count = mark_ref.shape[1]
+        start(mark_ref.at[q], out_ref.at[pl.ds(held * rows, count)])
+    for copy in copies:
+        copy.wait()
+    if not layer:
+        end = slice(cols - LANES, cols)
+        weight_plus, weight_minus = face_weights(rate_ref[1, :, end], flag_ref[1, :, end])
+        columns = [first_ref[plane][:, :1] for plane in range(planes)]
+        columns += [last_ref[plane][:, LANES - 1 :] for plane in range(planes)]
         columns += [weight_plus[:, LANES - 1 :], weight_minus[:, LANES - 1 :]]
         edge_ref[...] = gather_columns(columns, rows)
-    for copy in copies:
-        copy.wait()
-
-
-def pack(concentration, stiff_mask, layer, ranks, after, faces):
+
+
+def pack(concentration, stiff_mask, layer, ranks, others):
     planes, rows, cols = concentration.shape
     held = planes // NZ
     block = stiff_mask.shape[1]
-    message = jax.ShapeDtypeStruct((held * rows + block, cols), jnp.float32)
+    extra = block + (bands(rows, cols) if layer else 0)
+    message = jax.ShapeDtypeStruct((held * rows + extra, cols), jnp.float32)
     out_shape, out_specs = [message] * ranks, [any_spec()] * ranks
-    if faces:
+    if not layer:
         out_shape.append(jax.ShapeDtypeStruct((rows, LANES), jnp.float32))
         out_specs.append(whole_spec())
     results = pl.pallas_call(
-        functools.partial(pack_kernel, ranks, layer, bool(faces)),
+        functools.partial(pack_kernel, layer),
         out_shape=out_shape,
-        in_specs=[any_spec(), whole_spec(), any_spec()] + [whole_spec()] * len(faces),
+        in_specs=[hbm_spec()] * 2 + [whole_spec()] * 2,
         out_specs=out_specs,
         scratch_shapes=[
-            pltpu.VMEM((ranks, block, cols), jnp.float32),
+            pltpu.VMEM((ranks, block, cols), jnp.int32),
+            pltpu.VMEM((ranks, extra, cols), jnp.float32),
             pltpu.VMEM((planes, rows, LANES), jnp.float32),
             pltpu.VMEM((planes, rows, LANES), jnp.float32),
+            pltpu.SemaphoreType.DMA((ranks,)),
             pltpu.SemaphoreType.DMA((ranks * (held + 1) + 2,)),
         ],
+        compiler_params=pltpu.CompilerParams(vmem_limit_bytes=VMEM_LIMIT if layer else MOST_VMEM),
+        cost_estimate=pl.CostEstimate(flops=0, bytes_accessed=0, transcendentals=0),
+        name="pack",
+    )(concentration, stiff_mask, *others)
+    return list(results[:ranks]), results[ranks:]
+
+
+def edges_kernel(held, *refs):
+    half = (len(refs) - 4) // 2
+    low_refs, high_refs, (rate_ref, flag_ref, _, out_ref) = refs[:half], refs[half:-4], refs[-4:]
+    rows = rate_ref.shape[1]
+    weight_plus, weight_minus = face_weights(rate_ref[1], flag_ref[1])
+    spots = [slice(index * rows, (index + 1) * rows) for index in range(held)]
+    columns = [ref[spot, :][:, :1] for ref in low_refs for spot in spots]
+    columns += [ref[spot, :][:, LANES - 1 :] for ref in high_refs for spot in spots]
+    columns += [weight_plus[:, LANES - 1 :], weight_minus[:, LANES - 1 :]]
+    out_ref[...] = gather_columns(columns, rows)
+
+
+def edges_of(values, face_rate, face_flag, after):
+    rows, cols = face_rate.shape[1:]
+    last = cols // LANES - 1
+    size = values[0].shape[0]
+    low = pl.BlockSpec((size, LANES), lambda i: (0, 0))
+    high = pl.BlockSpec((size, LANES), lambda i: (0, last))
+    face = pl.BlockSpec((2, rows, LANES), lambda i: (0, 0, last))
+    return pl.pallas_call(
+        functools.partial(edges_kernel, size // rows),
+        grid=(1,),
+        out_shape=jax.ShapeDtypeStruct((rows, LANES), jnp.float32),
+        in_specs=[low] * len(values) + [high] * len(values) + [face, face, hbm_spec()],
+        out_specs=pl.BlockSpec((rows, LANES), lambda i: (0, 0)),
         compiler_params=pltpu.CompilerParams(vmem_limit_bytes=VMEM_LIMIT),
-        cost_estimate=pl.CostEstimate(
-            flops=0, bytes_accessed=8 * ranks * held * rows * cols, transcendentals=0
-        ),
-        name="pack",
-    )(concentration, stiff_mask, after, *faces)
-    return list(results[:ranks]), results[ranks:]
+        cost_estimate=pl.CostEstimate(flops=0, bytes_accessed=0, transcendentals=0),
+        name="edges",
+    )(*values, *values, face_rate, face_flag, after)
 
 
 def spread_kernel(ranks, mixing_ref, inverse_ref, affinity_ref, mineral_ref, *refs):
@@ -296,16 +351,12 @@
         in_specs=[whole_spec()] * 4 + [any_spec()],
         out_specs=[whole_spec()] * 3,
         compiler_params=pltpu.CompilerParams(vmem_limit_bytes=VMEM_LIMIT),
-        cost_estimate=pl.CostEstimate(
-            flops=12 * stacked * stacked * components,
-            bytes_accessed=32 * stacked * stacked,
-            transcendentals=0,
-        ),
+        cost_estimate=pl.CostEstimate(flops=0, bytes_accessed=0, transcendentals=0),
         name="spread_parameters",
     )(mixing, mixing_inverse, affinity.reshape(1, -1), mineral.reshape(1, -1), after)
 
 
-def step_kernel(pieces, is_first, with_rim, layer, layers, spread_ref, retard_ref, *refs):
+def step_kernel(pieces, layer, is_first, with_rim, spread_ref, retard_ref, *refs):
     value_refs, refs = refs[:pieces], refs[pieces:]
     (low_ref, high_ref, rate_ref, flag_ref, ratio_ref, first_ref, both_ref), refs = (
         refs[:7],
@@ -350,24 +401,31 @@
     def from_upper_col(value, edge):
         return jnp.where(col_at == cols - 1, edge, pltpu.roll(value, cols - 1, 1))
 
-    if is_first:
-        planes = held * layers * pieces
-        rim_side, rim_at = low_ref[0], 2 * planes
-        turn = LANES - (me * layers + layer)
+    block = rows // pieces
+    low_side, high_side = low_ref[...], high_ref[...]
+    rim_at = 2 * components
+    sides = [(low_side, components + at, high_side, at) for at in range(components)]
+    if is_first and layer:
         sides = []
-        for rank in ranks:
-            side = pltpu.roll(low_ref[jnp.bitwise_xor(me, rank)], turn, 1)
+        rim_at = 2 * held * NZ
+        turn = LANES - (me * (NZ // pieces) + layer)
+        for value_ref in value_refs:
+            start = held * rows + block
+            side = jnp.concatenate(
+                [
+                    value_ref[start + row : start + row + TILE, lane : lane + LANES]
+                    for _, row, lane in band_spots(rows, cols)
+                ]
+            )
+            if not sides:
+                low_side = side
+            side = pltpu.roll(side, turn, 1)
             for index in range(held):
-                at = index * layers * pieces
-                sides.append((side, planes + at, side, at))
-    else:
-        rim_side, rim_at = low_ref[...], 2 * components
-        low_side, high_side = low_ref[...], high_ref[...]
-        sides = [(low_side, components + at, high_side, at) for at in range(components)]
+                sides.append((side, (held + index) * NZ, side, index * NZ))
     down_plus = from_lower_row(weight_plus[0])
     down_minus = from_lower_row(weight_minus[0])
-    side_plus = from_lower_col(weight_plus[1], column(rim_side, rim_at))
-    side_minus = from_lower_col(weight_minus[1], column(rim_side, rim_at + 1))
+    side_plus = from_lower_col(weight_plus[1], column(low_side, rim_at))
+    side_minus = from_lower_col(weight_minus[1], column(low_side, rim_at + 1))
     centre = down_minus + weight_plus[0] + side_minus + weight_plus[1]
     for at, (low_side, low_at, high_side, high_at) in enumerate(sides):
         q, index = divmod(at, held)
@@ -412,10 +470,9 @@
 
     lax.fori_loop(0, STIFF, stiff_step, 0)
     if is_first:
-        block = rows // pieces
         for rank, value_ref in zip(ranks, value_refs):
             spot = pl.ds(pl.multiple_of(rank * block, TILE), block)
-            stiff_ref[spot, :] = value_ref[held * rows :, :]
+            stiff_ref[spot, :] = value_ref[held * rows : held * rows + block, :]
     for group in range(groups):
         spot = slice(group * TILE, (group + 1) * TILE)
         stiff = stiff_ref[spot, :] > 0.0
@@ -432,7 +489,7 @@
         rim_ref[...] = gather_columns(columns, rows)
 
 
-def layer_step(values, stiff, low, high, shared, layer, layers, with_rim):
+def layer_step(values, stiff, low, high, shared, layer, with_rim):
     dispersion, retardation, face_rate, face_flag, ratio, first, both = shared
     pieces = len(values)
     rows, cols = face_rate.shape[1:]
@@ -453,15 +510,13 @@
     if stiff is not None:
         operands.append(stiff)
     results = pl.pallas_call(
-        functools.partial(step_kernel, pieces, stiff is None, with_rim, layer, layers),
+        functools.partial(step_kernel, pieces, layer, stiff is None, with_rim),
         out_shape=out_shape,
         in_specs=[scalar, scalar] + [whole_spec()] * (len(operands) - 2),
         out_specs=[whole_spec()] * len(out_shape),
         scratch_shapes=[field, field, field],
         compiler_params=pltpu.CompilerParams(vmem_limit_bytes=VMEM_LIMIT),
-        cost_estimate=pl.CostEstimate(
-            flops=0, bytes_accessed=8 * components * cells, transcendentals=0
-        ),
+        cost_estimate=pl.CostEstimate(flops=0, bytes_accessed=0, transcendentals=0),
         name="layer_step",
     )(*operands)
     values, results = results[:pieces], results[pieces:]
@@ -490,38 +545,29 @@
     def send(value, by):
         return lax.ppermute(value, "comp", [(i, (i + by) % ranks) for i in range(ranks)])
 
-    faces = (face_rate, face_flag)
-    messages, (edges,) = pack(concentration, stiff_mask, 0, ranks, face_rate, faces)
-    arrived = [[send(part, q) if q else part for q, part in enumerate(messages)]]
-
-    from_low, from_high = shifted(edges, "space", 1), shifted(edges, "space", -1)
-    lane_at = lax.broadcasted_iota(jnp.int32, edges.shape, 1)
-    sides = jnp.where(lane_at < planes, from_high, from_low)[None]
-    span = 1
-    while span < ranks:
-        other = lax.ppermute(sides, "comp", [(i, i ^ span) for i in range(ranks)])
-        sides = jnp.concatenate([sides, other])
-        span *= 2
-
-    first, both, ratio = spread_parameters(
-        ranks, mixing, mixing_inverse, affinity, mineral, edges
-    )
+    arrived, others = [], (face_rate, face_flag)
+    for layer in range(layers):
+        messages, edges = pack(concentration, stiff_mask, layer, ranks, others)
+        arrived.append([send(part, q) if q else part for q, part in enumerate(messages)])
+        if edges:
+            others = (shifted(edges[0], "space", 1), shifted(edges[0], "space", -1))
+        after = messages[0]
+
+    first, both, ratio = spread_parameters(ranks, mixing, mixing_inverse, affinity, mineral, after)
     shared = (dispersion, retardation, face_rate, face_flag, ratio, first, both)
-
-    for layer in range(1, layers):
-        messages, _ = pack(concentration, stiff_mask, layer, ranks, sides, ())
-        arrived.append([send(part, q) if q else part for q, part in enumerate(messages)])
 
     result = jnp.zeros((held, NZ, rows, cols), jnp.float32)
     for layer in range(layers):
-        values, stiff, low, high = arrived[layer], None, sides, sides
+        values, stiff = arrived[layer], None
+        rims = None if layer else edges_of(values, face_rate, face_flag, after)
         for step in range(STEPS):
-            last = step == STEPS - 1
+            if rims is None:
+                low, high = others
+            else:
+                low, high = shifted(rims, "space", 1), shifted(rims, "space", -1)
             values, stiff, rims = layer_step(
-                values, stiff, low, high, shared, layer, layers, not last
+                values, stiff, low, high, shared, layer, step < STEPS - 1
             )
-            if not last:
-                low, high = shifted(rims, "space", 1), shifted(rims, "space", -1)
         for q in range(ranks):
             piece = send(values[q], -q) if q else values[q]
             result = lax.dynamic_update_slice(
@@ -535,7 +581,7 @@
 def shards(concentration, face_rate, face_flag, *parameters):
     ranks = lax.axis_size("comp")
     planes, rows, cols = concentration.shape
-    whole = NZ % ranks == 0 and planes % NZ == 0 and ranks & (ranks - 1) == 0
+    whole = NZ % ranks == 0 and planes % NZ == 0
     narrow = 2 * max(NC, planes) + 2 <= LANES
     even = rows % (ranks * TILE) == 0 and cols % LANES == 0
     plan = by_layers if whole and narrow and even else by_rows

time: 122 us -> 160 us (1.31)
  Pallas kernels: 34.8 us -> 68.2 us
  starting transfers between devices: 29.8 us -> 56.7 us
  waiting for transfers between devices: 49 us -> 30.8 us
  local copies, waits for them, and re-layouts: 7.98 us -> 3.69 us
    pallas_call x6 -> x7, Pallas kernels: 34 us -> 67.4 us  [the longest x2 37.1 us: pack(): pl.pallas_call(functools.partial(pack_kernel, layer), out_shape=out_shape...]
    ppermute x2 -> x0, waiting for transfers between devices: 23.8 us -> none  [by_layers(): other = lax.ppermute(sides, 'comp', [(i, i ^ span) for i in range(ranks)])]
    ppermute x6 -> x8, starting transfers between devices: 15.6 us -> 30.2 us  [shifted(): return lax.ppermute(shard, axis, pairs)]
    ppermute x12, starting transfers between devices: 12.1 us -> 26.5 us  [send(): lax.ppermute(value, 'comp', [(i, (i + by) % ranks) for i in range(ranks)])]
    unnamed x26 -> x24, local copies, waits for them, and re-layouts: 5.65 us -> 1.36 us
    ppermute x12, waiting for transfers between devices: 18.7 us -> 22 us  [send(): lax.ppermute(value, 'comp', [(i, (i + by) % ranks) for i in range(ranks)])]
    ppermute x6 -> x8, waiting for transfers between devices: 6.47 us -> 8.79 us  [shifted(): return lax.ppermute(shard, axis, pairs)]
    ppermute x2 -> x0, starting transfers between devices: 2.08 us -> none  [by_layers(): other = lax.ppermute(sides, 'comp', [(i, i ^ span) for i in range(ranks)])]
  transfers between devices with their start and end apart: 20 -> 20, of which waited for: 6 -> 6; matrix products, arithmetic and copies ran while one was open for 2% -> 1% of each run, Pallas kernels for 27% -> 21%
where the time goes in v3:
time: 160 us
  Pallas kernels  68.2 us (43%)
  starting transfers between devices  56.7 us (35%)
  waiting for transfers between devices  30.8 us (19%)
  local copies, waits for them, and re-layouts  3.69 us (2%)
    pallas_call x2, Pallas kernels, pack(): pl.pallas_call(functools.partial(pack_kernel, layer), out_shape=out_shape...  37.1 us
    ppermute x8, starting transfers between devices, shifted(): return lax.ppermute(shard, axis, pairs)  30.2 us
    pallas_call x4, Pallas kernels, layer_step(): pl.pallas_call(functools.partial(step_kernel, pieces, layer, stiff is Non...  30.1 us
    ppermute x12, starting transfers between devices, send(): lax.ppermute(value, 'comp', [(i, (i + by) % ranks) for i in range(ranks)])  26.5 us
    ppermute x12, waiting for transfers between devices, send(): lax.ppermute(value, 'comp', [(i, (i + by) % ranks) for i in range(ranks)])  22 us
    ppermute x8, waiting for transfers between devices, shifted(): return lax.ppermute(shard, axis, pairs)  8.79 us
  transfers between devices with their start and end apart: 20, of which 6 were waited for; matrix products, arithmetic and copies ran while one was open for 1% of the time, Pallas kernels for 21%

profile of v3, /device:TPU:1, one launch (start us, length us, event | category | flops | bytes accessed | tf_op | source)
XLA Modules:
  0.0 159.7 jit_solution(13180980340780166452)
XLA Ops:
  0.0 35.2 %pack.2 = (f32[136,512]{1,0:T(8,128)}, f32[136,512]{1,0:T(8,128)}, f32[136,512]{1,0:T(8,128)}, f32[136,512]{1,0:T(8,128)}, f32[32,128]{1,0:T(8,128)}) custom-call(f32[32,32,512]{2,1,0:T(8,128)} %plane_ref.3, s32[8,8,512]{2,1,0:T(8,128)} %mask_ref.3, f32[2,32,512]{2,1,0:T(8,128)} %refs_6_.7, s32[2,32,512]{2,1,0:T(8,128)} %refs_7_.7), custom_call_target="tpu_custom_call" | custom-call | tf_op jit(solution)/shard_map/pack/pallas_call | solution.py:246
  35.2 2.2 %collective-permute-start = (f32[136,512]{1,0:T(8,128)}, f32[136,512]{1,0:T(8,128)S(1)}, u32[]{:S(2)}, u32[]{:S(2)}) collective-permute-start(f32[136,512]{1,0:T(8,128)} %get-tuple-element.38), channel_id=1, source_target_pairs={{0,4},{4,8},{8,12},{12,0},{1,5},{5,9},{9,13},{13,1},{2,6},{6,10},{... | collective-permute-start | bytes 835592 | tf_op jit(solution)/shard_map/ppermute | solution.py:546
  37.4 2.3 %collective-permute-start.1 = (f32[136,512]{1,0:T(8,128)}, f32[136,512]{1,0:T(8,128)S(1)}, u32[]{:S(2)}, u32[]{:S(2)}) collective-permute-start(f32[136,512]{1,0:T(8,128)} %get-tuple-element.39), channel_id=1, source_target_pairs={{0,8},{4,12},{8,0},{12,4},{1,9},{5,13},{9,1},{13,5},{2,10},{6,14},... | collective-permute-start | bytes 835592 | tf_op jit(solution)/shard_map/ppermute | solution.py:546
  40.8 4.7 %collective-permute-start.3 = (f32[32,128]{1,0:T(8,128)}, f32[32,128]{1,0:T(8,128)S(1)}, u32[]{:S(2)}, u32[]{:S(2)}) collective-permute-start(f32[32,128]{1,0:T(8,128)} %get-tuple-element.41), channel_id=1, source_target_pairs={{0,1},{1,2},{2,3},{4,5},{5,6},{6,7},{8,9},{9,10},{10,11},{12,13},{... | collective-permute-start | bytes 49160 | tf_op jit(solution)/shard_map/ppermute | solution.py:23
  45.5 1.9 %collective-permute-start.4 = (f32[32,128]{1,0:T(8,128)}, f32[32,128]{1,0:T(8,128)S(1)}, u32[]{:S(2)}, u32[]{:S(2)}) collective-permute-start(f32[32,128]{1,0:T(8,128)} %get-tuple-element.41), channel_id=1, source_target_pairs={{1,0},{2,1},{3,2},{5,4},{6,5},{7,6},{9,8},{10,9},{11,10},{13,12},{... | collective-permute-start | bytes 49160 | tf_op jit(solution)/shard_map/ppermute | solution.py:23
  47.4 3.6 %collective-permute-done.4.refs_1_.refs_5_ = f32[32,128]{1,0:T(8,128)S(1)} collective-permute-done((f32[32,128]{1,0:T(8,128)}, f32[32,128]{1,0:T(8,128)S(1)}, u32[]{:S(2)}, u32[]{:S(2)}) %collective-permute-start.4) | collective-permute-done | bytes 16416 | tf_op jit(solution)/shard_map/ppermute | solution.py:23
  51.0 1.9 %pack.3 = (f32[144,512]{1,0:T(8,128)S(1)}, f32[144,512]{1,0:T(8,128)S(1)}, f32[144,512]{1,0:T(8,128)S(1)}, f32[144,512]{1,0:T(8,128)S(1)}) custom-call(f32[32,32,512]{2,1,0:T(8,128)S(1)} %copy-done, s32[8,8,512]{2,1,0:T(8,128)S(1)} %copy-done.4, f32[32,128]{1,0:T(8,128)S(1)} %collective-permute-done.3.refs_0_.refs_4_, ...), custom_call_target="tpu_custom_call" | custom-call | tf_op jit(solution)/shard_map/pack/pallas_call | solution.py:246
  53.4 2.9 %collective-permute-start.14 = (f32[144,512]{1,0:T(8,128)S(1)}, f32[144,512]{1,0:T(8,128)S(1)}, u32[]{:S(2)}, u32[]{:S(2)}) collective-permute-start(f32[144,512]{1,0:T(8,128)S(1)} %get-tuple-element.58), channel_id=1, source_target_pairs={{0,12},{4,0},{8,4},{12,8},{1,13},{5,1},{9,5},{13,9},{2,14},{6,2},{... | collective-permute-start | bytes 884744 | tf_op jit(solution)/shard_map/ppermute | solution.py:546
  56.3 3.1 %collective-permute-done.1.refs_2_.refs_6_ = f32[136,512]{1,0:T(8,128)S(1)} collective-permute-done((f32[136,512]{1,0:T(8,128)}, f32[136,512]{1,0:T(8,128)S(1)}, u32[]{:S(2)}, u32[]{:S(2)}) %collective-permute-start.1) | collective-permute-done | bytes 278560 | tf_op jit(solution)/shard_map/ppermute | solution.py:546
  59.6 4.1 %collective-permute-start.5 = (f32[32,128]{1,0:T(8,128)S(1)}, f32[32,128]{1,0:T(8,128)S(1)}, u32[]{:S(2)}, u32[]{:S(2)}) collective-permute-start(f32[32,128]{1,0:T(8,128)S(1)} %edges.1), channel_id=1, source_target_pairs={{0,1},{1,2},{2,3},{4,5},{5,6},{6,7},{8,9},{9,10},{10,11},{12,13},{... | collective-permute-start | bytes 49160 | tf_op jit(solution)/shard_map/ppermute | solution.py:23
  63.7 10.9 %collective-permute-start.6 = (f32[32,128]{1,0:T(8,128)S(1)}, f32[32,128]{1,0:T(8,128)S(1)}, u32[]{:S(2)}, u32[]{:S(2)}) collective-permute-start(f32[32,128]{1,0:T(8,128)S(1)} %edges.1), channel_id=1, source_target_pairs={{1,0},{2,1},{3,2},{5,4},{6,5},{7,6},{9,8},{10,9},{11,10},{13,12},{... | collective-permute-start | bytes 49160 | tf_op jit(solution)/shard_map/ppermute | solution.py:23
  75.6 7.4 %layer_step.4 = (f32[128,512]{1,0:T(8,128)S(1)}, f32[128,512]{1,0:T(8,128)S(1)}, f32[128,512]{1,0:T(8,128)S(1)}, f32[128,512]{1,0:T(8,128)S(1)}, f32[32,128]{1,0:T(8,128)S(1)}, /*index=5*/f32[32,512]{1,0:T(8,128)S(1)}) custom-call(f32[16]{0:T(128)S(1)} %copy-done.5, f32[16]{0:T(128)S(1)} %copy-done.6, f32[136,512]{1,0:T(8,128)S(1)} %copy-done.3, ...), custom_call_target="tpu_custom_call" | custom-call | tf_op jit(solution)/shard_map/layer_step/pallas_call | solution.py:512
  83.0 1.9 %collective-permute-start.7 = (f32[32,128]{1,0:T(8,128)S(1)}, f32[32,128]{1,0:T(8,128)S(1)}, u32[]{:S(2)}, u32[]{:S(2)}) collective-permute-start(f32[32,128]{1,0:T(8,128)S(1)} %get-tuple-element.50), channel_id=1, source_target_pairs={{0,1},{1,2},{2,3},{4,5},{5,6},{6,7},{8,9},{9,10},{10,11},{12,13},{... | collective-permute-start | bytes 49160 | tf_op jit(solution)/shard_map/ppermute | solution.py:23
  84.9 2.4 %collective-permute-start.8 = (f32[32,128]{1,0:T(8,128)S(1)}, f32[32,128]{1,0:T(8,128)S(1)}, u32[]{:S(2)}, u32[]{:S(2)}) collective-permute-start(f32[32,128]{1,0:T(8,128)S(1)} %get-tuple-element.50), channel_id=1, source_target_pairs={{1,0},{2,1},{3,2},{5,4},{6,5},{7,6},{9,8},{10,9},{11,10},{13,12},{... | collective-permute-start | bytes 49160 | tf_op jit(solution)/shard_map/ppermute | solution.py:23
  87.3 2.6 %collective-permute-done.8.refs_5_ = f32[32,128]{1,0:T(8,128)S(1)} collective-permute-done((f32[32,128]{1,0:T(8,128)S(1)}, f32[32,128]{1,0:T(8,128)S(1)}, u32[]{:S(2)}, u32[]{:S(2)}) %collective-permute-start.8) | collective-permute-done | bytes 16416 | tf_op jit(solution)/shard_map/ppermute | solution.py:23
  90.0 8.0 %layer_step.5 = (f32[128,512]{1,0:T(8,128)S(1)}, f32[128,512]{1,0:T(8,128)}, f32[128,512]{1,0:T(8,128)}, f32[128,512]{1,0:T(8,128)S(1)}) custom-call(f32[16]{0:T(128)S(1)} %copy-done.5, f32[16]{0:T(128)S(1)} %copy-done.6, f32[128,512]{1,0:T(8,128)S(1)} %get-tuple-element.46.refs_0_, f32[128,512]{1,0:T(8,128)S(1)} %get-tuple-element.47.refs_1_, ...), custom_call_target="tpu_custom_call" | custom-call | tf_op jit(solution)/shard_map/layer_step/pallas_call | solution.py:512
  98.0 13.4 %collective-permute-start.9 = (f32[128,512]{1,0:T(8,128)}, f32[128,512]{1,0:T(8,128)}, u32[]{:S(2)}, u32[]{:S(2)}) collective-permute-start(f32[128,512]{1,0:T(8,128)} %get-tuple-element.53), channel_id=1, source_target_pairs={{0,12},{4,0},{8,4},{12,8},{1,13},{5,1},{9,5},{13,9},{2,14},{6,2},{... | collective-permute-start | bytes 786440 | tf_op jit(solution)/shard_map/ppermute | solution.py:546
  111.4 7.4 %layer_step.6 = (f32[128,512]{1,0:T(8,128)S(1)}, f32[128,512]{1,0:T(8,128)S(1)}, f32[128,512]{1,0:T(8,128)S(1)}, f32[128,512]{1,0:T(8,128)S(1)}, f32[32,128]{1,0:T(8,128)S(1)}, /*index=5*/f32[32,512]{1,0:T(8,128)S(1)}) custom-call(f32[16]{0:T(128)S(1)} %copy-done.5, f32[16]{0:T(128)S(1)} %copy-done.6, f32[144,512]{1,0:T(8,128)S(1)} %get-tuple-element.42.refs_10_.refs_0_, ...), custom_call_target="tpu_custom_call" | custom-call | tf_op jit(solution)/shard_map/layer_step/pallas_call | solution.py:512
  118.8 2.2 %collective-permute-start.15 = (f32[32,128]{1,0:T(8,128)S(1)}, f32[32,128]{1,0:T(8,128)S(1)}, u32[]{:S(2)}, u32[]{:S(2)}) collective-permute-start(f32[32,128]{1,0:T(8,128)S(1)} %get-tuple-element.63), channel_id=1, source_target_pairs={{0,1},{1,2},{2,3},{4,5},{5,6},{6,7},{8,9},{9,10},{10,11},{12,13},{... | collective-permute-start | bytes 49160 | tf_op jit(solution)/shard_map/ppermute | solution.py:23
  121.0 2.1 %collective-permute-start.16 = (f32[32,128]{1,0:T(8,128)S(1)}, f32[32,128]{1,0:T(8,128)S(1)}, u32[]{:S(2)}, u32[]{:S(2)}) collective-permute-start(f32[32,128]{1,0:T(8,128)S(1)} %get-tuple-element.63), channel_id=1, source_target_pairs={{1,0},{2,1},{3,2},{5,4},{6,5},{7,6},{9,8},{10,9},{11,10},{13,12},{... | collective-permute-start | bytes 49160 | tf_op jit(solution)/shard_map/ppermute | solution.py:23
  123.9 2.5 %collective-permute-done.16.refs_5_ = f32[32,128]{1,0:T(8,128)S(1)} collective-permute-done((f32[32,128]{1,0:T(8,128)S(1)}, f32[32,128]{1,0:T(8,128)S(1)}, u32[]{:S(2)}, u32[]{:S(2)}) %collective-permute-start.16) | collective-permute-done | bytes 16416 | tf_op jit(solution)/shard_map/ppermute | solution.py:23
  126.5 7.2 %layer_step.7 = (f32[128,512]{1,0:T(8,128)S(1)}, f32[128,512]{1,0:T(8,128)S(1)}, f32[128,512]{1,0:T(8,128)S(1)}, f32[128,512]{1,0:T(8,128)S(1)}) custom-call(f32[16]{0:T(128)S(1)} %copy-done.5, f32[16]{0:T(128)S(1)} %copy-done.6, f32[128,512]{1,0:T(8,128)S(1)} %get-tuple-element.59.refs_0_, f32[128,512]{1,0:T(8,128)S(1)} %get-tuple-element.60.refs_1_, ...), custom_call_target="tpu_custom_call" | custom-call | tf_op jit(solution)/shard_map/layer_step/pallas_call | solution.py:512
  134.3 1.8 %collective-permute-start.18 = (f32[128,512]{1,0:T(8,128)S(1)}, f32[128,512]{1,0:T(8,128)S(1)}, u32[]{:S(2)}, u32[]{:S(2)}) collective-permute-start(f32[128,512]{1,0:T(8,128)S(1)} %get-tuple-element.67), channel_id=1, source_target_pairs={{0,8},{4,12},{8,0},{12,4},{1,9},{5,13},{9,1},{13,5},{2,10},{6,14},... | collective-permute-start | bytes 786440 | tf_op jit(solution)/shard_map/ppermute | solution.py:546
  140.4 18.0 %collective-permute-done.18 = f32[128,512]{1,0:T(8,128)S(1)} collective-permute-done((f32[128,512]{1,0:T(8,128)S(1)}, f32[128,512]{1,0:T(8,128)S(1)}, u32[]{:S(2)}, u32[]{:S(2)}) %collective-permute-start.18) | collective-permute-done | bytes 262176 | tf_op jit(solution)/shard_map/ppermute | solution.py:546
  (57 shorter events, 9.6 us)
Async XLA Ops:
  0.0 51.0 %copy-start = (f32[32,32,512]{2,1,0:T(8,128)S(1)}, f32[32,32,512]{2,1,0:T(8,128)}, u32[]{:S(2)}) copy-start(f32[32,32,512]{2,1,0:T(8,128)} %plane_ref.3) | copy-start | bytes 6291460
  0.0 59.4 %copy-start.1 = (f32[2,32,512]{2,1,0:T(8,128)S(1)}, f32[2,32,512]{2,1,0:T(8,128)}, u32[]{:S(2)}) copy-start(f32[2,32,512]{2,1,0:T(8,128)} %refs_6_.7) | copy-start | bytes 393220
  0.0 59.4 %copy-start.2 = (s32[2,32,512]{2,1,0:T(8,128)S(1)}, s32[2,32,512]{2,1,0:T(8,128)}, u32[]{:S(2)}) copy-start(s32[2,32,512]{2,1,0:T(8,128)} %refs_7_.7) | copy-start | bytes 393220
  0.0 51.0 %copy-start.4 = (s32[8,8,512]{2,1,0:T(8,128)S(1)}, s32[8,8,512]{2,1,0:T(8,128)}, u32[]{:S(2)}) copy-start(s32[8,8,512]{2,1,0:T(8,128)} %mask_ref.3) | copy-start | bytes 393220
  35.2 18.2 %collective-permute-start = (f32[136,512]{1,0:T(8,128)}, f32[136,512]{1,0:T(8,128)S(1)}, u32[]{:S(2)}, u32[]{:S(2)}) collective-permute-start(f32[136,512]{1,0:T(8,128)} %get-tuple-element.38), channel_id=1, source_target_pairs={{0,4},{4,8},{8,12},{12,0},{1,5},{5,9},{9,13},{13,1},{2,6},{6,10},{... | collective-permute-start | bytes 835592 | tf_op jit(solution)/shard_map/ppermute | solution.py:546
  37.4 22.0 %collective-permute-start.1 = (f32[136,512]{1,0:T(8,128)}, f32[136,512]{1,0:T(8,128)S(1)}, u32[]{:S(2)}, u32[]{:S(2)}) collective-permute-start(f32[136,512]{1,0:T(8,128)} %get-tuple-element.39), channel_id=1, source_target_pairs={{0,8},{4,12},{8,0},{12,4},{1,9},{5,13},{9,1},{13,5},{2,10},{6,14},... | collective-permute-start | bytes 835592 | tf_op jit(solution)/shard_map/ppermute | solution.py:546
  39.7 19.7 %collective-permute-start.2 = (f32[136,512]{1,0:T(8,128)}, f32[136,512]{1,0:T(8,128)S(1)}, u32[]{:S(2)}, u32[]{:S(2)}) collective-permute-start(f32[136,512]{1,0:T(8,128)} %get-tuple-element.40), channel_id=1, source_target_pairs={{0,12},{4,0},{8,4},{12,8},{1,13},{5,1},{9,5},{13,9},{2,14},{6,2},{... | collective-permute-start | bytes 835592 | tf_op jit(solution)/shard_map/ppermute | solution.py:546
  40.8 6.6 %collective-permute-start.3 = (f32[32,128]{1,0:T(8,128)}, f32[32,128]{1,0:T(8,128)S(1)}, u32[]{:S(2)}, u32[]{:S(2)}) collective-permute-start(f32[32,128]{1,0:T(8,128)} %get-tuple-element.41), channel_id=1, source_target_pairs={{0,1},{1,2},{2,3},{4,5},{5,6},{6,7},{8,9},{9,10},{10,11},{12,13},{... | collective-permute-start | bytes 49160 | tf_op jit(solution)/shard_map/ppermute | solution.py:23
  45.5 5.6 %collective-permute-start.4 = (f32[32,128]{1,0:T(8,128)}, f32[32,128]{1,0:T(8,128)S(1)}, u32[]{:S(2)}, u32[]{:S(2)}) collective-permute-start(f32[32,128]{1,0:T(8,128)} %get-tuple-element.41), channel_id=1, source_target_pairs={{1,0},{2,1},{3,2},{5,4},{6,5},{7,6},{9,8},{10,9},{11,10},{13,12},{... | collective-permute-start | bytes 49160 | tf_op jit(solution)/shard_map/ppermute | solution.py:23
  53.0 58.4 %collective-permute-start.12 = (f32[144,512]{1,0:T(8,128)S(1)}, f32[144,512]{1,0:T(8,128)S(1)}, u32[]{:S(2)}, u32[]{:S(2)}) collective-permute-start(f32[144,512]{1,0:T(8,128)S(1)} %get-tuple-element.56), channel_id=1, source_target_pairs={{0,4},{4,8},{8,12},{12,0},{1,5},{5,9},{9,13},{13,1},{2,6},{6,10},{... | collective-permute-start | bytes 884744 | tf_op jit(solution)/shard_map/ppermute | solution.py:546
  53.4 57.9 %collective-permute-start.13 = (f32[144,512]{1,0:T(8,128)S(1)}, f32[144,512]{1,0:T(8,128)S(1)}, u32[]{:S(2)}, u32[]{:S(2)}) collective-permute-start(f32[144,512]{1,0:T(8,128)S(1)} %get-tuple-element.57), channel_id=1, source_target_pairs={{0,8},{4,12},{8,0},{12,4},{1,9},{5,13},{9,1},{13,5},{2,10},{6,14},... | collective-permute-start | bytes 884744 | tf_op jit(solution)/shard_map/ppermute | solution.py:546
  53.4 57.9 %collective-permute-start.14 = (f32[144,512]{1,0:T(8,128)S(1)}, f32[144,512]{1,0:T(8,128)S(1)}, u32[]{:S(2)}, u32[]{:S(2)}) collective-permute-start(f32[144,512]{1,0:T(8,128)S(1)} %get-tuple-element.58), channel_id=1, source_target_pairs={{0,12},{4,0},{8,4},{12,8},{1,13},{5,1},{9,5},{13,9},{2,14},{6,2},{... | collective-permute-start | bytes 884744 | tf_op jit(solution)/shard_map/ppermute | solution.py:546
  59.6 15.9 %collective-permute-start.5 = (f32[32,128]{1,0:T(8,128)S(1)}, f32[32,128]{1,0:T(8,128)S(1)}, u32[]{:S(2)}, u32[]{:S(2)}) collective-permute-start(f32[32,128]{1,0:T(8,128)S(1)} %edges.1), channel_id=1, source_target_pairs={{0,1},{1,2},{2,3},{4,5},{5,6},{6,7},{8,9},{9,10},{10,11},{12,13},{... | collective-permute-start | bytes 49160 | tf_op jit(solution)/shard_map/ppermute | solution.py:23
  63.7 11.8 %collective-permute-start.6 = (f32[32,128]{1,0:T(8,128)S(1)}, f32[32,128]{1,0:T(8,128)S(1)}, u32[]{:S(2)}, u32[]{:S(2)}) collective-permute-start(f32[32,128]{1,0:T(8,128)S(1)} %edges.1), channel_id=1, source_target_pairs={{1,0},{2,1},{3,2},{5,4},{6,5},{7,6},{9,8},{10,9},{11,10},{13,12},{... | collective-permute-start | bytes 49160 | tf_op jit(solution)/shard_map/ppermute | solution.py:23
  83.0 4.3 %collective-permute-start.7 = (f32[32,128]{1,0:T(8,128)S(1)}, f32[32,128]{1,0:T(8,128)S(1)}, u32[]{:S(2)}, u32[]{:S(2)}) collective-permute-start(f32[32,128]{1,0:T(8,128)S(1)} %get-tuple-element.50), channel_id=1, source_target_pairs={{0,1},{1,2},{2,3},{4,5},{5,6},{6,7},{8,9},{9,10},{10,11},{12,13},{... | collective-permute-start | bytes 49160 | tf_op jit(solution)/shard_map/ppermute | solution.py:23
  84.9 5.1 %collective-permute-start.8 = (f32[32,128]{1,0:T(8,128)S(1)}, f32[32,128]{1,0:T(8,128)S(1)}, u32[]{:S(2)}, u32[]{:S(2)}) collective-permute-start(f32[32,128]{1,0:T(8,128)S(1)} %get-tuple-element.50), channel_id=1, source_target_pairs={{1,0},{2,1},{3,2},{5,4},{6,5},{7,6},{9,8},{10,9},{11,10},{13,12},{... | collective-permute-start | bytes 49160 | tf_op jit(solution)/shard_map/ppermute | solution.py:23
  98.0 38.1 %collective-permute-start.9 = (f32[128,512]{1,0:T(8,128)}, f32[128,512]{1,0:T(8,128)}, u32[]{:S(2)}, u32[]{:S(2)}) collective-permute-start(f32[128,512]{1,0:T(8,128)} %get-tuple-element.53), channel_id=1, source_target_pairs={{0,12},{4,0},{8,4},{12,8},{1,13},{5,1},{9,5},{13,9},{2,14},{6,2},{... | collective-permute-start | bytes 786440 | tf_op jit(solution)/shard_map/ppermute | solution.py:546
  111.3 27.1 %collective-permute-start.10 = (f32[128,512]{1,0:T(8,128)}, f32[128,512]{1,0:T(8,128)}, u32[]{:S(2)}, u32[]{:S(2)}) collective-permute-start(f32[128,512]{1,0:T(8,128)} %get-tuple-element.54), channel_id=1, source_target_pairs={{0,8},{4,12},{8,0},{12,4},{1,9},{5,13},{9,1},{13,5},{2,10},{6,14},... | collective-permute-start | bytes 786440 | tf_op jit(solution)/shard_map/ppermute | solution.py:546
  118.8 5.1 %collective-permute-start.15 = (f32[32,128]{1,0:T(8,128)S(1)}, f32[32,128]{1,0:T(8,128)S(1)}, u32[]{:S(2)}, u32[]{:S(2)}) collective-permute-start(f32[32,128]{1,0:T(8,128)S(1)} %get-tuple-element.63), channel_id=1, source_target_pairs={{0,1},{1,2},{2,3},{4,5},{5,6},{6,7},{8,9},{9,10},{10,11},{12,13},{... | collective-permute-start | bytes 49160 | tf_op jit(solution)/shard_map/ppermute | solution.py:23
  121.0 5.5 %collective-permute-start.16 = (f32[32,128]{1,0:T(8,128)S(1)}, f32[32,128]{1,0:T(8,128)S(1)}, u32[]{:S(2)}, u32[]{:S(2)}) collective-permute-start(f32[32,128]{1,0:T(8,128)S(1)} %get-tuple-element.63), channel_id=1, source_target_pairs={{1,0},{2,1},{3,2},{5,4},{6,5},{7,6},{9,8},{10,9},{11,10},{13,12},{... | collective-permute-start | bytes 49160 | tf_op jit(solution)/shard_map/ppermute | solution.py:23
  123.1 16.3 %collective-permute-start.11 = (f32[128,512]{1,0:T(8,128)S(1)}, f32[128,512]{1,0:T(8,128)S(1)}, u32[]{:S(2)}, u32[]{:S(2)}) collective-permute-start(f32[128,512]{1,0:T(8,128)S(1)} %get-tuple-element.55), channel_id=1, source_target_pairs={{0,4},{4,8},{8,12},{12,0},{1,5},{5,9},{9,13},{13,1},{2,6},{6,10},{... | collective-permute-start | bytes 786440 | tf_op jit(solution)/shard_map/ppermute | solution.py:546
  133.7 6.6 %collective-permute-start.17 = (f32[128,512]{1,0:T(8,128)S(1)}, f32[128,512]{1,0:T(8,128)S(1)}, u32[]{:S(2)}, u32[]{:S(2)}) collective-permute-start(f32[128,512]{1,0:T(8,128)S(1)} %get-tuple-element.66), channel_id=1, source_target_pairs={{0,12},{4,0},{8,4},{12,8},{1,13},{5,1},{9,5},{13,9},{2,14},{6,2},{... | collective-permute-start | bytes 786440 | tf_op jit(solution)/shard_map/ppermute | solution.py:546
  134.3 24.1 %collective-permute-start.18 = (f32[128,512]{1,0:T(8,128)S(1)}, f32[128,512]{1,0:T(8,128)S(1)}, u32[]{:S(2)}, u32[]{:S(2)}) collective-permute-start(f32[128,512]{1,0:T(8,128)S(1)} %get-tuple-element.67), channel_id=1, source_target_pairs={{0,8},{4,12},{8,0},{12,4},{1,9},{5,13},{9,1},{13,5},{2,10},{6,14},... | collective-permute-start | bytes 786440 | tf_op jit(solution)/shard_map/ppermute | solution.py:546
  136.1 22.3 %collective-permute-start.19 = (f32[128,512]{1,0:T(8,128)S(1)}, f32[128,512]{1,0:T(8,128)S(1)}, u32[]{:S(2)}, u32[]{:S(2)}) collective-permute-start(f32[128,512]{1,0:T(8,128)S(1)} %get-tuple-element.68), channel_id=1, source_target_pairs={{0,4},{4,8},{8,12},{12,0},{1,5},{5,9},{9,13},{13,1},{2,6},{6,10},{... | collective-permute-start | bytes 786440 | tf_op jit(solution)/shard_map/ppermute | solution.py:546
  (8 other events, 206.3 us)

commit v4 on v3

--- a/solution.py
+++ b/solution.py
@@ -184,8 +184,7 @@
         (low_ref, high_ref), refs = refs[:2], refs[2:]
     else:
         (rate_ref, flag_ref), refs = refs[:2], refs[2:]
-    refs, scratch = refs[:-6], refs[-6:]
-    mask_part, mark_ref, first_ref, last_ref, mask_sems, sems = scratch
+    refs, (mask_part, first_ref, last_ref, mask_sems, sems) = refs[:-5], refs[-5:]
     if layer:
         out_refs = refs
     else:
@@ -201,6 +200,9 @@
         copies.append(pltpu.make_async_copy(source, target, sems.at[len(copies)]))
         copies[-1].start()
 
+    if not layer:
+        start(plane_ref.at[:, :, pl.ds(0, LANES)], first_ref)
+        start(plane_ref.at[:, :, pl.ds(cols - LANES, LANES)], last_ref)
     for q, out_ref in enumerate(out_refs):
         at = lax.rem(me + q, ranks) * (levels // ranks) + layer
         masks.append(pltpu.make_async_copy(mask_ref.at[at], mask_part.at[q], mask_sems.at[q]))
@@ -212,25 +214,23 @@
         sides = jnp.where(lane_at < planes, high_ref[...], low_ref[...])
         for group, row, lane in band_spots(rows, cols):
             part = sides[group * TILE : (group + 1) * TILE]
-            for q in range(ranks):
-                mark_ref[q, block + row : block + row + TILE, lane : lane + LANES] = part
+            row += held * rows + block
+            for out_ref in out_refs:
+                out_ref[row : row + TILE, lane : lane + LANES] = part
     else:
-        start(plane_ref.at[:, :, pl.ds(0, LANES)], first_ref)
-        start(plane_ref.at[:, :, pl.ds(cols - LANES, LANES)], last_ref)
-    for q, out_ref in enumerate(out_refs):
-        masks[q].wait()
-        mark_ref[q, :block, :] = mask_part[q].astype(jnp.float32)
-        count = mark_ref.shape[1]
-        start(mark_ref.at[q], out_ref.at[pl.ds(held * rows, count)])
-    for copy in copies:
-        copy.wait()
-    if not layer:
+        copies[0].wait()
+        copies[1].wait()
         end = slice(cols - LANES, cols)
         weight_plus, weight_minus = face_weights(rate_ref[1, :, end], flag_ref[1, :, end])
         columns = [first_ref[plane][:, :1] for plane in range(planes)]
         columns += [last_ref[plane][:, LANES - 1 :] for plane in range(planes)]
         columns += [weight_plus[:, LANES - 1 :], weight_minus[:, LANES - 1 :]]
         edge_ref[...] = gather_columns(columns, rows)
+    for q, out_ref in enumerate(out_refs):
+        masks[q].wait()
+        out_ref[held * rows : held * rows + block, :] = mask_part[q].astype(jnp.float32)
+    for copy in copies[0 if layer else 2 :]:
+        copy.wait()
 
 
 def pack(concentration, stiff_mask, layer, ranks, others):
@@ -239,22 +239,20 @@
     block = stiff_mask.shape[1]
     extra = block + (bands(rows, cols) if layer else 0)
     message = jax.ShapeDtypeStruct((held * rows + extra, cols), jnp.float32)
-    out_shape, out_specs = [message] * ranks, [any_spec()] * ranks
+    out_shape = [message] * ranks
     if not layer:
         out_shape.append(jax.ShapeDtypeStruct((rows, LANES), jnp.float32))
-        out_specs.append(whole_spec())
     results = pl.pallas_call(
         functools.partial(pack_kernel, layer),
         out_shape=out_shape,
         in_specs=[hbm_spec()] * 2 + [whole_spec()] * 2,
-        out_specs=out_specs,
+        out_specs=[whole_spec()] * len(out_shape),
         scratch_shapes=[
             pltpu.VMEM((ranks, block, cols), jnp.int32),
-            pltpu.VMEM((ranks, extra, cols), jnp.float32),
             pltpu.VMEM((planes, rows, LANES), jnp.float32),
             pltpu.VMEM((planes, rows, LANES), jnp.float32),
             pltpu.SemaphoreType.DMA((ranks,)),
-            pltpu.SemaphoreType.DMA((ranks * (held + 1) + 2,)),
+            pltpu.SemaphoreType.DMA((ranks * held + 2,)),
         ],
         compiler_params=pltpu.CompilerParams(vmem_limit_bytes=VMEM_LIMIT if layer else MOST_VMEM),
         cost_estimate=pl.CostEstimate(flops=0, bytes_accessed=0, transcendentals=0),
@@ -548,6 +546,8 @@
     arrived, others = [], (face_rate, face_flag)
     for layer in range(layers):
         messages, edges = pack(concentration, stiff_mask, layer, ranks, others)
+        for q in range(1, ranks if layer else 0):
+            messages[q], arrived[-1][q] = lax.optimization_barrier((messages[q], arrived[-1][q]))
         arrived.append([send(part, q) if q else part for q, part in enumerate(messages)])
         if edges:
             others = (shifted(edges[0], "space", 1), shifted(edges[0], "space", -1))

time: 160 us -> 131 us (0.82)
  Pallas kernels: 68.2 us -> 36.7 us
  waiting for transfers between devices: 30.8 us -> 33.6 us
    pallas_call x2, Pallas kernels: 37.1 us -> 5.61 us  [pack(): pl.pallas_call(functools.partial(pack_kernel, layer), out_shape=out_shape...]
    ppermute x8, starting transfers between devices: 30.2 us -> 23.8 us  [shifted(): return lax.ppermute(shard, axis, pairs)]
    ppermute x12, starting transfers between devices: 26.5 us -> 31.9 us  [send(): lax.ppermute(value, 'comp', [(i, (i + by) % ranks) for i in range(ranks)])]
    ppermute x12, waiting for transfers between devices: 22 us -> 24.5 us  [send(): lax.ppermute(value, 'comp', [(i, (i + by) % ranks) for i in range(ranks)])]
  transfers between devices with their start and end apart: 20 -> 20, of which waited for: 6 -> 6; matrix products, arithmetic and copies ran while one was open for 1% -> 2% of each run, Pallas kernels for 21% -> 25%
where the time goes in v4:
time: 131 us; the launch traced here: 130 us
  starting transfers between devices  55.8 us (43%)
  Pallas kernels  36.7 us (28%)
  waiting for transfers between devices  33.6 us (26%)
  local copies, waits for them, and re-layouts  3.69 us (3%)
    ppermute x12, starting transfers between devices, send(): lax.ppermute(value, 'comp', [(i, (i + by) % ranks) for i in range(ranks)])  31.9 us
    pallas_call x4, Pallas kernels, layer_step(): pl.pallas_call(functools.partial(step_kernel, pieces, layer, stiff is Non...  30.1 us
    ppermute x12, waiting for transfers between devices, send(): lax.ppermute(value, 'comp', [(i, (i + by) % ranks) for i in range(ranks)])  24.5 us
    ppermute x8, starting transfers between devices, shifted(): return lax.ppermute(shard, axis, pairs)  23.8 us
    ppermute x8, waiting for transfers between devices, shifted(): return lax.ppermute(shard, axis, pairs)  9.11 us
    pallas_call x2, Pallas kernels, pack(): pl.pallas_call(functools.partial(pack_kernel, layer), out_shape=out_shape...  5.61 us
  transfers between devices with their start and end apart: 20, of which 6 were waited for; matrix products, arithmetic and copies ran while one was open for 2% of the time, Pallas kernels for 25%

profile of v4, /device:TPU:1, one launch (start us, length us, event | category | flops | bytes accessed | tf_op | source)
XLA Modules:
  0.0 130.1 jit_solution(5870752677859800244)
XLA Ops:
  0.0 3.9 %pack.2 = (f32[136,512]{1,0:T(8,128)}, f32[136,512]{1,0:T(8,128)}, f32[136,512]{1,0:T(8,128)}, f32[136,512]{1,0:T(8,128)}, f32[32,128]{1,0:T(8,128)}) custom-call(f32[32,32,512]{2,1,0:T(8,128)} %plane_ref.3, s32[8,8,512]{2,1,0:T(8,128)} %mask_ref.3, f32[2,32,512]{2,1,0:T(8,128)} %refs_6_.7, s32[2,32,512]{2,1,0:T(8,128)} %refs_7_.7), custom_call_target="tpu_custom_call" | custom-call | tf_op jit(solution)/shard_map/pack/pallas_call | solution.py:245
  4.0 3.2 %collective-permute-start.3 = (f32[136,512]{1,0:T(8,128)}, f32[136,512]{1,0:T(8,128)S(1)}, u32[]{:S(2)}, u32[]{:S(2)}) collective-permute-start(f32[136,512]{1,0:T(8,128)} %get-tuple-element.49), channel_id=1, source_target_pairs={{0,8},{4,12},{8,0},{12,4},{1,9},{5,13},{9,1},{13,5},{2,10},{6,14},... | collective-permute-start | bytes 835592 | tf_op jit(solution)/shard_map/ppermute | solution.py:544
  8.6 4.7 %collective-permute-start = (f32[32,128]{1,0:T(8,128)}, f32[32,128]{1,0:T(8,128)S(1)}, u32[]{:S(2)}, u32[]{:S(2)}) collective-permute-start(f32[32,128]{1,0:T(8,128)} %get-tuple-element.44), channel_id=1, source_target_pairs={{0,1},{1,2},{2,3},{4,5},{5,6},{6,7},{8,9},{9,10},{10,11},{12,13},{... | collective-permute-start | bytes 49160 | tf_op jit(solution)/shard_map/ppermute | solution.py:23
  13.3 1.9 %collective-permute-start.1 = (f32[32,128]{1,0:T(8,128)}, f32[32,128]{1,0:T(8,128)S(1)}, u32[]{:S(2)}, u32[]{:S(2)}) collective-permute-start(f32[32,128]{1,0:T(8,128)} %get-tuple-element.44), channel_id=1, source_target_pairs={{1,0},{2,1},{3,2},{5,4},{6,5},{7,6},{9,8},{10,9},{11,10},{13,12},{... | collective-permute-start | bytes 49160 | tf_op jit(solution)/shard_map/ppermute | solution.py:23
  15.2 3.6 %collective-permute-done.1.refs_1_.refs_5_ = f32[32,128]{1,0:T(8,128)S(1)} collective-permute-done((f32[32,128]{1,0:T(8,128)}, f32[32,128]{1,0:T(8,128)S(1)}, u32[]{:S(2)}, u32[]{:S(2)}) %collective-permute-start.1) | collective-permute-done | bytes 16416 | tf_op jit(solution)/shard_map/ppermute | solution.py:23
  18.9 1.7 %pack.3 = (f32[144,512]{1,0:T(8,128)S(1)}, f32[144,512]{1,0:T(8,128)S(1)}, f32[144,512]{1,0:T(8,128)S(1)}, f32[144,512]{1,0:T(8,128)S(1)}) custom-call(f32[32,32,512]{2,1,0:T(8,128)S(1)} %copy-done, s32[8,8,512]{2,1,0:T(8,128)S(1)} %copy-done.4, f32[32,128]{1,0:T(8,128)S(1)} %collective-permute-done.refs_0_.refs_4_, ...), custom_call_target="tpu_custom_call" | custom-call | tf_op jit(solution)/shard_map/pack/pallas_call | solution.py:245
  21.4 5.2 %collective-permute-done.2.refs_1_.refs_5_ = f32[136,512]{1,0:T(8,128)S(1)} collective-permute-done((f32[136,512]{1,0:T(8,128)}, f32[136,512]{1,0:T(8,128)S(1)}, u32[]{:S(2)}, u32[]{:S(2)}) %collective-permute-start.2) | collective-permute-done | bytes 278560 | tf_op jit(solution)/shard_map/ppermute | solution.py:544
  26.8 4.6 %collective-permute-start.5 = (f32[32,128]{1,0:T(8,128)S(1)}, f32[32,128]{1,0:T(8,128)S(1)}, u32[]{:S(2)}, u32[]{:S(2)}) collective-permute-start(f32[32,128]{1,0:T(8,128)S(1)} %edges.1), channel_id=1, source_target_pairs={{0,1},{1,2},{2,3},{4,5},{5,6},{6,7},{8,9},{9,10},{10,11},{12,13},{... | collective-permute-start | bytes 49160 | tf_op jit(solution)/shard_map/ppermute | solution.py:23
  31.4 1.9 %collective-permute-start.6 = (f32[32,128]{1,0:T(8,128)S(1)}, f32[32,128]{1,0:T(8,128)S(1)}, u32[]{:S(2)}, u32[]{:S(2)}) collective-permute-start(f32[32,128]{1,0:T(8,128)S(1)} %edges.1), channel_id=1, source_target_pairs={{1,0},{2,1},{3,2},{5,4},{6,5},{7,6},{9,8},{10,9},{11,10},{13,12},{... | collective-permute-start | bytes 49160 | tf_op jit(solution)/shard_map/ppermute | solution.py:23
  33.3 3.4 %collective-permute-start.14 = (f32[144,512]{1,0:T(8,128)S(1)}, f32[144,512]{1,0:T(8,128)S(1)}, u32[]{:S(2)}, u32[]{:S(2)}) collective-permute-start(f32[144,512]{1,0:T(8,128)S(1)} %get-tuple-element.70), channel_id=1, source_target_pairs={{0,12},{4,0},{8,4},{12,8},{1,13},{5,1},{9,5},{13,9},{2,14},{6,2},{... | collective-permute-start | bytes 884744 | tf_op jit(solution)/shard_map/ppermute | solution.py:544
  36.7 14.8 %collective-permute-start.12 = (f32[144,512]{1,0:T(8,128)S(1)}, f32[144,512]{1,0:T(8,128)S(1)}, u32[]{:S(2)}, u32[]{:S(2)}) collective-permute-start(f32[144,512]{1,0:T(8,128)S(1)} %get-tuple-element.68), channel_id=1, source_target_pairs={{0,4},{4,8},{8,12},{12,0},{1,5},{5,9},{9,13},{13,1},{2,6},{6,10},{... | collective-permute-start | bytes 884744 | tf_op jit(solution)/shard_map/ppermute | solution.py:544
  52.4 7.4 %layer_step.4 = (f32[128,512]{1,0:T(8,128)S(1)}, f32[128,512]{1,0:T(8,128)S(1)}, f32[128,512]{1,0:T(8,128)S(1)}, f32[128,512]{1,0:T(8,128)S(1)}, f32[32,128]{1,0:T(8,128)S(1)}, /*index=5*/f32[32,512]{1,0:T(8,128)S(1)}) custom-call(f32[16]{0:T(128)S(1)} %copy-done.5, f32[16]{0:T(128)S(1)} %copy-done.6, f32[136,512]{1,0:T(8,128)S(1)} %copy-done.3, ...), custom_call_target="tpu_custom_call" | custom-call | tf_op jit(solution)/shard_map/layer_step/pallas_call | solution.py:510
  59.8 3.9 %collective-permute-start.7 = (f32[32,128]{1,0:T(8,128)S(1)}, f32[32,128]{1,0:T(8,128)S(1)}, u32[]{:S(2)}, u32[]{:S(2)}) collective-permute-start(f32[32,128]{1,0:T(8,128)S(1)} %get-tuple-element.62), channel_id=1, source_target_pairs={{0,1},{1,2},{2,3},{4,5},{5,6},{6,7},{8,9},{9,10},{10,11},{12,13},{... | collective-permute-start | bytes 49160 | tf_op jit(solution)/shard_map/ppermute | solution.py:23
  63.7 1.9 %collective-permute-start.8 = (f32[32,128]{1,0:T(8,128)S(1)}, f32[32,128]{1,0:T(8,128)S(1)}, u32[]{:S(2)}, u32[]{:S(2)}) collective-permute-start(f32[32,128]{1,0:T(8,128)S(1)} %get-tuple-element.62), channel_id=1, source_target_pairs={{1,0},{2,1},{3,2},{5,4},{6,5},{7,6},{9,8},{10,9},{11,10},{13,12},{... | collective-permute-start | bytes 49160 | tf_op jit(solution)/shard_map/ppermute | solution.py:23
  65.6 3.1 %collective-permute-done.8.refs_5_ = f32[32,128]{1,0:T(8,128)S(1)} collective-permute-done((f32[32,128]{1,0:T(8,128)S(1)}, f32[32,128]{1,0:T(8,128)S(1)}, u32[]{:S(2)}, u32[]{:S(2)}) %collective-permute-start.8) | collective-permute-done | bytes 16416 | tf_op jit(solution)/shard_map/ppermute | solution.py:23
  68.8 8.0 %layer_step.5 = (f32[128,512]{1,0:T(8,128)S(1)}, f32[128,512]{1,0:T(8,128)}, f32[128,512]{1,0:T(8,128)}, f32[128,512]{1,0:T(8,128)S(1)}) custom-call(f32[16]{0:T(128)S(1)} %copy-done.5, f32[16]{0:T(128)S(1)} %copy-done.6, f32[128,512]{1,0:T(8,128)S(1)} %get-tuple-element.58.refs_0_, f32[128,512]{1,0:T(8,128)S(1)} %get-tuple-element.59.refs_1_, ...), custom_call_target="tpu_custom_call" | custom-call | tf_op jit(solution)/shard_map/layer_step/pallas_call | solution.py:510
  76.8 3.0 %collective-permute-start.9 = (f32[128,512]{1,0:T(8,128)}, f32[128,512]{1,0:T(8,128)}, u32[]{:S(2)}, u32[]{:S(2)}) collective-permute-start(f32[128,512]{1,0:T(8,128)} %get-tuple-element.65), channel_id=1, source_target_pairs={{0,12},{4,0},{8,4},{12,8},{1,13},{5,1},{9,5},{13,9},{2,14},{6,2},{... | collective-permute-start | bytes 786440 | tf_op jit(solution)/shard_map/ppermute | solution.py:544
  82.0 7.4 %layer_step.6 = (f32[128,512]{1,0:T(8,128)S(1)}, f32[128,512]{1,0:T(8,128)S(1)}, f32[128,512]{1,0:T(8,128)S(1)}, f32[128,512]{1,0:T(8,128)S(1)}, f32[32,128]{1,0:T(8,128)S(1)}, /*index=5*/f32[32,512]{1,0:T(8,128)S(1)}) custom-call(f32[16]{0:T(128)S(1)} %copy-done.5, f32[16]{0:T(128)S(1)} %copy-done.6, f32[144,512]{1,0:T(8,128)S(1)} %get-tuple-element.54.refs_10_.refs_0_, ...), custom_call_target="tpu_custom_call" | custom-call | tf_op jit(solution)/shard_map/layer_step/pallas_call | solution.py:510
  89.5 2.8 %collective-permute-start.15 = (f32[32,128]{1,0:T(8,128)S(1)}, f32[32,128]{1,0:T(8,128)S(1)}, u32[]{:S(2)}, u32[]{:S(2)}) collective-permute-start(f32[32,128]{1,0:T(8,128)S(1)} %get-tuple-element.75), channel_id=1, source_target_pairs={{0,1},{1,2},{2,3},{4,5},{5,6},{6,7},{8,9},{9,10},{10,11},{12,13},{... | collective-permute-start | bytes 49160 | tf_op jit(solution)/shard_map/ppermute | solution.py:23
  92.3 2.1 %collective-permute-start.16 = (f32[32,128]{1,0:T(8,128)S(1)}, f32[32,128]{1,0:T(8,128)S(1)}, u32[]{:S(2)}, u32[]{:S(2)}) collective-permute-start(f32[32,128]{1,0:T(8,128)S(1)} %get-tuple-element.75), channel_id=1, source_target_pairs={{1,0},{2,1},{3,2},{5,4},{6,5},{7,6},{9,8},{10,9},{11,10},{13,12},{... | collective-permute-start | bytes 49160 | tf_op jit(solution)/shard_map/ppermute | solution.py:23
  95.4 2.4 %collective-permute-done.16.refs_5_ = f32[32,128]{1,0:T(8,128)S(1)} collective-permute-done((f32[32,128]{1,0:T(8,128)S(1)}, f32[32,128]{1,0:T(8,128)S(1)}, u32[]{:S(2)}, u32[]{:S(2)}) %collective-permute-start.16) | collective-permute-done | bytes 16416 | tf_op jit(solution)/shard_map/ppermute | solution.py:23
  97.7 7.2 %layer_step.7 = (f32[128,512]{1,0:T(8,128)S(1)}, f32[128,512]{1,0:T(8,128)S(1)}, f32[128,512]{1,0:T(8,128)S(1)}, f32[128,512]{1,0:T(8,128)S(1)}) custom-call(f32[16]{0:T(128)S(1)} %copy-done.5, f32[16]{0:T(128)S(1)} %copy-done.6, f32[128,512]{1,0:T(8,128)S(1)} %get-tuple-element.71.refs_0_, f32[128,512]{1,0:T(8,128)S(1)} %get-tuple-element.72.refs_1_, ...), custom_call_target="tpu_custom_call" | custom-call | tf_op jit(solution)/shard_map/layer_step/pallas_call | solution.py:510
  109.4 3.5 %collective-permute-done.17 = f32[128,512]{1,0:T(8,128)S(1)} collective-permute-done((f32[128,512]{1,0:T(8,128)S(1)}, f32[128,512]{1,0:T(8,128)S(1)}, u32[]{:S(2)}, u32[]{:S(2)}) %collective-permute-start.17) | collective-permute-done | bytes 262176 | tf_op jit(solution)/shard_map/ppermute | solution.py:544
  112.9 15.8 %collective-permute-done.18 = f32[128,512]{1,0:T(8,128)S(1)} collective-permute-done((f32[128,512]{1,0:T(8,128)S(1)}, f32[128,512]{1,0:T(8,128)S(1)}, u32[]{:S(2)}, u32[]{:S(2)}) %collective-permute-start.18) | collective-permute-done | bytes 262176 | tf_op jit(solution)/shard_map/ppermute | solution.py:544
  (57 shorter events, 12.4 us)
Async XLA Ops:
  4.0 16.6 %collective-permute-start.3 = (f32[136,512]{1,0:T(8,128)}, f32[136,512]{1,0:T(8,128)S(1)}, u32[]{:S(2)}, u32[]{:S(2)}) collective-permute-start(f32[136,512]{1,0:T(8,128)} %get-tuple-element.49), channel_id=1, source_target_pairs={{0,8},{4,12},{8,0},{12,4},{1,9},{5,13},{9,1},{13,5},{2,10},{6,14},... | collective-permute-start | bytes 835592 | tf_op jit(solution)/shard_map/ppermute | solution.py:544
  7.2 14.3 %collective-permute-start.4 = (f32[136,512]{1,0:T(8,128)}, f32[136,512]{1,0:T(8,128)S(1)}, u32[]{:S(2)}, u32[]{:S(2)}) collective-permute-start(f32[136,512]{1,0:T(8,128)} %get-tuple-element.52), channel_id=1, source_target_pairs={{0,12},{4,0},{8,4},{12,8},{1,13},{5,1},{9,5},{13,9},{2,14},{6,2},{... | collective-permute-start | bytes 835592 | tf_op jit(solution)/shard_map/ppermute | solution.py:544
  8.2 18.3 %collective-permute-start.2 = (f32[136,512]{1,0:T(8,128)}, f32[136,512]{1,0:T(8,128)S(1)}, u32[]{:S(2)}, u32[]{:S(2)}) collective-permute-start(f32[136,512]{1,0:T(8,128)} %get-tuple-element.46), channel_id=1, source_target_pairs={{0,4},{4,8},{8,12},{12,0},{1,5},{5,9},{9,13},{13,1},{2,6},{6,10},{... | collective-permute-start | bytes 835592 | tf_op jit(solution)/shard_map/ppermute | solution.py:544
  8.6 42.9 %copy-start.7 = (f32[16,16]{1,0:T(8,128)S(1)}, f32[16,16]{1,0:T(8,128)}, u32[]{:S(2)}) copy-start(f32[16,16]{1,0:T(8,128)} %mixing_ref.1) | copy-start | bytes 3076
  8.6 42.9 %copy-start.8 = (f32[16,16]{1,0:T(8,128)S(1)}, f32[16,16]{1,0:T(8,128)}, u32[]{:S(2)}) copy-start(f32[16,16]{1,0:T(8,128)} %inverse_ref.1) | copy-start | bytes 3076
  8.6 42.9 %copy-start.9 = (f32[16]{0:T(128)S(1)}, f32[16]{0:T(128)}, u32[]{:S(2)}) copy-start(f32[16]{0:T(128)} %param.17) | copy-start | bytes 196
  8.6 42.9 %copy-start.10 = (f32[16]{0:T(128)S(1)}, f32[16]{0:T(128)}, u32[]{:S(2)}) copy-start(f32[16]{0:T(128)} %param.18) | copy-start | bytes 196
  8.6 6.6 %collective-permute-start = (f32[32,128]{1,0:T(8,128)}, f32[32,128]{1,0:T(8,128)S(1)}, u32[]{:S(2)}, u32[]{:S(2)}) collective-permute-start(f32[32,128]{1,0:T(8,128)} %get-tuple-element.44), channel_id=1, source_target_pairs={{0,1},{1,2},{2,3},{4,5},{5,6},{6,7},{8,9},{9,10},{10,11},{12,13},{... | collective-permute-start | bytes 49160 | tf_op jit(solution)/shard_map/ppermute | solution.py:23
  13.3 5.6 %collective-permute-start.1 = (f32[32,128]{1,0:T(8,128)}, f32[32,128]{1,0:T(8,128)S(1)}, u32[]{:S(2)}, u32[]{:S(2)}) collective-permute-start(f32[32,128]{1,0:T(8,128)} %get-tuple-element.44), channel_id=1, source_target_pairs={{1,0},{2,1},{3,2},{5,4},{6,5},{7,6},{9,8},{10,9},{11,10},{13,12},{... | collective-permute-start | bytes 49160 | tf_op jit(solution)/shard_map/ppermute | solution.py:23
  20.6 59.7 %collective-permute-start.13 = (f32[144,512]{1,0:T(8,128)S(1)}, f32[144,512]{1,0:T(8,128)S(1)}, u32[]{:S(2)}, u32[]{:S(2)}) collective-permute-start(f32[144,512]{1,0:T(8,128)S(1)} %get-tuple-element.69), channel_id=1, source_target_pairs={{0,8},{4,12},{8,0},{12,4},{1,9},{5,13},{9,1},{13,5},{2,10},{6,14},... | collective-permute-start | bytes 884744 | tf_op jit(solution)/shard_map/ppermute | solution.py:544
  26.8 25.5 %collective-permute-start.5 = (f32[32,128]{1,0:T(8,128)S(1)}, f32[32,128]{1,0:T(8,128)S(1)}, u32[]{:S(2)}, u32[]{:S(2)}) collective-permute-start(f32[32,128]{1,0:T(8,128)S(1)} %edges.1), channel_id=1, source_target_pairs={{0,1},{1,2},{2,3},{4,5},{5,6},{6,7},{8,9},{9,10},{10,11},{12,13},{... | collective-permute-start | bytes 49160 | tf_op jit(solution)/shard_map/ppermute | solution.py:23
  31.4 20.9 %collective-permute-start.6 = (f32[32,128]{1,0:T(8,128)S(1)}, f32[32,128]{1,0:T(8,128)S(1)}, u32[]{:S(2)}, u32[]{:S(2)}) collective-permute-start(f32[32,128]{1,0:T(8,128)S(1)} %edges.1), channel_id=1, source_target_pairs={{1,0},{2,1},{3,2},{5,4},{6,5},{7,6},{9,8},{10,9},{11,10},{13,12},{... | collective-permute-start | bytes 49160 | tf_op jit(solution)/shard_map/ppermute | solution.py:23
  33.3 48.7 %collective-permute-start.14 = (f32[144,512]{1,0:T(8,128)S(1)}, f32[144,512]{1,0:T(8,128)S(1)}, u32[]{:S(2)}, u32[]{:S(2)}) collective-permute-start(f32[144,512]{1,0:T(8,128)S(1)} %get-tuple-element.70), channel_id=1, source_target_pairs={{0,12},{4,0},{8,4},{12,8},{1,13},{5,1},{9,5},{13,9},{2,14},{6,2},{... | collective-permute-start | bytes 884744 | tf_op jit(solution)/shard_map/ppermute | solution.py:544
  36.7 45.3 %collective-permute-start.12 = (f32[144,512]{1,0:T(8,128)S(1)}, f32[144,512]{1,0:T(8,128)S(1)}, u32[]{:S(2)}, u32[]{:S(2)}) collective-permute-start(f32[144,512]{1,0:T(8,128)S(1)} %get-tuple-element.68), channel_id=1, source_target_pairs={{0,4},{4,8},{8,12},{12,0},{1,5},{5,9},{9,13},{13,1},{2,6},{6,10},{... | collective-permute-start | bytes 884744 | tf_op jit(solution)/shard_map/ppermute | solution.py:544
  59.8 5.9 %collective-permute-start.7 = (f32[32,128]{1,0:T(8,128)S(1)}, f32[32,128]{1,0:T(8,128)S(1)}, u32[]{:S(2)}, u32[]{:S(2)}) collective-permute-start(f32[32,128]{1,0:T(8,128)S(1)} %get-tuple-element.62), channel_id=1, source_target_pairs={{0,1},{1,2},{2,3},{4,5},{5,6},{6,7},{8,9},{9,10},{10,11},{12,13},{... | collective-permute-start | bytes 49160 | tf_op jit(solution)/shard_map/ppermute | solution.py:23
  63.7 5.1 %collective-permute-start.8 = (f32[32,128]{1,0:T(8,128)S(1)}, f32[32,128]{1,0:T(8,128)S(1)}, u32[]{:S(2)}, u32[]{:S(2)}) collective-permute-start(f32[32,128]{1,0:T(8,128)S(1)} %get-tuple-element.62), channel_id=1, source_target_pairs={{1,0},{2,1},{3,2},{5,4},{6,5},{7,6},{9,8},{10,9},{11,10},{13,12},{... | collective-permute-start | bytes 49160 | tf_op jit(solution)/shard_map/ppermute | solution.py:23
  76.8 17.6 %collective-permute-start.9 = (f32[128,512]{1,0:T(8,128)}, f32[128,512]{1,0:T(8,128)}, u32[]{:S(2)}, u32[]{:S(2)}) collective-permute-start(f32[128,512]{1,0:T(8,128)} %get-tuple-element.65), channel_id=1, source_target_pairs={{0,12},{4,0},{8,4},{12,8},{1,13},{5,1},{9,5},{13,9},{2,14},{6,2},{... | collective-permute-start | bytes 786440 | tf_op jit(solution)/shard_map/ppermute | solution.py:544
  79.7 26.9 %collective-permute-start.10 = (f32[128,512]{1,0:T(8,128)}, f32[128,512]{1,0:T(8,128)}, u32[]{:S(2)}, u32[]{:S(2)}) collective-permute-start(f32[128,512]{1,0:T(8,128)} %get-tuple-element.66), channel_id=1, source_target_pairs={{0,8},{4,12},{8,0},{12,4},{1,9},{5,13},{9,1},{13,5},{2,10},{6,14},... | collective-permute-start | bytes 786440 | tf_op jit(solution)/shard_map/ppermute | solution.py:544
  80.3 29.0 %collective-permute-start.11 = (f32[128,512]{1,0:T(8,128)S(1)}, f32[128,512]{1,0:T(8,128)S(1)}, u32[]{:S(2)}, u32[]{:S(2)}) collective-permute-start(f32[128,512]{1,0:T(8,128)S(1)} %get-tuple-element.67), channel_id=1, source_target_pairs={{0,4},{4,8},{8,12},{12,0},{1,5},{5,9},{9,13},{13,1},{2,6},{6,10},{... | collective-permute-start | bytes 786440 | tf_op jit(solution)/shard_map/ppermute | solution.py:544
  89.5 5.9 %collective-permute-start.15 = (f32[32,128]{1,0:T(8,128)S(1)}, f32[32,128]{1,0:T(8,128)S(1)}, u32[]{:S(2)}, u32[]{:S(2)}) collective-permute-start(f32[32,128]{1,0:T(8,128)S(1)} %get-tuple-element.75), channel_id=1, source_target_pairs={{0,1},{1,2},{2,3},{4,5},{5,6},{6,7},{8,9},{9,10},{10,11},{12,13},{... | collective-permute-start | bytes 49160 | tf_op jit(solution)/shard_map/ppermute | solution.py:23
  92.3 5.5 %collective-permute-start.16 = (f32[32,128]{1,0:T(8,128)S(1)}, f32[32,128]{1,0:T(8,128)S(1)}, u32[]{:S(2)}, u32[]{:S(2)}) collective-permute-start(f32[32,128]{1,0:T(8,128)S(1)} %get-tuple-element.75), channel_id=1, source_target_pairs={{1,0},{2,1},{3,2},{5,4},{6,5},{7,6},{9,8},{10,9},{11,10},{13,12},{... | collective-permute-start | bytes 49160 | tf_op jit(solution)/shard_map/ppermute | solution.py:23
  105.0 7.9 %collective-permute-start.17 = (f32[128,512]{1,0:T(8,128)S(1)}, f32[128,512]{1,0:T(8,128)S(1)}, u32[]{:S(2)}, u32[]{:S(2)}) collective-permute-start(f32[128,512]{1,0:T(8,128)S(1)} %get-tuple-element.78), channel_id=1, source_target_pairs={{0,12},{4,0},{8,4},{12,8},{1,13},{5,1},{9,5},{13,9},{2,14},{6,2},{... | collective-permute-start | bytes 786440 | tf_op jit(solution)/shard_map/ppermute | solution.py:544
  107.6 21.1 %collective-permute-start.18 = (f32[128,512]{1,0:T(8,128)S(1)}, f32[128,512]{1,0:T(8,128)S(1)}, u32[]{:S(2)}, u32[]{:S(2)}) collective-permute-start(f32[128,512]{1,0:T(8,128)S(1)} %get-tuple-element.79), channel_id=1, source_target_pairs={{0,8},{4,12},{8,0},{12,4},{1,9},{5,13},{9,1},{13,5},{2,10},{6,14},... | collective-permute-start | bytes 786440 | tf_op jit(solution)/shard_map/ppermute | solution.py:544
  109.3 19.5 %collective-permute-start.19 = (f32[128,512]{1,0:T(8,128)S(1)}, f32[128,512]{1,0:T(8,128)S(1)}, u32[]{:S(2)}, u32[]{:S(2)}) collective-permute-start(f32[128,512]{1,0:T(8,128)S(1)} %get-tuple-element.80), channel_id=1, source_target_pairs={{0,4},{4,8},{8,12},{12,0},{1,5},{5,9},{9,13},{13,1},{2,6},{6,10},{... | collective-permute-start | bytes 786440 | tf_op jit(solution)/shard_map/ppermute | solution.py:544
  (8 other events, 178.4 us)

commit v5 on v4

--- a/solution.py
+++ b/solution.py
@@ -204,7 +204,7 @@
         start(plane_ref.at[:, :, pl.ds(0, LANES)], first_ref)
         start(plane_ref.at[:, :, pl.ds(cols - LANES, LANES)], last_ref)
     for q, out_ref in enumerate(out_refs):
-        at = lax.rem(me + q, ranks) * (levels // ranks) + layer
+        at = jnp.bitwise_xor(me, q) * (levels // ranks) + layer
         masks.append(pltpu.make_async_copy(mask_ref.at[at], mask_part.at[q], mask_sems.at[q]))
         masks[-1].start()
         for index in range(held):
@@ -304,7 +304,7 @@
 
     def pick(shape, stacked_dim):
         at = lax.broadcasted_iota(jnp.int32, shape, stacked_dim) // TILE
-        component = lax.rem(me + ranks - at // held, ranks) * held + lax.rem(at, held)
+        component = jnp.bitwise_xor(me, at // held) * held + lax.rem(at, held)
         held_at = lax.broadcasted_iota(jnp.int32, shape, 1 - stacked_dim)
         return jnp.where(component == held_at, 1.0, 0.0)
 
@@ -373,7 +373,7 @@
     components = stacked // TILE
     held = components // pieces
     me = lax.axis_index("comp")
-    ranks = [lax.rem(me + pieces - q, pieces) for q in range(pieces)]
+    ranks = [jnp.bitwise_xor(me, q) for q in range(pieces)]
     row_at = lax.broadcasted_iota(jnp.int32, (rows, cols), 0)
     col_at = lax.broadcasted_iota(jnp.int32, (rows, cols), 1)
 
@@ -541,14 +541,14 @@
     layers = NZ // ranks
 
     def send(value, by):
-        return lax.ppermute(value, "comp", [(i, (i + by) % ranks) for i in range(ranks)])
+        return lax.ppermute(value, "comp", [(i, i ^ by) for i in range(ranks)]) if by else value
 
     arrived, others = [], (face_rate, face_flag)
     for layer in range(layers):
         messages, edges = pack(concentration, stiff_mask, layer, ranks, others)
-        for q in range(1, ranks if layer else 0):
-            messages[q], arrived[-1][q] = lax.optimization_barrier((messages[q], arrived[-1][q]))
-        arrived.append([send(part, q) if q else part for q, part in enumerate(messages)])
+        if layer:
+            messages, arrived[-1] = lax.optimization_barrier((messages, arrived[-1]))
+        arrived.append([send(part, q) for q, part in enumerate(messages)])
         if edges:
             others = (shifted(edges[0], "space", 1), shifted(edges[0], "space", -1))
         after = messages[0]
@@ -569,11 +569,11 @@
                 values, stiff, low, high, shared, layer, step < STEPS - 1
             )
         for q in range(ranks):
-            piece = send(values[q], -q) if q else values[q]
+            piece = send(values[q], q)
             result = lax.dynamic_update_slice(
                 result,
                 piece.reshape(held, 1, rows, cols),
-                (0, (me + q) % ranks * layers + layer, 0, 0),
+                (0, (me ^ q) * layers + layer, 0, 0),
             )
     return result.reshape(planes, rows, cols)
 
@@ -581,7 +581,7 @@
 def shards(concentration, face_rate, face_flag, *parameters):
     ranks = lax.axis_size("comp")
     planes, rows, cols = concentration.shape
-    whole = NZ % ranks == 0 and planes % NZ == 0
+    whole = NZ % ranks == 0 and planes % NZ == 0 and ranks & (ranks - 1) == 0
     narrow = 2 * max(NC, planes) + 2 <= LANES
     even = rows % (ranks * TILE) == 0 and cols % LANES == 0
     plan = by_layers if whole and narrow and even else by_rows

time: 131 us -> 119 us (0.908)
  the two profiles are of different devices: /device:TPU:1 before, /device:TPU:9 now
where the time goes in v5:
time: 119 us
  waiting for transfers between devices  43.1 us (36%)
  Pallas kernels  36.5 us (31%)
  starting transfers between devices  35.2 us (30%)
  local copies, waits for them, and re-layouts  3.68 us (3%)
    ppermute x12, waiting for transfers between devices, send(): lax.ppermute(value, 'comp', [(i, i ^ by) for i in range(ranks)])  33.8 us
    pallas_call x4, Pallas kernels, layer_step(): pl.pallas_call(functools.partial(step_kernel, pieces, layer, stiff is Non...  29.9 us
    ppermute x8, starting transfers between devices, shifted(): return lax.ppermute(shard, axis, pairs)  24 us
    ppermute x12, starting transfers between devices, send(): lax.ppermute(value, 'comp', [(i, i ^ by) for i in range(ranks)])  11.2 us
    ppermute x8, waiting for transfers between devices, shifted(): return lax.ppermute(shard, axis, pairs)  9.3 us
    pallas_call x2, Pallas kernels, pack(): pl.pallas_call(functools.partial(pack_kernel, layer), out_shape=out_shape...  5.6 us
  transfers between devices with their start and end apart: 20, of which 8 were waited for; matrix products, arithmetic and copies ran while one was open for 2% of the time, Pallas kernels for 27%

profile of v5, /device:TPU:9, one launch (start us, length us, event | category | flops | bytes accessed | tf_op | source)
XLA Modules:
  0.0 118.9 jit_solution(10733618203849287641)
XLA Ops:
  0.0 3.9 %pack.2 = (f32[136,512]{1,0:T(8,128)}, f32[136,512]{1,0:T(8,128)}, f32[136,512]{1,0:T(8,128)}, f32[136,512]{1,0:T(8,128)}, f32[32,128]{1,0:T(8,128)}) custom-call(f32[32,32,512]{2,1,0:T(8,128)} %plane_ref.3, s32[8,8,512]{2,1,0:T(8,128)} %mask_ref.3, f32[2,32,512]{2,1,0:T(8,128)} %refs_6_.7, s32[2,32,512]{2,1,0:T(8,128)} %refs_7_.7), custom_call_target="tpu_custom_call" | custom-call | tf_op jit(solution)/shard_map/pack/pallas_call | solution.py:245
  4.0 2.5 %collective-permute-start.3 = (f32[136,512]{1,0:T(8,128)}, f32[136,512]{1,0:T(8,128)S(1)}, u32[]{:S(2)}, u32[]{:S(2)}) collective-permute-start(f32[136,512]{1,0:T(8,128)} %get-tuple-element.52), channel_id=1, source_target_pairs={{0,8},{4,12},{8,0},{12,4},{1,9},{5,13},{9,1},{13,5},{2,10},{6,14},... | collective-permute-start | bytes 835592 | tf_op jit(solution)/shard_map/ppermute | solution.py:544
  6.7 4.7 %collective-permute-start = (f32[32,128]{1,0:T(8,128)}, f32[32,128]{1,0:T(8,128)S(1)}, u32[]{:S(2)}, u32[]{:S(2)}) collective-permute-start(f32[32,128]{1,0:T(8,128)} %get-tuple-element.45), channel_id=1, source_target_pairs={{0,1},{1,2},{2,3},{4,5},{5,6},{6,7},{8,9},{9,10},{10,11},{12,13},{... | collective-permute-start | bytes 49160 | tf_op jit(solution)/shard_map/ppermute | solution.py:23
  11.3 1.9 %collective-permute-start.1 = (f32[32,128]{1,0:T(8,128)}, f32[32,128]{1,0:T(8,128)S(1)}, u32[]{:S(2)}, u32[]{:S(2)}) collective-permute-start(f32[32,128]{1,0:T(8,128)} %get-tuple-element.45), channel_id=1, source_target_pairs={{1,0},{2,1},{3,2},{5,4},{6,5},{7,6},{9,8},{10,9},{11,10},{13,12},{... | collective-permute-start | bytes 49160 | tf_op jit(solution)/shard_map/ppermute | solution.py:23
  13.3 3.6 %collective-permute-done.1.refs_1_.refs_5_ = f32[32,128]{1,0:T(8,128)S(1)} collective-permute-done((f32[32,128]{1,0:T(8,128)}, f32[32,128]{1,0:T(8,128)S(1)}, u32[]{:S(2)}, u32[]{:S(2)}) %collective-permute-start.1) | collective-permute-done | bytes 16416 | tf_op jit(solution)/shard_map/ppermute | solution.py:23
  16.9 1.7 %pack.3 = (f32[144,512]{1,0:T(8,128)S(1)}, f32[144,512]{1,0:T(8,128)S(1)}, f32[144,512]{1,0:T(8,128)S(1)}, f32[144,512]{1,0:T(8,128)S(1)}) custom-call(f32[32,32,512]{2,1,0:T(8,128)S(1)} %copy-done, s32[8,8,512]{2,1,0:T(8,128)S(1)} %copy-done.4, f32[32,128]{1,0:T(8,128)S(1)} %collective-permute-done.refs_0_.refs_4_, ...), custom_call_target="tpu_custom_call" | custom-call | tf_op jit(solution)/shard_map/pack/pallas_call | solution.py:245
  18.8 11.8 %collective-permute-done.4.refs_3_.refs_7_ = f32[136,512]{1,0:T(8,128)S(1)} collective-permute-done((f32[136,512]{1,0:T(8,128)}, f32[136,512]{1,0:T(8,128)S(1)}, u32[]{:S(2)}, u32[]{:S(2)}) %collective-permute-start.4) | collective-permute-done | bytes 278560 | tf_op jit(solution)/shard_map/ppermute | solution.py:544
  30.9 4.8 %collective-permute-start.5 = (f32[32,128]{1,0:T(8,128)S(1)}, f32[32,128]{1,0:T(8,128)S(1)}, u32[]{:S(2)}, u32[]{:S(2)}) collective-permute-start(f32[32,128]{1,0:T(8,128)S(1)} %edges.1), channel_id=1, source_target_pairs={{0,1},{1,2},{2,3},{4,5},{5,6},{6,7},{8,9},{9,10},{10,11},{12,13},{... | collective-permute-start | bytes 49160 | tf_op jit(solution)/shard_map/ppermute | solution.py:23
  35.7 1.9 %collective-permute-start.6 = (f32[32,128]{1,0:T(8,128)S(1)}, f32[32,128]{1,0:T(8,128)S(1)}, u32[]{:S(2)}, u32[]{:S(2)}) collective-permute-start(f32[32,128]{1,0:T(8,128)S(1)} %edges.1), channel_id=1, source_target_pairs={{1,0},{2,1},{3,2},{5,4},{6,5},{7,6},{9,8},{10,9},{11,10},{13,12},{... | collective-permute-start | bytes 49160 | tf_op jit(solution)/shard_map/ppermute | solution.py:23
  37.6 2.8 %collective-permute-start.13 = (f32[144,512]{1,0:T(8,128)S(1)}, f32[144,512]{1,0:T(8,128)S(1)}, u32[]{:S(2)}, u32[]{:S(2)}) collective-permute-start(f32[144,512]{1,0:T(8,128)S(1)} %get-tuple-element.73), channel_id=1, source_target_pairs={{0,8},{4,12},{8,0},{12,4},{1,9},{5,13},{9,1},{13,5},{2,10},{6,14},... | collective-permute-start | bytes 884744 | tf_op jit(solution)/shard_map/ppermute | solution.py:544
  41.5 7.4 %layer_step.4 = (f32[128,512]{1,0:T(8,128)S(1)}, f32[128,512]{1,0:T(8,128)S(1)}, f32[128,512]{1,0:T(8,128)S(1)}, f32[128,512]{1,0:T(8,128)S(1)}, f32[32,128]{1,0:T(8,128)S(1)}, /*index=5*/f32[32,512]{1,0:T(8,128)S(1)}) custom-call(f32[16]{0:T(128)S(1)} %copy-done.5, f32[16]{0:T(128)S(1)} %copy-done.6, f32[136,512]{1,0:T(8,128)S(1)} %copy-done.3, ...), custom_call_target="tpu_custom_call" | custom-call | tf_op jit(solution)/shard_map/layer_step/pallas_call | solution.py:510
  48.8 4.2 %collective-permute-start.7 = (f32[32,128]{1,0:T(8,128)S(1)}, f32[32,128]{1,0:T(8,128)S(1)}, u32[]{:S(2)}, u32[]{:S(2)}) collective-permute-start(f32[32,128]{1,0:T(8,128)S(1)} %get-tuple-element.66), channel_id=1, source_target_pairs={{0,1},{1,2},{2,3},{4,5},{5,6},{6,7},{8,9},{9,10},{10,11},{12,13},{... | collective-permute-start | bytes 49160 | tf_op jit(solution)/shard_map/ppermute | solution.py:23
  53.1 1.9 %collective-permute-start.8 = (f32[32,128]{1,0:T(8,128)S(1)}, f32[32,128]{1,0:T(8,128)S(1)}, u32[]{:S(2)}, u32[]{:S(2)}) collective-permute-start(f32[32,128]{1,0:T(8,128)S(1)} %get-tuple-element.66), channel_id=1, source_target_pairs={{1,0},{2,1},{3,2},{5,4},{6,5},{7,6},{9,8},{10,9},{11,10},{13,12},{... | collective-permute-start | bytes 49160 | tf_op jit(solution)/shard_map/ppermute | solution.py:23
  55.0 3.4 %collective-permute-done.8.refs_5_ = f32[32,128]{1,0:T(8,128)S(1)} collective-permute-done((f32[32,128]{1,0:T(8,128)S(1)}, f32[32,128]{1,0:T(8,128)S(1)}, u32[]{:S(2)}, u32[]{:S(2)}) %collective-permute-start.8) | collective-permute-done | bytes 16416 | tf_op jit(solution)/shard_map/ppermute | solution.py:23
  58.4 8.0 %layer_step.5 = (f32[128,512]{1,0:T(8,128)S(1)}, f32[128,512]{1,0:T(8,128)}, f32[128,512]{1,0:T(8,128)}, f32[128,512]{1,0:T(8,128)S(1)}) custom-call(f32[16]{0:T(128)S(1)} %copy-done.5, f32[16]{0:T(128)S(1)} %copy-done.6, f32[128,512]{1,0:T(8,128)S(1)} %get-tuple-element.62.refs_0_, f32[128,512]{1,0:T(8,128)S(1)} %get-tuple-element.63.refs_1_, ...), custom_call_target="tpu_custom_call" | custom-call | tf_op jit(solution)/shard_map/layer_step/pallas_call | solution.py:510
  67.2 1.7 %collective-permute-start.10 = (f32[128,512]{1,0:T(8,128)}, f32[128,512]{1,0:T(8,128)}, u32[]{:S(2)}, u32[]{:S(2)}) collective-permute-start(f32[128,512]{1,0:T(8,128)} %get-tuple-element.70), channel_id=1, source_target_pairs={{0,8},{4,12},{8,0},{12,4},{1,9},{5,13},{9,1},{13,5},{2,10},{6,14},... | collective-permute-start | bytes 786440 | tf_op jit(solution)/shard_map/ppermute | solution.py:544
  69.4 7.4 %layer_step.6 = (f32[128,512]{1,0:T(8,128)S(1)}, f32[128,512]{1,0:T(8,128)S(1)}, f32[128,512]{1,0:T(8,128)S(1)}, f32[128,512]{1,0:T(8,128)S(1)}, f32[32,128]{1,0:T(8,128)S(1)}, /*index=5*/f32[32,512]{1,0:T(8,128)S(1)}) custom-call(f32[16]{0:T(128)S(1)} %copy-done.5, f32[16]{0:T(128)S(1)} %copy-done.6, f32[144,512]{1,0:T(8,128)S(1)} %get-tuple-element.58.refs_10_.refs_0_, ...), custom_call_target="tpu_custom_call" | custom-call | tf_op jit(solution)/shard_map/layer_step/pallas_call | solution.py:510
  76.7 2.5 %collective-permute-start.15 = (f32[32,128]{1,0:T(8,128)S(1)}, f32[32,128]{1,0:T(8,128)S(1)}, u32[]{:S(2)}, u32[]{:S(2)}) collective-permute-start(f32[32,128]{1,0:T(8,128)S(1)} %get-tuple-element.79), channel_id=1, source_target_pairs={{0,1},{1,2},{2,3},{4,5},{5,6},{6,7},{8,9},{9,10},{10,11},{12,13},{... | collective-permute-start | bytes 49160 | tf_op jit(solution)/shard_map/ppermute | solution.py:23
  79.2 2.1 %collective-permute-start.16 = (f32[32,128]{1,0:T(8,128)S(1)}, f32[32,128]{1,0:T(8,128)S(1)}, u32[]{:S(2)}, u32[]{:S(2)}) collective-permute-start(f32[32,128]{1,0:T(8,128)S(1)} %get-tuple-element.79), channel_id=1, source_target_pairs={{1,0},{2,1},{3,2},{5,4},{6,5},{7,6},{9,8},{10,9},{11,10},{13,12},{... | collective-permute-start | bytes 49160 | tf_op jit(solution)/shard_map/ppermute | solution.py:23
  82.3 2.2 %collective-permute-done.16.refs_5_ = f32[32,128]{1,0:T(8,128)S(1)} collective-permute-done((f32[32,128]{1,0:T(8,128)S(1)}, f32[32,128]{1,0:T(8,128)S(1)}, u32[]{:S(2)}, u32[]{:S(2)}) %collective-permute-start.16) | collective-permute-done | bytes 16416 | tf_op jit(solution)/shard_map/ppermute | solution.py:23
  84.6 7.2 %layer_step.7 = (f32[128,512]{1,0:T(8,128)S(1)}, f32[128,512]{1,0:T(8,128)S(1)}, f32[128,512]{1,0:T(8,128)S(1)}, f32[128,512]{1,0:T(8,128)S(1)}) custom-call(f32[16]{0:T(128)S(1)} %copy-done.5, f32[16]{0:T(128)S(1)} %copy-done.6, f32[128,512]{1,0:T(8,128)S(1)} %get-tuple-element.75.refs_0_, f32[128,512]{1,0:T(8,128)S(1)} %get-tuple-element.76.refs_1_, ...), custom_call_target="tpu_custom_call" | custom-call | tf_op jit(solution)/shard_map/layer_step/pallas_call | solution.py:510
  95.7 6.4 %collective-permute-done.17 = f32[128,512]{1,0:T(8,128)S(1)} collective-permute-done((f32[128,512]{1,0:T(8,128)S(1)}, f32[128,512]{1,0:T(8,128)S(1)}, u32[]{:S(2)}, u32[]{:S(2)}) %collective-permute-start.17) | collective-permute-done | bytes 262176 | tf_op jit(solution)/shard_map/ppermute | solution.py:544
  102.1 10.6 %collective-permute-done.18 = f32[128,512]{1,0:T(8,128)S(1)} collective-permute-done((f32[128,512]{1,0:T(8,128)S(1)}, f32[128,512]{1,0:T(8,128)S(1)}, u32[]{:S(2)}, u32[]{:S(2)}) %collective-permute-start.18) | collective-permute-done | bytes 262176 | tf_op jit(solution)/shard_map/ppermute | solution.py:544
  112.7 4.8 %collective-permute-done.19 = f32[128,512]{1,0:T(8,128)S(1)} collective-permute-done((f32[128,512]{1,0:T(8,128)S(1)}, f32[128,512]{1,0:T(8,128)S(1)}, u32[]{:S(2)}, u32[]{:S(2)}) %collective-permute-start.19) | collective-permute-done | bytes 262176 | tf_op jit(solution)/shard_map/ppermute | solution.py:544
  (57 shorter events, 9.1 us)
Async XLA Ops:
  4.0 14.7 %collective-permute-start.2 = (f32[136,512]{1,0:T(8,128)}, f32[136,512]{1,0:T(8,128)S(1)}, u32[]{:S(2)}, u32[]{:S(2)}) collective-permute-start(f32[136,512]{1,0:T(8,128)} %get-tuple-element.51), channel_id=1, source_target_pairs={{0,4},{4,0},{8,12},{12,8},{1,5},{5,1},{9,13},{13,9},{2,6},{6,2},{1... | collective-permute-start | bytes 835592 | tf_op jit(solution)/shard_map/ppermute | solution.py:544
  4.0 14.8 %collective-permute-start.3 = (f32[136,512]{1,0:T(8,128)}, f32[136,512]{1,0:T(8,128)S(1)}, u32[]{:S(2)}, u32[]{:S(2)}) collective-permute-start(f32[136,512]{1,0:T(8,128)} %get-tuple-element.52), channel_id=1, source_target_pairs={{0,8},{4,12},{8,0},{12,4},{1,9},{5,13},{9,1},{13,5},{2,10},{6,14},... | collective-permute-start | bytes 835592 | tf_op jit(solution)/shard_map/ppermute | solution.py:544
  6.5 24.1 %collective-permute-start.4 = (f32[136,512]{1,0:T(8,128)}, f32[136,512]{1,0:T(8,128)S(1)}, u32[]{:S(2)}, u32[]{:S(2)}) collective-permute-start(f32[136,512]{1,0:T(8,128)} %get-tuple-element.53), channel_id=1, source_target_pairs={{0,12},{4,8},{8,4},{12,0},{1,13},{5,9},{9,5},{13,1},{2,14},{6,10},... | collective-permute-start | bytes 835592 | tf_op jit(solution)/shard_map/ppermute | solution.py:544
  6.7 33.9 %copy-start.7 = (f32[16,16]{1,0:T(8,128)S(1)}, f32[16,16]{1,0:T(8,128)}, u32[]{:S(2)}) copy-start(f32[16,16]{1,0:T(8,128)} %mixing_ref.1) | copy-start | bytes 3076
  6.7 33.9 %copy-start.8 = (f32[16,16]{1,0:T(8,128)S(1)}, f32[16,16]{1,0:T(8,128)}, u32[]{:S(2)}) copy-start(f32[16,16]{1,0:T(8,128)} %inverse_ref.1) | copy-start | bytes 3076
  6.7 33.9 %copy-start.9 = (f32[16]{0:T(128)S(1)}, f32[16]{0:T(128)}, u32[]{:S(2)}) copy-start(f32[16]{0:T(128)} %param.17) | copy-start | bytes 196
  6.7 33.9 %copy-start.10 = (f32[16]{0:T(128)S(1)}, f32[16]{0:T(128)}, u32[]{:S(2)}) copy-start(f32[16]{0:T(128)} %param.18) | copy-start | bytes 196
  6.7 6.6 %collective-permute-start = (f32[32,128]{1,0:T(8,128)}, f32[32,128]{1,0:T(8,128)S(1)}, u32[]{:S(2)}, u32[]{:S(2)}) collective-permute-start(f32[32,128]{1,0:T(8,128)} %get-tuple-element.45), channel_id=1, source_target_pairs={{0,1},{1,2},{2,3},{4,5},{5,6},{6,7},{8,9},{9,10},{10,11},{12,13},{... | collective-permute-start | bytes 49160 | tf_op jit(solution)/shard_map/ppermute | solution.py:23
  11.3 5.6 %collective-permute-start.1 = (f32[32,128]{1,0:T(8,128)}, f32[32,128]{1,0:T(8,128)S(1)}, u32[]{:S(2)}, u32[]{:S(2)}) collective-permute-start(f32[32,128]{1,0:T(8,128)} %get-tuple-element.45), channel_id=1, source_target_pairs={{1,0},{2,1},{3,2},{5,4},{6,5},{7,6},{9,8},{10,9},{11,10},{13,12},{... | collective-permute-start | bytes 49160 | tf_op jit(solution)/shard_map/ppermute | solution.py:23
  30.6 38.3 %collective-permute-start.12 = (f32[144,512]{1,0:T(8,128)S(1)}, f32[144,512]{1,0:T(8,128)S(1)}, u32[]{:S(2)}, u32[]{:S(2)}) collective-permute-start(f32[144,512]{1,0:T(8,128)S(1)} %get-tuple-element.72), channel_id=1, source_target_pairs={{0,4},{4,0},{8,12},{12,8},{1,5},{5,1},{9,13},{13,9},{2,6},{6,2},{1... | collective-permute-start | bytes 884744 | tf_op jit(solution)/shard_map/ppermute | solution.py:544
  30.9 10.6 %collective-permute-start.5 = (f32[32,128]{1,0:T(8,128)S(1)}, f32[32,128]{1,0:T(8,128)S(1)}, u32[]{:S(2)}, u32[]{:S(2)}) collective-permute-start(f32[32,128]{1,0:T(8,128)S(1)} %edges.1), channel_id=1, source_target_pairs={{0,1},{1,2},{2,3},{4,5},{5,6},{6,7},{8,9},{9,10},{10,11},{12,13},{... | collective-permute-start | bytes 49160 | tf_op jit(solution)/shard_map/ppermute | solution.py:23
  35.7 5.7 %collective-permute-start.6 = (f32[32,128]{1,0:T(8,128)S(1)}, f32[32,128]{1,0:T(8,128)S(1)}, u32[]{:S(2)}, u32[]{:S(2)}) collective-permute-start(f32[32,128]{1,0:T(8,128)S(1)} %edges.1), channel_id=1, source_target_pairs={{1,0},{2,1},{3,2},{5,4},{6,5},{7,6},{9,8},{10,9},{11,10},{13,12},{... | collective-permute-start | bytes 49160 | tf_op jit(solution)/shard_map/ppermute | solution.py:23
  37.6 31.7 %collective-permute-start.13 = (f32[144,512]{1,0:T(8,128)S(1)}, f32[144,512]{1,0:T(8,128)S(1)}, u32[]{:S(2)}, u32[]{:S(2)}) collective-permute-start(f32[144,512]{1,0:T(8,128)S(1)} %get-tuple-element.73), channel_id=1, source_target_pairs={{0,8},{4,12},{8,0},{12,4},{1,9},{5,13},{9,1},{13,5},{2,10},{6,14},... | collective-permute-start | bytes 884744 | tf_op jit(solution)/shard_map/ppermute | solution.py:544
  40.4 28.9 %collective-permute-start.14 = (f32[144,512]{1,0:T(8,128)S(1)}, f32[144,512]{1,0:T(8,128)S(1)}, u32[]{:S(2)}, u32[]{:S(2)}) collective-permute-start(f32[144,512]{1,0:T(8,128)S(1)} %get-tuple-element.74), channel_id=1, source_target_pairs={{0,12},{4,8},{8,4},{12,0},{1,13},{5,9},{9,5},{13,1},{2,14},{6,10},... | collective-permute-start | bytes 884744 | tf_op jit(solution)/shard_map/ppermute | solution.py:544
  48.8 6.2 %collective-permute-start.7 = (f32[32,128]{1,0:T(8,128)S(1)}, f32[32,128]{1,0:T(8,128)S(1)}, u32[]{:S(2)}, u32[]{:S(2)}) collective-permute-start(f32[32,128]{1,0:T(8,128)S(1)} %get-tuple-element.66), channel_id=1, source_target_pairs={{0,1},{1,2},{2,3},{4,5},{5,6},{6,7},{8,9},{9,10},{10,11},{12,13},{... | collective-permute-start | bytes 49160 | tf_op jit(solution)/shard_map/ppermute | solution.py:23
  53.1 5.4 %collective-permute-start.8 = (f32[32,128]{1,0:T(8,128)S(1)}, f32[32,128]{1,0:T(8,128)S(1)}, u32[]{:S(2)}, u32[]{:S(2)}) collective-permute-start(f32[32,128]{1,0:T(8,128)S(1)} %get-tuple-element.66), channel_id=1, source_target_pairs={{1,0},{2,1},{3,2},{5,4},{6,5},{7,6},{9,8},{10,9},{11,10},{13,12},{... | collective-permute-start | bytes 49160 | tf_op jit(solution)/shard_map/ppermute | solution.py:23
  66.4 14.9 %collective-permute-start.9 = (f32[128,512]{1,0:T(8,128)}, f32[128,512]{1,0:T(8,128)}, u32[]{:S(2)}, u32[]{:S(2)}) collective-permute-start(f32[128,512]{1,0:T(8,128)} %get-tuple-element.69), channel_id=1, source_target_pairs={{0,4},{4,0},{8,12},{12,8},{1,5},{5,1},{9,13},{13,9},{2,6},{6,2},{1... | collective-permute-start | bytes 786440 | tf_op jit(solution)/shard_map/ppermute | solution.py:544
  67.2 26.1 %collective-permute-start.10 = (f32[128,512]{1,0:T(8,128)}, f32[128,512]{1,0:T(8,128)}, u32[]{:S(2)}, u32[]{:S(2)}) collective-permute-start(f32[128,512]{1,0:T(8,128)} %get-tuple-element.70), channel_id=1, source_target_pairs={{0,8},{4,12},{8,0},{12,4},{1,9},{5,13},{9,1},{13,5},{2,10},{6,14},... | collective-permute-start | bytes 786440 | tf_op jit(solution)/shard_map/ppermute | solution.py:544
  68.9 26.5 %collective-permute-start.11 = (f32[128,512]{1,0:T(8,128)S(1)}, f32[128,512]{1,0:T(8,128)S(1)}, u32[]{:S(2)}, u32[]{:S(2)}) collective-permute-start(f32[128,512]{1,0:T(8,128)S(1)} %get-tuple-element.71), channel_id=1, source_target_pairs={{0,12},{4,8},{8,4},{12,0},{1,13},{5,9},{9,5},{13,1},{2,14},{6,10},... | collective-permute-start | bytes 786440 | tf_op jit(solution)/shard_map/ppermute | solution.py:544
  76.7 5.6 %collective-permute-start.15 = (f32[32,128]{1,0:T(8,128)S(1)}, f32[32,128]{1,0:T(8,128)S(1)}, u32[]{:S(2)}, u32[]{:S(2)}) collective-permute-start(f32[32,128]{1,0:T(8,128)S(1)} %get-tuple-element.79), channel_id=1, source_target_pairs={{0,1},{1,2},{2,3},{4,5},{5,6},{6,7},{8,9},{9,10},{10,11},{12,13},{... | collective-permute-start | bytes 49160 | tf_op jit(solution)/shard_map/ppermute | solution.py:23
  79.2 5.4 %collective-permute-start.16 = (f32[32,128]{1,0:T(8,128)S(1)}, f32[32,128]{1,0:T(8,128)S(1)}, u32[]{:S(2)}, u32[]{:S(2)}) collective-permute-start(f32[32,128]{1,0:T(8,128)S(1)} %get-tuple-element.79), channel_id=1, source_target_pairs={{1,0},{2,1},{3,2},{5,4},{6,5},{7,6},{9,8},{10,9},{11,10},{13,12},{... | collective-permute-start | bytes 49160 | tf_op jit(solution)/shard_map/ppermute | solution.py:23
  91.8 10.2 %collective-permute-start.17 = (f32[128,512]{1,0:T(8,128)S(1)}, f32[128,512]{1,0:T(8,128)S(1)}, u32[]{:S(2)}, u32[]{:S(2)}) collective-permute-start(f32[128,512]{1,0:T(8,128)S(1)} %get-tuple-element.82), channel_id=1, source_target_pairs={{0,4},{4,0},{8,12},{12,8},{1,5},{5,1},{9,13},{13,9},{2,6},{6,2},{1... | collective-permute-start | bytes 786440 | tf_op jit(solution)/shard_map/ppermute | solution.py:544
  94.2 18.4 %collective-permute-start.18 = (f32[128,512]{1,0:T(8,128)S(1)}, f32[128,512]{1,0:T(8,128)S(1)}, u32[]{:S(2)}, u32[]{:S(2)}) collective-permute-start(f32[128,512]{1,0:T(8,128)S(1)} %get-tuple-element.83), channel_id=1, source_target_pairs={{0,8},{4,12},{8,0},{12,4},{1,9},{5,13},{9,1},{13,5},{2,10},{6,14},... | collective-permute-start | bytes 786440 | tf_op jit(solution)/shard_map/ppermute | solution.py:544
  95.4 22.1 %collective-permute-start.19 = (f32[128,512]{1,0:T(8,128)S(1)}, f32[128,512]{1,0:T(8,128)S(1)}, u32[]{:S(2)}, u32[]{:S(2)}) collective-permute-start(f32[128,512]{1,0:T(8,128)S(1)} %get-tuple-element.84), channel_id=1, source_target_pairs={{0,12},{4,8},{8,4},{12,0},{1,13},{5,9},{9,5},{13,1},{2,14},{6,10},... | collective-permute-start | bytes 786440 | tf_op jit(solution)/shard_map/ppermute | solution.py:544
  (8 other events, 168.7 us)

commit v6 on v2

--- a/solution.py
+++ b/solution.py
@@ -140,6 +140,7 @@
 TILE = 8
 LANES = 128
 VMEM_LIMIT = 24 * 1024 * 1024
+MOST_VMEM = 60 * 1024 * 1024
 
 
 def whole_spec():
@@ -148,6 +149,14 @@
 
 def any_spec():
     return pl.BlockSpec(memory_space=pl.ANY)
+
+
+def hbm_spec():
+    return pl.BlockSpec(memory_space=pltpu.HBM)
+
+
+def pair(q, ranks):
+    return (ranks - q) % ranks
 
 
 def split(value):
@@ -163,79 +172,86 @@
     return gathered
 
 
-def pack_kernel(ranks, layer, with_edges, plane_ref, mask_ref, after_ref, *refs):
-    if with_edges:
+def pack_kernel(layer, plane_ref, mask_ref, *refs):
+    if not layer:
         (rate_ref, flag_ref), refs = refs[:2], refs[2:]
-    out_refs, refs = refs[:ranks], refs[ranks:]
-    if with_edges:
-        (edge_ref,), refs = refs[:1], refs[1:]
-    mark_ref, low_ref, high_ref, sems = refs
+    refs, (part_ref, mask_part, first_ref, last_ref, mask_sems, in_sems, out_sems) = (
+        refs[:-7],
+        refs[-7:],
+    )
+    out_refs = refs[: part_ref.shape[0]]
+    ranks = len(out_refs)
     planes, rows, cols = plane_ref.shape
-    layers = mask_ref.shape[0] // ranks
-    block = mask_ref.shape[1]
-    held = planes // mask_ref.shape[0]
+    levels, block, _ = mask_ref.shape
+    held = planes // levels
     me = lax.axis_index("comp")
     copies = []
-
-    def start(source, target):
-        copies.append(pltpu.make_async_copy(source, target, sems.at[len(copies)]))
+    order = [*range(1, ranks), 0]
+
+    def start(source, target, sem):
+        copies.append(pltpu.make_async_copy(source, target, sem))
         copies[-1].start()
-        return copies[-1]
-
-    if with_edges:
-        low = start(plane_ref.at[:, :, pl.ds(0, LANES)], low_ref)
-        high = start(plane_ref.at[:, :, pl.ds(cols - LANES, LANES)], high_ref)
-    for q, out_ref in enumerate(out_refs):
-        at = lax.rem(me + q, ranks) * layers + layer
+
+    for q in order:
+        at = jnp.bitwise_xor(me, pair(q, ranks)) * (levels // ranks) + layer
         for index in range(held):
-            start(
-                plane_ref.at[index * mask_ref.shape[0] + at],
-                out_ref.at[pl.ds(index * rows, rows)],
-            )
-    for q, out_ref in enumerate(out_refs):
-        at = lax.rem(me + q, ranks) * layers + layer
-        mark_ref[q] = mask_ref[at].astype(jnp.float32)
-        start(mark_ref.at[q], out_ref.at[pl.ds(held * rows, block)])
-    if with_edges:
-        low.wait()
-        high.wait()
-        copies = copies[2:]
-        last = pl.ds(cols - LANES, LANES)
-        weight_plus, weight_minus = face_weights(rate_ref[1, :, last], flag_ref[1, :, last])
-        columns = [low_ref[plane][:, :1] for plane in range(planes)]
-        columns += [high_ref[plane][:, LANES - 1 :] for plane in range(planes)]
+            spot = pl.ds(index * rows, rows)
+            start(plane_ref.at[index * levels + at], part_ref.at[q, spot], in_sems.at[len(copies)])
+        start(mask_ref.at[at], mask_part.at[q], mask_sems.at[q])
+    arrivals = list(copies)
+    if not layer:
+        start(plane_ref.at[:, :, pl.ds(0, LANES)], first_ref, in_sems.at[len(copies)])
+        start(
+            plane_ref.at[:, :, pl.ds(cols - LANES, LANES)], last_ref, in_sems.at[len(copies)]
+        )
+    edges = copies[len(arrivals) :]
+    copies.clear()
+    for position, q in enumerate(order):
+        for copy in arrivals[position * (held + 1) : (position + 1) * (held + 1)]:
+            copy.wait()
+        part_ref[q, held * rows :, :] = mask_part[q].astype(jnp.float32)
+        start(part_ref.at[q], out_refs[q], out_sems.at[q])
+    for copy in edges:
+        copy.wait()
+    if not layer:
+        end = slice(cols - LANES, cols)
+        weight_plus, weight_minus = face_weights(rate_ref[1, :, end], flag_ref[1, :, end])
+        columns = [first_ref[plane][:, :1] for plane in range(planes)]
+        columns += [last_ref[plane][:, LANES - 1 :] for plane in range(planes)]
         columns += [weight_plus[:, LANES - 1 :], weight_minus[:, LANES - 1 :]]
-        edge_ref[...] = gather_columns(columns, rows)
+        refs[ranks][...] = gather_columns(columns, rows)
     for copy in copies:
         copy.wait()
 
 
-def pack(concentration, stiff_mask, layer, ranks, after, faces):
+def pack(concentration, stiff_mask, layer, ranks, faces):
     planes, rows, cols = concentration.shape
     held = planes // NZ
     block = stiff_mask.shape[1]
-    message = jax.ShapeDtypeStruct((held * rows + block, cols), jnp.float32)
-    out_shape, out_specs = [message] * ranks, [any_spec()] * ranks
-    if faces:
+    size = held * rows + block
+    out_shape = [jax.ShapeDtypeStruct((size, cols), jnp.float32)] * ranks
+    out_specs = [any_spec()] * ranks
+    if not layer:
         out_shape.append(jax.ShapeDtypeStruct((rows, LANES), jnp.float32))
         out_specs.append(whole_spec())
     results = pl.pallas_call(
-        functools.partial(pack_kernel, ranks, layer, bool(faces)),
+        functools.partial(pack_kernel, layer),
         out_shape=out_shape,
-        in_specs=[any_spec(), whole_spec(), any_spec()] + [whole_spec()] * len(faces),
+        in_specs=[hbm_spec()] * 2 + [whole_spec()] * len(faces),
         out_specs=out_specs,
         scratch_shapes=[
-            pltpu.VMEM((ranks, block, cols), jnp.float32),
+            pltpu.VMEM((ranks, size, cols), jnp.float32),
+            pltpu.VMEM((ranks, block, cols), jnp.int32),
             pltpu.VMEM((planes, rows, LANES), jnp.float32),
             pltpu.VMEM((planes, rows, LANES), jnp.float32),
+            pltpu.SemaphoreType.DMA((ranks,)),
             pltpu.SemaphoreType.DMA((ranks * (held + 1) + 2,)),
+            pltpu.SemaphoreType.DMA((ranks,)),
         ],
-        compiler_params=pltpu.CompilerParams(vmem_limit_bytes=VMEM_LIMIT),
-        cost_estimate=pl.CostEstimate(
-            flops=0, bytes_accessed=8 * ranks * held * rows * cols, transcendentals=0
-        ),
+        compiler_params=pltpu.CompilerParams(vmem_limit_bytes=VMEM_LIMIT if layer else MOST_VMEM),
+        cost_estimate=pl.CostEstimate(flops=0, bytes_accessed=0, transcendentals=0),
         name="pack",
-    )(concentration, stiff_mask, after, *faces)
+    )(concentration, stiff_mask, *faces)
     return list(results[:ranks]), results[ranks:]
 
 
@@ -251,7 +267,7 @@
 
     def pick(shape, stacked_dim):
         at = lax.broadcasted_iota(jnp.int32, shape, stacked_dim) // TILE
-        component = lax.rem(me + ranks - at // held, ranks) * held + lax.rem(at, held)
+        component = jnp.bitwise_xor(me, pair(at // held, ranks)) * held + lax.rem(at, held)
         held_at = lax.broadcasted_iota(jnp.int32, shape, 1 - stacked_dim)
         return jnp.where(component == held_at, 1.0, 0.0)
 
@@ -296,16 +312,12 @@
         in_specs=[whole_spec()] * 4 + [any_spec()],
         out_specs=[whole_spec()] * 3,
         compiler_params=pltpu.CompilerParams(vmem_limit_bytes=VMEM_LIMIT),
-        cost_estimate=pl.CostEstimate(
-            flops=12 * stacked * stacked * components,
-            bytes_accessed=32 * stacked * stacked,
-            transcendentals=0,
-        ),
+        cost_estimate=pl.CostEstimate(flops=0, bytes_accessed=0, transcendentals=0),
         name="spread_parameters",
     )(mixing, mixing_inverse, affinity.reshape(1, -1), mineral.reshape(1, -1), after)
 
 
-def step_kernel(pieces, is_first, with_rim, layer, layers, spread_ref, retard_ref, *refs):
+def step_kernel(pieces, layer, is_first, with_rim, spread_ref, retard_ref, *refs):
     value_refs, refs = refs[:pieces], refs[pieces:]
     (low_ref, high_ref, rate_ref, flag_ref, ratio_ref, first_ref, both_ref), refs = (
         refs[:7],
@@ -324,7 +336,7 @@
     components = stacked // TILE
     held = components // pieces
     me = lax.axis_index("comp")
-    ranks = [lax.rem(me + pieces - q, pieces) for q in range(pieces)]
+    ranks = [jnp.bitwise_xor(me, pair(q, pieces)) for q in range(pieces)]
     row_at = lax.broadcasted_iota(jnp.int32, (rows, cols), 0)
     col_at = lax.broadcasted_iota(jnp.int32, (rows, cols), 1)
 
@@ -350,31 +362,30 @@
     def from_upper_col(value, edge):
         return jnp.where(col_at == cols - 1, edge, pltpu.roll(value, cols - 1, 1))
 
+    block = rows // pieces
     if is_first:
-        planes = held * layers * pieces
-        rim_side, rim_at = low_ref[0], 2 * planes
-        turn = LANES - (me * layers + layer)
         sides = []
-        for rank in ranks:
-            side = pltpu.roll(low_ref[jnp.bitwise_xor(me, rank)], turn, 1)
+        low_side, rim_at = low_ref[0], 2 * held * NZ
+        turn = LANES - (me * (NZ // pieces) + layer)
+        for q in range(pieces):
+            side = pltpu.roll(low_ref[pair(q, pieces)], turn, 1)
             for index in range(held):
-                at = index * layers * pieces
-                sides.append((side, planes + at, side, at))
+                sides.append((side, (held + index) * NZ, side, index * NZ))
     else:
-        rim_side, rim_at = low_ref[...], 2 * components
-        low_side, high_side = low_ref[...], high_ref[...]
+        low_side, high_side, rim_at = low_ref[...], high_ref[...], 2 * components
         sides = [(low_side, components + at, high_side, at) for at in range(components)]
     down_plus = from_lower_row(weight_plus[0])
     down_minus = from_lower_row(weight_minus[0])
-    side_plus = from_lower_col(weight_plus[1], column(rim_side, rim_at))
-    side_minus = from_lower_col(weight_minus[1], column(rim_side, rim_at + 1))
+    side_plus = from_lower_col(weight_plus[1], column(low_side, rim_at))
+    side_minus = from_lower_col(weight_minus[1], column(low_side, rim_at + 1))
     centre = down_minus + weight_plus[0] + side_minus + weight_plus[1]
     for at, (low_side, low_at, high_side, high_at) in enumerate(sides):
         q, index = divmod(at, held)
         value = value_refs[q][index * rows : (index + 1) * rows, :]
         component = ranks[q] * held + index
         spread = spread_ref[component]
-        retard = 1.0 / jnp.full((rows, cols), retard_ref[component], jnp.float32)
+        retard = 1.0 / jnp.full((rows, LANES), retard_ref[component], jnp.float32)
+        retard = jnp.concatenate([retard] * (cols // LANES), axis=1)
         change = (
             (down_plus + spread) * from_lower_row(value)
             + (weight_minus[0] + spread) * from_upper_row(value)
@@ -412,10 +423,9 @@
 
     lax.fori_loop(0, STIFF, stiff_step, 0)
     if is_first:
-        block = rows // pieces
         for rank, value_ref in zip(ranks, value_refs):
             spot = pl.ds(pl.multiple_of(rank * block, TILE), block)
-            stiff_ref[spot, :] = value_ref[held * rows :, :]
+            stiff_ref[spot, :] = value_ref[held * rows : held * rows + block, :]
     for group in range(groups):
         spot = slice(group * TILE, (group + 1) * TILE)
         stiff = stiff_ref[spot, :] > 0.0
@@ -432,7 +442,7 @@
         rim_ref[...] = gather_columns(columns, rows)
 
 
-def layer_step(values, stiff, low, high, shared, layer, layers, with_rim):
+def layer_step(values, stiff, low, high, shared, layer, with_rim):
     dispersion, retardation, face_rate, face_flag, ratio, first, both = shared
     pieces = len(values)
     rows, cols = face_rate.shape[1:]
@@ -453,15 +463,13 @@
     if stiff is not None:
         operands.append(stiff)
     results = pl.pallas_call(
-        functools.partial(step_kernel, pieces, stiff is None, with_rim, layer, layers),
+        functools.partial(step_kernel, pieces, layer, stiff is None, with_rim),
         out_shape=out_shape,
         in_specs=[scalar, scalar] + [whole_spec()] * (len(operands) - 2),
         out_specs=[whole_spec()] * len(out_shape),
         scratch_shapes=[field, field, field],
         compiler_params=pltpu.CompilerParams(vmem_limit_bytes=VMEM_LIMIT),
-        cost_estimate=pl.CostEstimate(
-            flops=0, bytes_accessed=8 * components * cells, transcendentals=0
-        ),
+        cost_estimate=pl.CostEstimate(flops=0, bytes_accessed=0, transcendentals=0),
         name="layer_step",
     )(*operands)
     values, results = results[:pieces], results[pieces:]
@@ -488,46 +496,44 @@
     layers = NZ // ranks
 
     def send(value, by):
-        return lax.ppermute(value, "comp", [(i, (i + by) % ranks) for i in range(ranks)])
-
-    faces = (face_rate, face_flag)
-    messages, (edges,) = pack(concentration, stiff_mask, 0, ranks, face_rate, faces)
-    arrived = [[send(part, q) if q else part for q, part in enumerate(messages)]]
+        return lax.ppermute(value, "comp", [(i, i ^ by) for i in range(ranks)]) if by else value
+
+    def send_all(parts):
+        return [send(part, pair(q, ranks)) for q, part in enumerate(parts)]
+
+    messages, (edges,) = pack(concentration, stiff_mask, 0, ranks, (face_rate, face_flag))
+    arrived = [send_all(messages)]
 
     from_low, from_high = shifted(edges, "space", 1), shifted(edges, "space", -1)
     lane_at = lax.broadcasted_iota(jnp.int32, edges.shape, 1)
     sides = jnp.where(lane_at < planes, from_high, from_low)[None]
     span = 1
     while span < ranks:
-        other = lax.ppermute(sides, "comp", [(i, i ^ span) for i in range(ranks)])
-        sides = jnp.concatenate([sides, other])
+        sides = jnp.concatenate([sides, send(sides, span)])
         span *= 2
 
-    first, both, ratio = spread_parameters(
-        ranks, mixing, mixing_inverse, affinity, mineral, edges
-    )
+    for layer in range(1, layers):
+        messages, _ = pack(concentration, stiff_mask, layer, ranks, ())
+        messages, sides = lax.optimization_barrier((messages, sides))
+        arrived.append(send_all(messages))
+
+    first, both, ratio = spread_parameters(ranks, mixing, mixing_inverse, affinity, mineral, edges)
     shared = (dispersion, retardation, face_rate, face_flag, ratio, first, both)
-
-    for layer in range(1, layers):
-        messages, _ = pack(concentration, stiff_mask, layer, ranks, sides, ())
-        arrived.append([send(part, q) if q else part for q, part in enumerate(messages)])
 
     result = jnp.zeros((held, NZ, rows, cols), jnp.float32)
     for layer in range(layers):
-        values, stiff, low, high = arrived[layer], None, sides, sides
+        values, stiff = arrived[layer], None
+        low, high = sides, sides
         for step in range(STEPS):
             last = step == STEPS - 1
-            values, stiff, rims = layer_step(
-                values, stiff, low, high, shared, layer, layers, not last
-            )
+            values, stiff, rims = layer_step(values, stiff, low, high, shared, layer, not last)
             if not last:
                 low, high = shifted(rims, "space", 1), shifted(rims, "space", -1)
-        for q in range(ranks):
-            piece = send(values[q], -q) if q else values[q]
+        for q, piece in enumerate(send_all(values)):
             result = lax.dynamic_update_slice(
                 result,
                 piece.reshape(held, 1, rows, cols),
-                (0, (me + q) % ranks * layers + layer, 0, 0),
+                (0, (me ^ pair(q, ranks)) * layers + layer, 0, 0),
             )
     return result.reshape(planes, rows, cols)
 

time: 122 us -> 119 us (0.975)
  local copies, waits for them, and re-layouts: 7.98 us -> 3.7 us
  waiting for transfers between devices: 49 us -> 45.1 us
  starting transfers between devices: 29.8 us -> 32.4 us
  Pallas kernels: 34.8 us -> 36.9 us
    unnamed x26, local copies, waits for them, and re-layouts: 5.65 us -> 1.36 us
    ppermute x14, waiting for transfers between devices: 42.5 us -> 38.9 us  [send(): lax.ppermute(value, 'comp', [(i, i ^ by) for i in range(ranks)])]
    pallas_call x6, Pallas kernels: 34 us -> 36.1 us  [the longest x4 30.1 us: layer_step(): pl.pallas_call(functools.partial(step_kernel, pieces, layer, stiff is Non...]
    ppermute x14, starting transfers between devices: 14.2 us -> 16.3 us  [send(): lax.ppermute(value, 'comp', [(i, i ^ by) for i in range(ranks)])]
  transfers between devices with their start and end apart: 20 -> 20, of which waited for: 6 -> 6; matrix products, arithmetic and copies ran while one was open for 2% -> 2% of each run, Pallas kernels for 27% -> 28%
where the time goes in v6:
time: 119 us; the launch traced here: 118 us
  waiting for transfers between devices  45.1 us (38%)
  Pallas kernels  36.9 us (31%)
  starting transfers between devices  32.4 us (27%)
  local copies, waits for them, and re-layouts  3.7 us (3%)
    ppermute x14, waiting for transfers between devices, send(): lax.ppermute(value, 'comp', [(i, i ^ by) for i in range(ranks)])  38.9 us
    pallas_call x4, Pallas kernels, layer_step(): pl.pallas_call(functools.partial(step_kernel, pieces, layer, stiff is Non...  30.1 us
    ppermute x14, starting transfers between devices, send(): lax.ppermute(value, 'comp', [(i, i ^ by) for i in range(ranks)])  16.3 us
    ppermute x6, starting transfers between devices, shifted(): return lax.ppermute(shard, axis, pairs)  16.1 us
    ppermute x6, waiting for transfers between devices, shifted(): return lax.ppermute(shard, axis, pairs)  6.18 us
    pallas_call x2, Pallas kernels, pack(): pl.pallas_call(functools.partial(pack_kernel, layer), out_shape=out_shape...  5.96 us
  transfers between devices with their start and end apart: 20, of which 6 were waited for; matrix products, arithmetic and copies ran while one was open for 2% of the time, Pallas kernels for 28%

profile of v6, /device:TPU:1, one launch (start us, length us, event | category | flops | bytes accessed | tf_op | source)
XLA Modules:
  0.0 118.5 jit_solution(3834832063687507545)
XLA Ops:
  0.1 4.1 %pack.2 = (f32[136,512]{1,0:T(8,128)}, f32[136,512]{1,0:T(8,128)}, f32[136,512]{1,0:T(8,128)}, f32[136,512]{1,0:T(8,128)}, f32[32,128]{1,0:T(8,128)}) custom-call(f32[32,32,512]{2,1,0:T(8,128)} %plane_ref.3, s32[8,8,512]{2,1,0:T(8,128)} %mask_ref.3, f32[2,32,512]{2,1,0:T(8,128)} %refs_6_.7, s32[2,32,512]{2,1,0:T(8,128)} %refs_7_.7), custom_call_target="tpu_custom_call" | custom-call | tf_op jit(solution)/shard_map/pack/pallas_call | solution.py:237
  4.2 2.1 %collective-permute-start.3 = (f32[32,128]{1,0:T(8,128)}, f32[32,128]{1,0:T(8,128)S(1)}, u32[]{:S(2)}, u32[]{:S(2)}) collective-permute-start(f32[32,128]{1,0:T(8,128)} %get-tuple-element.50.refs_0_), channel_id=1, source_target_pairs={{1,0},{2,1},{3,2},{5,4},{6,5},{7,6},{9,8},{10,9},{11,10},{13,12},{... | collective-permute-start | bytes 49160 | tf_op jit(solution)/shard_map/ppermute | solution.py:23
  6.3 4.5 %collective-permute-start.4 = (f32[32,128]{1,0:T(8,128)}, f32[32,128]{1,0:T(8,128)S(1)}, u32[]{:S(2)}, u32[]{:S(2)}) collective-permute-start(f32[32,128]{1,0:T(8,128)} %get-tuple-element.50.refs_0_), channel_id=1, source_target_pairs={{0,1},{1,2},{2,3},{4,5},{5,6},{6,7},{8,9},{9,10},{10,11},{12,13},{... | collective-permute-start | bytes 49160 | tf_op jit(solution)/shard_map/ppermute | solution.py:23
  10.7 3.4 %collective-permute-start = (f32[136,512]{1,0:T(8,128)}, f32[136,512]{1,0:T(8,128)S(1)}, u32[]{:S(2)}, u32[]{:S(2)}) collective-permute-start(f32[136,512]{1,0:T(8,128)} %get-tuple-element.43), channel_id=1, source_target_pairs={{0,12},{4,8},{8,4},{12,0},{1,13},{5,9},{9,5},{13,1},{2,14},{6,10},... | collective-permute-start | bytes 835592 | tf_op jit(solution)/shard_map/ppermute | solution.py:499
  15.7 5.9 %collective-permute-done.5 = f32[1,32,128]{2,1,0:T(8,128)S(1)} collective-permute-done((f32[1,32,128]{2,1,0:T(8,128)S(1)}, f32[1,32,128]{2,1,0:T(8,128)S(1)}, u32[]{:S(2)}, u32[]{:S(2)}) %collective-permute-start.5) | collective-permute-done | bytes 16416 | tf_op jit(solution)/shard_map/ppermute | solution.py:499
  22.2 1.9 %pack.3 = (f32[136,512]{1,0:T(8,128)S(1)}, f32[136,512]{1,0:T(8,128)S(1)}, f32[136,512]{1,0:T(8,128)S(1)}, f32[136,512]{1,0:T(8,128)S(1)}) custom-call(f32[32,32,512]{2,1,0:T(8,128)S(1)} %copy-done, s32[8,8,512]{2,1,0:T(8,128)S(1)} %copy-done.3), custom_call_target="tpu_custom_call" | custom-call | tf_op jit(solution)/shard_map/pack/pallas_call | solution.py:237
  24.1 15.6 %collective-permute-done.6 = f32[2,32,128]{2,1,0:T(8,128)S(1)} collective-permute-done((f32[2,32,128]{2,1,0:T(8,128)S(1)}, f32[2,32,128]{2,1,0:T(8,128)S(1)}, u32[]{:S(2)}, u32[]{:S(2)}) %collective-permute-start.6) | collective-permute-done | bytes 32800 | tf_op jit(solution)/shard_map/ppermute | solution.py:499
  39.7 2.2 %collective-permute-start.12 = (f32[136,512]{1,0:T(8,128)S(1)}, f32[136,512]{1,0:T(8,128)S(1)}, u32[]{:S(2)}, u32[]{:S(2)}) collective-permute-start(f32[136,512]{1,0:T(8,128)S(1)} %get-tuple-element.66), channel_id=1, source_target_pairs={{0,12},{4,8},{8,4},{12,0},{1,13},{5,9},{9,5},{13,1},{2,14},{6,10},... | collective-permute-start | bytes 835592 | tf_op jit(solution)/shard_map/ppermute | solution.py:499
  41.9 1.4 %collective-permute-start.14 = (f32[136,512]{1,0:T(8,128)S(1)}, f32[136,512]{1,0:T(8,128)S(1)}, u32[]{:S(2)}, u32[]{:S(2)}) collective-permute-start(f32[136,512]{1,0:T(8,128)S(1)} %get-tuple-element.68), channel_id=1, source_target_pairs={{0,4},{4,0},{8,12},{12,8},{1,5},{5,1},{9,13},{13,9},{2,6},{6,2},{1... | collective-permute-start | bytes 835592 | tf_op jit(solution)/shard_map/ppermute | solution.py:499
  44.2 7.5 %layer_step.4 = (f32[128,512]{1,0:T(8,128)S(1)}, f32[128,512]{1,0:T(8,128)S(1)}, f32[128,512]{1,0:T(8,128)S(1)}, f32[128,512]{1,0:T(8,128)S(1)}, f32[32,128]{1,0:T(8,128)S(1)}, /*index=5*/f32[32,512]{1,0:T(8,128)S(1)}) custom-call(f32[16]{0:T(128)S(1)} %copy-done.6, f32[16]{0:T(128)S(1)} %copy-done.7, f32[136,512]{1,0:T(8,128)S(1)} %copy-done.4, ...), custom_call_target="tpu_custom_call" | custom-call | tf_op jit(solution)/shard_map/layer_step/pallas_call | solution.py:465
  51.7 2.8 %collective-permute-start.7 = (f32[32,128]{1,0:T(8,128)S(1)}, f32[32,128]{1,0:T(8,128)S(1)}, u32[]{:S(2)}, u32[]{:S(2)}) collective-permute-start(f32[32,128]{1,0:T(8,128)S(1)} %get-tuple-element.59), channel_id=1, source_target_pairs={{0,1},{1,2},{2,3},{4,5},{5,6},{6,7},{8,9},{9,10},{10,11},{12,13},{... | collective-permute-start | bytes 49160 | tf_op jit(solution)/shard_map/ppermute | solution.py:23
  54.5 1.9 %collective-permute-start.8 = (f32[32,128]{1,0:T(8,128)S(1)}, f32[32,128]{1,0:T(8,128)S(1)}, u32[]{:S(2)}, u32[]{:S(2)}) collective-permute-start(f32[32,128]{1,0:T(8,128)S(1)} %get-tuple-element.59), channel_id=1, source_target_pairs={{1,0},{2,1},{3,2},{5,4},{6,5},{7,6},{9,8},{10,9},{11,10},{13,12},{... | collective-permute-start | bytes 49160 | tf_op jit(solution)/shard_map/ppermute | solution.py:23
  56.5 3.1 %collective-permute-done.8.refs_5_ = f32[32,128]{1,0:T(8,128)S(1)} collective-permute-done((f32[32,128]{1,0:T(8,128)S(1)}, f32[32,128]{1,0:T(8,128)S(1)}, u32[]{:S(2)}, u32[]{:S(2)}) %collective-permute-start.8) | collective-permute-done | bytes 16416 | tf_op jit(solution)/shard_map/ppermute | solution.py:23
  59.6 8.0 %layer_step.5 = (f32[128,512]{1,0:T(8,128)S(1)}, f32[128,512]{1,0:T(8,128)}, f32[128,512]{1,0:T(8,128)}, f32[128,512]{1,0:T(8,128)S(1)}) custom-call(f32[16]{0:T(128)S(1)} %copy-done.6, f32[16]{0:T(128)S(1)} %copy-done.7, f32[128,512]{1,0:T(8,128)S(1)} %get-tuple-element.55.refs_0_, f32[128,512]{1,0:T(8,128)S(1)} %get-tuple-element.56.refs_1_, ...), custom_call_target="tpu_custom_call" | custom-call | tf_op jit(solution)/shard_map/layer_step/pallas_call | solution.py:465
  67.6 2.7 %collective-permute-start.9 = (f32[128,512]{1,0:T(8,128)}, f32[128,512]{1,0:T(8,128)}, u32[]{:S(2)}, u32[]{:S(2)}) collective-permute-start(f32[128,512]{1,0:T(8,128)} %get-tuple-element.62), channel_id=1, source_target_pairs={{0,12},{4,8},{8,4},{12,0},{1,13},{5,9},{9,5},{13,1},{2,14},{6,10},... | collective-permute-start | bytes 786440 | tf_op jit(solution)/shard_map/ppermute | solution.py:499
  71.1 7.4 %layer_step.6 = (f32[128,512]{1,0:T(8,128)S(1)}, f32[128,512]{1,0:T(8,128)S(1)}, f32[128,512]{1,0:T(8,128)S(1)}, f32[128,512]{1,0:T(8,128)S(1)}, f32[32,128]{1,0:T(8,128)S(1)}, /*index=5*/f32[32,512]{1,0:T(8,128)S(1)}) custom-call(f32[16]{0:T(128)S(1)} %copy-done.6, f32[16]{0:T(128)S(1)} %copy-done.7, f32[136,512]{1,0:T(8,128)S(1)} %get-tuple-element.65.refs_0_, ...), custom_call_target="tpu_custom_call" | custom-call | tf_op jit(solution)/shard_map/layer_step/pallas_call | solution.py:465
  78.5 2.8 %collective-permute-start.15 = (f32[32,128]{1,0:T(8,128)S(1)}, f32[32,128]{1,0:T(8,128)S(1)}, u32[]{:S(2)}, u32[]{:S(2)}) collective-permute-start(f32[32,128]{1,0:T(8,128)S(1)} %get-tuple-element.73), channel_id=1, source_target_pairs={{0,1},{1,2},{2,3},{4,5},{5,6},{6,7},{8,9},{9,10},{10,11},{12,13},{... | collective-permute-start | bytes 49160 | tf_op jit(solution)/shard_map/ppermute | solution.py:23
  81.3 2.1 %collective-permute-start.16 = (f32[32,128]{1,0:T(8,128)S(1)}, f32[32,128]{1,0:T(8,128)S(1)}, u32[]{:S(2)}, u32[]{:S(2)}) collective-permute-start(f32[32,128]{1,0:T(8,128)S(1)} %get-tuple-element.73), channel_id=1, source_target_pairs={{1,0},{2,1},{3,2},{5,4},{6,5},{7,6},{9,8},{10,9},{11,10},{13,12},{... | collective-permute-start | bytes 49160 | tf_op jit(solution)/shard_map/ppermute | solution.py:23
  83.7 3.0 %collective-permute-done.16.refs_5_ = f32[32,128]{1,0:T(8,128)S(1)} collective-permute-done((f32[32,128]{1,0:T(8,128)S(1)}, f32[32,128]{1,0:T(8,128)S(1)}, u32[]{:S(2)}, u32[]{:S(2)}) %collective-permute-start.16) | collective-permute-done | bytes 16416 | tf_op jit(solution)/shard_map/ppermute | solution.py:23
  86.7 7.3 %layer_step.7 = (f32[128,512]{1,0:T(8,128)S(1)}, f32[128,512]{1,0:T(8,128)S(1)}, f32[128,512]{1,0:T(8,128)S(1)}, f32[128,512]{1,0:T(8,128)S(1)}) custom-call(f32[16]{0:T(128)S(1)} %copy-done.6, f32[16]{0:T(128)S(1)} %copy-done.7, f32[128,512]{1,0:T(8,128)S(1)} %get-tuple-element.69.refs_0_, f32[128,512]{1,0:T(8,128)S(1)} %get-tuple-element.70.refs_1_, ...), custom_call_target="tpu_custom_call" | custom-call | tf_op jit(solution)/shard_map/layer_step/pallas_call | solution.py:465
  94.0 2.5 %collective-permute-start.17 = (f32[128,512]{1,0:T(8,128)S(1)}, f32[128,512]{1,0:T(8,128)S(1)}, u32[]{:S(2)}, u32[]{:S(2)}) collective-permute-start(f32[128,512]{1,0:T(8,128)S(1)} %get-tuple-element.76), channel_id=1, source_target_pairs={{0,12},{4,8},{8,4},{12,0},{1,13},{5,9},{9,5},{13,1},{2,14},{6,10},... | collective-permute-start | bytes 786440 | tf_op jit(solution)/shard_map/ppermute | solution.py:499
  99.7 4.4 %collective-permute-done.17 = f32[128,512]{1,0:T(8,128)S(1)} collective-permute-done((f32[128,512]{1,0:T(8,128)S(1)}, f32[128,512]{1,0:T(8,128)S(1)}, u32[]{:S(2)}, u32[]{:S(2)}) %collective-permute-start.17) | collective-permute-done | bytes 262176 | tf_op jit(solution)/shard_map/ppermute | solution.py:499
  104.1 13.0 %collective-permute-done.18 = f32[128,512]{1,0:T(8,128)S(1)} collective-permute-done((f32[128,512]{1,0:T(8,128)S(1)}, f32[128,512]{1,0:T(8,128)S(1)}, u32[]{:S(2)}, u32[]{:S(2)}) %collective-permute-start.18) | collective-permute-done | bytes 262176 | tf_op jit(solution)/shard_map/ppermute | solution.py:499
  117.2 1.3 %copy-done.12 = f32[4,8,32,512]{3,2,1,0:T(8,128)} copy-done((f32[4,8,32,512]{3,2,1,0:T(8,128)}, f32[4,8,32,512]{3,2,1,0:T(8,128)S(1)}, u32[]{:S(2)}) %copy-start.12) | copy-done | bytes 2097176
  (62 shorter events, 7.3 us)
Async XLA Ops:
  0.0 44.2 %copy-start.1 = (f32[2,32,512]{2,1,0:T(8,128)S(1)}, f32[2,32,512]{2,1,0:T(8,128)}, u32[]{:S(2)}) copy-start(f32[2,32,512]{2,1,0:T(8,128)} %refs_6_.7) | copy-start | bytes 393220
  0.0 44.2 %copy-start.2 = (s32[2,32,512]{2,1,0:T(8,128)S(1)}, s32[2,32,512]{2,1,0:T(8,128)}, u32[]{:S(2)}) copy-start(s32[2,32,512]{2,1,0:T(8,128)} %refs_7_.7) | copy-start | bytes 393220
  0.1 44.1 %copy-start.7 = (f32[16]{0:T(128)S(1)}, f32[16]{0:T(128)}, u32[]{:S(2)}) copy-start(f32[16]{0:T(128)} %retard_ref.7) | copy-start | bytes 196
  0.1 44.1 %copy-start.6 = (f32[16]{0:T(128)S(1)}, f32[16]{0:T(128)}, u32[]{:S(2)}) copy-start(f32[16]{0:T(128)} %spread_ref.7) | copy-start | bytes 196
  4.2 10.0 %collective-permute-start.3 = (f32[32,128]{1,0:T(8,128)}, f32[32,128]{1,0:T(8,128)S(1)}, u32[]{:S(2)}, u32[]{:S(2)}) collective-permute-start(f32[32,128]{1,0:T(8,128)} %get-tuple-element.50.refs_0_), channel_id=1, source_target_pairs={{1,0},{2,1},{3,2},{5,4},{6,5},{7,6},{9,8},{10,9},{11,10},{13,12},{... | collective-permute-start | bytes 49160 | tf_op jit(solution)/shard_map/ppermute | solution.py:23
  6.3 7.9 %collective-permute-start.4 = (f32[32,128]{1,0:T(8,128)}, f32[32,128]{1,0:T(8,128)S(1)}, u32[]{:S(2)}, u32[]{:S(2)}) collective-permute-start(f32[32,128]{1,0:T(8,128)} %get-tuple-element.50.refs_0_), channel_id=1, source_target_pairs={{0,1},{1,2},{2,3},{4,5},{5,6},{6,7},{8,9},{9,10},{10,11},{12,13},{... | collective-permute-start | bytes 49160 | tf_op jit(solution)/shard_map/ppermute | solution.py:23
  10.7 31.2 %collective-permute-start = (f32[136,512]{1,0:T(8,128)}, f32[136,512]{1,0:T(8,128)S(1)}, u32[]{:S(2)}, u32[]{:S(2)}) collective-permute-start(f32[136,512]{1,0:T(8,128)} %get-tuple-element.43), channel_id=1, source_target_pairs={{0,12},{4,8},{8,4},{12,0},{1,13},{5,9},{9,5},{13,1},{2,14},{6,10},... | collective-permute-start | bytes 835592 | tf_op jit(solution)/shard_map/ppermute | solution.py:499
  14.2 7.4 %collective-permute-start.5 = (f32[1,32,128]{2,1,0:T(8,128)S(1)}, f32[1,32,128]{2,1,0:T(8,128)S(1)}, u32[]{:S(2)}, u32[]{:S(2)}) collective-permute-start(f32[1,32,128]{2,1,0:T(8,128)S(1)} %select_bitcast_fusion), channel_id=1, source_target_pairs={{0,4},{4,0},{8,12},{12,8},{1,5},{5,1},{9,13},{13,9},{2,6},{6,2},{1... | collective-permute-start | bytes 49160 | tf_op jit(solution)/shard_map/ppermute | solution.py:499
  14.2 29.9 %collective-permute-start.1 = (f32[136,512]{1,0:T(8,128)}, f32[136,512]{1,0:T(8,128)S(1)}, u32[]{:S(2)}, u32[]{:S(2)}) collective-permute-start(f32[136,512]{1,0:T(8,128)} %get-tuple-element.44), channel_id=1, source_target_pairs={{0,8},{4,12},{8,0},{12,4},{1,9},{5,13},{9,1},{13,5},{2,10},{6,14},... | collective-permute-start | bytes 835592 | tf_op jit(solution)/shard_map/ppermute | solution.py:499
  15.4 28.7 %collective-permute-start.2 = (f32[136,512]{1,0:T(8,128)}, f32[136,512]{1,0:T(8,128)S(1)}, u32[]{:S(2)}, u32[]{:S(2)}) collective-permute-start(f32[136,512]{1,0:T(8,128)} %get-tuple-element.45), channel_id=1, source_target_pairs={{0,4},{4,0},{8,12},{12,8},{1,5},{5,1},{9,13},{13,9},{2,6},{6,2},{1... | collective-permute-start | bytes 835592 | tf_op jit(solution)/shard_map/ppermute | solution.py:499
  21.6 18.2 %collective-permute-start.6 = (f32[2,32,128]{2,1,0:T(8,128)S(1)}, f32[2,32,128]{2,1,0:T(8,128)S(1)}, u32[]{:S(2)}, u32[]{:S(2)}) collective-permute-start(f32[2,32,128]{2,1,0:T(8,128)S(1)} %pad_maximum_fusion.1), channel_id=1, source_target_pairs={{0,8},{4,12},{8,0},{12,4},{1,9},{5,13},{9,1},{13,5},{2,10},{6,14},... | collective-permute-start | bytes 98312 | tf_op jit(solution)/shard_map/ppermute | solution.py:499
  39.7 30.6 %collective-permute-start.12 = (f32[136,512]{1,0:T(8,128)S(1)}, f32[136,512]{1,0:T(8,128)S(1)}, u32[]{:S(2)}, u32[]{:S(2)}) collective-permute-start(f32[136,512]{1,0:T(8,128)S(1)} %get-tuple-element.66), channel_id=1, source_target_pairs={{0,12},{4,8},{8,4},{12,0},{1,13},{5,9},{9,5},{13,1},{2,14},{6,10},... | collective-permute-start | bytes 835592 | tf_op jit(solution)/shard_map/ppermute | solution.py:499
  41.9 29.2 %collective-permute-start.13 = (f32[136,512]{1,0:T(8,128)S(1)}, f32[136,512]{1,0:T(8,128)S(1)}, u32[]{:S(2)}, u32[]{:S(2)}) collective-permute-start(f32[136,512]{1,0:T(8,128)S(1)} %get-tuple-element.67), channel_id=1, source_target_pairs={{0,8},{4,12},{8,0},{12,4},{1,9},{5,13},{9,1},{13,5},{2,10},{6,14},... | collective-permute-start | bytes 835592 | tf_op jit(solution)/shard_map/ppermute | solution.py:499
  41.9 29.2 %collective-permute-start.14 = (f32[136,512]{1,0:T(8,128)S(1)}, f32[136,512]{1,0:T(8,128)S(1)}, u32[]{:S(2)}, u32[]{:S(2)}) collective-permute-start(f32[136,512]{1,0:T(8,128)S(1)} %get-tuple-element.68), channel_id=1, source_target_pairs={{0,4},{4,0},{8,12},{12,8},{1,5},{5,1},{9,13},{13,9},{2,6},{6,2},{1... | collective-permute-start | bytes 835592 | tf_op jit(solution)/shard_map/ppermute | solution.py:499
  51.7 4.7 %collective-permute-start.7 = (f32[32,128]{1,0:T(8,128)S(1)}, f32[32,128]{1,0:T(8,128)S(1)}, u32[]{:S(2)}, u32[]{:S(2)}) collective-permute-start(f32[32,128]{1,0:T(8,128)S(1)} %get-tuple-element.59), channel_id=1, source_target_pairs={{0,1},{1,2},{2,3},{4,5},{5,6},{6,7},{8,9},{9,10},{10,11},{12,13},{... | collective-permute-start | bytes 49160 | tf_op jit(solution)/shard_map/ppermute | solution.py:23
  54.5 5.1 %collective-permute-start.8 = (f32[32,128]{1,0:T(8,128)S(1)}, f32[32,128]{1,0:T(8,128)S(1)}, u32[]{:S(2)}, u32[]{:S(2)}) collective-permute-start(f32[32,128]{1,0:T(8,128)S(1)} %get-tuple-element.59), channel_id=1, source_target_pairs={{1,0},{2,1},{3,2},{5,4},{6,5},{7,6},{9,8},{10,9},{11,10},{13,12},{... | collective-permute-start | bytes 49160 | tf_op jit(solution)/shard_map/ppermute | solution.py:23
  67.6 29.0 %collective-permute-start.9 = (f32[128,512]{1,0:T(8,128)}, f32[128,512]{1,0:T(8,128)}, u32[]{:S(2)}, u32[]{:S(2)}) collective-permute-start(f32[128,512]{1,0:T(8,128)} %get-tuple-element.62), channel_id=1, source_target_pairs={{0,12},{4,8},{8,4},{12,0},{1,13},{5,9},{9,5},{13,1},{2,14},{6,10},... | collective-permute-start | bytes 786440 | tf_op jit(solution)/shard_map/ppermute | solution.py:499
  70.3 28.3 %collective-permute-start.10 = (f32[128,512]{1,0:T(8,128)}, f32[128,512]{1,0:T(8,128)}, u32[]{:S(2)}, u32[]{:S(2)}) collective-permute-start(f32[128,512]{1,0:T(8,128)} %get-tuple-element.63), channel_id=1, source_target_pairs={{0,8},{4,12},{8,0},{12,4},{1,9},{5,13},{9,1},{13,5},{2,10},{6,14},... | collective-permute-start | bytes 786440 | tf_op jit(solution)/shard_map/ppermute | solution.py:499
  70.3 29.3 %collective-permute-start.11 = (f32[128,512]{1,0:T(8,128)S(1)}, f32[128,512]{1,0:T(8,128)S(1)}, u32[]{:S(2)}, u32[]{:S(2)}) collective-permute-start(f32[128,512]{1,0:T(8,128)S(1)} %get-tuple-element.64), channel_id=1, source_target_pairs={{0,4},{4,0},{8,12},{12,8},{1,5},{5,1},{9,13},{13,9},{2,6},{6,2},{1... | collective-permute-start | bytes 786440 | tf_op jit(solution)/shard_map/ppermute | solution.py:499
  78.5 5.2 %collective-permute-start.15 = (f32[32,128]{1,0:T(8,128)S(1)}, f32[32,128]{1,0:T(8,128)S(1)}, u32[]{:S(2)}, u32[]{:S(2)}) collective-permute-start(f32[32,128]{1,0:T(8,128)S(1)} %get-tuple-element.73), channel_id=1, source_target_pairs={{0,1},{1,2},{2,3},{4,5},{5,6},{6,7},{8,9},{9,10},{10,11},{12,13},{... | collective-permute-start | bytes 49160 | tf_op jit(solution)/shard_map/ppermute | solution.py:23
  81.3 5.5 %collective-permute-start.16 = (f32[32,128]{1,0:T(8,128)S(1)}, f32[32,128]{1,0:T(8,128)S(1)}, u32[]{:S(2)}, u32[]{:S(2)}) collective-permute-start(f32[32,128]{1,0:T(8,128)S(1)} %get-tuple-element.73), channel_id=1, source_target_pairs={{1,0},{2,1},{3,2},{5,4},{6,5},{7,6},{9,8},{10,9},{11,10},{13,12},{... | collective-permute-start | bytes 49160 | tf_op jit(solution)/shard_map/ppermute | solution.py:23
  94.0 10.1 %collective-permute-start.17 = (f32[128,512]{1,0:T(8,128)S(1)}, f32[128,512]{1,0:T(8,128)S(1)}, u32[]{:S(2)}, u32[]{:S(2)}) collective-permute-start(f32[128,512]{1,0:T(8,128)S(1)} %get-tuple-element.76), channel_id=1, source_target_pairs={{0,12},{4,8},{8,4},{12,0},{1,13},{5,9},{9,5},{13,1},{2,14},{6,10},... | collective-permute-start | bytes 786440 | tf_op jit(solution)/shard_map/ppermute | solution.py:499
  96.5 20.5 %collective-permute-start.18 = (f32[128,512]{1,0:T(8,128)S(1)}, f32[128,512]{1,0:T(8,128)S(1)}, u32[]{:S(2)}, u32[]{:S(2)}) collective-permute-start(f32[128,512]{1,0:T(8,128)S(1)} %get-tuple-element.77), channel_id=1, source_target_pairs={{0,8},{4,12},{8,0},{12,4},{1,9},{5,13},{9,1},{13,5},{2,10},{6,14},... | collective-permute-start | bytes 786440 | tf_op jit(solution)/shard_map/ppermute | solution.py:499
  96.5 20.6 %collective-permute-start.19 = (f32[128,512]{1,0:T(8,128)S(1)}, f32[128,512]{1,0:T(8,128)S(1)}, u32[]{:S(2)}, u32[]{:S(2)}) collective-permute-start(f32[128,512]{1,0:T(8,128)S(1)} %get-tuple-element.78), channel_id=1, source_target_pairs={{0,4},{4,0},{8,12},{12,8},{1,5},{5,1},{9,13},{13,9},{2,6},{6,2},{1... | collective-permute-start | bytes 786440 | tf_op jit(solution)/shard_map/ppermute | solution.py:499
  (9 other events, 298.0 us)

commit v7 on v6

--- a/solution.py
+++ b/solution.py
@@ -159,6 +159,17 @@
     return (ranks - q) % ranks
 
 
+def spans(ranks):
+    return [ranks >> bit for bit in range(1, ranks.bit_length())]
+
+
+def doubled(ranks):
+    places = [0]
+    for by in spans(ranks):
+        places += [place ^ by for place in places]
+    return places
+
+
 def split(value):
     high = value.astype(jnp.bfloat16)
     return high, (value - high.astype(jnp.float32)).astype(jnp.bfloat16)
@@ -368,7 +379,7 @@
         low_side, rim_at = low_ref[0], 2 * held * NZ
         turn = LANES - (me * (NZ // pieces) + layer)
         for q in range(pieces):
-            side = pltpu.roll(low_ref[pair(q, pieces)], turn, 1)
+            side = pltpu.roll(low_ref[doubled(pieces).index(pair(q, pieces))], turn, 1)
             for index in range(held):
                 sides.append((side, (held + index) * NZ, side, index * NZ))
     else:
@@ -507,14 +518,16 @@
     from_low, from_high = shifted(edges, "space", 1), shifted(edges, "space", -1)
     lane_at = lax.broadcasted_iota(jnp.int32, edges.shape, 1)
     sides = jnp.where(lane_at < planes, from_high, from_low)[None]
-    span = 1
-    while span < ranks:
-        sides = jnp.concatenate([sides, send(sides, span)])
-        span *= 2
-
-    for layer in range(1, layers):
-        messages, _ = pack(concentration, stiff_mask, layer, ranks, ())
-        messages, sides = lax.optimization_barrier((messages, sides))
+    later = [pack(concentration, stiff_mask, layer, ranks, ())[0] for layer in range(1, layers)]
+    sides, later = lax.optimization_barrier((sides, later))
+    for by in spans(ranks):
+        if by == 1:
+            sides, arrived[0] = lax.optimization_barrier((sides, arrived[0]))
+        sides = jnp.concatenate([sides, send(sides, by)])
+
+    for messages in later:
+        messages[:-1], arrived[-1] = lax.optimization_barrier((messages[:-1], arrived[-1]))
+        messages[-1], sides = lax.optimization_barrier((messages[-1], sides))
         arrived.append(send_all(messages))
 
     first, both, ratio = spread_parameters(ranks, mixing, mixing_inverse, affinity, mineral, edges)

time: 119 us -> 120 us (level)
  starting transfers between devices: 32.4 us -> 34.2 us
    ppermute x14, starting transfers between devices: 16.3 us -> 18.2 us  [send(): lax.ppermute(value, 'comp', [(i, i ^ by) for i in range(ranks)])]
  transfers between devices with their start and end apart: 20 -> 20, of which waited for: 6 -> 5; matrix products, arithmetic and copies ran while one was open for 2% -> 2% of each run, Pallas kernels for 28% -> 27%
where the time goes in v7:
time: 120 us
  waiting for transfers between devices  44.7 us (37%)
  Pallas kernels  36.9 us (31%)
  starting transfers between devices  34.2 us (29%)
  local copies, waits for them, and re-layouts  3.69 us (3%)
    ppermute x14, waiting for transfers between devices, send(): lax.ppermute(value, 'comp', [(i, i ^ by) for i in range(ranks)])  39.5 us
    pallas_call x4, Pallas kernels, layer_step(): pl.pallas_call(functools.partial(step_kernel, pieces, layer, stiff is Non...  30.1 us
    ppermute x14, starting transfers between devices, send(): lax.ppermute(value, 'comp', [(i, i ^ by) for i in range(ranks)])  18.2 us
    ppermute x6, starting transfers between devices, shifted(): return lax.ppermute(shard, axis, pairs)  16.1 us
    pallas_call x2, Pallas kernels, pack(): pl.pallas_call(functools.partial(pack_kernel, layer), out_shape=out_shape...  5.99 us
    ppermute x6, waiting for transfers between devices, shifted(): return lax.ppermute(shard, axis, pairs)  5.23 us
  transfers between devices with their start and end apart: 20, of which 5 were waited for; matrix products, arithmetic and copies ran while one was open for 2% of the time, Pallas kernels for 27%

profile of v7, /device:TPU:1, one launch (start us, length us, event | category | flops | bytes accessed | tf_op | source)
XLA Modules:
  0.0 120.0 jit_solution(17537050509479243793)
XLA Ops:
  0.1 4.1 %pack.2 = (f32[136,512]{1,0:T(8,128)}, f32[136,512]{1,0:T(8,128)}, f32[136,512]{1,0:T(8,128)}, f32[136,512]{1,0:T(8,128)}, f32[32,128]{1,0:T(8,128)}) custom-call(f32[32,32,512]{2,1,0:T(8,128)} %plane_ref.3, s32[8,8,512]{2,1,0:T(8,128)} %mask_ref.3, f32[2,32,512]{2,1,0:T(8,128)} %refs_6_.7, s32[2,32,512]{2,1,0:T(8,128)} %refs_7_.7), custom_call_target="tpu_custom_call" | custom-call | tf_op jit(solution)/shard_map/pack/pallas_call | solution.py:248
  4.2 2.1 %collective-permute-start = (f32[32,128]{1,0:T(8,128)}, f32[32,128]{1,0:T(8,128)S(1)}, u32[]{:S(2)}, u32[]{:S(2)}) collective-permute-start(f32[32,128]{1,0:T(8,128)} %get-tuple-element.56.refs_0_), channel_id=1, source_target_pairs={{1,0},{2,1},{3,2},{5,4},{6,5},{7,6},{9,8},{10,9},{11,10},{13,12},{... | collective-permute-start | bytes 49160 | tf_op jit(solution)/shard_map/ppermute | solution.py:23
  6.3 4.5 %collective-permute-start.1 = (f32[32,128]{1,0:T(8,128)}, f32[32,128]{1,0:T(8,128)S(1)}, u32[]{:S(2)}, u32[]{:S(2)}) collective-permute-start(f32[32,128]{1,0:T(8,128)} %get-tuple-element.56.refs_0_), channel_id=1, source_target_pairs={{0,1},{1,2},{2,3},{4,5},{5,6},{6,7},{8,9},{9,10},{10,11},{12,13},{... | collective-permute-start | bytes 49160 | tf_op jit(solution)/shard_map/ppermute | solution.py:23
  10.7 3.4 %collective-permute-start.3 = (f32[136,512]{1,0:T(8,128)}, f32[136,512]{1,0:T(8,128)S(1)}, u32[]{:S(2)}, u32[]{:S(2)}) collective-permute-start(f32[136,512]{1,0:T(8,128)} %get-tuple-element.66), channel_id=1, source_target_pairs={{0,12},{4,8},{8,4},{12,0},{1,13},{5,9},{9,5},{13,1},{2,14},{6,10},... | collective-permute-start | bytes 835592 | tf_op jit(solution)/shard_map/ppermute | solution.py:510
  14.5 1.9 %pack.3 = (f32[136,512]{1,0:T(8,128)S(1)}, f32[136,512]{1,0:T(8,128)S(1)}, f32[136,512]{1,0:T(8,128)S(1)}, f32[136,512]{1,0:T(8,128)S(1)}) custom-call(f32[32,32,512]{2,1,0:T(8,128)S(1)} %copy-done, s32[8,8,512]{2,1,0:T(8,128)S(1)} %copy-done.3), custom_call_target="tpu_custom_call" | custom-call | tf_op jit(solution)/shard_map/pack/pallas_call | solution.py:248
  16.5 2.1 %collective-permute-start.2 = (f32[1,32,128]{2,1,0:T(8,128)S(1)}, f32[1,32,128]{2,1,0:T(8,128)S(1)}, u32[]{:S(2)}, u32[]{:S(2)}) collective-permute-start(f32[1,32,128]{2,1,0:T(8,128)S(1)} %select_bitcast_fusion), channel_id=1, source_target_pairs={{0,8},{4,12},{8,0},{12,4},{1,9},{5,13},{9,1},{13,5},{2,10},{6,14},... | collective-permute-start | bytes 49160 | tf_op jit(solution)/shard_map/ppermute | solution.py:510
  18.6 20.5 %collective-permute-done.2 = f32[1,32,128]{2,1,0:T(8,128)S(1)} collective-permute-done((f32[1,32,128]{2,1,0:T(8,128)S(1)}, f32[1,32,128]{2,1,0:T(8,128)S(1)}, u32[]{:S(2)}, u32[]{:S(2)}) %collective-permute-start.2) | collective-permute-done | bytes 16416 | tf_op jit(solution)/shard_map/ppermute | solution.py:510
  39.1 2.3 %collective-permute-start.12 = (f32[136,512]{1,0:T(8,128)S(1)}, f32[136,512]{1,0:T(8,128)S(1)}, u32[]{:S(2)}, u32[]{:S(2)}) collective-permute-start(f32[136,512]{1,0:T(8,128)S(1)} %get-tuple-element.94), channel_id=1, source_target_pairs={{0,12},{4,8},{8,4},{12,0},{1,13},{5,9},{9,5},{13,1},{2,14},{6,10},... | collective-permute-start | bytes 835592 | tf_op jit(solution)/shard_map/ppermute | solution.py:510
  42.8 7.5 %layer_step.4 = (f32[128,512]{1,0:T(8,128)S(1)}, f32[128,512]{1,0:T(8,128)S(1)}, f32[128,512]{1,0:T(8,128)S(1)}, f32[128,512]{1,0:T(8,128)S(1)}, f32[32,128]{1,0:T(8,128)S(1)}, /*index=5*/f32[32,512]{1,0:T(8,128)S(1)}) custom-call(f32[16]{0:T(128)S(1)} %copy-done.6, f32[16]{0:T(128)S(1)} %copy-done.7, f32[136,512]{1,0:T(8,128)S(1)} %copy-done.4, ...), custom_call_target="tpu_custom_call" | custom-call | tf_op jit(solution)/shard_map/layer_step/pallas_call | solution.py:476
  50.2 3.0 %collective-permute-start.7 = (f32[32,128]{1,0:T(8,128)S(1)}, f32[32,128]{1,0:T(8,128)S(1)}, u32[]{:S(2)}, u32[]{:S(2)}) collective-permute-start(f32[32,128]{1,0:T(8,128)S(1)} %get-tuple-element.87), channel_id=1, source_target_pairs={{0,1},{1,2},{2,3},{4,5},{5,6},{6,7},{8,9},{9,10},{10,11},{12,13},{... | collective-permute-start | bytes 49160 | tf_op jit(solution)/shard_map/ppermute | solution.py:23
  53.3 1.9 %collective-permute-start.8 = (f32[32,128]{1,0:T(8,128)S(1)}, f32[32,128]{1,0:T(8,128)S(1)}, u32[]{:S(2)}, u32[]{:S(2)}) collective-permute-start(f32[32,128]{1,0:T(8,128)S(1)} %get-tuple-element.87), channel_id=1, source_target_pairs={{1,0},{2,1},{3,2},{5,4},{6,5},{7,6},{9,8},{10,9},{11,10},{13,12},{... | collective-permute-start | bytes 49160 | tf_op jit(solution)/shard_map/ppermute | solution.py:23
  55.7 2.9 %collective-permute-done.8.refs_5_ = f32[32,128]{1,0:T(8,128)S(1)} collective-permute-done((f32[32,128]{1,0:T(8,128)S(1)}, f32[32,128]{1,0:T(8,128)S(1)}, u32[]{:S(2)}, u32[]{:S(2)}) %collective-permute-start.8) | collective-permute-done | bytes 16416 | tf_op jit(solution)/shard_map/ppermute | solution.py:23
  58.6 8.0 %layer_step.5 = (f32[128,512]{1,0:T(8,128)S(1)}, f32[128,512]{1,0:T(8,128)}, f32[128,512]{1,0:T(8,128)}, f32[128,512]{1,0:T(8,128)S(1)}) custom-call(f32[16]{0:T(128)S(1)} %copy-done.6, f32[16]{0:T(128)S(1)} %copy-done.7, f32[128,512]{1,0:T(8,128)S(1)} %get-tuple-element.83.refs_0_, f32[128,512]{1,0:T(8,128)S(1)} %get-tuple-element.84.refs_1_, ...), custom_call_target="tpu_custom_call" | custom-call | tf_op jit(solution)/shard_map/layer_step/pallas_call | solution.py:476
  66.6 4.8 %collective-permute-start.9 = (f32[128,512]{1,0:T(8,128)}, f32[128,512]{1,0:T(8,128)}, u32[]{:S(2)}, u32[]{:S(2)}) collective-permute-start(f32[128,512]{1,0:T(8,128)} %get-tuple-element.90), channel_id=1, source_target_pairs={{0,12},{4,8},{8,4},{12,0},{1,13},{5,9},{9,5},{13,1},{2,14},{6,10},... | collective-permute-start | bytes 786440 | tf_op jit(solution)/shard_map/ppermute | solution.py:510
  72.0 7.4 %layer_step.6 = (f32[128,512]{1,0:T(8,128)S(1)}, f32[128,512]{1,0:T(8,128)S(1)}, f32[128,512]{1,0:T(8,128)S(1)}, f32[128,512]{1,0:T(8,128)S(1)}, f32[32,128]{1,0:T(8,128)S(1)}, /*index=5*/f32[32,512]{1,0:T(8,128)S(1)}) custom-call(f32[16]{0:T(128)S(1)} %copy-done.6, f32[16]{0:T(128)S(1)} %copy-done.7, f32[136,512]{1,0:T(8,128)S(1)} %get-tuple-element.93.refs_0_, ...), custom_call_target="tpu_custom_call" | custom-call | tf_op jit(solution)/shard_map/layer_step/pallas_call | solution.py:476
  79.4 2.5 %collective-permute-start.15 = (f32[32,128]{1,0:T(8,128)S(1)}, f32[32,128]{1,0:T(8,128)S(1)}, u32[]{:S(2)}, u32[]{:S(2)}) collective-permute-start(f32[32,128]{1,0:T(8,128)S(1)} %get-tuple-element.101), channel_id=1, source_target_pairs={{0,1},{1,2},{2,3},{4,5},{5,6},{6,7},{8,9},{9,10},{10,11},{12,13},{... | collective-permute-start | bytes 49160 | tf_op jit(solution)/shard_map/ppermute | solution.py:23
  81.9 2.1 %collective-permute-start.16 = (f32[32,128]{1,0:T(8,128)S(1)}, f32[32,128]{1,0:T(8,128)S(1)}, u32[]{:S(2)}, u32[]{:S(2)}) collective-permute-start(f32[32,128]{1,0:T(8,128)S(1)} %get-tuple-element.101), channel_id=1, source_target_pairs={{1,0},{2,1},{3,2},{5,4},{6,5},{7,6},{9,8},{10,9},{11,10},{13,12},{... | collective-permute-start | bytes 49160 | tf_op jit(solution)/shard_map/ppermute | solution.py:23
  84.0 1.0 constant_dynamic-update-slice_fusion.6
  85.0 2.4 %collective-permute-done.16.refs_5_ = f32[32,128]{1,0:T(8,128)S(1)} collective-permute-done((f32[32,128]{1,0:T(8,128)S(1)}, f32[32,128]{1,0:T(8,128)S(1)}, u32[]{:S(2)}, u32[]{:S(2)}) %collective-permute-start.16) | collective-permute-done | bytes 16416 | tf_op jit(solution)/shard_map/ppermute | solution.py:23
  87.4 7.3 %layer_step.7 = (f32[128,512]{1,0:T(8,128)S(1)}, f32[128,512]{1,0:T(8,128)S(1)}, f32[128,512]{1,0:T(8,128)S(1)}, f32[128,512]{1,0:T(8,128)S(1)}) custom-call(f32[16]{0:T(128)S(1)} %copy-done.6, f32[16]{0:T(128)S(1)} %copy-done.7, f32[128,512]{1,0:T(8,128)S(1)} %get-tuple-element.97.refs_0_, f32[128,512]{1,0:T(8,128)S(1)} %get-tuple-element.98.refs_1_, ...), custom_call_target="tpu_custom_call" | custom-call | tf_op jit(solution)/shard_map/layer_step/pallas_call | solution.py:476
  94.6 3.5 %collective-permute-start.17 = (f32[128,512]{1,0:T(8,128)S(1)}, f32[128,512]{1,0:T(8,128)S(1)}, u32[]{:S(2)}, u32[]{:S(2)}) collective-permute-start(f32[128,512]{1,0:T(8,128)S(1)} %get-tuple-element.104), channel_id=1, source_target_pairs={{0,12},{4,8},{8,4},{12,0},{1,13},{5,9},{9,5},{13,1},{2,14},{6,10},... | collective-permute-start | bytes 786440 | tf_op jit(solution)/shard_map/ppermute | solution.py:510
  99.6 5.2 %collective-permute-done.17 = f32[128,512]{1,0:T(8,128)S(1)} collective-permute-done((f32[128,512]{1,0:T(8,128)S(1)}, f32[128,512]{1,0:T(8,128)S(1)}, u32[]{:S(2)}, u32[]{:S(2)}) %collective-permute-start.17) | collective-permute-done | bytes 262176 | tf_op jit(solution)/shard_map/ppermute | solution.py:510
  104.8 13.7 %collective-permute-done.18 = f32[128,512]{1,0:T(8,128)S(1)} collective-permute-done((f32[128,512]{1,0:T(8,128)S(1)}, f32[128,512]{1,0:T(8,128)S(1)}, u32[]{:S(2)}, u32[]{:S(2)}) %collective-permute-start.18) | collective-permute-done | bytes 262176 | tf_op jit(solution)/shard_map/ppermute | solution.py:510
  118.7 1.3 %copy-done.12 = f32[4,8,32,512]{3,2,1,0:T(8,128)} copy-done((f32[4,8,32,512]{3,2,1,0:T(8,128)}, f32[4,8,32,512]{3,2,1,0:T(8,128)S(1)}, u32[]{:S(2)}) %copy-start.12) | copy-done | bytes 2097176
  (62 shorter events, 4.4 us)
Async XLA Ops:
  0.0 42.7 %copy-start.1 = (f32[2,32,512]{2,1,0:T(8,128)S(1)}, f32[2,32,512]{2,1,0:T(8,128)}, u32[]{:S(2)}) copy-start(f32[2,32,512]{2,1,0:T(8,128)} %refs_6_.7) | copy-start | bytes 393220
  0.0 42.7 %copy-start.2 = (s32[2,32,512]{2,1,0:T(8,128)S(1)}, s32[2,32,512]{2,1,0:T(8,128)}, u32[]{:S(2)}) copy-start(s32[2,32,512]{2,1,0:T(8,128)} %refs_7_.7) | copy-start | bytes 393220
  0.1 42.7 %copy-start.7 = (f32[16]{0:T(128)S(1)}, f32[16]{0:T(128)}, u32[]{:S(2)}) copy-start(f32[16]{0:T(128)} %retard_ref.7) | copy-start | bytes 196
  0.1 42.7 %copy-start.6 = (f32[16]{0:T(128)S(1)}, f32[16]{0:T(128)}, u32[]{:S(2)}) copy-start(f32[16]{0:T(128)} %spread_ref.7) | copy-start | bytes 196
  4.2 12.3 %collective-permute-start = (f32[32,128]{1,0:T(8,128)}, f32[32,128]{1,0:T(8,128)S(1)}, u32[]{:S(2)}, u32[]{:S(2)}) collective-permute-start(f32[32,128]{1,0:T(8,128)} %get-tuple-element.56.refs_0_), channel_id=1, source_target_pairs={{1,0},{2,1},{3,2},{5,4},{6,5},{7,6},{9,8},{10,9},{11,10},{13,12},{... | collective-permute-start | bytes 49160 | tf_op jit(solution)/shard_map/ppermute | solution.py:23
  6.3 10.2 %collective-permute-start.1 = (f32[32,128]{1,0:T(8,128)}, f32[32,128]{1,0:T(8,128)S(1)}, u32[]{:S(2)}, u32[]{:S(2)}) collective-permute-start(f32[32,128]{1,0:T(8,128)} %get-tuple-element.56.refs_0_), channel_id=1, source_target_pairs={{0,1},{1,2},{2,3},{4,5},{5,6},{6,7},{8,9},{9,10},{10,11},{12,13},{... | collective-permute-start | bytes 49160 | tf_op jit(solution)/shard_map/ppermute | solution.py:23
  10.7 28.3 %collective-permute-start.3 = (f32[136,512]{1,0:T(8,128)}, f32[136,512]{1,0:T(8,128)S(1)}, u32[]{:S(2)}, u32[]{:S(2)}) collective-permute-start(f32[136,512]{1,0:T(8,128)} %get-tuple-element.66), channel_id=1, source_target_pairs={{0,12},{4,8},{8,4},{12,0},{1,13},{5,9},{9,5},{13,1},{2,14},{6,10},... | collective-permute-start | bytes 835592 | tf_op jit(solution)/shard_map/ppermute | solution.py:510
  14.1 24.9 %collective-permute-start.4 = (f32[136,512]{1,0:T(8,128)}, f32[136,512]{1,0:T(8,128)S(1)}, u32[]{:S(2)}, u32[]{:S(2)}) collective-permute-start(f32[136,512]{1,0:T(8,128)} %get-tuple-element.67), channel_id=1, source_target_pairs={{0,8},{4,12},{8,0},{12,4},{1,9},{5,13},{9,1},{13,5},{2,10},{6,14},... | collective-permute-start | bytes 835592 | tf_op jit(solution)/shard_map/ppermute | solution.py:510
  14.1 24.9 %collective-permute-start.5 = (f32[136,512]{1,0:T(8,128)}, f32[136,512]{1,0:T(8,128)S(1)}, u32[]{:S(2)}, u32[]{:S(2)}) collective-permute-start(f32[136,512]{1,0:T(8,128)} %get-tuple-element.68), channel_id=1, source_target_pairs={{0,4},{4,0},{8,12},{12,8},{1,5},{5,1},{9,13},{13,9},{2,6},{6,2},{1... | collective-permute-start | bytes 835592 | tf_op jit(solution)/shard_map/ppermute | solution.py:510
  16.5 22.6 %collective-permute-start.2 = (f32[1,32,128]{2,1,0:T(8,128)S(1)}, f32[1,32,128]{2,1,0:T(8,128)S(1)}, u32[]{:S(2)}, u32[]{:S(2)}) collective-permute-start(f32[1,32,128]{2,1,0:T(8,128)S(1)} %select_bitcast_fusion), channel_id=1, source_target_pairs={{0,8},{4,12},{8,0},{12,4},{1,9},{5,13},{9,1},{13,5},{2,10},{6,14},... | collective-permute-start | bytes 49160 | tf_op jit(solution)/shard_map/ppermute | solution.py:510
  39.1 3.6 %collective-permute-start.6 = (f32[2,32,128]{2,1,0:T(8,128)S(1)}, f32[2,32,128]{2,1,0:T(8,128)S(1)}, u32[]{:S(2)}, u32[]{:S(2)}) collective-permute-start(f32[2,32,128]{2,1,0:T(8,128)S(1)} %pad_maximum_fusion.1), channel_id=1, source_target_pairs={{0,4},{4,0},{8,12},{12,8},{1,5},{5,1},{9,13},{13,9},{2,6},{6,2},{1... | collective-permute-start | bytes 98312 | tf_op jit(solution)/shard_map/ppermute | solution.py:510
  39.1 32.3 %collective-permute-start.12 = (f32[136,512]{1,0:T(8,128)S(1)}, f32[136,512]{1,0:T(8,128)S(1)}, u32[]{:S(2)}, u32[]{:S(2)}) collective-permute-start(f32[136,512]{1,0:T(8,128)S(1)} %get-tuple-element.94), channel_id=1, source_target_pairs={{0,12},{4,8},{8,4},{12,0},{1,13},{5,9},{9,5},{13,1},{2,14},{6,10},... | collective-permute-start | bytes 835592 | tf_op jit(solution)/shard_map/ppermute | solution.py:510
  42.2 29.8 %collective-permute-start.13 = (f32[136,512]{1,0:T(8,128)S(1)}, f32[136,512]{1,0:T(8,128)S(1)}, u32[]{:S(2)}, u32[]{:S(2)}) collective-permute-start(f32[136,512]{1,0:T(8,128)S(1)} %get-tuple-element.95), channel_id=1, source_target_pairs={{0,8},{4,12},{8,0},{12,4},{1,9},{5,13},{9,1},{13,5},{2,10},{6,14},... | collective-permute-start | bytes 835592 | tf_op jit(solution)/shard_map/ppermute | solution.py:510
  50.2 5.5 %collective-permute-start.7 = (f32[32,128]{1,0:T(8,128)S(1)}, f32[32,128]{1,0:T(8,128)S(1)}, u32[]{:S(2)}, u32[]{:S(2)}) collective-permute-start(f32[32,128]{1,0:T(8,128)S(1)} %get-tuple-element.87), channel_id=1, source_target_pairs={{0,1},{1,2},{2,3},{4,5},{5,6},{6,7},{8,9},{9,10},{10,11},{12,13},{... | collective-permute-start | bytes 49160 | tf_op jit(solution)/shard_map/ppermute | solution.py:23
  53.3 5.4 %collective-permute-start.8 = (f32[32,128]{1,0:T(8,128)S(1)}, f32[32,128]{1,0:T(8,128)S(1)}, u32[]{:S(2)}, u32[]{:S(2)}) collective-permute-start(f32[32,128]{1,0:T(8,128)S(1)} %get-tuple-element.87), channel_id=1, source_target_pairs={{1,0},{2,1},{3,2},{5,4},{6,5},{7,6},{9,8},{10,9},{11,10},{13,12},{... | collective-permute-start | bytes 49160 | tf_op jit(solution)/shard_map/ppermute | solution.py:23
  55.2 16.8 %collective-permute-start.14 = (f32[136,512]{1,0:T(8,128)S(1)}, f32[136,512]{1,0:T(8,128)S(1)}, u32[]{:S(2)}, u32[]{:S(2)}) collective-permute-start(f32[136,512]{1,0:T(8,128)S(1)} %get-tuple-element.96), channel_id=1, source_target_pairs={{0,4},{4,0},{8,12},{12,8},{1,5},{5,1},{9,13},{13,9},{2,6},{6,2},{1... | collective-permute-start | bytes 835592 | tf_op jit(solution)/shard_map/ppermute | solution.py:510
  66.6 17.4 %collective-permute-start.9 = (f32[128,512]{1,0:T(8,128)}, f32[128,512]{1,0:T(8,128)}, u32[]{:S(2)}, u32[]{:S(2)}) collective-permute-start(f32[128,512]{1,0:T(8,128)} %get-tuple-element.90), channel_id=1, source_target_pairs={{0,12},{4,8},{8,4},{12,0},{1,13},{5,9},{9,5},{13,1},{2,14},{6,10},... | collective-permute-start | bytes 786440 | tf_op jit(solution)/shard_map/ppermute | solution.py:510
  71.4 26.7 %collective-permute-start.10 = (f32[128,512]{1,0:T(8,128)}, f32[128,512]{1,0:T(8,128)}, u32[]{:S(2)}, u32[]{:S(2)}) collective-permute-start(f32[128,512]{1,0:T(8,128)} %get-tuple-element.91), channel_id=1, source_target_pairs={{0,8},{4,12},{8,0},{12,4},{1,9},{5,13},{9,1},{13,5},{2,10},{6,14},... | collective-permute-start | bytes 786440 | tf_op jit(solution)/shard_map/ppermute | solution.py:510
  71.4 27.7 %collective-permute-start.11 = (f32[128,512]{1,0:T(8,128)S(1)}, f32[128,512]{1,0:T(8,128)S(1)}, u32[]{:S(2)}, u32[]{:S(2)}) collective-permute-start(f32[128,512]{1,0:T(8,128)S(1)} %get-tuple-element.92), channel_id=1, source_target_pairs={{0,4},{4,0},{8,12},{12,8},{1,5},{5,1},{9,13},{13,9},{2,6},{6,2},{1... | collective-permute-start | bytes 786440 | tf_op jit(solution)/shard_map/ppermute | solution.py:510
  79.4 5.6 %collective-permute-start.15 = (f32[32,128]{1,0:T(8,128)S(1)}, f32[32,128]{1,0:T(8,128)S(1)}, u32[]{:S(2)}, u32[]{:S(2)}) collective-permute-start(f32[32,128]{1,0:T(8,128)S(1)} %get-tuple-element.101), channel_id=1, source_target_pairs={{0,1},{1,2},{2,3},{4,5},{5,6},{6,7},{8,9},{9,10},{10,11},{12,13},{... | collective-permute-start | bytes 49160 | tf_op jit(solution)/shard_map/ppermute | solution.py:23
  81.9 5.5 %collective-permute-start.16 = (f32[32,128]{1,0:T(8,128)S(1)}, f32[32,128]{1,0:T(8,128)S(1)}, u32[]{:S(2)}, u32[]{:S(2)}) collective-permute-start(f32[32,128]{1,0:T(8,128)S(1)} %get-tuple-element.101), channel_id=1, source_target_pairs={{1,0},{2,1},{3,2},{5,4},{6,5},{7,6},{9,8},{10,9},{11,10},{13,12},{... | collective-permute-start | bytes 49160 | tf_op jit(solution)/shard_map/ppermute | solution.py:23
  94.6 10.2 %collective-permute-start.17 = (f32[128,512]{1,0:T(8,128)S(1)}, f32[128,512]{1,0:T(8,128)S(1)}, u32[]{:S(2)}, u32[]{:S(2)}) collective-permute-start(f32[128,512]{1,0:T(8,128)S(1)} %get-tuple-element.104), channel_id=1, source_target_pairs={{0,12},{4,8},{8,4},{12,0},{1,13},{5,9},{9,5},{13,1},{2,14},{6,10},... | collective-permute-start | bytes 786440 | tf_op jit(solution)/shard_map/ppermute | solution.py:510
  99.1 19.5 %collective-permute-start.18 = (f32[128,512]{1,0:T(8,128)S(1)}, f32[128,512]{1,0:T(8,128)S(1)}, u32[]{:S(2)}, u32[]{:S(2)}) collective-permute-start(f32[128,512]{1,0:T(8,128)S(1)} %get-tuple-element.105), channel_id=1, source_target_pairs={{0,8},{4,12},{8,0},{12,4},{1,9},{5,13},{9,1},{13,5},{2,10},{6,14},... | collective-permute-start | bytes 786440 | tf_op jit(solution)/shard_map/ppermute | solution.py:510
  99.2 19.4 %collective-permute-start.19 = (f32[128,512]{1,0:T(8,128)S(1)}, f32[128,512]{1,0:T(8,128)S(1)}, u32[]{:S(2)}, u32[]{:S(2)}) collective-permute-start(f32[128,512]{1,0:T(8,128)S(1)} %get-tuple-element.106), channel_id=1, source_target_pairs={{0,4},{4,0},{8,12},{12,8},{1,5},{5,1},{9,13},{13,9},{2,6},{6,2},{1... | collective-permute-start | bytes 786440 | tf_op jit(solution)/shard_map/ppermute | solution.py:510
  (9 other events, 271.7 us)

commit v8 on v6

--- a/solution.py
+++ b/solution.py
@@ -410,7 +410,7 @@
             species_ref[group] = offset_ref[group] + product(both_ref, [species, jnp.tanh(species)])
         return carry
 
-    lax.fori_loop(0, NEWT - 1, plain_step, 0)
+    lax.fori_loop(0, NEWT - 1, plain_step, 0, unroll=True)
     plain_ref[...] = species_ref[...]
     ratio = jnp.concatenate([ratio_ref[...]] * (cols // LANES), axis=1)
 
@@ -421,7 +421,7 @@
             species_ref[group] = offset_ref[group] + product(both_ref, [species, reaction])
         return carry
 
-    lax.fori_loop(0, STIFF, stiff_step, 0)
+    lax.fori_loop(0, STIFF, stiff_step, 0, unroll=True)
     if is_first:
         for rank, value_ref in zip(ranks, value_refs):
             spot = pl.ds(pl.multiple_of(rank * block, TILE), block)

time: 119 us -> 113 us (0.950)
  Pallas kernels: 36.9 us -> 31.1 us
    pallas_call x4, Pallas kernels: 30.1 us -> 24.2 us  [layer_step(): pl.pallas_call(functools.partial(step_kernel, pieces, layer, stiff is Non...]
  transfers between devices with their start and end apart: 20 -> 20, of which waited for: 6 -> 6; matrix products, arithmetic and copies ran while one was open for 2% -> 2% of each run, Pallas kernels for 28% -> 24%
where the time goes in v8:
time: 113 us; the launch traced here: 112 us
  waiting for transfers between devices  44.4 us (39%)
  starting transfers between devices  32.7 us (29%)
  Pallas kernels  31.1 us (28%)
  local copies, waits for them, and re-layouts  3.7 us (3%)
    ppermute x14, waiting for transfers between devices, send(): lax.ppermute(value, 'comp', [(i, i ^ by) for i in range(ranks)])  38.5 us
    pallas_call x4, Pallas kernels, layer_step(): pl.pallas_call(functools.partial(step_kernel, pieces, layer, stiff is Non...  24.2 us
    ppermute x6, starting transfers between devices, shifted(): return lax.ppermute(shard, axis, pairs)  16.4 us
    ppermute x14, starting transfers between devices, send(): lax.ppermute(value, 'comp', [(i, i ^ by) for i in range(ranks)])  16.3 us
    pallas_call x2, Pallas kernels, pack(): pl.pallas_call(functools.partial(pack_kernel, layer), out_shape=out_shape...  6.12 us
    ppermute x6, waiting for transfers between devices, shifted(): return lax.ppermute(shard, axis, pairs)  5.96 us
  transfers between devices with their start and end apart: 20, of which 6 were waited for; matrix products, arithmetic and copies ran while one was open for 2% of the time, Pallas kernels for 24%

profile of v8, /device:TPU:1, one launch (start us, length us, event | category | flops | bytes accessed | tf_op | source)
XLA Modules:
  0.0 112.3 jit_solution(11463274669302430696)
XLA Ops:
  0.1 4.2 %pack.2 = (f32[136,512]{1,0:T(8,128)}, f32[136,512]{1,0:T(8,128)}, f32[136,512]{1,0:T(8,128)}, f32[136,512]{1,0:T(8,128)}, f32[32,128]{1,0:T(8,128)}) custom-call(f32[32,32,512]{2,1,0:T(8,128)} %plane_ref.3, s32[8,8,512]{2,1,0:T(8,128)} %mask_ref.3, f32[2,32,512]{2,1,0:T(8,128)} %refs_6_.7, s32[2,32,512]{2,1,0:T(8,128)} %refs_7_.7), custom_call_target="tpu_custom_call" | custom-call | tf_op jit(solution)/shard_map/pack/pallas_call | solution.py:237
  4.3 2.1 %collective-permute-start.3 = (f32[32,128]{1,0:T(8,128)}, f32[32,128]{1,0:T(8,128)S(1)}, u32[]{:S(2)}, u32[]{:S(2)}) collective-permute-start(f32[32,128]{1,0:T(8,128)} %get-tuple-element.50.refs_0_), channel_id=1, source_target_pairs={{1,0},{2,1},{3,2},{5,4},{6,5},{7,6},{9,8},{10,9},{11,10},{13,12},{... | collective-permute-start | bytes 49160 | tf_op jit(solution)/shard_map/ppermute | solution.py:23
  6.4 4.5 %collective-permute-start.4 = (f32[32,128]{1,0:T(8,128)}, f32[32,128]{1,0:T(8,128)S(1)}, u32[]{:S(2)}, u32[]{:S(2)}) collective-permute-start(f32[32,128]{1,0:T(8,128)} %get-tuple-element.50.refs_0_), channel_id=1, source_target_pairs={{0,1},{1,2},{2,3},{4,5},{5,6},{6,7},{8,9},{9,10},{10,11},{12,13},{... | collective-permute-start | bytes 49160 | tf_op jit(solution)/shard_map/ppermute | solution.py:23
  10.9 3.2 %collective-permute-start = (f32[136,512]{1,0:T(8,128)}, f32[136,512]{1,0:T(8,128)S(1)}, u32[]{:S(2)}, u32[]{:S(2)}) collective-permute-start(f32[136,512]{1,0:T(8,128)} %get-tuple-element.43), channel_id=1, source_target_pairs={{0,12},{4,8},{8,4},{12,0},{1,13},{5,9},{9,5},{13,1},{2,14},{6,10},... | collective-permute-start | bytes 835592 | tf_op jit(solution)/shard_map/ppermute | solution.py:499
  15.7 5.8 %collective-permute-done.5 = f32[1,32,128]{2,1,0:T(8,128)S(1)} collective-permute-done((f32[1,32,128]{2,1,0:T(8,128)S(1)}, f32[1,32,128]{2,1,0:T(8,128)S(1)}, u32[]{:S(2)}, u32[]{:S(2)}) %collective-permute-start.5) | collective-permute-done | bytes 16416 | tf_op jit(solution)/shard_map/ppermute | solution.py:499
  22.3 1.9 %pack.3 = (f32[136,512]{1,0:T(8,128)S(1)}, f32[136,512]{1,0:T(8,128)S(1)}, f32[136,512]{1,0:T(8,128)S(1)}, f32[136,512]{1,0:T(8,128)S(1)}) custom-call(f32[32,32,512]{2,1,0:T(8,128)S(1)} %copy-done, s32[8,8,512]{2,1,0:T(8,128)S(1)} %copy-done.3), custom_call_target="tpu_custom_call" | custom-call | tf_op jit(solution)/shard_map/pack/pallas_call | solution.py:237
  24.2 15.6 %collective-permute-done.6 = f32[2,32,128]{2,1,0:T(8,128)S(1)} collective-permute-done((f32[2,32,128]{2,1,0:T(8,128)S(1)}, f32[2,32,128]{2,1,0:T(8,128)S(1)}, u32[]{:S(2)}, u32[]{:S(2)}) %collective-permute-start.6) | collective-permute-done | bytes 32800 | tf_op jit(solution)/shard_map/ppermute | solution.py:499
  39.8 2.1 %collective-permute-start.12 = (f32[136,512]{1,0:T(8,128)S(1)}, f32[136,512]{1,0:T(8,128)S(1)}, u32[]{:S(2)}, u32[]{:S(2)}) collective-permute-start(f32[136,512]{1,0:T(8,128)S(1)} %get-tuple-element.66), channel_id=1, source_target_pairs={{0,12},{4,8},{8,4},{12,0},{1,13},{5,9},{9,5},{13,1},{2,14},{6,10},... | collective-permute-start | bytes 835592 | tf_op jit(solution)/shard_map/ppermute | solution.py:499
  41.9 1.4 %collective-permute-start.14 = (f32[136,512]{1,0:T(8,128)S(1)}, f32[136,512]{1,0:T(8,128)S(1)}, u32[]{:S(2)}, u32[]{:S(2)}) collective-permute-start(f32[136,512]{1,0:T(8,128)S(1)} %get-tuple-element.68), channel_id=1, source_target_pairs={{0,4},{4,0},{8,12},{12,8},{1,5},{5,1},{9,13},{13,9},{2,6},{6,2},{1... | collective-permute-start | bytes 835592 | tf_op jit(solution)/shard_map/ppermute | solution.py:499
  44.3 5.9 %layer_step.4 = (f32[128,512]{1,0:T(8,128)S(1)}, f32[128,512]{1,0:T(8,128)S(1)}, f32[128,512]{1,0:T(8,128)S(1)}, f32[128,512]{1,0:T(8,128)S(1)}, f32[32,128]{1,0:T(8,128)S(1)}, /*index=5*/f32[32,512]{1,0:T(8,128)S(1)}) custom-call(f32[16]{0:T(128)S(1)} %copy-done.6, f32[16]{0:T(128)S(1)} %copy-done.7, f32[136,512]{1,0:T(8,128)S(1)} %copy-done.4, ...), custom_call_target="tpu_custom_call" | custom-call | tf_op jit(solution)/shard_map/layer_step/pallas_call | solution.py:465
  50.2 2.8 %collective-permute-start.7 = (f32[32,128]{1,0:T(8,128)S(1)}, f32[32,128]{1,0:T(8,128)S(1)}, u32[]{:S(2)}, u32[]{:S(2)}) collective-permute-start(f32[32,128]{1,0:T(8,128)S(1)} %get-tuple-element.59), channel_id=1, source_target_pairs={{0,1},{1,2},{2,3},{4,5},{5,6},{6,7},{8,9},{9,10},{10,11},{12,13},{... | collective-permute-start | bytes 49160 | tf_op jit(solution)/shard_map/ppermute | solution.py:23
  53.0 2.1 %collective-permute-start.8 = (f32[32,128]{1,0:T(8,128)S(1)}, f32[32,128]{1,0:T(8,128)S(1)}, u32[]{:S(2)}, u32[]{:S(2)}) collective-permute-start(f32[32,128]{1,0:T(8,128)S(1)} %get-tuple-element.59), channel_id=1, source_target_pairs={{1,0},{2,1},{3,2},{5,4},{6,5},{7,6},{9,8},{10,9},{11,10},{13,12},{... | collective-permute-start | bytes 49160 | tf_op jit(solution)/shard_map/ppermute | solution.py:23
  55.1 2.9 %collective-permute-done.8.refs_5_ = f32[32,128]{1,0:T(8,128)S(1)} collective-permute-done((f32[32,128]{1,0:T(8,128)S(1)}, f32[32,128]{1,0:T(8,128)S(1)}, u32[]{:S(2)}, u32[]{:S(2)}) %collective-permute-start.8) | collective-permute-done | bytes 16416 | tf_op jit(solution)/shard_map/ppermute | solution.py:23
  58.0 6.7 %layer_step.5 = (f32[128,512]{1,0:T(8,128)S(1)}, f32[128,512]{1,0:T(8,128)}, f32[128,512]{1,0:T(8,128)}, f32[128,512]{1,0:T(8,128)S(1)}) custom-call(f32[16]{0:T(128)S(1)} %copy-done.6, f32[16]{0:T(128)S(1)} %copy-done.7, f32[128,512]{1,0:T(8,128)S(1)} %get-tuple-element.55.refs_0_, f32[128,512]{1,0:T(8,128)S(1)} %get-tuple-element.56.refs_1_, ...), custom_call_target="tpu_custom_call" | custom-call | tf_op jit(solution)/shard_map/layer_step/pallas_call | solution.py:465
  64.7 2.4 %collective-permute-start.9 = (f32[128,512]{1,0:T(8,128)}, f32[128,512]{1,0:T(8,128)}, u32[]{:S(2)}, u32[]{:S(2)}) collective-permute-start(f32[128,512]{1,0:T(8,128)} %get-tuple-element.62), channel_id=1, source_target_pairs={{0,12},{4,8},{8,4},{12,0},{1,13},{5,9},{9,5},{13,1},{2,14},{6,10},... | collective-permute-start | bytes 786440 | tf_op jit(solution)/shard_map/ppermute | solution.py:499
  68.3 5.7 %layer_step.6 = (f32[128,512]{1,0:T(8,128)S(1)}, f32[128,512]{1,0:T(8,128)S(1)}, f32[128,512]{1,0:T(8,128)S(1)}, f32[128,512]{1,0:T(8,128)S(1)}, f32[32,128]{1,0:T(8,128)S(1)}, /*index=5*/f32[32,512]{1,0:T(8,128)S(1)}) custom-call(f32[16]{0:T(128)S(1)} %copy-done.6, f32[16]{0:T(128)S(1)} %copy-done.7, f32[136,512]{1,0:T(8,128)S(1)} %get-tuple-element.65.refs_0_, ...), custom_call_target="tpu_custom_call" | custom-call | tf_op jit(solution)/shard_map/layer_step/pallas_call | solution.py:465
  74.0 2.8 %collective-permute-start.15 = (f32[32,128]{1,0:T(8,128)S(1)}, f32[32,128]{1,0:T(8,128)S(1)}, u32[]{:S(2)}, u32[]{:S(2)}) collective-permute-start(f32[32,128]{1,0:T(8,128)S(1)} %get-tuple-element.73), channel_id=1, source_target_pairs={{0,1},{1,2},{2,3},{4,5},{5,6},{6,7},{8,9},{9,10},{10,11},{12,13},{... | collective-permute-start | bytes 49160 | tf_op jit(solution)/shard_map/ppermute | solution.py:23
  76.8 2.1 %collective-permute-start.16 = (f32[32,128]{1,0:T(8,128)S(1)}, f32[32,128]{1,0:T(8,128)S(1)}, u32[]{:S(2)}, u32[]{:S(2)}) collective-permute-start(f32[32,128]{1,0:T(8,128)S(1)} %get-tuple-element.73), channel_id=1, source_target_pairs={{1,0},{2,1},{3,2},{5,4},{6,5},{7,6},{9,8},{10,9},{11,10},{13,12},{... | collective-permute-start | bytes 49160 | tf_op jit(solution)/shard_map/ppermute | solution.py:23
  79.2 3.0 %collective-permute-done.16.refs_5_ = f32[32,128]{1,0:T(8,128)S(1)} collective-permute-done((f32[32,128]{1,0:T(8,128)S(1)}, f32[32,128]{1,0:T(8,128)S(1)}, u32[]{:S(2)}, u32[]{:S(2)}) %collective-permute-start.16) | collective-permute-done | bytes 16416 | tf_op jit(solution)/shard_map/ppermute | solution.py:23
  82.2 5.9 %layer_step.7 = (f32[128,512]{1,0:T(8,128)S(1)}, f32[128,512]{1,0:T(8,128)S(1)}, f32[128,512]{1,0:T(8,128)S(1)}, f32[128,512]{1,0:T(8,128)S(1)}) custom-call(f32[16]{0:T(128)S(1)} %copy-done.6, f32[16]{0:T(128)S(1)} %copy-done.7, f32[128,512]{1,0:T(8,128)S(1)} %get-tuple-element.69.refs_0_, f32[128,512]{1,0:T(8,128)S(1)} %get-tuple-element.70.refs_1_, ...), custom_call_target="tpu_custom_call" | custom-call | tf_op jit(solution)/shard_map/layer_step/pallas_call | solution.py:465
  88.1 2.5 %collective-permute-start.17 = (f32[128,512]{1,0:T(8,128)S(1)}, f32[128,512]{1,0:T(8,128)S(1)}, u32[]{:S(2)}, u32[]{:S(2)}) collective-permute-start(f32[128,512]{1,0:T(8,128)S(1)} %get-tuple-element.76), channel_id=1, source_target_pairs={{0,12},{4,8},{8,4},{12,0},{1,13},{5,9},{9,5},{13,1},{2,14},{6,10},... | collective-permute-start | bytes 786440 | tf_op jit(solution)/shard_map/ppermute | solution.py:499
  93.8 4.4 %collective-permute-done.17 = f32[128,512]{1,0:T(8,128)S(1)} collective-permute-done((f32[128,512]{1,0:T(8,128)S(1)}, f32[128,512]{1,0:T(8,128)S(1)}, u32[]{:S(2)}, u32[]{:S(2)}) %collective-permute-start.17) | collective-permute-done | bytes 262176 | tf_op jit(solution)/shard_map/ppermute | solution.py:499
  98.2 12.7 %collective-permute-done.18 = f32[128,512]{1,0:T(8,128)S(1)} collective-permute-done((f32[128,512]{1,0:T(8,128)S(1)}, f32[128,512]{1,0:T(8,128)S(1)}, u32[]{:S(2)}, u32[]{:S(2)}) %collective-permute-start.18) | collective-permute-done | bytes 262176 | tf_op jit(solution)/shard_map/ppermute | solution.py:499
  111.0 1.3 %copy-done.12 = f32[4,8,32,512]{3,2,1,0:T(8,128)} copy-done((f32[4,8,32,512]{3,2,1,0:T(8,128)}, f32[4,8,32,512]{3,2,1,0:T(8,128)S(1)}, u32[]{:S(2)}) %copy-start.12) | copy-done | bytes 2097176
  (62 shorter events, 8.0 us)
Async XLA Ops:
  0.0 44.2 %copy-start.1 = (f32[2,32,512]{2,1,0:T(8,128)S(1)}, f32[2,32,512]{2,1,0:T(8,128)}, u32[]{:S(2)}) copy-start(f32[2,32,512]{2,1,0:T(8,128)} %refs_6_.7) | copy-start | bytes 393220
  0.0 44.2 %copy-start.2 = (s32[2,32,512]{2,1,0:T(8,128)S(1)}, s32[2,32,512]{2,1,0:T(8,128)}, u32[]{:S(2)}) copy-start(s32[2,32,512]{2,1,0:T(8,128)} %refs_7_.7) | copy-start | bytes 393220
  0.1 44.2 %copy-start.7 = (f32[16]{0:T(128)S(1)}, f32[16]{0:T(128)}, u32[]{:S(2)}) copy-start(f32[16]{0:T(128)} %retard_ref.7) | copy-start | bytes 196
  0.1 44.2 %copy-start.6 = (f32[16]{0:T(128)S(1)}, f32[16]{0:T(128)}, u32[]{:S(2)}) copy-start(f32[16]{0:T(128)} %spread_ref.7) | copy-start | bytes 196
  4.3 9.8 %collective-permute-start.3 = (f32[32,128]{1,0:T(8,128)}, f32[32,128]{1,0:T(8,128)S(1)}, u32[]{:S(2)}, u32[]{:S(2)}) collective-permute-start(f32[32,128]{1,0:T(8,128)} %get-tuple-element.50.refs_0_), channel_id=1, source_target_pairs={{1,0},{2,1},{3,2},{5,4},{6,5},{7,6},{9,8},{10,9},{11,10},{13,12},{... | collective-permute-start | bytes 49160 | tf_op jit(solution)/shard_map/ppermute | solution.py:23
  6.4 7.7 %collective-permute-start.4 = (f32[32,128]{1,0:T(8,128)}, f32[32,128]{1,0:T(8,128)S(1)}, u32[]{:S(2)}, u32[]{:S(2)}) collective-permute-start(f32[32,128]{1,0:T(8,128)} %get-tuple-element.50.refs_0_), channel_id=1, source_target_pairs={{0,1},{1,2},{2,3},{4,5},{5,6},{6,7},{8,9},{9,10},{10,11},{12,13},{... | collective-permute-start | bytes 49160 | tf_op jit(solution)/shard_map/ppermute | solution.py:23
  10.9 31.0 %collective-permute-start = (f32[136,512]{1,0:T(8,128)}, f32[136,512]{1,0:T(8,128)S(1)}, u32[]{:S(2)}, u32[]{:S(2)}) collective-permute-start(f32[136,512]{1,0:T(8,128)} %get-tuple-element.43), channel_id=1, source_target_pairs={{0,12},{4,8},{8,4},{12,0},{1,13},{5,9},{9,5},{13,1},{2,14},{6,10},... | collective-permute-start | bytes 835592 | tf_op jit(solution)/shard_map/ppermute | solution.py:499
  14.2 7.3 %collective-permute-start.5 = (f32[1,32,128]{2,1,0:T(8,128)S(1)}, f32[1,32,128]{2,1,0:T(8,128)S(1)}, u32[]{:S(2)}, u32[]{:S(2)}) collective-permute-start(f32[1,32,128]{2,1,0:T(8,128)S(1)} %select_bitcast_fusion), channel_id=1, source_target_pairs={{0,4},{4,0},{8,12},{12,8},{1,5},{5,1},{9,13},{13,9},{2,6},{6,2},{1... | collective-permute-start | bytes 49160 | tf_op jit(solution)/shard_map/ppermute | solution.py:499
  14.2 30.0 %collective-permute-start.1 = (f32[136,512]{1,0:T(8,128)}, f32[136,512]{1,0:T(8,128)S(1)}, u32[]{:S(2)}, u32[]{:S(2)}) collective-permute-start(f32[136,512]{1,0:T(8,128)} %get-tuple-element.44), channel_id=1, source_target_pairs={{0,8},{4,12},{8,0},{12,4},{1,9},{5,13},{9,1},{13,5},{2,10},{6,14},... | collective-permute-start | bytes 835592 | tf_op jit(solution)/shard_map/ppermute | solution.py:499
  15.4 28.8 %collective-permute-start.2 = (f32[136,512]{1,0:T(8,128)}, f32[136,512]{1,0:T(8,128)S(1)}, u32[]{:S(2)}, u32[]{:S(2)}) collective-permute-start(f32[136,512]{1,0:T(8,128)} %get-tuple-element.45), channel_id=1, source_target_pairs={{0,4},{4,0},{8,12},{12,8},{1,5},{5,1},{9,13},{13,9},{2,6},{6,2},{1... | collective-permute-start | bytes 835592 | tf_op jit(solution)/shard_map/ppermute | solution.py:499
  21.5 18.3 %collective-permute-start.6 = (f32[2,32,128]{2,1,0:T(8,128)S(1)}, f32[2,32,128]{2,1,0:T(8,128)S(1)}, u32[]{:S(2)}, u32[]{:S(2)}) collective-permute-start(f32[2,32,128]{2,1,0:T(8,128)S(1)} %pad_maximum_fusion.1), channel_id=1, source_target_pairs={{0,8},{4,12},{8,0},{12,4},{1,9},{5,13},{9,1},{13,5},{2,10},{6,14},... | collective-permute-start | bytes 98312 | tf_op jit(solution)/shard_map/ppermute | solution.py:499
  39.8 27.3 %collective-permute-start.12 = (f32[136,512]{1,0:T(8,128)S(1)}, f32[136,512]{1,0:T(8,128)S(1)}, u32[]{:S(2)}, u32[]{:S(2)}) collective-permute-start(f32[136,512]{1,0:T(8,128)S(1)} %get-tuple-element.66), channel_id=1, source_target_pairs={{0,12},{4,8},{8,4},{12,0},{1,13},{5,9},{9,5},{13,1},{2,14},{6,10},... | collective-permute-start | bytes 835592 | tf_op jit(solution)/shard_map/ppermute | solution.py:499
  41.9 26.3 %collective-permute-start.13 = (f32[136,512]{1,0:T(8,128)S(1)}, f32[136,512]{1,0:T(8,128)S(1)}, u32[]{:S(2)}, u32[]{:S(2)}) collective-permute-start(f32[136,512]{1,0:T(8,128)S(1)} %get-tuple-element.67), channel_id=1, source_target_pairs={{0,8},{4,12},{8,0},{12,4},{1,9},{5,13},{9,1},{13,5},{2,10},{6,14},... | collective-permute-start | bytes 835592 | tf_op jit(solution)/shard_map/ppermute | solution.py:499
  41.9 26.3 %collective-permute-start.14 = (f32[136,512]{1,0:T(8,128)S(1)}, f32[136,512]{1,0:T(8,128)S(1)}, u32[]{:S(2)}, u32[]{:S(2)}) collective-permute-start(f32[136,512]{1,0:T(8,128)S(1)} %get-tuple-element.68), channel_id=1, source_target_pairs={{0,4},{4,0},{8,12},{12,8},{1,5},{5,1},{9,13},{13,9},{2,6},{6,2},{1... | collective-permute-start | bytes 835592 | tf_op jit(solution)/shard_map/ppermute | solution.py:499
  50.2 4.9 %collective-permute-start.7 = (f32[32,128]{1,0:T(8,128)S(1)}, f32[32,128]{1,0:T(8,128)S(1)}, u32[]{:S(2)}, u32[]{:S(2)}) collective-permute-start(f32[32,128]{1,0:T(8,128)S(1)} %get-tuple-element.59), channel_id=1, source_target_pairs={{0,1},{1,2},{2,3},{4,5},{5,6},{6,7},{8,9},{9,10},{10,11},{12,13},{... | collective-permute-start | bytes 49160 | tf_op jit(solution)/shard_map/ppermute | solution.py:23
  53.0 5.1 %collective-permute-start.8 = (f32[32,128]{1,0:T(8,128)S(1)}, f32[32,128]{1,0:T(8,128)S(1)}, u32[]{:S(2)}, u32[]{:S(2)}) collective-permute-start(f32[32,128]{1,0:T(8,128)S(1)} %get-tuple-element.59), channel_id=1, source_target_pairs={{1,0},{2,1},{3,2},{5,4},{6,5},{7,6},{9,8},{10,9},{11,10},{13,12},{... | collective-permute-start | bytes 49160 | tf_op jit(solution)/shard_map/ppermute | solution.py:23
  64.7 25.9 %collective-permute-start.9 = (f32[128,512]{1,0:T(8,128)}, f32[128,512]{1,0:T(8,128)}, u32[]{:S(2)}, u32[]{:S(2)}) collective-permute-start(f32[128,512]{1,0:T(8,128)} %get-tuple-element.62), channel_id=1, source_target_pairs={{0,12},{4,8},{8,4},{12,0},{1,13},{5,9},{9,5},{13,1},{2,14},{6,10},... | collective-permute-start | bytes 786440 | tf_op jit(solution)/shard_map/ppermute | solution.py:499
  67.1 25.6 %collective-permute-start.10 = (f32[128,512]{1,0:T(8,128)}, f32[128,512]{1,0:T(8,128)}, u32[]{:S(2)}, u32[]{:S(2)}) collective-permute-start(f32[128,512]{1,0:T(8,128)} %get-tuple-element.63), channel_id=1, source_target_pairs={{0,8},{4,12},{8,0},{12,4},{1,9},{5,13},{9,1},{13,5},{2,10},{6,14},... | collective-permute-start | bytes 786440 | tf_op jit(solution)/shard_map/ppermute | solution.py:499
  67.1 26.6 %collective-permute-start.11 = (f32[128,512]{1,0:T(8,128)S(1)}, f32[128,512]{1,0:T(8,128)S(1)}, u32[]{:S(2)}, u32[]{:S(2)}) collective-permute-start(f32[128,512]{1,0:T(8,128)S(1)} %get-tuple-element.64), channel_id=1, source_target_pairs={{0,4},{4,0},{8,12},{12,8},{1,5},{5,1},{9,13},{13,9},{2,6},{6,2},{1... | collective-permute-start | bytes 786440 | tf_op jit(solution)/shard_map/ppermute | solution.py:499
  74.0 5.2 %collective-permute-start.15 = (f32[32,128]{1,0:T(8,128)S(1)}, f32[32,128]{1,0:T(8,128)S(1)}, u32[]{:S(2)}, u32[]{:S(2)}) collective-permute-start(f32[32,128]{1,0:T(8,128)S(1)} %get-tuple-element.73), channel_id=1, source_target_pairs={{0,1},{1,2},{2,3},{4,5},{5,6},{6,7},{8,9},{9,10},{10,11},{12,13},{... | collective-permute-start | bytes 49160 | tf_op jit(solution)/shard_map/ppermute | solution.py:23
  76.8 5.5 %collective-permute-start.16 = (f32[32,128]{1,0:T(8,128)S(1)}, f32[32,128]{1,0:T(8,128)S(1)}, u32[]{:S(2)}, u32[]{:S(2)}) collective-permute-start(f32[32,128]{1,0:T(8,128)S(1)} %get-tuple-element.73), channel_id=1, source_target_pairs={{1,0},{2,1},{3,2},{5,4},{6,5},{7,6},{9,8},{10,9},{11,10},{13,12},{... | collective-permute-start | bytes 49160 | tf_op jit(solution)/shard_map/ppermute | solution.py:23
  88.1 10.1 %collective-permute-start.17 = (f32[128,512]{1,0:T(8,128)S(1)}, f32[128,512]{1,0:T(8,128)S(1)}, u32[]{:S(2)}, u32[]{:S(2)}) collective-permute-start(f32[128,512]{1,0:T(8,128)S(1)} %get-tuple-element.76), channel_id=1, source_target_pairs={{0,12},{4,8},{8,4},{12,0},{1,13},{5,9},{9,5},{13,1},{2,14},{6,10},... | collective-permute-start | bytes 786440 | tf_op jit(solution)/shard_map/ppermute | solution.py:499
  90.6 20.4 %collective-permute-start.18 = (f32[128,512]{1,0:T(8,128)S(1)}, f32[128,512]{1,0:T(8,128)S(1)}, u32[]{:S(2)}, u32[]{:S(2)}) collective-permute-start(f32[128,512]{1,0:T(8,128)S(1)} %get-tuple-element.77), channel_id=1, source_target_pairs={{0,8},{4,12},{8,0},{12,4},{1,9},{5,13},{9,1},{13,5},{2,10},{6,14},... | collective-permute-start | bytes 786440 | tf_op jit(solution)/shard_map/ppermute | solution.py:499
  90.6 20.4 %collective-permute-start.19 = (f32[128,512]{1,0:T(8,128)S(1)}, f32[128,512]{1,0:T(8,128)S(1)}, u32[]{:S(2)}, u32[]{:S(2)}) collective-permute-start(f32[128,512]{1,0:T(8,128)S(1)} %get-tuple-element.78), channel_id=1, source_target_pairs={{0,4},{4,0},{8,12},{12,8},{1,5},{5,1},{9,13},{13,9},{2,6},{6,2},{1... | collective-permute-start | bytes 786440 | tf_op jit(solution)/shard_map/ppermute | solution.py:499
  (9 other events, 298.2 us)

commit v9 on v5

--- a/solution.py
+++ b/solution.py
@@ -155,6 +155,10 @@
     return pl.BlockSpec(memory_space=pltpu.HBM)
 
 
+def pair(q, ranks):
+    return (ranks - q) % ranks
+
+
 def split(value):
     high = value.astype(jnp.bfloat16)
     return high, (value - high.astype(jnp.float32)).astype(jnp.bfloat16)
@@ -182,83 +186,98 @@
 def pack_kernel(layer, plane_ref, mask_ref, *refs):
     if layer:
         (low_ref, high_ref), refs = refs[:2], refs[2:]
-    else:
-        (rate_ref, flag_ref), refs = refs[:2], refs[2:]
-    refs, (mask_part, first_ref, last_ref, mask_sems, sems) = refs[:-5], refs[-5:]
-    if layer:
-        out_refs = refs
-    else:
-        out_refs, edge_ref = refs[:-1], refs[-1]
+    out_refs, (part_ref, mask_part, mask_sems, in_sems, out_sems) = refs[:-5], refs[-5:]
     ranks = len(out_refs)
     planes, rows, cols = plane_ref.shape
     levels, block, _ = mask_ref.shape
     held = planes // levels
     me = lax.axis_index("comp")
-    copies, masks = [], []
-
-    def start(source, target):
-        copies.append(pltpu.make_async_copy(source, target, sems.at[len(copies)]))
+    copies = []
+    order = [*range(1, ranks), 0]
+
+    def start(source, target, sem):
+        copies.append(pltpu.make_async_copy(source, target, sem))
         copies[-1].start()
 
-    if not layer:
-        start(plane_ref.at[:, :, pl.ds(0, LANES)], first_ref)
-        start(plane_ref.at[:, :, pl.ds(cols - LANES, LANES)], last_ref)
-    for q, out_ref in enumerate(out_refs):
-        at = jnp.bitwise_xor(me, q) * (levels // ranks) + layer
-        masks.append(pltpu.make_async_copy(mask_ref.at[at], mask_part.at[q], mask_sems.at[q]))
-        masks[-1].start()
+    for q in order:
+        at = jnp.bitwise_xor(me, pair(q, ranks)) * (levels // ranks) + layer
         for index in range(held):
-            start(plane_ref.at[index * levels + at], out_ref.at[pl.ds(index * rows, rows)])
+            spot = pl.ds(index * rows, rows)
+            start(plane_ref.at[index * levels + at], part_ref.at[q, spot], in_sems.at[len(copies)])
+        start(mask_ref.at[at], mask_part.at[q], mask_sems.at[q])
+    arrivals = list(copies)
+    copies.clear()
     if layer:
         lane_at = lax.broadcasted_iota(jnp.int32, (rows, LANES), 1)
         sides = jnp.where(lane_at < planes, high_ref[...], low_ref[...])
         for group, row, lane in band_spots(rows, cols):
-            part = sides[group * TILE : (group + 1) * TILE]
             row += held * rows + block
-            for out_ref in out_refs:
-                out_ref[row : row + TILE, lane : lane + LANES] = part
-    else:
-        copies[0].wait()
-        copies[1].wait()
-        end = slice(cols - LANES, cols)
-        weight_plus, weight_minus = face_weights(rate_ref[1, :, end], flag_ref[1, :, end])
-        columns = [first_ref[plane][:, :1] for plane in range(planes)]
-        columns += [last_ref[plane][:, LANES - 1 :] for plane in range(planes)]
-        columns += [weight_plus[:, LANES - 1 :], weight_minus[:, LANES - 1 :]]
-        edge_ref[...] = gather_columns(columns, rows)
-    for q, out_ref in enumerate(out_refs):
-        masks[q].wait()
-        out_ref[held * rows : held * rows + block, :] = mask_part[q].astype(jnp.float32)
-    for copy in copies[0 if layer else 2 :]:
+            for q in order:
+                part_ref[q, row : row + TILE, lane : lane + LANES] = sides[
+                    group * TILE : (group + 1) * TILE
+                ]
+    for position, q in enumerate(order):
+        for copy in arrivals[position * (held + 1) : (position + 1) * (held + 1)]:
+            copy.wait()
+        part_ref[q, held * rows : held * rows + block, :] = mask_part[q].astype(jnp.float32)
+        start(part_ref.at[q], out_refs[q], out_sems.at[q])
+    for copy in copies:
         copy.wait()
 
 
-def pack(concentration, stiff_mask, layer, ranks, others):
+def pack(concentration, stiff_mask, layer, ranks, sides):
     planes, rows, cols = concentration.shape
     held = planes // NZ
     block = stiff_mask.shape[1]
-    extra = block + (bands(rows, cols) if layer else 0)
-    message = jax.ShapeDtypeStruct((held * rows + extra, cols), jnp.float32)
-    out_shape = [message] * ranks
-    if not layer:
-        out_shape.append(jax.ShapeDtypeStruct((rows, LANES), jnp.float32))
+    size = held * rows + block + (bands(rows, cols) if layer else 0)
     results = pl.pallas_call(
         functools.partial(pack_kernel, layer),
-        out_shape=out_shape,
-        in_specs=[hbm_spec()] * 2 + [whole_spec()] * 2,
-        out_specs=[whole_spec()] * len(out_shape),
+        out_shape=[jax.ShapeDtypeStruct((size, cols), jnp.float32)] * ranks,
+        in_specs=[hbm_spec()] * 2 + [whole_spec()] * len(sides),
+        out_specs=[any_spec()] * ranks,
         scratch_shapes=[
+            pltpu.VMEM((ranks, size, cols), jnp.float32),
             pltpu.VMEM((ranks, block, cols), jnp.int32),
-            pltpu.VMEM((planes, rows, LANES), jnp.float32),
-            pltpu.VMEM((planes, rows, LANES), jnp.float32),
             pltpu.SemaphoreType.DMA((ranks,)),
-            pltpu.SemaphoreType.DMA((ranks * held + 2,)),
+            pltpu.SemaphoreType.DMA((ranks * (held + 1),)),
+            pltpu.SemaphoreType.DMA((ranks,)),
         ],
         compiler_params=pltpu.CompilerParams(vmem_limit_bytes=VMEM_LIMIT if layer else MOST_VMEM),
         cost_estimate=pl.CostEstimate(flops=0, bytes_accessed=0, transcendentals=0),
         name="pack",
-    )(concentration, stiff_mask, *others)
-    return list(results[:ranks]), results[ranks:]
+    )(concentration, stiff_mask, *sides)
+    return list(results)
+
+
+def plane_edges_kernel(first_ref, last_ref, rate_ref, flag_ref, *refs):
+    planes, rows, _ = first_ref.shape
+    weight_plus, weight_minus = face_weights(rate_ref[1], flag_ref[1])
+    columns = [first_ref[plane][:, :1] for plane in range(planes)]
+    columns += [last_ref[plane][:, LANES - 1 :] for plane in range(planes)]
+    columns += [weight_plus[:, LANES - 1 :], weight_minus[:, LANES - 1 :]]
+    refs[-1][...] = gather_columns(columns, rows)
+
+
+def plane_edges(concentration, face_rate, face_flag, after):
+    planes, rows, cols = concentration.shape
+    last = cols // LANES - 1
+    face = pl.BlockSpec((2, rows, LANES), lambda i: (0, 0, last))
+    return pl.pallas_call(
+        plane_edges_kernel,
+        grid=(1,),
+        out_shape=jax.ShapeDtypeStruct((rows, LANES), jnp.float32),
+        in_specs=[
+            pl.BlockSpec((planes, rows, LANES), lambda i: (0, 0, 0)),
+            pl.BlockSpec((planes, rows, LANES), lambda i: (0, 0, last)),
+            face,
+            face,
+        ]
+        + [any_spec()] * len(after),
+        out_specs=pl.BlockSpec((rows, LANES), lambda i: (0, 0)),
+        compiler_params=pltpu.CompilerParams(vmem_limit_bytes=VMEM_LIMIT),
+        cost_estimate=pl.CostEstimate(flops=0, bytes_accessed=0, transcendentals=0),
+        name="plane_edges",
+    )(concentration, concentration, face_rate, face_flag, *after)
 
 
 def edges_kernel(held, *refs):
@@ -304,7 +323,7 @@
 
     def pick(shape, stacked_dim):
         at = lax.broadcasted_iota(jnp.int32, shape, stacked_dim) // TILE
-        component = jnp.bitwise_xor(me, at // held) * held + lax.rem(at, held)
+        component = jnp.bitwise_xor(me, pair(at // held, ranks)) * held + lax.rem(at, held)
         held_at = lax.broadcasted_iota(jnp.int32, shape, 1 - stacked_dim)
         return jnp.where(component == held_at, 1.0, 0.0)
 
@@ -373,7 +392,7 @@
     components = stacked // TILE
     held = components // pieces
     me = lax.axis_index("comp")
-    ranks = [jnp.bitwise_xor(me, q) for q in range(pieces)]
+    ranks = [jnp.bitwise_xor(me, pair(q, pieces)) for q in range(pieces)]
     row_at = lax.broadcasted_iota(jnp.int32, (rows, cols), 0)
     col_at = lax.broadcasted_iota(jnp.int32, (rows, cols), 1)
 
@@ -400,12 +419,8 @@
         return jnp.where(col_at == cols - 1, edge, pltpu.roll(value, cols - 1, 1))
 
     block = rows // pieces
-    low_side, high_side = low_ref[...], high_ref[...]
-    rim_at = 2 * components
-    sides = [(low_side, components + at, high_side, at) for at in range(components)]
     if is_first and layer:
-        sides = []
-        rim_at = 2 * held * NZ
+        sides, rim_at = [], 2 * held * NZ
         turn = LANES - (me * (NZ // pieces) + layer)
         for value_ref in value_refs:
             start = held * rows + block
@@ -420,6 +435,9 @@
             side = pltpu.roll(side, turn, 1)
             for index in range(held):
                 sides.append((side, (held + index) * NZ, side, index * NZ))
+    else:
+        low_side, high_side, rim_at = low_ref[...], high_ref[...], 2 * components
+        sides = [(low_side, components + at, high_side, at) for at in range(components)]
     down_plus = from_lower_row(weight_plus[0])
     down_minus = from_lower_row(weight_minus[0])
     side_plus = from_lower_col(weight_plus[1], column(low_side, rim_at))
@@ -430,7 +448,8 @@
         value = value_refs[q][index * rows : (index + 1) * rows, :]
         component = ranks[q] * held + index
         spread = spread_ref[component]
-        retard = 1.0 / jnp.full((rows, cols), retard_ref[component], jnp.float32)
+        retard = 1.0 / jnp.full((rows, LANES), retard_ref[component], jnp.float32)
+        retard = jnp.concatenate([retard] * (cols // LANES), axis=1)
         change = (
             (down_plus + spread) * from_lower_row(value)
             + (weight_minus[0] + spread) * from_upper_row(value)
@@ -455,7 +474,7 @@
             species_ref[group] = offset_ref[group] + product(both_ref, [species, jnp.tanh(species)])
         return carry
 
-    lax.fori_loop(0, NEWT - 1, plain_step, 0)
+    lax.fori_loop(0, NEWT - 1, plain_step, 0, unroll=True)
     plain_ref[...] = species_ref[...]
     ratio = jnp.concatenate([ratio_ref[...]] * (cols // LANES), axis=1)
 
@@ -466,7 +485,7 @@
             species_ref[group] = offset_ref[group] + product(both_ref, [species, reaction])
         return carry
 
-    lax.fori_loop(0, STIFF, stiff_step, 0)
+    lax.fori_loop(0, STIFF, stiff_step, 0, unroll=True)
     if is_first:
         for rank, value_ref in zip(ranks, value_refs):
             spot = pl.ds(pl.multiple_of(rank * block, TILE), block)
@@ -543,37 +562,40 @@
     def send(value, by):
         return lax.ppermute(value, "comp", [(i, i ^ by) for i in range(ranks)]) if by else value
 
-    arrived, others = [], (face_rate, face_flag)
-    for layer in range(layers):
-        messages, edges = pack(concentration, stiff_mask, layer, ranks, others)
-        if layer:
-            messages, arrived[-1] = lax.optimization_barrier((messages, arrived[-1]))
-        arrived.append([send(part, q) for q, part in enumerate(messages)])
-        if edges:
-            others = (shifted(edges[0], "space", 1), shifted(edges[0], "space", -1))
-        after = messages[0]
-
-    first, both, ratio = spread_parameters(ranks, mixing, mixing_inverse, affinity, mineral, after)
+    def send_all(parts):
+        return [send(part, pair(q, ranks)) for q, part in enumerate(parts)]
+
+    messages = pack(concentration, stiff_mask, 0, ranks, ())
+    arrived = [send_all(messages)]
+    if layers > 1:
+        edges = plane_edges(concentration, face_rate, face_flag, messages[:1])
+        sides = (shifted(edges, "space", 1), shifted(edges, "space", -1))
+    for layer in range(1, layers):
+        messages = pack(concentration, stiff_mask, layer, ranks, sides)
+        messages, arrived[-1] = lax.optimization_barrier((messages, arrived[-1]))
+        arrived.append(send_all(messages))
+
+    first, both, ratio = spread_parameters(ranks, mixing, mixing_inverse, affinity, mineral, messages[0]
+    )
     shared = (dispersion, retardation, face_rate, face_flag, ratio, first, both)
 
     result = jnp.zeros((held, NZ, rows, cols), jnp.float32)
     for layer in range(layers):
         values, stiff = arrived[layer], None
-        rims = None if layer else edges_of(values, face_rate, face_flag, after)
+        rims = None if layer else edges_of(values, face_rate, face_flag, messages[0])
         for step in range(STEPS):
             if rims is None:
-                low, high = others
+                low, high = sides
             else:
                 low, high = shifted(rims, "space", 1), shifted(rims, "space", -1)
             values, stiff, rims = layer_step(
                 values, stiff, low, high, shared, layer, step < STEPS - 1
             )
-        for q in range(ranks):
-            piece = send(values[q], q)
+        for q, piece in enumerate(send_all(values)):
             result = lax.dynamic_update_slice(
                 result,
                 piece.reshape(held, 1, rows, cols),
-                (0, (me ^ q) * layers + layer, 0, 0),
+                (0, (me ^ pair(q, ranks)) * layers + layer, 0, 0),
             )
     return result.reshape(planes, rows, cols)
 

time: 119 us -> 114 us (0.958)
  the two profiles are of different devices: /device:TPU:9 before, /device:TPU:1 now
where the time goes in v9:
time: 114 us; the launch traced here: 113 us
  waiting for transfers between devices  39 us (34%)
  starting transfers between devices  38.6 us (34%)
  Pallas kernels  29.6 us (26%)
  local copies, waits for them, and re-layouts  5.56 us (5%)
    ppermute x12, waiting for transfers between devices, send(): lax.ppermute(value, 'comp', [(i, i ^ by) for i in range(ranks)])  28.7 us
    pallas_call x4, Pallas kernels, layer_step(): pl.pallas_call(functools.partial(step_kernel, pieces, layer, stiff is Non...  23.8 us
    ppermute x8, starting transfers between devices, shifted(): return lax.ppermute(shard, axis, pairs)  23 us
    ppermute x12, starting transfers between devices, send(): lax.ppermute(value, 'comp', [(i, i ^ by) for i in range(ranks)])  15.7 us
    ppermute x8, waiting for transfers between devices, shifted(): return lax.ppermute(shard, axis, pairs)  10.2 us
    pallas_call x2, Pallas kernels, pack(): pl.pallas_call(functools.partial(pack_kernel, layer), out_shape=[jax.Shap...  4.39 us
    unnamed x28, local copies, waits for them, and re-layouts  3.24 us
  transfers between devices with their start and end apart: 20, of which 7 were waited for; matrix products, arithmetic and copies ran while one was open for 2% of the time, Pallas kernels for 24%

profile of v9, /device:TPU:1, one launch (start us, length us, event | category | flops | bytes accessed | tf_op | source)
XLA Modules:
  0.0 113.1 jit_solution(3093891583605644111)
XLA Ops:
  0.0 2.4 %pack.2 = (f32[136,512]{1,0:T(8,128)}, f32[136,512]{1,0:T(8,128)}, f32[136,512]{1,0:T(8,128)}, f32[136,512]{1,0:T(8,128)}) custom-call(f32[32,32,512]{2,1,0:T(8,128)} %plane_ref.3, s32[8,8,512]{2,1,0:T(8,128)} %mask_ref.3), custom_call_target="tpu_custom_call" | custom-call | tf_op jit(solution)/shard_map/pack/pallas_call | solution.py:233
  2.4 4.2 %collective-permute-start.2 = (f32[136,512]{1,0:T(8,128)}, f32[136,512]{1,0:T(8,128)S(1)}, u32[]{:S(2)}, u32[]{:S(2)}) collective-permute-start(f32[136,512]{1,0:T(8,128)} %get-tuple-element.49), channel_id=1, source_target_pairs={{0,12},{4,8},{8,4},{12,0},{1,13},{5,9},{9,5},{13,1},{2,14},{6,10},... | collective-permute-start | bytes 835592 | tf_op jit(solution)/shard_map/ppermute | solution.py:563
  9.3 4.5 %collective-permute-start = (f32[32,128]{1,0:T(8,128)S(1)}, f32[32,128]{1,0:T(8,128)S(1)}, u32[]{:S(2)}, u32[]{:S(2)}) collective-permute-start(f32[32,128]{1,0:T(8,128)S(1)} %plane_edges.1), channel_id=1, source_target_pairs={{0,1},{1,2},{2,3},{4,5},{5,6},{6,7},{8,9},{9,10},{10,11},{12,13},{... | collective-permute-start | bytes 49160 | tf_op jit(solution)/shard_map/ppermute | solution.py:23
  13.8 1.9 %collective-permute-start.1 = (f32[32,128]{1,0:T(8,128)S(1)}, f32[32,128]{1,0:T(8,128)S(1)}, u32[]{:S(2)}, u32[]{:S(2)}) collective-permute-start(f32[32,128]{1,0:T(8,128)S(1)} %plane_edges.1), channel_id=1, source_target_pairs={{1,0},{2,1},{3,2},{5,4},{6,5},{7,6},{9,8},{10,9},{11,10},{13,12},{... | collective-permute-start | bytes 49160 | tf_op jit(solution)/shard_map/ppermute | solution.py:23
  15.8 3.4 %collective-permute-done.1.refs_1_.refs_5_ = f32[32,128]{1,0:T(8,128)S(1)} collective-permute-done((f32[32,128]{1,0:T(8,128)S(1)}, f32[32,128]{1,0:T(8,128)S(1)}, u32[]{:S(2)}, u32[]{:S(2)}) %collective-permute-start.1) | collective-permute-done | bytes 16416 | tf_op jit(solution)/shard_map/ppermute | solution.py:23
  19.2 2.0 %pack.3 = (f32[144,512]{1,0:T(8,128)S(1)}, f32[144,512]{1,0:T(8,128)S(1)}, f32[144,512]{1,0:T(8,128)S(1)}, f32[144,512]{1,0:T(8,128)S(1)}) custom-call(f32[32,32,512]{2,1,0:T(8,128)S(1)} %copy-done, s32[8,8,512]{2,1,0:T(8,128)S(1)} %copy-done.6, f32[32,128]{1,0:T(8,128)S(1)} %collective-permute-done.refs_0_.refs_4_, ...), custom_call_target="tpu_custom_call" | custom-call | tf_op jit(solution)/shard_map/pack/pallas_call | solution.py:233
  21.2 9.0 %collective-permute-done.3.refs_2_.refs_6_ = f32[136,512]{1,0:T(8,128)S(1)} collective-permute-done((f32[136,512]{1,0:T(8,128)}, f32[136,512]{1,0:T(8,128)S(1)}, u32[]{:S(2)}, u32[]{:S(2)}) %collective-permute-start.3) | collective-permute-done | bytes 278560 | tf_op jit(solution)/shard_map/ppermute | solution.py:563
  30.2 2.0 %collective-permute-start.12 = (f32[144,512]{1,0:T(8,128)S(1)}, f32[144,512]{1,0:T(8,128)S(1)}, u32[]{:S(2)}, u32[]{:S(2)}) collective-permute-start(f32[144,512]{1,0:T(8,128)S(1)} %get-tuple-element.70), channel_id=1, source_target_pairs={{0,12},{4,8},{8,4},{12,0},{1,13},{5,9},{9,5},{13,1},{2,14},{6,10},... | collective-permute-start | bytes 884744 | tf_op jit(solution)/shard_map/ppermute | solution.py:563
  32.4 4.9 %collective-permute-start.5 = (f32[32,128]{1,0:T(8,128)S(1)}, f32[32,128]{1,0:T(8,128)S(1)}, u32[]{:S(2)}, u32[]{:S(2)}) collective-permute-start(f32[32,128]{1,0:T(8,128)S(1)} %edges.1), channel_id=1, source_target_pairs={{0,1},{1,2},{2,3},{4,5},{5,6},{6,7},{8,9},{9,10},{10,11},{12,13},{... | collective-permute-start | bytes 49160 | tf_op jit(solution)/shard_map/ppermute | solution.py:23
  37.4 1.9 %collective-permute-start.6 = (f32[32,128]{1,0:T(8,128)S(1)}, f32[32,128]{1,0:T(8,128)S(1)}, u32[]{:S(2)}, u32[]{:S(2)}) collective-permute-start(f32[32,128]{1,0:T(8,128)S(1)} %edges.1), channel_id=1, source_target_pairs={{1,0},{2,1},{3,2},{5,4},{6,5},{7,6},{9,8},{10,9},{11,10},{13,12},{... | collective-permute-start | bytes 49160 | tf_op jit(solution)/shard_map/ppermute | solution.py:23
  42.7 5.7 %layer_step.4 = (f32[128,512]{1,0:T(8,128)S(1)}, f32[128,512]{1,0:T(8,128)S(1)}, f32[128,512]{1,0:T(8,128)S(1)}, f32[128,512]{1,0:T(8,128)S(1)}, f32[32,128]{1,0:T(8,128)S(1)}, /*index=5*/f32[32,512]{1,0:T(8,128)S(1)}) custom-call(f32[16]{0:T(128)S(1)} %copy-done.7, f32[16]{0:T(128)S(1)} %copy-done.8, f32[136,512]{1,0:T(8,128)S(1)} %copy-done.5, ...), custom_call_target="tpu_custom_call" | custom-call | tf_op jit(solution)/shard_map/layer_step/pallas_call | solution.py:529
  48.4 3.0 %collective-permute-start.7 = (f32[32,128]{1,0:T(8,128)S(1)}, f32[32,128]{1,0:T(8,128)S(1)}, u32[]{:S(2)}, u32[]{:S(2)}) collective-permute-start(f32[32,128]{1,0:T(8,128)S(1)} %get-tuple-element.64), channel_id=1, source_target_pairs={{0,1},{1,2},{2,3},{4,5},{5,6},{6,7},{8,9},{9,10},{10,11},{12,13},{... | collective-permute-start | bytes 49160 | tf_op jit(solution)/shard_map/ppermute | solution.py:23
  51.4 2.1 %collective-permute-start.8 = (f32[32,128]{1,0:T(8,128)S(1)}, f32[32,128]{1,0:T(8,128)S(1)}, u32[]{:S(2)}, u32[]{:S(2)}) collective-permute-start(f32[32,128]{1,0:T(8,128)S(1)} %get-tuple-element.64), channel_id=1, source_target_pairs={{1,0},{2,1},{3,2},{5,4},{6,5},{7,6},{9,8},{10,9},{11,10},{13,12},{... | collective-permute-start | bytes 49160 | tf_op jit(solution)/shard_map/ppermute | solution.py:23
  53.5 3.2 %collective-permute-done.8.refs_5_ = f32[32,128]{1,0:T(8,128)S(1)} collective-permute-done((f32[32,128]{1,0:T(8,128)S(1)}, f32[32,128]{1,0:T(8,128)S(1)}, u32[]{:S(2)}, u32[]{:S(2)}) %collective-permute-start.8) | collective-permute-done | bytes 16416 | tf_op jit(solution)/shard_map/ppermute | solution.py:23
  56.8 6.5 %layer_step.5 = (f32[128,512]{1,0:T(8,128)S(1)}, f32[128,512]{1,0:T(8,128)}, f32[128,512]{1,0:T(8,128)S(1)}, f32[128,512]{1,0:T(8,128)S(1)}) custom-call(f32[16]{0:T(128)S(1)} %copy-done.7, f32[16]{0:T(128)S(1)} %copy-done.8, f32[128,512]{1,0:T(8,128)S(1)} %get-tuple-element.60.refs_0_, f32[128,512]{1,0:T(8,128)S(1)} %get-tuple-element.61.refs_1_, ...), custom_call_target="tpu_custom_call" | custom-call | tf_op jit(solution)/shard_map/layer_step/pallas_call | solution.py:529
  63.3 2.0 %collective-permute-start.9 = (f32[128,512]{1,0:T(8,128)}, f32[128,512]{1,0:T(8,128)}, u32[]{:S(2)}, u32[]{:S(2)}) collective-permute-start(f32[128,512]{1,0:T(8,128)} %get-tuple-element.67), channel_id=1, source_target_pairs={{0,12},{4,8},{8,4},{12,0},{1,13},{5,9},{9,5},{13,1},{2,14},{6,10},... | collective-permute-start | bytes 786440 | tf_op jit(solution)/shard_map/ppermute | solution.py:563
  67.2 5.7 %layer_step.6 = (f32[128,512]{1,0:T(8,128)S(1)}, f32[128,512]{1,0:T(8,128)S(1)}, f32[128,512]{1,0:T(8,128)S(1)}, f32[128,512]{1,0:T(8,128)S(1)}, f32[32,128]{1,0:T(8,128)S(1)}, /*index=5*/f32[32,512]{1,0:T(8,128)S(1)}) custom-call(f32[16]{0:T(128)S(1)} %copy-done.7, f32[16]{0:T(128)S(1)} %copy-done.8, f32[144,512]{1,0:T(8,128)S(1)} %get-tuple-element.56.refs_10_.refs_0_, ...), custom_call_target="tpu_custom_call" | custom-call | tf_op jit(solution)/shard_map/layer_step/pallas_call | solution.py:529
  72.9 2.5 %collective-permute-start.15 = (f32[32,128]{1,0:T(8,128)S(1)}, f32[32,128]{1,0:T(8,128)S(1)}, u32[]{:S(2)}, u32[]{:S(2)}) collective-permute-start(f32[32,128]{1,0:T(8,128)S(1)} %get-tuple-element.77), channel_id=1, source_target_pairs={{0,1},{1,2},{2,3},{4,5},{5,6},{6,7},{8,9},{9,10},{10,11},{12,13},{... | collective-permute-start | bytes 49160 | tf_op jit(solution)/shard_map/ppermute | solution.py:23
  75.4 2.1 %collective-permute-start.16 = (f32[32,128]{1,0:T(8,128)S(1)}, f32[32,128]{1,0:T(8,128)S(1)}, u32[]{:S(2)}, u32[]{:S(2)}) collective-permute-start(f32[32,128]{1,0:T(8,128)S(1)} %get-tuple-element.77), channel_id=1, source_target_pairs={{1,0},{2,1},{3,2},{5,4},{6,5},{7,6},{9,8},{10,9},{11,10},{13,12},{... | collective-permute-start | bytes 49160 | tf_op jit(solution)/shard_map/ppermute | solution.py:23
  78.5 2.3 %collective-permute-done.16.refs_5_ = f32[32,128]{1,0:T(8,128)S(1)} collective-permute-done((f32[32,128]{1,0:T(8,128)S(1)}, f32[32,128]{1,0:T(8,128)S(1)}, u32[]{:S(2)}, u32[]{:S(2)}) %collective-permute-start.16) | collective-permute-done | bytes 16416 | tf_op jit(solution)/shard_map/ppermute | solution.py:23
  80.8 5.8 %layer_step.7 = (f32[128,512]{1,0:T(8,128)S(1)}, f32[128,512]{1,0:T(8,128)S(1)}, f32[128,512]{1,0:T(8,128)S(1)}, f32[128,512]{1,0:T(8,128)S(1)}) custom-call(f32[16]{0:T(128)S(1)} %copy-done.7, f32[16]{0:T(128)S(1)} %copy-done.8, f32[128,512]{1,0:T(8,128)S(1)} %get-tuple-element.73.refs_0_, f32[128,512]{1,0:T(8,128)S(1)} %get-tuple-element.74.refs_1_, ...), custom_call_target="tpu_custom_call" | custom-call | tf_op jit(solution)/shard_map/layer_step/pallas_call | solution.py:529
  86.6 2.4 %collective-permute-start.17 = (f32[128,512]{1,0:T(8,128)S(1)}, f32[128,512]{1,0:T(8,128)S(1)}, u32[]{:S(2)}, u32[]{:S(2)}) collective-permute-start(f32[128,512]{1,0:T(8,128)S(1)} %get-tuple-element.80), channel_id=1, source_target_pairs={{0,12},{4,8},{8,4},{12,0},{1,13},{5,9},{9,5},{13,1},{2,14},{6,10},... | collective-permute-start | bytes 786440 | tf_op jit(solution)/shard_map/ppermute | solution.py:563
  91.9 4.4 %collective-permute-done.17 = f32[128,512]{1,0:T(8,128)S(1)} collective-permute-done((f32[128,512]{1,0:T(8,128)S(1)}, f32[128,512]{1,0:T(8,128)S(1)}, u32[]{:S(2)}, u32[]{:S(2)}) %collective-permute-start.17) | collective-permute-done | bytes 262176 | tf_op jit(solution)/shard_map/ppermute | solution.py:563
  96.3 15.4 %collective-permute-done.18 = f32[128,512]{1,0:T(8,128)S(1)} collective-permute-done((f32[128,512]{1,0:T(8,128)S(1)}, f32[128,512]{1,0:T(8,128)S(1)}, u32[]{:S(2)}, u32[]{:S(2)}) %collective-permute-start.18) | collective-permute-done | bytes 262176 | tf_op jit(solution)/shard_map/ppermute | solution.py:563
  (62 shorter events, 13.3 us)
Async XLA Ops:
  2.4 18.8 %collective-permute-start.2 = (f32[136,512]{1,0:T(8,128)}, f32[136,512]{1,0:T(8,128)S(1)}, u32[]{:S(2)}, u32[]{:S(2)}) collective-permute-start(f32[136,512]{1,0:T(8,128)} %get-tuple-element.49), channel_id=1, source_target_pairs={{0,12},{4,8},{8,4},{12,0},{1,13},{5,9},{9,5},{13,1},{2,14},{6,10},... | collective-permute-start | bytes 835592 | tf_op jit(solution)/shard_map/ppermute | solution.py:563
  6.7 23.5 %collective-permute-start.3 = (f32[136,512]{1,0:T(8,128)}, f32[136,512]{1,0:T(8,128)S(1)}, u32[]{:S(2)}, u32[]{:S(2)}) collective-permute-start(f32[136,512]{1,0:T(8,128)} %get-tuple-element.50), channel_id=1, source_target_pairs={{0,8},{4,12},{8,0},{12,4},{1,9},{5,13},{9,1},{13,5},{2,10},{6,14},... | collective-permute-start | bytes 835592 | tf_op jit(solution)/shard_map/ppermute | solution.py:563
  6.7 23.5 %collective-permute-start.4 = (f32[136,512]{1,0:T(8,128)}, f32[136,512]{1,0:T(8,128)S(1)}, u32[]{:S(2)}, u32[]{:S(2)}) collective-permute-start(f32[136,512]{1,0:T(8,128)} %get-tuple-element.51), channel_id=1, source_target_pairs={{0,4},{4,0},{8,12},{12,8},{1,5},{5,1},{9,13},{13,9},{2,6},{6,2},{1... | collective-permute-start | bytes 835592 | tf_op jit(solution)/shard_map/ppermute | solution.py:563
  9.2 31.3 %copy-start.9 = (f32[16,16]{1,0:T(8,128)S(1)}, f32[16,16]{1,0:T(8,128)}, u32[]{:S(2)}) copy-start(f32[16,16]{1,0:T(8,128)} %mixing_ref.1) | copy-start | bytes 3076
  9.3 31.3 %copy-start.10 = (f32[16,16]{1,0:T(8,128)S(1)}, f32[16,16]{1,0:T(8,128)}, u32[]{:S(2)}) copy-start(f32[16,16]{1,0:T(8,128)} %inverse_ref.1) | copy-start | bytes 3076
  9.3 31.3 %copy-start.11 = (f32[16]{0:T(128)S(1)}, f32[16]{0:T(128)}, u32[]{:S(2)}) copy-start(f32[16]{0:T(128)} %param.17) | copy-start | bytes 196
  9.3 31.3 %copy-start.12 = (f32[16]{0:T(128)S(1)}, f32[16]{0:T(128)}, u32[]{:S(2)}) copy-start(f32[16]{0:T(128)} %param.18) | copy-start | bytes 196
  9.3 6.5 %collective-permute-start = (f32[32,128]{1,0:T(8,128)S(1)}, f32[32,128]{1,0:T(8,128)S(1)}, u32[]{:S(2)}, u32[]{:S(2)}) collective-permute-start(f32[32,128]{1,0:T(8,128)S(1)} %plane_edges.1), channel_id=1, source_target_pairs={{0,1},{1,2},{2,3},{4,5},{5,6},{6,7},{8,9},{9,10},{10,11},{12,13},{... | collective-permute-start | bytes 49160 | tf_op jit(solution)/shard_map/ppermute | solution.py:23
  13.8 5.4 %collective-permute-start.1 = (f32[32,128]{1,0:T(8,128)S(1)}, f32[32,128]{1,0:T(8,128)S(1)}, u32[]{:S(2)}, u32[]{:S(2)}) collective-permute-start(f32[32,128]{1,0:T(8,128)S(1)} %plane_edges.1), channel_id=1, source_target_pairs={{1,0},{2,1},{3,2},{5,4},{6,5},{7,6},{9,8},{10,9},{11,10},{13,12},{... | collective-permute-start | bytes 49160 | tf_op jit(solution)/shard_map/ppermute | solution.py:23
  30.2 35.1 %collective-permute-start.12 = (f32[144,512]{1,0:T(8,128)S(1)}, f32[144,512]{1,0:T(8,128)S(1)}, u32[]{:S(2)}, u32[]{:S(2)}) collective-permute-start(f32[144,512]{1,0:T(8,128)S(1)} %get-tuple-element.70), channel_id=1, source_target_pairs={{0,12},{4,8},{8,4},{12,0},{1,13},{5,9},{9,5},{13,1},{2,14},{6,10},... | collective-permute-start | bytes 884744 | tf_op jit(solution)/shard_map/ppermute | solution.py:563
  32.4 9.0 %collective-permute-start.5 = (f32[32,128]{1,0:T(8,128)S(1)}, f32[32,128]{1,0:T(8,128)S(1)}, u32[]{:S(2)}, u32[]{:S(2)}) collective-permute-start(f32[32,128]{1,0:T(8,128)S(1)} %edges.1), channel_id=1, source_target_pairs={{0,1},{1,2},{2,3},{4,5},{5,6},{6,7},{8,9},{9,10},{10,11},{12,13},{... | collective-permute-start | bytes 49160 | tf_op jit(solution)/shard_map/ppermute | solution.py:23
  37.4 5.4 %collective-permute-start.6 = (f32[32,128]{1,0:T(8,128)S(1)}, f32[32,128]{1,0:T(8,128)S(1)}, u32[]{:S(2)}, u32[]{:S(2)}) collective-permute-start(f32[32,128]{1,0:T(8,128)S(1)} %edges.1), channel_id=1, source_target_pairs={{1,0},{2,1},{3,2},{5,4},{6,5},{7,6},{9,8},{10,9},{11,10},{13,12},{... | collective-permute-start | bytes 49160 | tf_op jit(solution)/shard_map/ppermute | solution.py:23
  39.3 27.9 %collective-permute-start.13 = (f32[144,512]{1,0:T(8,128)S(1)}, f32[144,512]{1,0:T(8,128)S(1)}, u32[]{:S(2)}, u32[]{:S(2)}) collective-permute-start(f32[144,512]{1,0:T(8,128)S(1)} %get-tuple-element.71), channel_id=1, source_target_pairs={{0,8},{4,12},{8,0},{12,4},{1,9},{5,13},{9,1},{13,5},{2,10},{6,14},... | collective-permute-start | bytes 884744 | tf_op jit(solution)/shard_map/ppermute | solution.py:563
  39.4 27.8 %collective-permute-start.14 = (f32[144,512]{1,0:T(8,128)S(1)}, f32[144,512]{1,0:T(8,128)S(1)}, u32[]{:S(2)}, u32[]{:S(2)}) collective-permute-start(f32[144,512]{1,0:T(8,128)S(1)} %get-tuple-element.72), channel_id=1, source_target_pairs={{0,4},{4,0},{8,12},{12,8},{1,5},{5,1},{9,13},{13,9},{2,6},{6,2},{1... | collective-permute-start | bytes 884744 | tf_op jit(solution)/shard_map/ppermute | solution.py:563
  48.4 5.1 %collective-permute-start.7 = (f32[32,128]{1,0:T(8,128)S(1)}, f32[32,128]{1,0:T(8,128)S(1)}, u32[]{:S(2)}, u32[]{:S(2)}) collective-permute-start(f32[32,128]{1,0:T(8,128)S(1)} %get-tuple-element.64), channel_id=1, source_target_pairs={{0,1},{1,2},{2,3},{4,5},{5,6},{6,7},{8,9},{9,10},{10,11},{12,13},{... | collective-permute-start | bytes 49160 | tf_op jit(solution)/shard_map/ppermute | solution.py:23
  51.4 5.4 %collective-permute-start.8 = (f32[32,128]{1,0:T(8,128)S(1)}, f32[32,128]{1,0:T(8,128)S(1)}, u32[]{:S(2)}, u32[]{:S(2)}) collective-permute-start(f32[32,128]{1,0:T(8,128)S(1)} %get-tuple-element.64), channel_id=1, source_target_pairs={{1,0},{2,1},{3,2},{5,4},{6,5},{7,6},{9,8},{10,9},{11,10},{13,12},{... | collective-permute-start | bytes 49160 | tf_op jit(solution)/shard_map/ppermute | solution.py:23
  63.3 14.2 %collective-permute-start.9 = (f32[128,512]{1,0:T(8,128)}, f32[128,512]{1,0:T(8,128)}, u32[]{:S(2)}, u32[]{:S(2)}) collective-permute-start(f32[128,512]{1,0:T(8,128)} %get-tuple-element.67), channel_id=1, source_target_pairs={{0,12},{4,8},{8,4},{12,0},{1,13},{5,9},{9,5},{13,1},{2,14},{6,10},... | collective-permute-start | bytes 786440 | tf_op jit(solution)/shard_map/ppermute | solution.py:563
  65.3 23.7 %collective-permute-start.10 = (f32[128,512]{1,0:T(8,128)S(1)}, f32[128,512]{1,0:T(8,128)}, u32[]{:S(2)}, u32[]{:S(2)}) collective-permute-start(f32[128,512]{1,0:T(8,128)S(1)} %get-tuple-element.68), channel_id=1, source_target_pairs={{0,8},{4,12},{8,0},{12,4},{1,9},{5,13},{9,1},{13,5},{2,10},{6,14},... | collective-permute-start | bytes 786440 | tf_op jit(solution)/shard_map/ppermute | solution.py:563
  65.3 26.4 %collective-permute-start.11 = (f32[128,512]{1,0:T(8,128)S(1)}, f32[128,512]{1,0:T(8,128)S(1)}, u32[]{:S(2)}, u32[]{:S(2)}) collective-permute-start(f32[128,512]{1,0:T(8,128)S(1)} %get-tuple-element.69), channel_id=1, source_target_pairs={{0,4},{4,0},{8,12},{12,8},{1,5},{5,1},{9,13},{13,9},{2,6},{6,2},{1... | collective-permute-start | bytes 786440 | tf_op jit(solution)/shard_map/ppermute | solution.py:563
  72.9 5.6 %collective-permute-start.15 = (f32[32,128]{1,0:T(8,128)S(1)}, f32[32,128]{1,0:T(8,128)S(1)}, u32[]{:S(2)}, u32[]{:S(2)}) collective-permute-start(f32[32,128]{1,0:T(8,128)S(1)} %get-tuple-element.77), channel_id=1, source_target_pairs={{0,1},{1,2},{2,3},{4,5},{5,6},{6,7},{8,9},{9,10},{10,11},{12,13},{... | collective-permute-start | bytes 49160 | tf_op jit(solution)/shard_map/ppermute | solution.py:23
  75.4 5.5 %collective-permute-start.16 = (f32[32,128]{1,0:T(8,128)S(1)}, f32[32,128]{1,0:T(8,128)S(1)}, u32[]{:S(2)}, u32[]{:S(2)}) collective-permute-start(f32[32,128]{1,0:T(8,128)S(1)} %get-tuple-element.77), channel_id=1, source_target_pairs={{1,0},{2,1},{3,2},{5,4},{6,5},{7,6},{9,8},{10,9},{11,10},{13,12},{... | collective-permute-start | bytes 49160 | tf_op jit(solution)/shard_map/ppermute | solution.py:23
  86.6 9.6 %collective-permute-start.17 = (f32[128,512]{1,0:T(8,128)S(1)}, f32[128,512]{1,0:T(8,128)S(1)}, u32[]{:S(2)}, u32[]{:S(2)}) collective-permute-start(f32[128,512]{1,0:T(8,128)S(1)} %get-tuple-element.80), channel_id=1, source_target_pairs={{0,12},{4,8},{8,4},{12,0},{1,13},{5,9},{9,5},{13,1},{2,14},{6,10},... | collective-permute-start | bytes 786440 | tf_op jit(solution)/shard_map/ppermute | solution.py:563
  90.0 21.7 %collective-permute-start.18 = (f32[128,512]{1,0:T(8,128)S(1)}, f32[128,512]{1,0:T(8,128)S(1)}, u32[]{:S(2)}, u32[]{:S(2)}) collective-permute-start(f32[128,512]{1,0:T(8,128)S(1)} %get-tuple-element.81), channel_id=1, source_target_pairs={{0,8},{4,12},{8,0},{12,4},{1,9},{5,13},{9,1},{13,5},{2,10},{6,14},... | collective-permute-start | bytes 786440 | tf_op jit(solution)/shard_map/ppermute | solution.py:563
  91.8 19.9 %collective-permute-start.19 = (f32[128,512]{1,0:T(8,128)S(1)}, f32[128,512]{1,0:T(8,128)S(1)}, u32[]{:S(2)}, u32[]{:S(2)}) collective-permute-start(f32[128,512]{1,0:T(8,128)S(1)} %get-tuple-element.82), channel_id=1, source_target_pairs={{0,4},{4,0},{8,12},{12,8},{1,5},{5,1},{9,13},{13,9},{2,6},{6,2},{1... | collective-permute-start | bytes 786440 | tf_op jit(solution)/shard_map/ppermute | solution.py:563
  (10 other events, 115.1 us)

commit v10 on v9

--- a/solution.py
+++ b/solution.py
@@ -159,6 +159,17 @@
     return (ranks - q) % ranks
 
 
+def paired(value, first):
+    low = range(first, lax.axis_size("space") - 1, 2)
+    return lax.ppermute(value, "space", [(i, i + 1) for i in low] + [(i + 1, i) for i in low])
+
+
+def by_side(even_ref, odd_ref):
+    upward = lax.rem(lax.axis_index("space"), 2) == 0
+    even, odd = even_ref[...], odd_ref[...]
+    return jnp.where(upward, odd, even), jnp.where(upward, even, odd)
+
+
 def split(value):
     high = value.astype(jnp.bfloat16)
     return high, (value - high.astype(jnp.float32)).astype(jnp.bfloat16)
@@ -209,7 +220,8 @@
     copies.clear()
     if layer:
         lane_at = lax.broadcasted_iota(jnp.int32, (rows, LANES), 1)
-        sides = jnp.where(lane_at < planes, high_ref[...], low_ref[...])
+        low_side, high_side = by_side(low_ref, high_ref)
+        sides = jnp.where(lane_at < planes, high_side, low_side)
         for group, row, lane in band_spots(rows, cols):
             row += held * rows + block
             for q in order:
@@ -436,7 +448,8 @@
             for index in range(held):
                 sides.append((side, (held + index) * NZ, side, index * NZ))
     else:
-        low_side, high_side, rim_at = low_ref[...], high_ref[...], 2 * components
+        low_side, high_side = by_side(low_ref, high_ref)
+        rim_at = 2 * components
         sides = [(low_side, components + at, high_side, at) for at in range(components)]
     down_plus = from_lower_row(weight_plus[0])
     down_minus = from_lower_row(weight_minus[0])
@@ -569,7 +582,7 @@
     arrived = [send_all(messages)]
     if layers > 1:
         edges = plane_edges(concentration, face_rate, face_flag, messages[:1])
-        sides = (shifted(edges, "space", 1), shifted(edges, "space", -1))
+        sides = (paired(edges, 0), paired(edges, 1))
     for layer in range(1, layers):
         messages = pack(concentration, stiff_mask, layer, ranks, sides)
         messages, arrived[-1] = lax.optimization_barrier((messages, arrived[-1]))
@@ -587,7 +600,7 @@
             if rims is None:
                 low, high = sides
             else:
-                low, high = shifted(rims, "space", 1), shifted(rims, "space", -1)
+                low, high = paired(rims, 0), paired(rims, 1)
             values, stiff, rims = layer_step(
                 values, stiff, low, high, shared, layer, step < STEPS - 1
             )

time: 114 us -> 105 us (0.921)
  waiting for transfers between devices: 39 us -> 31.2 us
  starting transfers between devices: 38.6 us -> 37 us
    ppermute x8, waiting for transfers between devices: 10.2 us -> 4.81 us  [paired(): lax.ppermute(value, 'space', [(i, i + 1) for i in low] + [(i + 1, i) for...]
    ppermute x12, waiting for transfers between devices: 28.7 us -> 26.3 us  [send(): lax.ppermute(value, 'comp', [(i, i ^ by) for i in range(ranks)])]
  transfers between devices with their start and end apart: 20 -> 20, of which waited for: 7 -> 7; matrix products, arithmetic and copies ran while one was open for 2% -> 2% of each run, Pallas kernels for 24% -> 26%
where the time goes in v10:
time: 105 us; the launch traced here: 104 us
  starting transfers between devices  37 us (35%)
  waiting for transfers between devices  31.2 us (30%)
  Pallas kernels  29.5 us (28%)
  local copies, waits for them, and re-layouts  5.56 us (5%)
    ppermute x12, waiting for transfers between devices, send(): lax.ppermute(value, 'comp', [(i, i ^ by) for i in range(ranks)])  26.3 us
    pallas_call x4, Pallas kernels, layer_step(): pl.pallas_call(functools.partial(step_kernel, pieces, layer, stiff is Non...  23.7 us
    ppermute x8, starting transfers between devices, paired(): lax.ppermute(value, 'space', [(i, i + 1) for i in low] + [(i + 1, i) for...  21.9 us
    ppermute x12, starting transfers between devices, send(): lax.ppermute(value, 'comp', [(i, i ^ by) for i in range(ranks)])  15.2 us
    ppermute x8, waiting for transfers between devices, paired(): lax.ppermute(value, 'space', [(i, i + 1) for i in low] + [(i + 1, i) for...  4.81 us
    pallas_call x2, Pallas kernels, pack(): pl.pallas_call(functools.partial(pack_kernel, layer), out_shape=[jax.Shap...  4.4 us
    unnamed x28, local copies, waits for them, and re-layouts  3.24 us
  transfers between devices with their start and end apart: 20, of which 7 were waited for; matrix products, arithmetic and copies ran while one was open for 2% of the time, Pallas kernels for 26%

profile of v10, /device:TPU:1, one launch (start us, length us, event | category | flops | bytes accessed | tf_op | source)
XLA Modules:
  0.0 103.6 jit_solution(14071356383733264513)
XLA Ops:
  0.0 2.4 %pack.2 = (f32[136,512]{1,0:T(8,128)}, f32[136,512]{1,0:T(8,128)}, f32[136,512]{1,0:T(8,128)}, f32[136,512]{1,0:T(8,128)}) custom-call(f32[32,32,512]{2,1,0:T(8,128)} %plane_ref.3, s32[8,8,512]{2,1,0:T(8,128)} %mask_ref.3), custom_call_target="tpu_custom_call" | custom-call | tf_op jit(solution)/shard_map/pack/pallas_call | solution.py:245
  2.4 4.2 %collective-permute-start.2 = (f32[136,512]{1,0:T(8,128)}, f32[136,512]{1,0:T(8,128)S(1)}, u32[]{:S(2)}, u32[]{:S(2)}) collective-permute-start(f32[136,512]{1,0:T(8,128)} %get-tuple-element.49), channel_id=1, source_target_pairs={{0,12},{4,8},{8,4},{12,0},{1,13},{5,9},{9,5},{13,1},{2,14},{6,10},... | collective-permute-start | bytes 835592 | tf_op jit(solution)/shard_map/ppermute | solution.py:576
  9.3 1.3 %collective-permute-start = (f32[32,128]{1,0:T(8,128)S(1)}, f32[32,128]{1,0:T(8,128)S(1)}, u32[]{:S(2)}, u32[]{:S(2)}) collective-permute-start(f32[32,128]{1,0:T(8,128)S(1)} %plane_edges.1), channel_id=1, source_target_pairs={{0,1},{2,3},{1,0},{3,2},{4,5},{6,7},{5,4},{7,6},{8,9},{10,11},{9,8... | collective-permute-start | bytes 49160 | tf_op jit(solution)/shard_map/ppermute | solution.py:164
  10.6 3.2 %collective-permute-start.1 = (f32[32,128]{1,0:T(8,128)S(1)}, f32[32,128]{1,0:T(8,128)S(1)}, u32[]{:S(2)}, u32[]{:S(2)}) collective-permute-start(f32[32,128]{1,0:T(8,128)S(1)} %plane_edges.1), channel_id=1, source_target_pairs={{1,2},{2,1},{5,6},{6,5},{9,10},{10,9},{13,14},{14,13},{17,18},{18,... | collective-permute-start | bytes 49160 | tf_op jit(solution)/shard_map/ppermute | solution.py:164
  13.8 2.2 %collective-permute-done.1.refs_1_.refs_5_ = f32[32,128]{1,0:T(8,128)S(1)} collective-permute-done((f32[32,128]{1,0:T(8,128)S(1)}, f32[32,128]{1,0:T(8,128)S(1)}, u32[]{:S(2)}, u32[]{:S(2)}) %collective-permute-start.1) | collective-permute-done | bytes 16416 | tf_op jit(solution)/shard_map/ppermute | solution.py:164
  15.9 2.0 %pack.3 = (f32[144,512]{1,0:T(8,128)S(1)}, f32[144,512]{1,0:T(8,128)S(1)}, f32[144,512]{1,0:T(8,128)S(1)}, f32[144,512]{1,0:T(8,128)S(1)}) custom-call(f32[32,32,512]{2,1,0:T(8,128)S(1)} %copy-done, s32[8,8,512]{2,1,0:T(8,128)S(1)} %copy-done.6, f32[32,128]{1,0:T(8,128)S(1)} %collective-permute-done.refs_0_.refs_4_, ...), custom_call_target="tpu_custom_call" | custom-call | tf_op jit(solution)/shard_map/pack/pallas_call | solution.py:245
  18.0 12.2 %collective-permute-done.3.refs_2_.refs_6_ = f32[136,512]{1,0:T(8,128)S(1)} collective-permute-done((f32[136,512]{1,0:T(8,128)}, f32[136,512]{1,0:T(8,128)S(1)}, u32[]{:S(2)}, u32[]{:S(2)}) %collective-permute-start.3) | collective-permute-done | bytes 278560 | tf_op jit(solution)/shard_map/ppermute | solution.py:576
  30.2 2.0 %collective-permute-start.12 = (f32[144,512]{1,0:T(8,128)S(1)}, f32[144,512]{1,0:T(8,128)S(1)}, u32[]{:S(2)}, u32[]{:S(2)}) collective-permute-start(f32[144,512]{1,0:T(8,128)S(1)} %get-tuple-element.70), channel_id=1, source_target_pairs={{0,12},{4,8},{8,4},{12,0},{1,13},{5,9},{9,5},{13,1},{2,14},{6,10},... | collective-permute-start | bytes 884744 | tf_op jit(solution)/shard_map/ppermute | solution.py:576
  32.4 2.0 %collective-permute-start.5 = (f32[32,128]{1,0:T(8,128)S(1)}, f32[32,128]{1,0:T(8,128)S(1)}, u32[]{:S(2)}, u32[]{:S(2)}) collective-permute-start(f32[32,128]{1,0:T(8,128)S(1)} %edges.1), channel_id=1, source_target_pairs={{0,1},{2,3},{1,0},{3,2},{4,5},{6,7},{5,4},{7,6},{8,9},{10,11},{9,8... | collective-permute-start | bytes 49160 | tf_op jit(solution)/shard_map/ppermute | solution.py:164
  34.4 3.0 %collective-permute-start.6 = (f32[32,128]{1,0:T(8,128)S(1)}, f32[32,128]{1,0:T(8,128)S(1)}, u32[]{:S(2)}, u32[]{:S(2)}) collective-permute-start(f32[32,128]{1,0:T(8,128)S(1)} %edges.1), channel_id=1, source_target_pairs={{1,2},{2,1},{5,6},{6,5},{9,10},{10,9},{13,14},{14,13},{17,18},{18,... | collective-permute-start | bytes 49160 | tf_op jit(solution)/shard_map/ppermute | solution.py:164
  37.5 1.2 %collective-permute-start.14 = (f32[144,512]{1,0:T(8,128)S(1)}, f32[144,512]{1,0:T(8,128)S(1)}, u32[]{:S(2)}, u32[]{:S(2)}) collective-permute-start(f32[144,512]{1,0:T(8,128)S(1)} %get-tuple-element.72), channel_id=1, source_target_pairs={{0,4},{4,0},{8,12},{12,8},{1,5},{5,1},{9,13},{13,9},{2,6},{6,2},{1... | collective-permute-start | bytes 884744 | tf_op jit(solution)/shard_map/ppermute | solution.py:576
  39.8 5.7 %layer_step.4 = (f32[128,512]{1,0:T(8,128)S(1)}, f32[128,512]{1,0:T(8,128)S(1)}, f32[128,512]{1,0:T(8,128)S(1)}, f32[128,512]{1,0:T(8,128)S(1)}, f32[32,128]{1,0:T(8,128)S(1)}, /*index=5*/f32[32,512]{1,0:T(8,128)S(1)}) custom-call(f32[16]{0:T(128)S(1)} %copy-done.7, f32[16]{0:T(128)S(1)} %copy-done.8, f32[136,512]{1,0:T(8,128)S(1)} %copy-done.5, ...), custom_call_target="tpu_custom_call" | custom-call | tf_op jit(solution)/shard_map/layer_step/pallas_call | solution.py:542
  45.6 3.1 %collective-permute-start.8 = (f32[32,128]{1,0:T(8,128)S(1)}, f32[32,128]{1,0:T(8,128)S(1)}, u32[]{:S(2)}, u32[]{:S(2)}) collective-permute-start(f32[32,128]{1,0:T(8,128)S(1)} %get-tuple-element.64), channel_id=1, source_target_pairs={{1,2},{2,1},{5,6},{6,5},{9,10},{10,9},{13,14},{14,13},{17,18},{18,... | collective-permute-start | bytes 49160 | tf_op jit(solution)/shard_map/ppermute | solution.py:164
  48.7 1.9 %collective-permute-done.8.refs_5_ = f32[32,128]{1,0:T(8,128)S(1)} collective-permute-done((f32[32,128]{1,0:T(8,128)S(1)}, f32[32,128]{1,0:T(8,128)S(1)}, u32[]{:S(2)}, u32[]{:S(2)}) %collective-permute-start.8) | collective-permute-done | bytes 16416 | tf_op jit(solution)/shard_map/ppermute | solution.py:164
  50.6 6.5 %layer_step.5 = (f32[128,512]{1,0:T(8,128)S(1)}, f32[128,512]{1,0:T(8,128)}, f32[128,512]{1,0:T(8,128)S(1)}, f32[128,512]{1,0:T(8,128)S(1)}) custom-call(f32[16]{0:T(128)S(1)} %copy-done.7, f32[16]{0:T(128)S(1)} %copy-done.8, f32[128,512]{1,0:T(8,128)S(1)} %get-tuple-element.60.refs_0_, f32[128,512]{1,0:T(8,128)S(1)} %get-tuple-element.61.refs_1_, ...), custom_call_target="tpu_custom_call" | custom-call | tf_op jit(solution)/shard_map/layer_step/pallas_call | solution.py:542
  57.1 2.2 %collective-permute-start.9 = (f32[128,512]{1,0:T(8,128)}, f32[128,512]{1,0:T(8,128)}, u32[]{:S(2)}, u32[]{:S(2)}) collective-permute-start(f32[128,512]{1,0:T(8,128)} %get-tuple-element.67), channel_id=1, source_target_pairs={{0,12},{4,8},{8,4},{12,0},{1,13},{5,9},{9,5},{13,1},{2,14},{6,10},... | collective-permute-start | bytes 786440 | tf_op jit(solution)/shard_map/ppermute | solution.py:576
  59.3 1.4 %collective-permute-start.11 = (f32[128,512]{1,0:T(8,128)S(1)}, f32[128,512]{1,0:T(8,128)S(1)}, u32[]{:S(2)}, u32[]{:S(2)}) collective-permute-start(f32[128,512]{1,0:T(8,128)S(1)} %get-tuple-element.69), channel_id=1, source_target_pairs={{0,4},{4,0},{8,12},{12,8},{1,5},{5,1},{9,13},{13,9},{2,6},{6,2},{1... | collective-permute-start | bytes 786440 | tf_op jit(solution)/shard_map/ppermute | solution.py:576
  61.0 5.7 %layer_step.6 = (f32[128,512]{1,0:T(8,128)S(1)}, f32[128,512]{1,0:T(8,128)S(1)}, f32[128,512]{1,0:T(8,128)S(1)}, f32[128,512]{1,0:T(8,128)S(1)}, f32[32,128]{1,0:T(8,128)S(1)}, /*index=5*/f32[32,512]{1,0:T(8,128)S(1)}) custom-call(f32[16]{0:T(128)S(1)} %copy-done.7, f32[16]{0:T(128)S(1)} %copy-done.8, f32[144,512]{1,0:T(8,128)S(1)} %get-tuple-element.56.refs_10_.refs_0_, ...), custom_call_target="tpu_custom_call" | custom-call | tf_op jit(solution)/shard_map/layer_step/pallas_call | solution.py:542
  66.8 9.1 %collective-permute-start.16 = (f32[32,128]{1,0:T(8,128)S(1)}, f32[32,128]{1,0:T(8,128)S(1)}, u32[]{:S(2)}, u32[]{:S(2)}) collective-permute-start(f32[32,128]{1,0:T(8,128)S(1)} %get-tuple-element.77), channel_id=1, source_target_pairs={{1,2},{2,1},{5,6},{6,5},{9,10},{10,9},{13,14},{14,13},{17,18},{18,... | collective-permute-start | bytes 49160 | tf_op jit(solution)/shard_map/ppermute | solution.py:164
  77.5 5.8 %layer_step.7 = (f32[128,512]{1,0:T(8,128)S(1)}, f32[128,512]{1,0:T(8,128)S(1)}, f32[128,512]{1,0:T(8,128)S(1)}, f32[128,512]{1,0:T(8,128)S(1)}) custom-call(f32[16]{0:T(128)S(1)} %copy-done.7, f32[16]{0:T(128)S(1)} %copy-done.8, f32[128,512]{1,0:T(8,128)S(1)} %get-tuple-element.73.refs_0_, f32[128,512]{1,0:T(8,128)S(1)} %get-tuple-element.74.refs_1_, ...), custom_call_target="tpu_custom_call" | custom-call | tf_op jit(solution)/shard_map/layer_step/pallas_call | solution.py:542
  84.8 3.2 %collective-permute-start.19 = (f32[128,512]{1,0:T(8,128)S(1)}, f32[128,512]{1,0:T(8,128)S(1)}, u32[]{:S(2)}, u32[]{:S(2)}) collective-permute-start(f32[128,512]{1,0:T(8,128)S(1)} %get-tuple-element.82), channel_id=1, source_target_pairs={{0,4},{4,0},{8,12},{12,8},{1,5},{5,1},{9,13},{13,9},{2,6},{6,2},{1... | collective-permute-start | bytes 786440 | tf_op jit(solution)/shard_map/ppermute | solution.py:576
  88.0 4.5 %collective-permute-done.17 = f32[128,512]{1,0:T(8,128)S(1)} collective-permute-done((f32[128,512]{1,0:T(8,128)S(1)}, f32[128,512]{1,0:T(8,128)S(1)}, u32[]{:S(2)}, u32[]{:S(2)}) %collective-permute-start.17) | collective-permute-done | bytes 262176 | tf_op jit(solution)/shard_map/ppermute | solution.py:576
  92.5 9.6 %collective-permute-done.18 = f32[128,512]{1,0:T(8,128)S(1)} collective-permute-done((f32[128,512]{1,0:T(8,128)S(1)}, f32[128,512]{1,0:T(8,128)S(1)}, u32[]{:S(2)}, u32[]{:S(2)}) %collective-permute-start.18) | collective-permute-done | bytes 262176 | tf_op jit(solution)/shard_map/ppermute | solution.py:576
  102.3 1.3 %copy-done.13 = f32[4,8,32,512]{3,2,1,0:T(8,128)} copy-done((f32[4,8,32,512]{3,2,1,0:T(8,128)}, f32[4,8,32,512]{3,2,1,0:T(8,128)S(1)}, u32[]{:S(2)}) %copy-start.13) | copy-done | bytes 2097176
  (62 shorter events, 7.5 us)
Async XLA Ops:
  2.4 15.5 %collective-permute-start.2 = (f32[136,512]{1,0:T(8,128)}, f32[136,512]{1,0:T(8,128)S(1)}, u32[]{:S(2)}, u32[]{:S(2)}) collective-permute-start(f32[136,512]{1,0:T(8,128)} %get-tuple-element.49), channel_id=1, source_target_pairs={{0,12},{4,8},{8,4},{12,0},{1,13},{5,9},{9,5},{13,1},{2,14},{6,10},... | collective-permute-start | bytes 835592 | tf_op jit(solution)/shard_map/ppermute | solution.py:576
  6.7 23.5 %collective-permute-start.3 = (f32[136,512]{1,0:T(8,128)}, f32[136,512]{1,0:T(8,128)S(1)}, u32[]{:S(2)}, u32[]{:S(2)}) collective-permute-start(f32[136,512]{1,0:T(8,128)} %get-tuple-element.50), channel_id=1, source_target_pairs={{0,8},{4,12},{8,0},{12,4},{1,9},{5,13},{9,1},{13,5},{2,10},{6,14},... | collective-permute-start | bytes 835592 | tf_op jit(solution)/shard_map/ppermute | solution.py:576
  6.7 23.5 %collective-permute-start.4 = (f32[136,512]{1,0:T(8,128)}, f32[136,512]{1,0:T(8,128)S(1)}, u32[]{:S(2)}, u32[]{:S(2)}) collective-permute-start(f32[136,512]{1,0:T(8,128)} %get-tuple-element.51), channel_id=1, source_target_pairs={{0,4},{4,0},{8,12},{12,8},{1,5},{5,1},{9,13},{13,9},{2,6},{6,2},{1... | collective-permute-start | bytes 835592 | tf_op jit(solution)/shard_map/ppermute | solution.py:576
  9.2 29.5 %copy-start.9 = (f32[16,16]{1,0:T(8,128)S(1)}, f32[16,16]{1,0:T(8,128)}, u32[]{:S(2)}) copy-start(f32[16,16]{1,0:T(8,128)} %mixing_ref.1) | copy-start | bytes 3076
  9.3 29.5 %copy-start.10 = (f32[16,16]{1,0:T(8,128)S(1)}, f32[16,16]{1,0:T(8,128)}, u32[]{:S(2)}) copy-start(f32[16,16]{1,0:T(8,128)} %inverse_ref.1) | copy-start | bytes 3076
  9.3 29.5 %copy-start.11 = (f32[16]{0:T(128)S(1)}, f32[16]{0:T(128)}, u32[]{:S(2)}) copy-start(f32[16]{0:T(128)} %param.17) | copy-start | bytes 196
  9.3 29.5 %copy-start.12 = (f32[16]{0:T(128)S(1)}, f32[16]{0:T(128)}, u32[]{:S(2)}) copy-start(f32[16]{0:T(128)} %param.18) | copy-start | bytes 196
  9.3 4.5 %collective-permute-start = (f32[32,128]{1,0:T(8,128)S(1)}, f32[32,128]{1,0:T(8,128)S(1)}, u32[]{:S(2)}, u32[]{:S(2)}) collective-permute-start(f32[32,128]{1,0:T(8,128)S(1)} %plane_edges.1), channel_id=1, source_target_pairs={{0,1},{2,3},{1,0},{3,2},{4,5},{6,7},{5,4},{7,6},{8,9},{10,11},{9,8... | collective-permute-start | bytes 49160 | tf_op jit(solution)/shard_map/ppermute | solution.py:164
  10.6 5.3 %collective-permute-start.1 = (f32[32,128]{1,0:T(8,128)S(1)}, f32[32,128]{1,0:T(8,128)S(1)}, u32[]{:S(2)}, u32[]{:S(2)}) collective-permute-start(f32[32,128]{1,0:T(8,128)S(1)} %plane_edges.1), channel_id=1, source_target_pairs={{1,2},{2,1},{5,6},{6,5},{9,10},{10,9},{13,14},{14,13},{17,18},{18,... | collective-permute-start | bytes 49160 | tf_op jit(solution)/shard_map/ppermute | solution.py:164
  30.2 29.1 %collective-permute-start.12 = (f32[144,512]{1,0:T(8,128)S(1)}, f32[144,512]{1,0:T(8,128)S(1)}, u32[]{:S(2)}, u32[]{:S(2)}) collective-permute-start(f32[144,512]{1,0:T(8,128)S(1)} %get-tuple-element.70), channel_id=1, source_target_pairs={{0,12},{4,8},{8,4},{12,0},{1,13},{5,9},{9,5},{13,1},{2,14},{6,10},... | collective-permute-start | bytes 884744 | tf_op jit(solution)/shard_map/ppermute | solution.py:576
  32.4 7.2 %collective-permute-start.5 = (f32[32,128]{1,0:T(8,128)S(1)}, f32[32,128]{1,0:T(8,128)S(1)}, u32[]{:S(2)}, u32[]{:S(2)}) collective-permute-start(f32[32,128]{1,0:T(8,128)S(1)} %edges.1), channel_id=1, source_target_pairs={{0,1},{2,3},{1,0},{3,2},{4,5},{6,7},{5,4},{7,6},{8,9},{10,11},{9,8... | collective-permute-start | bytes 49160 | tf_op jit(solution)/shard_map/ppermute | solution.py:164
  34.4 5.3 %collective-permute-start.6 = (f32[32,128]{1,0:T(8,128)S(1)}, f32[32,128]{1,0:T(8,128)S(1)}, u32[]{:S(2)}, u32[]{:S(2)}) collective-permute-start(f32[32,128]{1,0:T(8,128)S(1)} %edges.1), channel_id=1, source_target_pairs={{1,2},{2,1},{5,6},{6,5},{9,10},{10,9},{13,14},{14,13},{17,18},{18,... | collective-permute-start | bytes 49160 | tf_op jit(solution)/shard_map/ppermute | solution.py:164
  37.4 23.5 %collective-permute-start.13 = (f32[144,512]{1,0:T(8,128)S(1)}, f32[144,512]{1,0:T(8,128)S(1)}, u32[]{:S(2)}, u32[]{:S(2)}) collective-permute-start(f32[144,512]{1,0:T(8,128)S(1)} %get-tuple-element.71), channel_id=1, source_target_pairs={{0,8},{4,12},{8,0},{12,4},{1,9},{5,13},{9,1},{13,5},{2,10},{6,14},... | collective-permute-start | bytes 884744 | tf_op jit(solution)/shard_map/ppermute | solution.py:576
  37.5 23.5 %collective-permute-start.14 = (f32[144,512]{1,0:T(8,128)S(1)}, f32[144,512]{1,0:T(8,128)S(1)}, u32[]{:S(2)}, u32[]{:S(2)}) collective-permute-start(f32[144,512]{1,0:T(8,128)S(1)} %get-tuple-element.72), channel_id=1, source_target_pairs={{0,4},{4,0},{8,12},{12,8},{1,5},{5,1},{9,13},{13,9},{2,6},{6,2},{1... | collective-permute-start | bytes 884744 | tf_op jit(solution)/shard_map/ppermute | solution.py:576
  45.5 3.2 %collective-permute-start.7 = (f32[32,128]{1,0:T(8,128)S(1)}, f32[32,128]{1,0:T(8,128)S(1)}, u32[]{:S(2)}, u32[]{:S(2)}) collective-permute-start(f32[32,128]{1,0:T(8,128)S(1)} %get-tuple-element.64), channel_id=1, source_target_pairs={{0,1},{2,3},{1,0},{3,2},{4,5},{6,7},{5,4},{7,6},{8,9},{10,11},{9,8... | collective-permute-start | bytes 49160 | tf_op jit(solution)/shard_map/ppermute | solution.py:164
  45.6 5.1 %collective-permute-start.8 = (f32[32,128]{1,0:T(8,128)S(1)}, f32[32,128]{1,0:T(8,128)S(1)}, u32[]{:S(2)}, u32[]{:S(2)}) collective-permute-start(f32[32,128]{1,0:T(8,128)S(1)} %get-tuple-element.64), channel_id=1, source_target_pairs={{1,2},{2,1},{5,6},{6,5},{9,10},{10,9},{13,14},{14,13},{17,18},{18,... | collective-permute-start | bytes 49160 | tf_op jit(solution)/shard_map/ppermute | solution.py:164
  57.1 18.8 %collective-permute-start.9 = (f32[128,512]{1,0:T(8,128)}, f32[128,512]{1,0:T(8,128)}, u32[]{:S(2)}, u32[]{:S(2)}) collective-permute-start(f32[128,512]{1,0:T(8,128)} %get-tuple-element.67), channel_id=1, source_target_pairs={{0,12},{4,8},{8,4},{12,0},{1,13},{5,9},{9,5},{13,1},{2,14},{6,10},... | collective-permute-start | bytes 786440 | tf_op jit(solution)/shard_map/ppermute | solution.py:576
  59.3 24.0 %collective-permute-start.10 = (f32[128,512]{1,0:T(8,128)S(1)}, f32[128,512]{1,0:T(8,128)}, u32[]{:S(2)}, u32[]{:S(2)}) collective-permute-start(f32[128,512]{1,0:T(8,128)S(1)} %get-tuple-element.68), channel_id=1, source_target_pairs={{0,8},{4,12},{8,0},{12,4},{1,9},{5,13},{9,1},{13,5},{2,10},{6,14},... | collective-permute-start | bytes 786440 | tf_op jit(solution)/shard_map/ppermute | solution.py:576
  59.3 25.5 %collective-permute-start.11 = (f32[128,512]{1,0:T(8,128)S(1)}, f32[128,512]{1,0:T(8,128)S(1)}, u32[]{:S(2)}, u32[]{:S(2)}) collective-permute-start(f32[128,512]{1,0:T(8,128)S(1)} %get-tuple-element.69), channel_id=1, source_target_pairs={{0,4},{4,0},{8,12},{12,8},{1,5},{5,1},{9,13},{13,9},{2,6},{6,2},{1... | collective-permute-start | bytes 786440 | tf_op jit(solution)/shard_map/ppermute | solution.py:576
  66.7 10.2 %collective-permute-start.15 = (f32[32,128]{1,0:T(8,128)S(1)}, f32[32,128]{1,0:T(8,128)S(1)}, u32[]{:S(2)}, u32[]{:S(2)}) collective-permute-start(f32[32,128]{1,0:T(8,128)S(1)} %get-tuple-element.77), channel_id=1, source_target_pairs={{0,1},{2,3},{1,0},{3,2},{4,5},{6,7},{5,4},{7,6},{8,9},{10,11},{9,8... | collective-permute-start | bytes 49160 | tf_op jit(solution)/shard_map/ppermute | solution.py:164
  66.8 10.7 %collective-permute-start.16 = (f32[32,128]{1,0:T(8,128)S(1)}, f32[32,128]{1,0:T(8,128)S(1)}, u32[]{:S(2)}, u32[]{:S(2)}) collective-permute-start(f32[32,128]{1,0:T(8,128)S(1)} %get-tuple-element.77), channel_id=1, source_target_pairs={{1,2},{2,1},{5,6},{6,5},{9,10},{10,9},{13,14},{14,13},{17,18},{18,... | collective-permute-start | bytes 49160 | tf_op jit(solution)/shard_map/ppermute | solution.py:164
  83.3 9.3 %collective-permute-start.17 = (f32[128,512]{1,0:T(8,128)S(1)}, f32[128,512]{1,0:T(8,128)S(1)}, u32[]{:S(2)}, u32[]{:S(2)}) collective-permute-start(f32[128,512]{1,0:T(8,128)S(1)} %get-tuple-element.80), channel_id=1, source_target_pairs={{0,12},{4,8},{8,4},{12,0},{1,13},{5,9},{9,5},{13,1},{2,14},{6,10},... | collective-permute-start | bytes 786440 | tf_op jit(solution)/shard_map/ppermute | solution.py:576
  84.3 17.9 %collective-permute-start.18 = (f32[128,512]{1,0:T(8,128)S(1)}, f32[128,512]{1,0:T(8,128)S(1)}, u32[]{:S(2)}, u32[]{:S(2)}) collective-permute-start(f32[128,512]{1,0:T(8,128)S(1)} %get-tuple-element.81), channel_id=1, source_target_pairs={{0,8},{4,12},{8,0},{12,4},{1,9},{5,13},{9,1},{13,5},{2,10},{6,14},... | collective-permute-start | bytes 786440 | tf_op jit(solution)/shard_map/ppermute | solution.py:576
  84.8 17.4 %collective-permute-start.19 = (f32[128,512]{1,0:T(8,128)S(1)}, f32[128,512]{1,0:T(8,128)S(1)}, u32[]{:S(2)}, u32[]{:S(2)}) collective-permute-start(f32[128,512]{1,0:T(8,128)S(1)} %get-tuple-element.82), channel_id=1, source_target_pairs={{0,4},{4,0},{8,12},{12,8},{1,5},{5,1},{9,13},{13,9},{2,6},{6,2},{1... | collective-permute-start | bytes 786440 | tf_op jit(solution)/shard_map/ppermute | solution.py:576
  (10 other events, 112.7 us)

commit v11 on v10

--- a/solution.py
+++ b/solution.py
@@ -604,7 +604,7 @@
             values, stiff, rims = layer_step(
                 values, stiff, low, high, shared, layer, step < STEPS - 1
             )
-        for q, piece in enumerate(send_all(values)):
+        for q, piece in reversed(list(enumerate(send_all(values)))):
             result = lax.dynamic_update_slice(
                 result,
                 piece.reshape(held, 1, rows, cols),

time: 105 us -> 104 us (level)
  the two profiles are of different devices: /device:TPU:1 before, /device:TPU:13 now
where the time goes in v11:
time: 104 us
  waiting for transfers between devices  37.7 us (36%)
  starting transfers between devices  30.3 us (29%)
  Pallas kernels  28.8 us (28%)
  local copies, waits for them, and re-layouts  6.5 us (6%)
    ppermute x12, waiting for transfers between devices, send(): lax.ppermute(value, 'comp', [(i, i ^ by) for i in range(ranks)])  32.5 us
    pallas_call x4, Pallas kernels, layer_step(): pl.pallas_call(functools.partial(step_kernel, pieces, layer, stiff is Non...  23.1 us
    ppermute x8, starting transfers between devices, paired(): lax.ppermute(value, 'space', [(i, i + 1) for i in low] + [(i + 1, i) for...  15.8 us
    ppermute x12, starting transfers between devices, send(): lax.ppermute(value, 'comp', [(i, i ^ by) for i in range(ranks)])  14.5 us
    ppermute x8, waiting for transfers between devices, paired(): lax.ppermute(value, 'space', [(i, i + 1) for i in low] + [(i + 1, i) for...  5.27 us
    pallas_call x2, Pallas kernels, pack(): pl.pallas_call(functools.partial(pack_kernel, layer), out_shape=[jax.Shap...  4.4 us
    unnamed x28, local copies, waits for them, and re-layouts  3.24 us
    dynamic_update_slice x8, local copies, waits for them, and re-layouts, by_layers(): lax.dynamic_update_slice(result, piece.reshape(held, 1, rows, cols), (0,...  3.02 us
  transfers between devices with their start and end apart: 20, of which 8 were waited for; matrix products, arithmetic and copies ran while one was open for 3% of the time, Pallas kernels for 25%

profile of v11, /device:TPU:13, one launch (start us, length us, event | category | flops | bytes accessed | tf_op | source)
XLA Modules:
  0.0 103.7 jit_solution(13025576424091352019)
XLA Ops:
  0.0 2.4 %pack.2 = (f32[136,512]{1,0:T(8,128)}, f32[136,512]{1,0:T(8,128)}, f32[136,512]{1,0:T(8,128)}, f32[136,512]{1,0:T(8,128)}) custom-call(f32[32,32,512]{2,1,0:T(8,128)} %plane_ref.3, s32[8,8,512]{2,1,0:T(8,128)} %mask_ref.3), custom_call_target="tpu_custom_call" | custom-call | tf_op jit(solution)/shard_map/pack/pallas_call | solution.py:245
  2.4 1.4 %collective-permute-start.2 = (f32[136,512]{1,0:T(8,128)}, f32[136,512]{1,0:T(8,128)S(1)}, u32[]{:S(2)}, u32[]{:S(2)}) collective-permute-start(f32[136,512]{1,0:T(8,128)} %get-tuple-element.49), channel_id=1, source_target_pairs={{0,12},{4,8},{8,4},{12,0},{1,13},{5,9},{9,5},{13,1},{2,14},{6,10},... | collective-permute-start | bytes 835592 | tf_op jit(solution)/shard_map/ppermute | solution.py:576
  8.3 1.3 %collective-permute-start = (f32[32,128]{1,0:T(8,128)S(1)}, f32[32,128]{1,0:T(8,128)S(1)}, u32[]{:S(2)}, u32[]{:S(2)}) collective-permute-start(f32[32,128]{1,0:T(8,128)S(1)} %plane_edges.1), channel_id=1, source_target_pairs={{0,1},{2,3},{1,0},{3,2},{4,5},{6,7},{5,4},{7,6},{8,9},{10,11},{9,8... | collective-permute-start | bytes 49160 | tf_op jit(solution)/shard_map/ppermute | solution.py:164
  9.6 3.0 %collective-permute-start.1 = (f32[32,128]{1,0:T(8,128)S(1)}, f32[32,128]{1,0:T(8,128)S(1)}, u32[]{:S(2)}, u32[]{:S(2)}) collective-permute-start(f32[32,128]{1,0:T(8,128)S(1)} %plane_edges.1), channel_id=1, source_target_pairs={{1,2},{2,1},{5,6},{6,5},{9,10},{10,9},{13,14},{14,13},{17,18},{18,... | collective-permute-start | bytes 49160 | tf_op jit(solution)/shard_map/ppermute | solution.py:164
  12.6 2.3 %collective-permute-done.1.refs_1_.refs_5_ = f32[32,128]{1,0:T(8,128)S(1)} collective-permute-done((f32[32,128]{1,0:T(8,128)S(1)}, f32[32,128]{1,0:T(8,128)S(1)}, u32[]{:S(2)}, u32[]{:S(2)}) %collective-permute-start.1) | collective-permute-done | bytes 16416 | tf_op jit(solution)/shard_map/ppermute | solution.py:164
  14.9 2.0 %pack.3 = (f32[144,512]{1,0:T(8,128)S(1)}, f32[144,512]{1,0:T(8,128)S(1)}, f32[144,512]{1,0:T(8,128)S(1)}, f32[144,512]{1,0:T(8,128)S(1)}) custom-call(f32[32,32,512]{2,1,0:T(8,128)S(1)} %copy-done, s32[8,8,512]{2,1,0:T(8,128)S(1)} %copy-done.6, f32[32,128]{1,0:T(8,128)S(1)} %collective-permute-done.refs_0_.refs_4_, ...), custom_call_target="tpu_custom_call" | custom-call | tf_op jit(solution)/shard_map/pack/pallas_call | solution.py:245
  16.9 5.4 %collective-permute-done.2.refs_1_.refs_5_ = f32[136,512]{1,0:T(8,128)S(1)} collective-permute-done((f32[136,512]{1,0:T(8,128)}, f32[136,512]{1,0:T(8,128)S(1)}, u32[]{:S(2)}, u32[]{:S(2)}) %collective-permute-start.2) | collective-permute-done | bytes 278560 | tf_op jit(solution)/shard_map/ppermute | solution.py:576
  22.4 5.0 %collective-permute-done.3.refs_2_.refs_6_ = f32[136,512]{1,0:T(8,128)S(1)} collective-permute-done((f32[136,512]{1,0:T(8,128)}, f32[136,512]{1,0:T(8,128)S(1)}, u32[]{:S(2)}, u32[]{:S(2)}) %collective-permute-start.3) | collective-permute-done | bytes 278560 | tf_op jit(solution)/shard_map/ppermute | solution.py:576
  27.9 1.7 %collective-permute-start.5 = (f32[32,128]{1,0:T(8,128)S(1)}, f32[32,128]{1,0:T(8,128)S(1)}, u32[]{:S(2)}, u32[]{:S(2)}) collective-permute-start(f32[32,128]{1,0:T(8,128)S(1)} %edges.1), channel_id=1, source_target_pairs={{0,1},{2,3},{1,0},{3,2},{4,5},{6,7},{5,4},{7,6},{8,9},{10,11},{9,8... | collective-permute-start | bytes 49160 | tf_op jit(solution)/shard_map/ppermute | solution.py:164
  29.6 3.0 %collective-permute-start.6 = (f32[32,128]{1,0:T(8,128)S(1)}, f32[32,128]{1,0:T(8,128)S(1)}, u32[]{:S(2)}, u32[]{:S(2)}) collective-permute-start(f32[32,128]{1,0:T(8,128)S(1)} %edges.1), channel_id=1, source_target_pairs={{1,2},{2,1},{5,6},{6,5},{9,10},{10,9},{13,14},{14,13},{17,18},{18,... | collective-permute-start | bytes 49160 | tf_op jit(solution)/shard_map/ppermute | solution.py:164
  32.7 4.0 %collective-permute-start.13 = (f32[144,512]{1,0:T(8,128)S(1)}, f32[144,512]{1,0:T(8,128)S(1)}, u32[]{:S(2)}, u32[]{:S(2)}) collective-permute-start(f32[144,512]{1,0:T(8,128)S(1)} %get-tuple-element.71), channel_id=1, source_target_pairs={{0,8},{4,12},{8,0},{12,4},{1,9},{5,13},{9,1},{13,5},{2,10},{6,14},... | collective-permute-start | bytes 884744 | tf_op jit(solution)/shard_map/ppermute | solution.py:576
  37.8 5.7 %layer_step.4 = (f32[128,512]{1,0:T(8,128)S(1)}, f32[128,512]{1,0:T(8,128)S(1)}, f32[128,512]{1,0:T(8,128)S(1)}, f32[128,512]{1,0:T(8,128)S(1)}, f32[32,128]{1,0:T(8,128)S(1)}, /*index=5*/f32[32,512]{1,0:T(8,128)S(1)}) custom-call(f32[16]{0:T(128)S(1)} %copy-done.7, f32[16]{0:T(128)S(1)} %copy-done.8, f32[136,512]{1,0:T(8,128)S(1)} %copy-done.5, ...), custom_call_target="tpu_custom_call" | custom-call | tf_op jit(solution)/shard_map/layer_step/pallas_call | solution.py:542
  43.6 3.0 %collective-permute-start.8 = (f32[32,128]{1,0:T(8,128)S(1)}, f32[32,128]{1,0:T(8,128)S(1)}, u32[]{:S(2)}, u32[]{:S(2)}) collective-permute-start(f32[32,128]{1,0:T(8,128)S(1)} %get-tuple-element.64), channel_id=1, source_target_pairs={{1,2},{2,1},{5,6},{6,5},{9,10},{10,9},{13,14},{14,13},{17,18},{18,... | collective-permute-start | bytes 49160 | tf_op jit(solution)/shard_map/ppermute | solution.py:164
  46.6 2.3 %collective-permute-done.8.refs_5_ = f32[32,128]{1,0:T(8,128)S(1)} collective-permute-done((f32[32,128]{1,0:T(8,128)S(1)}, f32[32,128]{1,0:T(8,128)S(1)}, u32[]{:S(2)}, u32[]{:S(2)}) %collective-permute-start.8) | collective-permute-done | bytes 16416 | tf_op jit(solution)/shard_map/ppermute | solution.py:164
  49.0 5.8 %layer_step.5 = (f32[128,512]{1,0:T(8,128)S(1)}, f32[128,512]{1,0:T(8,128)S(1)}, f32[128,512]{1,0:T(8,128)S(1)}, f32[128,512]{1,0:T(8,128)S(1)}) custom-call(f32[16]{0:T(128)S(1)} %copy-done.7, f32[16]{0:T(128)S(1)} %copy-done.8, f32[128,512]{1,0:T(8,128)S(1)} %get-tuple-element.60.refs_0_, f32[128,512]{1,0:T(8,128)S(1)} %get-tuple-element.61.refs_1_, ...), custom_call_target="tpu_custom_call" | custom-call | tf_op jit(solution)/shard_map/layer_step/pallas_call | solution.py:542
  55.9 1.3 %collective-permute-start.10 = (f32[128,512]{1,0:T(8,128)S(1)}, f32[128,512]{1,0:T(8,128)}, u32[]{:S(2)}, u32[]{:S(2)}) collective-permute-start(f32[128,512]{1,0:T(8,128)S(1)} %get-tuple-element.67), channel_id=1, source_target_pairs={{0,8},{4,12},{8,0},{12,4},{1,9},{5,13},{9,1},{13,5},{2,10},{6,14},... | collective-permute-start | bytes 786440 | tf_op jit(solution)/shard_map/ppermute | solution.py:576
  57.5 5.7 %layer_step.6 = (f32[128,512]{1,0:T(8,128)S(1)}, f32[128,512]{1,0:T(8,128)S(1)}, f32[128,512]{1,0:T(8,128)S(1)}, f32[128,512]{1,0:T(8,128)S(1)}, f32[32,128]{1,0:T(8,128)S(1)}, /*index=5*/f32[32,512]{1,0:T(8,128)S(1)}) custom-call(f32[16]{0:T(128)S(1)} %copy-done.7, f32[16]{0:T(128)S(1)} %copy-done.8, f32[144,512]{1,0:T(8,128)S(1)} %get-tuple-element.56.refs_10_.refs_0_, ...), custom_call_target="tpu_custom_call" | custom-call | tf_op jit(solution)/shard_map/layer_step/pallas_call | solution.py:542
  63.3 3.6 %collective-permute-start.16 = (f32[32,128]{1,0:T(8,128)S(1)}, f32[32,128]{1,0:T(8,128)S(1)}, u32[]{:S(2)}, u32[]{:S(2)}) collective-permute-start(f32[32,128]{1,0:T(8,128)S(1)} %get-tuple-element.77), channel_id=1, source_target_pairs={{1,2},{2,1},{5,6},{6,5},{9,10},{10,9},{13,14},{14,13},{17,18},{18,... | collective-permute-start | bytes 49160 | tf_op jit(solution)/shard_map/ppermute | solution.py:164
  68.8 5.8 %layer_step.7 = (f32[128,512]{1,0:T(8,128)S(1)}, f32[128,512]{1,0:T(8,128)S(1)}, f32[128,512]{1,0:T(8,128)S(1)}, f32[128,512]{1,0:T(8,128)S(1)}) custom-call(f32[16]{0:T(128)S(1)} %copy-done.7, f32[16]{0:T(128)S(1)} %copy-done.8, f32[128,512]{1,0:T(8,128)S(1)} %get-tuple-element.73.refs_0_, f32[128,512]{1,0:T(8,128)S(1)} %get-tuple-element.74.refs_1_, ...), custom_call_target="tpu_custom_call" | custom-call | tf_op jit(solution)/shard_map/layer_step/pallas_call | solution.py:542
  74.6 1.8 %collective-permute-start.17 = (f32[128,512]{1,0:T(8,128)S(1)}, f32[128,512]{1,0:T(8,128)S(1)}, u32[]{:S(2)}, u32[]{:S(2)}) collective-permute-start(f32[128,512]{1,0:T(8,128)S(1)} %get-tuple-element.79), channel_id=1, source_target_pairs={{0,4},{4,0},{8,12},{12,8},{1,5},{5,1},{9,13},{13,9},{2,6},{6,2},{1... | collective-permute-start | bytes 786440 | tf_op jit(solution)/shard_map/ppermute | solution.py:576
  80.2 4.2 %collective-permute-done.17 = f32[128,512]{1,0:T(8,128)S(1)} collective-permute-done((f32[128,512]{1,0:T(8,128)S(1)}, f32[128,512]{1,0:T(8,128)S(1)}, u32[]{:S(2)}, u32[]{:S(2)}) %collective-permute-start.17) | collective-permute-done | bytes 262176 | tf_op jit(solution)/shard_map/ppermute | solution.py:576
  84.4 11.5 %collective-permute-done.18 = f32[128,512]{1,0:T(8,128)S(1)} collective-permute-done((f32[128,512]{1,0:T(8,128)S(1)}, f32[128,512]{1,0:T(8,128)S(1)}, u32[]{:S(2)}, u32[]{:S(2)}) %collective-permute-start.18) | collective-permute-done | bytes 262176 | tf_op jit(solution)/shard_map/ppermute | solution.py:576
  96.0 6.3 %collective-permute-done.19 = f32[128,512]{1,0:T(8,128)S(1)} collective-permute-done((f32[128,512]{1,0:T(8,128)S(1)}, f32[128,512]{1,0:T(8,128)S(1)}, u32[]{:S(2)}, u32[]{:S(2)}) %collective-permute-start.19) | collective-permute-done | bytes 262176 | tf_op jit(solution)/shard_map/ppermute | solution.py:576
  102.4 1.3 %copy-done.13 = f32[4,8,32,512]{3,2,1,0:T(8,128)} copy-done((f32[4,8,32,512]{3,2,1,0:T(8,128)}, f32[4,8,32,512]{3,2,1,0:T(8,128)S(1)}, u32[]{:S(2)}) %copy-start.13) | copy-done | bytes 2097176
  (62 shorter events, 13.4 us)
Async XLA Ops:
  2.4 19.9 %collective-permute-start.2 = (f32[136,512]{1,0:T(8,128)}, f32[136,512]{1,0:T(8,128)S(1)}, u32[]{:S(2)}, u32[]{:S(2)}) collective-permute-start(f32[136,512]{1,0:T(8,128)} %get-tuple-element.49), channel_id=1, source_target_pairs={{0,12},{4,8},{8,4},{12,0},{1,13},{5,9},{9,5},{13,1},{2,14},{6,10},... | collective-permute-start | bytes 835592 | tf_op jit(solution)/shard_map/ppermute | solution.py:576
  3.8 23.5 %collective-permute-start.3 = (f32[136,512]{1,0:T(8,128)}, f32[136,512]{1,0:T(8,128)S(1)}, u32[]{:S(2)}, u32[]{:S(2)}) collective-permute-start(f32[136,512]{1,0:T(8,128)} %get-tuple-element.50), channel_id=1, source_target_pairs={{0,8},{4,12},{8,0},{12,4},{1,9},{5,13},{9,1},{13,5},{2,10},{6,14},... | collective-permute-start | bytes 835592 | tf_op jit(solution)/shard_map/ppermute | solution.py:576
  4.9 22.5 %collective-permute-start.4 = (f32[136,512]{1,0:T(8,128)}, f32[136,512]{1,0:T(8,128)S(1)}, u32[]{:S(2)}, u32[]{:S(2)}) collective-permute-start(f32[136,512]{1,0:T(8,128)} %get-tuple-element.51), channel_id=1, source_target_pairs={{0,4},{4,0},{8,12},{12,8},{1,5},{5,1},{9,13},{13,9},{2,6},{6,2},{1... | collective-permute-start | bytes 835592 | tf_op jit(solution)/shard_map/ppermute | solution.py:576
  8.2 28.7 %copy-start.9 = (f32[16,16]{1,0:T(8,128)S(1)}, f32[16,16]{1,0:T(8,128)}, u32[]{:S(2)}) copy-start(f32[16,16]{1,0:T(8,128)} %mixing_ref.1) | copy-start | bytes 3076
  8.2 28.7 %copy-start.10 = (f32[16,16]{1,0:T(8,128)S(1)}, f32[16,16]{1,0:T(8,128)}, u32[]{:S(2)}) copy-start(f32[16,16]{1,0:T(8,128)} %inverse_ref.1) | copy-start | bytes 3076
  8.3 28.7 %copy-start.11 = (f32[16]{0:T(128)S(1)}, f32[16]{0:T(128)}, u32[]{:S(2)}) copy-start(f32[16]{0:T(128)} %param.17) | copy-start | bytes 196
  8.3 28.7 %copy-start.12 = (f32[16]{0:T(128)S(1)}, f32[16]{0:T(128)}, u32[]{:S(2)}) copy-start(f32[16]{0:T(128)} %param.18) | copy-start | bytes 196
  8.3 4.3 %collective-permute-start = (f32[32,128]{1,0:T(8,128)S(1)}, f32[32,128]{1,0:T(8,128)S(1)}, u32[]{:S(2)}, u32[]{:S(2)}) collective-permute-start(f32[32,128]{1,0:T(8,128)S(1)} %plane_edges.1), channel_id=1, source_target_pairs={{0,1},{2,3},{1,0},{3,2},{4,5},{6,7},{5,4},{7,6},{8,9},{10,11},{9,8... | collective-permute-start | bytes 49160 | tf_op jit(solution)/shard_map/ppermute | solution.py:164
  9.6 5.3 %collective-permute-start.1 = (f32[32,128]{1,0:T(8,128)S(1)}, f32[32,128]{1,0:T(8,128)S(1)}, u32[]{:S(2)}, u32[]{:S(2)}) collective-permute-start(f32[32,128]{1,0:T(8,128)S(1)} %plane_edges.1), channel_id=1, source_target_pairs={{1,2},{2,1},{5,6},{6,5},{9,10},{10,9},{13,14},{14,13},{17,18},{18,... | collective-permute-start | bytes 49160 | tf_op jit(solution)/shard_map/ppermute | solution.py:164
  27.4 29.8 %collective-permute-start.12 = (f32[144,512]{1,0:T(8,128)S(1)}, f32[144,512]{1,0:T(8,128)S(1)}, u32[]{:S(2)}, u32[]{:S(2)}) collective-permute-start(f32[144,512]{1,0:T(8,128)S(1)} %get-tuple-element.70), channel_id=1, source_target_pairs={{0,12},{4,8},{8,4},{12,0},{1,13},{5,9},{9,5},{13,1},{2,14},{6,10},... | collective-permute-start | bytes 884744 | tf_op jit(solution)/shard_map/ppermute | solution.py:576
  27.9 9.8 %collective-permute-start.5 = (f32[32,128]{1,0:T(8,128)S(1)}, f32[32,128]{1,0:T(8,128)S(1)}, u32[]{:S(2)}, u32[]{:S(2)}) collective-permute-start(f32[32,128]{1,0:T(8,128)S(1)} %edges.1), channel_id=1, source_target_pairs={{0,1},{2,3},{1,0},{3,2},{4,5},{6,7},{5,4},{7,6},{8,9},{10,11},{9,8... | collective-permute-start | bytes 49160 | tf_op jit(solution)/shard_map/ppermute | solution.py:164
  29.6 8.1 %collective-permute-start.6 = (f32[32,128]{1,0:T(8,128)S(1)}, f32[32,128]{1,0:T(8,128)S(1)}, u32[]{:S(2)}, u32[]{:S(2)}) collective-permute-start(f32[32,128]{1,0:T(8,128)S(1)} %edges.1), channel_id=1, source_target_pairs={{1,2},{2,1},{5,6},{6,5},{9,10},{10,9},{13,14},{14,13},{17,18},{18,... | collective-permute-start | bytes 49160 | tf_op jit(solution)/shard_map/ppermute | solution.py:164
  32.7 24.9 %collective-permute-start.13 = (f32[144,512]{1,0:T(8,128)S(1)}, f32[144,512]{1,0:T(8,128)S(1)}, u32[]{:S(2)}, u32[]{:S(2)}) collective-permute-start(f32[144,512]{1,0:T(8,128)S(1)} %get-tuple-element.71), channel_id=1, source_target_pairs={{0,8},{4,12},{8,0},{12,4},{1,9},{5,13},{9,1},{13,5},{2,10},{6,14},... | collective-permute-start | bytes 884744 | tf_op jit(solution)/shard_map/ppermute | solution.py:576
  36.6 20.9 %collective-permute-start.14 = (f32[144,512]{1,0:T(8,128)S(1)}, f32[144,512]{1,0:T(8,128)S(1)}, u32[]{:S(2)}, u32[]{:S(2)}) collective-permute-start(f32[144,512]{1,0:T(8,128)S(1)} %get-tuple-element.72), channel_id=1, source_target_pairs={{0,4},{4,0},{8,12},{12,8},{1,5},{5,1},{9,13},{13,9},{2,6},{6,2},{1... | collective-permute-start | bytes 884744 | tf_op jit(solution)/shard_map/ppermute | solution.py:576
  43.5 3.1 %collective-permute-start.7 = (f32[32,128]{1,0:T(8,128)S(1)}, f32[32,128]{1,0:T(8,128)S(1)}, u32[]{:S(2)}, u32[]{:S(2)}) collective-permute-start(f32[32,128]{1,0:T(8,128)S(1)} %get-tuple-element.64), channel_id=1, source_target_pairs={{0,1},{2,3},{1,0},{3,2},{4,5},{6,7},{5,4},{7,6},{8,9},{10,11},{9,8... | collective-permute-start | bytes 49160 | tf_op jit(solution)/shard_map/ppermute | solution.py:164
  43.6 5.4 %collective-permute-start.8 = (f32[32,128]{1,0:T(8,128)S(1)}, f32[32,128]{1,0:T(8,128)S(1)}, u32[]{:S(2)}, u32[]{:S(2)}) collective-permute-start(f32[32,128]{1,0:T(8,128)S(1)} %get-tuple-element.64), channel_id=1, source_target_pairs={{1,2},{2,1},{5,6},{6,5},{9,10},{10,9},{13,14},{14,13},{17,18},{18,... | collective-permute-start | bytes 49160 | tf_op jit(solution)/shard_map/ppermute | solution.py:164
  54.8 12.1 %collective-permute-start.9 = (f32[128,512]{1,0:T(8,128)S(1)}, f32[128,512]{1,0:T(8,128)}, u32[]{:S(2)}, u32[]{:S(2)}) collective-permute-start(f32[128,512]{1,0:T(8,128)S(1)} %get-tuple-element.66), channel_id=1, source_target_pairs={{0,4},{4,0},{8,12},{12,8},{1,5},{5,1},{9,13},{13,9},{2,6},{6,2},{1... | collective-permute-start | bytes 786440 | tf_op jit(solution)/shard_map/ppermute | solution.py:576
  55.9 20.6 %collective-permute-start.10 = (f32[128,512]{1,0:T(8,128)S(1)}, f32[128,512]{1,0:T(8,128)}, u32[]{:S(2)}, u32[]{:S(2)}) collective-permute-start(f32[128,512]{1,0:T(8,128)S(1)} %get-tuple-element.67), channel_id=1, source_target_pairs={{0,8},{4,12},{8,0},{12,4},{1,9},{5,13},{9,1},{13,5},{2,10},{6,14},... | collective-permute-start | bytes 786440 | tf_op jit(solution)/shard_map/ppermute | solution.py:576
  57.2 21.4 %collective-permute-start.11 = (f32[128,512]{1,0:T(8,128)S(1)}, f32[128,512]{1,0:T(8,128)}, u32[]{:S(2)}, u32[]{:S(2)}) collective-permute-start(f32[128,512]{1,0:T(8,128)S(1)} %get-tuple-element.68), channel_id=1, source_target_pairs={{0,12},{4,8},{8,4},{12,0},{1,13},{5,9},{9,5},{13,1},{2,14},{6,10},... | collective-permute-start | bytes 786440 | tf_op jit(solution)/shard_map/ppermute | solution.py:576
  63.2 4.9 %collective-permute-start.15 = (f32[32,128]{1,0:T(8,128)S(1)}, f32[32,128]{1,0:T(8,128)S(1)}, u32[]{:S(2)}, u32[]{:S(2)}) collective-permute-start(f32[32,128]{1,0:T(8,128)S(1)} %get-tuple-element.77), channel_id=1, source_target_pairs={{0,1},{2,3},{1,0},{3,2},{4,5},{6,7},{5,4},{7,6},{8,9},{10,11},{9,8... | collective-permute-start | bytes 49160 | tf_op jit(solution)/shard_map/ppermute | solution.py:164
  63.3 5.5 %collective-permute-start.16 = (f32[32,128]{1,0:T(8,128)S(1)}, f32[32,128]{1,0:T(8,128)S(1)}, u32[]{:S(2)}, u32[]{:S(2)}) collective-permute-start(f32[32,128]{1,0:T(8,128)S(1)} %get-tuple-element.77), channel_id=1, source_target_pairs={{1,2},{2,1},{5,6},{6,5},{9,10},{10,9},{13,14},{14,13},{17,18},{18,... | collective-permute-start | bytes 49160 | tf_op jit(solution)/shard_map/ppermute | solution.py:164
  74.6 9.8 %collective-permute-start.17 = (f32[128,512]{1,0:T(8,128)S(1)}, f32[128,512]{1,0:T(8,128)S(1)}, u32[]{:S(2)}, u32[]{:S(2)}) collective-permute-start(f32[128,512]{1,0:T(8,128)S(1)} %get-tuple-element.79), channel_id=1, source_target_pairs={{0,4},{4,0},{8,12},{12,8},{1,5},{5,1},{9,13},{13,9},{2,6},{6,2},{1... | collective-permute-start | bytes 786440 | tf_op jit(solution)/shard_map/ppermute | solution.py:576
  77.4 18.6 %collective-permute-start.18 = (f32[128,512]{1,0:T(8,128)S(1)}, f32[128,512]{1,0:T(8,128)S(1)}, u32[]{:S(2)}, u32[]{:S(2)}) collective-permute-start(f32[128,512]{1,0:T(8,128)S(1)} %get-tuple-element.80), channel_id=1, source_target_pairs={{0,8},{4,12},{8,0},{12,4},{1,9},{5,13},{9,1},{13,5},{2,10},{6,14},... | collective-permute-start | bytes 786440 | tf_op jit(solution)/shard_map/ppermute | solution.py:576
  79.6 22.7 %collective-permute-start.19 = (f32[128,512]{1,0:T(8,128)S(1)}, f32[128,512]{1,0:T(8,128)S(1)}, u32[]{:S(2)}, u32[]{:S(2)}) collective-permute-start(f32[128,512]{1,0:T(8,128)S(1)} %get-tuple-element.81), channel_id=1, source_target_pairs={{0,12},{4,8},{8,4},{12,0},{1,13},{5,9},{9,5},{13,1},{2,14},{6,10},... | collective-permute-start | bytes 786440 | tf_op jit(solution)/shard_map/ppermute | solution.py:576
  (10 other events, 104.4 us)

commit v12 on v11

--- a/solution.py
+++ b/solution.py
@@ -194,28 +194,26 @@
     ]
 
 
-def pack_kernel(layer, plane_ref, mask_ref, *refs):
+def pack_kernel(layer, ranks, order, plane_ref, mask_ref, *refs):
     if layer:
         (low_ref, high_ref), refs = refs[:2], refs[2:]
     out_refs, (part_ref, mask_part, mask_sems, in_sems, out_sems) = refs[:-5], refs[-5:]
-    ranks = len(out_refs)
     planes, rows, cols = plane_ref.shape
     levels, block, _ = mask_ref.shape
     held = planes // levels
     me = lax.axis_index("comp")
     copies = []
-    order = [*range(1, ranks), 0]
 
     def start(source, target, sem):
         copies.append(pltpu.make_async_copy(source, target, sem))
         copies[-1].start()
 
-    for q in order:
+    for place, q in enumerate(order):
         at = jnp.bitwise_xor(me, pair(q, ranks)) * (levels // ranks) + layer
         for index in range(held):
             spot = pl.ds(index * rows, rows)
-            start(plane_ref.at[index * levels + at], part_ref.at[q, spot], in_sems.at[len(copies)])
-        start(mask_ref.at[at], mask_part.at[q], mask_sems.at[q])
+            start(plane_ref.at[index * levels + at], part_ref.at[place, spot], in_sems.at[len(copies)])
+        start(mask_ref.at[at], mask_part.at[place], mask_sems.at[place])
     arrivals = list(copies)
     copies.clear()
     if layer:
@@ -224,35 +222,35 @@
         sides = jnp.where(lane_at < planes, high_side, low_side)
         for group, row, lane in band_spots(rows, cols):
             row += held * rows + block
-            for q in order:
-                part_ref[q, row : row + TILE, lane : lane + LANES] = sides[
+            for place in range(len(order)):
+                part_ref[place, row : row + TILE, lane : lane + LANES] = sides[
                     group * TILE : (group + 1) * TILE
                 ]
-    for position, q in enumerate(order):
-        for copy in arrivals[position * (held + 1) : (position + 1) * (held + 1)]:
+    for place, out_ref in enumerate(out_refs):
+        for copy in arrivals[place * (held + 1) : (place + 1) * (held + 1)]:
             copy.wait()
-        part_ref[q, held * rows : held * rows + block, :] = mask_part[q].astype(jnp.float32)
-        start(part_ref.at[q], out_refs[q], out_sems.at[q])
+        part_ref[place, held * rows : held * rows + block, :] = mask_part[place].astype(jnp.float32)
+        start(part_ref.at[place], out_ref, out_sems.at[place])
     for copy in copies:
         copy.wait()
 
 
-def pack(concentration, stiff_mask, layer, ranks, sides):
+def pack(concentration, stiff_mask, layer, ranks, order, sides):
     planes, rows, cols = concentration.shape
     held = planes // NZ
     block = stiff_mask.shape[1]
     size = held * rows + block + (bands(rows, cols) if layer else 0)
     results = pl.pallas_call(
-        functools.partial(pack_kernel, layer),
-        out_shape=[jax.ShapeDtypeStruct((size, cols), jnp.float32)] * ranks,
+        functools.partial(pack_kernel, layer, ranks, order),
+        out_shape=[jax.ShapeDtypeStruct((size, cols), jnp.float32)] * len(order),
         in_specs=[hbm_spec()] * 2 + [whole_spec()] * len(sides),
-        out_specs=[any_spec()] * ranks,
+        out_specs=[any_spec()] * len(order),
         scratch_shapes=[
-            pltpu.VMEM((ranks, size, cols), jnp.float32),
-            pltpu.VMEM((ranks, block, cols), jnp.int32),
-            pltpu.SemaphoreType.DMA((ranks,)),
-            pltpu.SemaphoreType.DMA((ranks * (held + 1),)),
-            pltpu.SemaphoreType.DMA((ranks,)),
+            pltpu.VMEM((len(order), size, cols), jnp.float32),
+            pltpu.VMEM((len(order), block, cols), jnp.int32),
+            pltpu.SemaphoreType.DMA((len(order),)),
+            pltpu.SemaphoreType.DMA((len(order) * (held + 1),)),
+            pltpu.SemaphoreType.DMA((len(order),)),
         ],
         compiler_params=pltpu.CompilerParams(vmem_limit_bytes=VMEM_LIMIT if layer else MOST_VMEM),
         cost_estimate=pl.CostEstimate(flops=0, bytes_accessed=0, transcendentals=0),
@@ -578,13 +576,16 @@
     def send_all(parts):
         return [send(part, pair(q, ranks)) for q, part in enumerate(parts)]
 
-    messages = pack(concentration, stiff_mask, 0, ranks, ())
+    far, near = list(range(1, ranks - 1)), list(range(1, ranks))[-1:] + [0]
+    parts = [pack(concentration, stiff_mask, 0, ranks, part, ()) for part in (far, near) if part]
+    messages = [message for _, message in sorted(zip(far + near, sum(parts, [])), key=lambda x: x[0])]
     arrived = [send_all(messages)]
     if layers > 1:
         edges = plane_edges(concentration, face_rate, face_flag, messages[:1])
         sides = (paired(edges, 0), paired(edges, 1))
     for layer in range(1, layers):
-        messages = pack(concentration, stiff_mask, layer, ranks, sides)
+        order = list(range(ranks))
+        messages = pack(concentration, stiff_mask, layer, ranks, order, sides)
         messages, arrived[-1] = lax.optimization_barrier((messages, arrived[-1]))
         arrived.append(send_all(messages))
 

time: 104 us -> 104 us (level)
  Pallas kernels: 28.8 us -> 30.4 us
  waiting for transfers between devices: 37.7 us -> 36.6 us
    pallas_call x2 -> x3, Pallas kernels: 4.4 us -> 5.96 us  [pack(): pl.pallas_call(functools.partial(pack_kernel, layer, ranks, order), out_s...]
    ppermute x12, waiting for transfers between devices: 32.5 us -> 31.4 us  [send(): lax.ppermute(value, 'comp', [(i, i ^ by) for i in range(ranks)])]
    unnamed x28 -> x26, local copies, waits for them, and re-layouts: 3.24 us -> 2.32 us
  transfers between devices with their start and end apart: 20 -> 20, of which waited for: 8 -> 8; matrix products, arithmetic and copies ran while one was open for 3% -> 3% of each run, Pallas kernels for 25% -> 27%
where the time goes in v12:
time: 104 us; the launch traced here: 103 us
  waiting for transfers between devices  36.6 us (35%)
  Pallas kernels  30.4 us (29%)
  starting transfers between devices  30.3 us (29%)
  local copies, waits for them, and re-layouts  5.59 us (5%)
    ppermute x12, waiting for transfers between devices, send(): lax.ppermute(value, 'comp', [(i, i ^ by) for i in range(ranks)])  31.4 us
    pallas_call x4, Pallas kernels, layer_step(): pl.pallas_call(functools.partial(step_kernel, pieces, layer, stiff is Non...  23.1 us
    ppermute x8, starting transfers between devices, paired(): lax.ppermute(value, 'space', [(i, i + 1) for i in low] + [(i + 1, i) for...  15.7 us
    ppermute x12, starting transfers between devices, send(): lax.ppermute(value, 'comp', [(i, i ^ by) for i in range(ranks)])  14.6 us
    pallas_call x3, Pallas kernels, pack(): pl.pallas_call(functools.partial(pack_kernel, layer, ranks, order), out_s...  5.96 us
    ppermute x8, waiting for transfers between devices, paired(): lax.ppermute(value, 'space', [(i, i + 1) for i in low] + [(i + 1, i) for...  5.28 us
    dynamic_update_slice x8, local copies, waits for them, and re-layouts, by_layers(): lax.dynamic_update_slice(result, piece.reshape(held, 1, rows, cols), (0,...  3.02 us
    unnamed x26, local copies, waits for them, and re-layouts  2.32 us
  transfers between devices with their start and end apart: 20, of which 8 were waited for; matrix products, arithmetic and copies ran while one was open for 3% of the time, Pallas kernels for 27%

profile of v12, /device:TPU:13, one launch (start us, length us, event | category | flops | bytes accessed | tf_op | source)
XLA Modules:
  0.0 103.3 jit_solution(8078009978156448807)
XLA Ops:
  0.0 2.1 %pack.5 = (f32[136,512]{1,0:T(8,128)}, f32[136,512]{1,0:T(8,128)}) custom-call(f32[32,32,512]{2,1,0:T(8,128)} %plane_ref.5, s32[8,8,512]{2,1,0:T(8,128)} %mask_ref.5), custom_call_target="tpu_custom_call" | custom-call | tf_op jit(solution)/shard_map/pack/pallas_call | solution.py:243
  2.1 1.4 %collective-permute-start.2 = (f32[136,512]{1,0:T(8,128)}, f32[136,512]{1,0:T(8,128)S(1)}, u32[]{:S(2)}, u32[]{:S(2)}) collective-permute-start(f32[136,512]{1,0:T(8,128)} %get-tuple-element.49), channel_id=1, source_target_pairs={{0,12},{4,8},{8,4},{12,0},{1,13},{5,9},{9,5},{13,1},{2,14},{6,10},... | collective-permute-start | bytes 835592 | tf_op jit(solution)/shard_map/ppermute | solution.py:574
  4.5 1.9 %pack.3 = (f32[136,512]{1,0:T(8,128)}, f32[136,512]{1,0:T(8,128)}) custom-call(f32[32,32,512]{2,1,0:T(8,128)} %plane_ref.5, s32[8,8,512]{2,1,0:T(8,128)} %mask_ref.5), custom_call_target="tpu_custom_call" | custom-call | tf_op jit(solution)/shard_map/pack/pallas_call | solution.py:243
  10.3 3.0 %collective-permute-start.1 = (f32[32,128]{1,0:T(8,128)S(1)}, f32[32,128]{1,0:T(8,128)S(1)}, u32[]{:S(2)}, u32[]{:S(2)}) collective-permute-start(f32[32,128]{1,0:T(8,128)S(1)} %plane_edges.1), channel_id=1, source_target_pairs={{1,2},{2,1},{5,6},{6,5},{9,10},{10,9},{13,14},{14,13},{17,18},{18,... | collective-permute-start | bytes 49160 | tf_op jit(solution)/shard_map/ppermute | solution.py:164
  13.3 2.3 %collective-permute-done.1.refs_1_.refs_5_ = f32[32,128]{1,0:T(8,128)S(1)} collective-permute-done((f32[32,128]{1,0:T(8,128)S(1)}, f32[32,128]{1,0:T(8,128)S(1)}, u32[]{:S(2)}, u32[]{:S(2)}) %collective-permute-start.1) | collective-permute-done | bytes 16416 | tf_op jit(solution)/shard_map/ppermute | solution.py:164
  15.6 2.0 %pack.4 = (f32[144,512]{1,0:T(8,128)S(1)}, f32[144,512]{1,0:T(8,128)S(1)}, f32[144,512]{1,0:T(8,128)S(1)}, f32[144,512]{1,0:T(8,128)S(1)}) custom-call(f32[32,32,512]{2,1,0:T(8,128)S(1)} %copy-done, s32[8,8,512]{2,1,0:T(8,128)S(1)} %copy-done.5, f32[32,128]{1,0:T(8,128)S(1)} %collective-permute-done.refs_0_.refs_4_, ...), custom_call_target="tpu_custom_call" | custom-call | tf_op jit(solution)/shard_map/pack/pallas_call | solution.py:243
  17.7 4.4 %collective-permute-done.2.refs_1_.refs_5_ = f32[136,512]{1,0:T(8,128)S(1)} collective-permute-done((f32[136,512]{1,0:T(8,128)}, f32[136,512]{1,0:T(8,128)S(1)}, u32[]{:S(2)}, u32[]{:S(2)}) %collective-permute-start.2) | collective-permute-done | bytes 278560 | tf_op jit(solution)/shard_map/ppermute | solution.py:574
  22.0 5.0 %collective-permute-done.3.refs_2_.refs_6_ = f32[136,512]{1,0:T(8,128)S(1)} collective-permute-done((f32[136,512]{1,0:T(8,128)}, f32[136,512]{1,0:T(8,128)S(1)}, u32[]{:S(2)}, u32[]{:S(2)}) %collective-permute-start.3) | collective-permute-done | bytes 278560 | tf_op jit(solution)/shard_map/ppermute | solution.py:574
  27.6 1.7 %collective-permute-start.5 = (f32[32,128]{1,0:T(8,128)S(1)}, f32[32,128]{1,0:T(8,128)S(1)}, u32[]{:S(2)}, u32[]{:S(2)}) collective-permute-start(f32[32,128]{1,0:T(8,128)S(1)} %edges.1), channel_id=1, source_target_pairs={{0,1},{2,3},{1,0},{3,2},{4,5},{6,7},{5,4},{7,6},{8,9},{10,11},{9,8... | collective-permute-start | bytes 49160 | tf_op jit(solution)/shard_map/ppermute | solution.py:164
  29.3 3.0 %collective-permute-start.6 = (f32[32,128]{1,0:T(8,128)S(1)}, f32[32,128]{1,0:T(8,128)S(1)}, u32[]{:S(2)}, u32[]{:S(2)}) collective-permute-start(f32[32,128]{1,0:T(8,128)S(1)} %edges.1), channel_id=1, source_target_pairs={{1,2},{2,1},{5,6},{6,5},{9,10},{10,9},{13,14},{14,13},{17,18},{18,... | collective-permute-start | bytes 49160 | tf_op jit(solution)/shard_map/ppermute | solution.py:164
  32.3 4.0 %collective-permute-start.13 = (f32[144,512]{1,0:T(8,128)S(1)}, f32[144,512]{1,0:T(8,128)S(1)}, u32[]{:S(2)}, u32[]{:S(2)}) collective-permute-start(f32[144,512]{1,0:T(8,128)S(1)} %get-tuple-element.71), channel_id=1, source_target_pairs={{0,8},{4,12},{8,0},{12,4},{1,9},{5,13},{9,1},{13,5},{2,10},{6,14},... | collective-permute-start | bytes 884744 | tf_op jit(solution)/shard_map/ppermute | solution.py:574
  37.5 5.7 %layer_step.4 = (f32[128,512]{1,0:T(8,128)S(1)}, f32[128,512]{1,0:T(8,128)S(1)}, f32[128,512]{1,0:T(8,128)S(1)}, f32[128,512]{1,0:T(8,128)S(1)}, f32[32,128]{1,0:T(8,128)S(1)}, /*index=5*/f32[32,512]{1,0:T(8,128)S(1)}) custom-call(f32[16]{0:T(128)S(1)} %copy-done.6, f32[16]{0:T(128)S(1)} %copy-done.7, f32[136,512]{1,0:T(8,128)S(1)} %copy-done.4, ...), custom_call_target="tpu_custom_call" | custom-call | tf_op jit(solution)/shard_map/layer_step/pallas_call | solution.py:540
  43.3 3.0 %collective-permute-start.8 = (f32[32,128]{1,0:T(8,128)S(1)}, f32[32,128]{1,0:T(8,128)S(1)}, u32[]{:S(2)}, u32[]{:S(2)}) collective-permute-start(f32[32,128]{1,0:T(8,128)S(1)} %get-tuple-element.64), channel_id=1, source_target_pairs={{1,2},{2,1},{5,6},{6,5},{9,10},{10,9},{13,14},{14,13},{17,18},{18,... | collective-permute-start | bytes 49160 | tf_op jit(solution)/shard_map/ppermute | solution.py:164
  46.3 2.3 %collective-permute-done.8.refs_5_ = f32[32,128]{1,0:T(8,128)S(1)} collective-permute-done((f32[32,128]{1,0:T(8,128)S(1)}, f32[32,128]{1,0:T(8,128)S(1)}, u32[]{:S(2)}, u32[]{:S(2)}) %collective-permute-start.8) | collective-permute-done | bytes 16416 | tf_op jit(solution)/shard_map/ppermute | solution.py:164
  48.6 5.8 %layer_step.5 = (f32[128,512]{1,0:T(8,128)S(1)}, f32[128,512]{1,0:T(8,128)S(1)}, f32[128,512]{1,0:T(8,128)S(1)}, f32[128,512]{1,0:T(8,128)S(1)}) custom-call(f32[16]{0:T(128)S(1)} %copy-done.6, f32[16]{0:T(128)S(1)} %copy-done.7, f32[128,512]{1,0:T(8,128)S(1)} %get-tuple-element.60.refs_0_, f32[128,512]{1,0:T(8,128)S(1)} %get-tuple-element.61.refs_1_, ...), custom_call_target="tpu_custom_call" | custom-call | tf_op jit(solution)/shard_map/layer_step/pallas_call | solution.py:540
  55.5 1.3 %collective-permute-start.10 = (f32[128,512]{1,0:T(8,128)S(1)}, f32[128,512]{1,0:T(8,128)}, u32[]{:S(2)}, u32[]{:S(2)}) collective-permute-start(f32[128,512]{1,0:T(8,128)S(1)} %get-tuple-element.67), channel_id=1, source_target_pairs={{0,8},{4,12},{8,0},{12,4},{1,9},{5,13},{9,1},{13,5},{2,10},{6,14},... | collective-permute-start | bytes 786440 | tf_op jit(solution)/shard_map/ppermute | solution.py:574
  57.2 5.7 %layer_step.6 = (f32[128,512]{1,0:T(8,128)S(1)}, f32[128,512]{1,0:T(8,128)S(1)}, f32[128,512]{1,0:T(8,128)S(1)}, f32[128,512]{1,0:T(8,128)S(1)}, f32[32,128]{1,0:T(8,128)S(1)}, /*index=5*/f32[32,512]{1,0:T(8,128)S(1)}) custom-call(f32[16]{0:T(128)S(1)} %copy-done.6, f32[16]{0:T(128)S(1)} %copy-done.7, f32[144,512]{1,0:T(8,128)S(1)} %get-tuple-element.56.refs_10_.refs_0_, ...), custom_call_target="tpu_custom_call" | custom-call | tf_op jit(solution)/shard_map/layer_step/pallas_call | solution.py:540
  63.0 3.6 %collective-permute-start.16 = (f32[32,128]{1,0:T(8,128)S(1)}, f32[32,128]{1,0:T(8,128)S(1)}, u32[]{:S(2)}, u32[]{:S(2)}) collective-permute-start(f32[32,128]{1,0:T(8,128)S(1)} %get-tuple-element.77), channel_id=1, source_target_pairs={{1,2},{2,1},{5,6},{6,5},{9,10},{10,9},{13,14},{14,13},{17,18},{18,... | collective-permute-start | bytes 49160 | tf_op jit(solution)/shard_map/ppermute | solution.py:164
  68.4 5.8 %layer_step.7 = (f32[128,512]{1,0:T(8,128)S(1)}, f32[128,512]{1,0:T(8,128)S(1)}, f32[128,512]{1,0:T(8,128)S(1)}, f32[128,512]{1,0:T(8,128)S(1)}) custom-call(f32[16]{0:T(128)S(1)} %copy-done.6, f32[16]{0:T(128)S(1)} %copy-done.7, f32[128,512]{1,0:T(8,128)S(1)} %get-tuple-element.73.refs_0_, f32[128,512]{1,0:T(8,128)S(1)} %get-tuple-element.74.refs_1_, ...), custom_call_target="tpu_custom_call" | custom-call | tf_op jit(solution)/shard_map/layer_step/pallas_call | solution.py:540
  74.3 1.8 %collective-permute-start.17 = (f32[128,512]{1,0:T(8,128)S(1)}, f32[128,512]{1,0:T(8,128)S(1)}, u32[]{:S(2)}, u32[]{:S(2)}) collective-permute-start(f32[128,512]{1,0:T(8,128)S(1)} %get-tuple-element.79), channel_id=1, source_target_pairs={{0,4},{4,0},{8,12},{12,8},{1,5},{5,1},{9,13},{13,9},{2,6},{6,2},{1... | collective-permute-start | bytes 786440 | tf_op jit(solution)/shard_map/ppermute | solution.py:574
  79.9 4.2 %collective-permute-done.17 = f32[128,512]{1,0:T(8,128)S(1)} collective-permute-done((f32[128,512]{1,0:T(8,128)S(1)}, f32[128,512]{1,0:T(8,128)S(1)}, u32[]{:S(2)}, u32[]{:S(2)}) %collective-permute-start.17) | collective-permute-done | bytes 262176 | tf_op jit(solution)/shard_map/ppermute | solution.py:574
  84.1 11.5 %collective-permute-done.18 = f32[128,512]{1,0:T(8,128)S(1)} collective-permute-done((f32[128,512]{1,0:T(8,128)S(1)}, f32[128,512]{1,0:T(8,128)S(1)}, u32[]{:S(2)}, u32[]{:S(2)}) %collective-permute-start.18) | collective-permute-done | bytes 262176 | tf_op jit(solution)/shard_map/ppermute | solution.py:574
  95.7 6.3 %collective-permute-done.19 = f32[128,512]{1,0:T(8,128)S(1)} collective-permute-done((f32[128,512]{1,0:T(8,128)S(1)}, f32[128,512]{1,0:T(8,128)S(1)}, u32[]{:S(2)}, u32[]{:S(2)}) %collective-permute-start.19) | collective-permute-done | bytes 262176 | tf_op jit(solution)/shard_map/ppermute | solution.py:574
  102.0 1.3 %copy-done.12 = f32[4,8,32,512]{3,2,1,0:T(8,128)} copy-done((f32[4,8,32,512]{3,2,1,0:T(8,128)}, f32[4,8,32,512]{3,2,1,0:T(8,128)S(1)}, u32[]{:S(2)}) %copy-start.12) | copy-done | bytes 2097176
  (61 shorter events, 13.9 us)
Async XLA Ops:
  2.1 19.9 %collective-permute-start.2 = (f32[136,512]{1,0:T(8,128)}, f32[136,512]{1,0:T(8,128)S(1)}, u32[]{:S(2)}, u32[]{:S(2)}) collective-permute-start(f32[136,512]{1,0:T(8,128)} %get-tuple-element.49), channel_id=1, source_target_pairs={{0,12},{4,8},{8,4},{12,0},{1,13},{5,9},{9,5},{13,1},{2,14},{6,10},... | collective-permute-start | bytes 835592 | tf_op jit(solution)/shard_map/ppermute | solution.py:574
  3.5 23.5 %collective-permute-start.3 = (f32[136,512]{1,0:T(8,128)}, f32[136,512]{1,0:T(8,128)S(1)}, u32[]{:S(2)}, u32[]{:S(2)}) collective-permute-start(f32[136,512]{1,0:T(8,128)} %get-tuple-element.50), channel_id=1, source_target_pairs={{0,8},{4,12},{8,0},{12,4},{1,9},{5,13},{9,1},{13,5},{2,10},{6,14},... | collective-permute-start | bytes 835592 | tf_op jit(solution)/shard_map/ppermute | solution.py:574
  6.5 20.5 %collective-permute-start.4 = (f32[136,512]{1,0:T(8,128)}, f32[136,512]{1,0:T(8,128)S(1)}, u32[]{:S(2)}, u32[]{:S(2)}) collective-permute-start(f32[136,512]{1,0:T(8,128)} %get-tuple-element.51), channel_id=1, source_target_pairs={{0,4},{4,0},{8,12},{12,8},{1,5},{5,1},{9,13},{13,9},{2,6},{6,2},{1... | collective-permute-start | bytes 835592 | tf_op jit(solution)/shard_map/ppermute | solution.py:574
  8.9 27.6 %copy-start.8 = (f32[16,16]{1,0:T(8,128)S(1)}, f32[16,16]{1,0:T(8,128)}, u32[]{:S(2)}) copy-start(f32[16,16]{1,0:T(8,128)} %mixing_ref.1) | copy-start | bytes 3076
  9.0 27.6 %copy-start.9 = (f32[16,16]{1,0:T(8,128)S(1)}, f32[16,16]{1,0:T(8,128)}, u32[]{:S(2)}) copy-start(f32[16,16]{1,0:T(8,128)} %inverse_ref.1) | copy-start | bytes 3076
  9.0 27.6 %copy-start.10 = (f32[16]{0:T(128)S(1)}, f32[16]{0:T(128)}, u32[]{:S(2)}) copy-start(f32[16]{0:T(128)} %param.17) | copy-start | bytes 196
  9.0 27.6 %copy-start.11 = (f32[16]{0:T(128)S(1)}, f32[16]{0:T(128)}, u32[]{:S(2)}) copy-start(f32[16]{0:T(128)} %param.18) | copy-start | bytes 196
  9.0 4.3 %collective-permute-start = (f32[32,128]{1,0:T(8,128)S(1)}, f32[32,128]{1,0:T(8,128)S(1)}, u32[]{:S(2)}, u32[]{:S(2)}) collective-permute-start(f32[32,128]{1,0:T(8,128)S(1)} %plane_edges.1), channel_id=1, source_target_pairs={{0,1},{2,3},{1,0},{3,2},{4,5},{6,7},{5,4},{7,6},{8,9},{10,11},{9,8... | collective-permute-start | bytes 49160 | tf_op jit(solution)/shard_map/ppermute | solution.py:164
  10.3 5.3 %collective-permute-start.1 = (f32[32,128]{1,0:T(8,128)S(1)}, f32[32,128]{1,0:T(8,128)S(1)}, u32[]{:S(2)}, u32[]{:S(2)}) collective-permute-start(f32[32,128]{1,0:T(8,128)S(1)} %plane_edges.1), channel_id=1, source_target_pairs={{1,2},{2,1},{5,6},{6,5},{9,10},{10,9},{13,14},{14,13},{17,18},{18,... | collective-permute-start | bytes 49160 | tf_op jit(solution)/shard_map/ppermute | solution.py:164
  27.0 29.8 %collective-permute-start.12 = (f32[144,512]{1,0:T(8,128)S(1)}, f32[144,512]{1,0:T(8,128)S(1)}, u32[]{:S(2)}, u32[]{:S(2)}) collective-permute-start(f32[144,512]{1,0:T(8,128)S(1)} %get-tuple-element.70), channel_id=1, source_target_pairs={{0,12},{4,8},{8,4},{12,0},{1,13},{5,9},{9,5},{13,1},{2,14},{6,10},... | collective-permute-start | bytes 884744 | tf_op jit(solution)/shard_map/ppermute | solution.py:574
  27.6 9.8 %collective-permute-start.5 = (f32[32,128]{1,0:T(8,128)S(1)}, f32[32,128]{1,0:T(8,128)S(1)}, u32[]{:S(2)}, u32[]{:S(2)}) collective-permute-start(f32[32,128]{1,0:T(8,128)S(1)} %edges.1), channel_id=1, source_target_pairs={{0,1},{2,3},{1,0},{3,2},{4,5},{6,7},{5,4},{7,6},{8,9},{10,11},{9,8... | collective-permute-start | bytes 49160 | tf_op jit(solution)/shard_map/ppermute | solution.py:164
  29.3 8.1 %collective-permute-start.6 = (f32[32,128]{1,0:T(8,128)S(1)}, f32[32,128]{1,0:T(8,128)S(1)}, u32[]{:S(2)}, u32[]{:S(2)}) collective-permute-start(f32[32,128]{1,0:T(8,128)S(1)} %edges.1), channel_id=1, source_target_pairs={{1,2},{2,1},{5,6},{6,5},{9,10},{10,9},{13,14},{14,13},{17,18},{18,... | collective-permute-start | bytes 49160 | tf_op jit(solution)/shard_map/ppermute | solution.py:164
  32.3 24.9 %collective-permute-start.13 = (f32[144,512]{1,0:T(8,128)S(1)}, f32[144,512]{1,0:T(8,128)S(1)}, u32[]{:S(2)}, u32[]{:S(2)}) collective-permute-start(f32[144,512]{1,0:T(8,128)S(1)} %get-tuple-element.71), channel_id=1, source_target_pairs={{0,8},{4,12},{8,0},{12,4},{1,9},{5,13},{9,1},{13,5},{2,10},{6,14},... | collective-permute-start | bytes 884744 | tf_op jit(solution)/shard_map/ppermute | solution.py:574
  36.3 20.9 %collective-permute-start.14 = (f32[144,512]{1,0:T(8,128)S(1)}, f32[144,512]{1,0:T(8,128)S(1)}, u32[]{:S(2)}, u32[]{:S(2)}) collective-permute-start(f32[144,512]{1,0:T(8,128)S(1)} %get-tuple-element.72), channel_id=1, source_target_pairs={{0,4},{4,0},{8,12},{12,8},{1,5},{5,1},{9,13},{13,9},{2,6},{6,2},{1... | collective-permute-start | bytes 884744 | tf_op jit(solution)/shard_map/ppermute | solution.py:574
  43.2 3.1 %collective-permute-start.7 = (f32[32,128]{1,0:T(8,128)S(1)}, f32[32,128]{1,0:T(8,128)S(1)}, u32[]{:S(2)}, u32[]{:S(2)}) collective-permute-start(f32[32,128]{1,0:T(8,128)S(1)} %get-tuple-element.64), channel_id=1, source_target_pairs={{0,1},{2,3},{1,0},{3,2},{4,5},{6,7},{5,4},{7,6},{8,9},{10,11},{9,8... | collective-permute-start | bytes 49160 | tf_op jit(solution)/shard_map/ppermute | solution.py:164
  43.3 5.4 %collective-permute-start.8 = (f32[32,128]{1,0:T(8,128)S(1)}, f32[32,128]{1,0:T(8,128)S(1)}, u32[]{:S(2)}, u32[]{:S(2)}) collective-permute-start(f32[32,128]{1,0:T(8,128)S(1)} %get-tuple-element.64), channel_id=1, source_target_pairs={{1,2},{2,1},{5,6},{6,5},{9,10},{10,9},{13,14},{14,13},{17,18},{18,... | collective-permute-start | bytes 49160 | tf_op jit(solution)/shard_map/ppermute | solution.py:164
  54.4 12.1 %collective-permute-start.9 = (f32[128,512]{1,0:T(8,128)S(1)}, f32[128,512]{1,0:T(8,128)}, u32[]{:S(2)}, u32[]{:S(2)}) collective-permute-start(f32[128,512]{1,0:T(8,128)S(1)} %get-tuple-element.66), channel_id=1, source_target_pairs={{0,4},{4,0},{8,12},{12,8},{1,5},{5,1},{9,13},{13,9},{2,6},{6,2},{1... | collective-permute-start | bytes 786440 | tf_op jit(solution)/shard_map/ppermute | solution.py:574
  55.5 20.6 %collective-permute-start.10 = (f32[128,512]{1,0:T(8,128)S(1)}, f32[128,512]{1,0:T(8,128)}, u32[]{:S(2)}, u32[]{:S(2)}) collective-permute-start(f32[128,512]{1,0:T(8,128)S(1)} %get-tuple-element.67), channel_id=1, source_target_pairs={{0,8},{4,12},{8,0},{12,4},{1,9},{5,13},{9,1},{13,5},{2,10},{6,14},... | collective-permute-start | bytes 786440 | tf_op jit(solution)/shard_map/ppermute | solution.py:574
  56.8 21.4 %collective-permute-start.11 = (f32[128,512]{1,0:T(8,128)S(1)}, f32[128,512]{1,0:T(8,128)}, u32[]{:S(2)}, u32[]{:S(2)}) collective-permute-start(f32[128,512]{1,0:T(8,128)S(1)} %get-tuple-element.68), channel_id=1, source_target_pairs={{0,12},{4,8},{8,4},{12,0},{1,13},{5,9},{9,5},{13,1},{2,14},{6,10},... | collective-permute-start | bytes 786440 | tf_op jit(solution)/shard_map/ppermute | solution.py:574
  62.9 4.9 %collective-permute-start.15 = (f32[32,128]{1,0:T(8,128)S(1)}, f32[32,128]{1,0:T(8,128)S(1)}, u32[]{:S(2)}, u32[]{:S(2)}) collective-permute-start(f32[32,128]{1,0:T(8,128)S(1)} %get-tuple-element.77), channel_id=1, source_target_pairs={{0,1},{2,3},{1,0},{3,2},{4,5},{6,7},{5,4},{7,6},{8,9},{10,11},{9,8... | collective-permute-start | bytes 49160 | tf_op jit(solution)/shard_map/ppermute | solution.py:164
  63.0 5.5 %collective-permute-start.16 = (f32[32,128]{1,0:T(8,128)S(1)}, f32[32,128]{1,0:T(8,128)S(1)}, u32[]{:S(2)}, u32[]{:S(2)}) collective-permute-start(f32[32,128]{1,0:T(8,128)S(1)} %get-tuple-element.77), channel_id=1, source_target_pairs={{1,2},{2,1},{5,6},{6,5},{9,10},{10,9},{13,14},{14,13},{17,18},{18,... | collective-permute-start | bytes 49160 | tf_op jit(solution)/shard_map/ppermute | solution.py:164
  74.3 9.9 %collective-permute-start.17 = (f32[128,512]{1,0:T(8,128)S(1)}, f32[128,512]{1,0:T(8,128)S(1)}, u32[]{:S(2)}, u32[]{:S(2)}) collective-permute-start(f32[128,512]{1,0:T(8,128)S(1)} %get-tuple-element.79), channel_id=1, source_target_pairs={{0,4},{4,0},{8,12},{12,8},{1,5},{5,1},{9,13},{13,9},{2,6},{6,2},{1... | collective-permute-start | bytes 786440 | tf_op jit(solution)/shard_map/ppermute | solution.py:574
  77.0 18.6 %collective-permute-start.18 = (f32[128,512]{1,0:T(8,128)S(1)}, f32[128,512]{1,0:T(8,128)S(1)}, u32[]{:S(2)}, u32[]{:S(2)}) collective-permute-start(f32[128,512]{1,0:T(8,128)S(1)} %get-tuple-element.80), channel_id=1, source_target_pairs={{0,8},{4,12},{8,0},{12,4},{1,9},{5,13},{9,1},{13,5},{2,10},{6,14},... | collective-permute-start | bytes 786440 | tf_op jit(solution)/shard_map/ppermute | solution.py:574
  79.2 22.7 %collective-permute-start.19 = (f32[128,512]{1,0:T(8,128)S(1)}, f32[128,512]{1,0:T(8,128)S(1)}, u32[]{:S(2)}, u32[]{:S(2)}) collective-permute-start(f32[128,512]{1,0:T(8,128)S(1)} %get-tuple-element.81), channel_id=1, source_target_pairs={{0,12},{4,8},{8,4},{12,0},{1,13},{5,9},{9,5},{13,1},{2,14},{6,10},... | collective-permute-start | bytes 786440 | tf_op jit(solution)/shard_map/ppermute | solution.py:574
  (9 other events, 91.6 us)
